TPU v7x, 32 devices: a whole 2x2x4 slice. The times are simulated.
32 devices in a mesh: dp: 16 (over z, y, x), head: 2 (over core).
Axes of the slice: x: 2, y: 2, z: 4, core: 2. Of those that a mesh axis runs over, the one named last changes fastest.
Arguments:
- tokens: bfloat16 [24576, 768], P('dp')
- cotangent: bfloat16 [24576, 768], P('dp'), may hold values from -6 to 6
- item_units: int32 [16, 2], P('dp'), may hold values from 1 to 23, as said below
- counted: int32 [24576], P('dp'), may hold values 0 or 1
- inputs_weight: float32 [3, 768, 768], P(None, 'dp', 'head'), may hold values from -0.21875 to 0.21875
- inputs_moment: float32 [3, 768, 768], P(None, 'dp', 'head'), may hold values from -0.00024414062 to 0.00024414062
- inputs_square: float32 [3, 768, 768], P(None, 'dp', 'head'), may hold values from 1.4391535e-09 to 2.2998236e-08
- mixing_weight: float32 [768, 768], P('head', 'dp'), may hold values from -0.21875 to 0.21875
- mixing_moment: float32 [768, 768], P('head', 'dp'), may hold values from -0.00024414062 to 0.00024414062
- mixing_square: float32 [768, 768], P('head', 'dp'), may hold values from 1.4391535e-09 to 2.2998236e-08
- expand_weight: float32 [768, 3072], P('dp', 'head'), may hold values from -0.21875 to 0.21875
- expand_moment: float32 [768, 3072], P('dp', 'head'), may hold values from -0.00024414062 to 0.00024414062
- expand_square: float32 [768, 3072], P('dp', 'head'), may hold values from 1.4391535e-09 to 2.2998236e-08
- reduce_weight: float32 [3072, 768], P('head', 'dp'), may hold values from -0.15625 to 0.15625
- reduce_moment: float32 [3072, 768], P('head', 'dp'), may hold values from -0.00024414062 to 0.00024414062
- reduce_square: float32 [3072, 768], P('head', 'dp'), may hold values from 1.4391535e-09 to 2.2998236e-08
- biases_weight: float32 [2, 2304], P('head', 'dp'), may hold values from -1.75 to 1.75
- biases_moment: float32 [2, 2304], P('head', 'dp'), may hold values from -0.00061035156 to 0.00061035156
- biases_square: float32 [2, 2304], P('head', 'dp'), may hold values from 1.41093475e-08 to 5.643739e-08
- shared_weight: float32 [6, 768], P(None, 'dp')
- shared_moment: float32 [6, 768], P(None, 'dp'), may hold values from -0.00061035156 to 0.00061035156
- shared_square: float32 [6, 768], P(None, 'dp'), may hold values from 1.41093475e-08 to 5.643739e-08
- kernel_weight: float32 [12, 33], P('head'), may hold values from -1 to 1
- kernel_moment: float32 [12, 33], P('head'), may hold values from -0.0012207031 to 0.0012207031
- kernel_square: float32 [12, 33], P('head'), may hold values from 3.5978836e-08 to 5.756614e-07
Outputs:
- output: float32 [24576, 768], P('dp')
- input_grad: float32 [24576, 768], P('dp')
- inputs_master: float32 [3, 768, 768], P(None, 'dp', 'head')
- inputs_momentum: float32 [3, 768, 768], P(None, 'dp', 'head')
- inputs_variance: float32 [3, 768, 768], P(None, 'dp', 'head')
- mixing_master: float32 [768, 768], P('head', 'dp')
- mixing_momentum: float32 [768, 768], P('head', 'dp')
- mixing_variance: float32 [768, 768], P('head', 'dp')
- expand_master: float32 [768, 3072], P('dp', 'head')
- expand_momentum: float32 [768, 3072], P('dp', 'head')
- expand_variance: float32 [768, 3072], P('dp', 'head')
- reduce_master: float32 [3072, 768], P('head', 'dp')
- reduce_momentum: float32 [3072, 768], P('head', 'dp')
- reduce_variance: float32 [3072, 768], P('head', 'dp')
- biases_master: float32 [2, 2304], P('head', 'dp')
- biases_momentum: float32 [2, 2304], P('head', 'dp')
- biases_variance: float32 [2, 2304], P('head', 'dp')
- shared_master: float32 [6, 768], P(None, 'dp')
- shared_momentum: float32 [6, 768], P(None, 'dp')
- shared_variance: float32 [6, 768], P(None, 'dp')
- kernel_master: float32 [12, 33], P('head')
- kernel_momentum: float32 [12, 33], P('head')
- kernel_variance: float32 [12, 33], P('head')
- grad_norm: float32 [], replicated
- sublayer_rms: float32 [2], replicated
Inputs may be any that keep to these rules, and one draw needn't show every extreme that they name: `item_units`: each row holds the lengths of one buffer's two items in blocks of 64 tokens; their sum is at most 24, and some buffer is filled to exactly that.
All inputs are finite; a program needn't handle non-finite values. No bound on the sum of `counted` on one device may be relied on, other than what follows from the above.
Results may differ from a plain program's by a relative error of at most 0.023.
Values may be sent and summed in bfloat16 or wider, within the bound.
No kernel may reach another device: no remote copies, remote signals or barrier semaphores. Data moves between devices by JAX's collectives and lax.ppermute only.
A program may use at most 320 MiB of HBM per device.

v0:
```python
import jax
import jax.numpy as jnp
from jax import lax
from jax.sharding import PartitionSpec as P

HEAD_DIM = 64
LANDMARKS = 64
PINV_STEPS = 6


PRECISE = lax.Precision.HIGHEST
NORM_EPS = 1e-05
CLIP_NORM = 1.0
CLIP_EPS = 1e-06
BETA_ONE = 0.9
BETA_TWO = 0.98
ADAM_EPS = 1e-08
RATE_MATRIX = 0.04
RATE_VECTOR = 0.5
WEIGHT_DECAY = 0.01
CORRECT_ONE = 1.0 - BETA_ONE**5
CORRECT_TWO = 1.0 - BETA_TWO**5


def softmax_rows(scores):
    peak = jnp.max(scores, axis=-1, keepdims=True)
    raised = jnp.exp(scores - peak)
    return raised / jnp.sum(raised, axis=-1, keepdims=True)


def layer_norm(summed_rows, gain_row, shift_row):
    center = summed_rows - jnp.mean(summed_rows, axis=-1, keepdims=True)
    spread = jnp.mean(center * center, axis=-1, keepdims=True)
    return center * lax.rsqrt(spread + NORM_EPS) * gain_row + shift_row


def gelu_tanh(values_in):
    return jax.nn.gelu(values_in, approximate=True)


def row_items(unit_pair, row_count, mark_count):
    position = lax.iota(jnp.int32, row_count)
    first_end = unit_pair[0] * mark_count
    second_end = first_end + unit_pair[1] * mark_count
    return jnp.where(position < first_end, 0, jnp.where(position < second_end, 1, 2)).astype(
        jnp.int32
    )


def landmark_select(unit_pair, row_item, mark_count):
    row_count = row_item.shape[0]
    position = lax.iota(jnp.int32, row_count)
    item_start = jnp.where(row_item == 1, unit_pair[0] * mark_count, 0)
    segment_size = jnp.where(row_item == 1, unit_pair[1], unit_pair[0])
    segment = (position - item_start) // segment_size
    landmark = lax.iota(jnp.int32, 2 * mark_count)
    member = (row_item[None, :] == landmark[:, None] // mark_count) & (
        segment[None, :] == landmark[:, None] % mark_count
    )
    per_item = jnp.where(landmark < mark_count, unit_pair[0], unit_pair[1]).astype(jnp.float32)
    return member.astype(jnp.float32) / per_item[:, None]


def pseudo_inverse(matrix, step_count):
    size_last = matrix.shape[-1]
    identity = jnp.eye(size_last, dtype=matrix.dtype)
    column_peak = jnp.max(jnp.sum(matrix, axis=-2), axis=-1)
    approx = jnp.swapaxes(matrix, -1, -2) / column_peak[..., None, None]
    for _ in range(step_count):
        product = jnp.matmul(matrix, approx, precision=PRECISE)
        inner_term = 7.0 * identity - product
        inner_term = 15.0 * identity - jnp.matmul(product, inner_term, precision=PRECISE)
        inner_term = 13.0 * identity - jnp.matmul(product, inner_term, precision=PRECISE)
        approx = jnp.matmul(0.25 * approx, inner_term, precision=PRECISE)
    return approx


def nystrom(queries, key_rows, value_rows, select, row_item, mark_count, step_count):
    head_count = queries.shape[1]
    head_size = queries.shape[2]
    scaling = head_size ** (-0.25)
    query_scaled = queries * scaling
    key_scaled = key_rows * scaling
    land_query = jnp.einsum("lr,rhe->lhe", select, query_scaled, precision=PRECISE)
    land_key = jnp.einsum("lr,rhe->lhe", select, key_scaled, precision=PRECISE)
    land_item = lax.iota(jnp.int32, 2 * mark_count) // mark_count
    own_item = jnp.minimum(row_item, 1)
    first_scores = jnp.einsum("rhe,lhe->hrl", query_scaled, land_key, precision=PRECISE)
    first_kernel = softmax_rows(
        jnp.where(own_item[None, :, None] == land_item[None, None, :], first_scores, -jnp.inf)
    )
    pair_query = land_query.reshape(2, mark_count, head_count, head_size)
    pair_key = land_key.reshape(2, mark_count, head_count, head_size)
    middle_kernel = softmax_rows(
        jnp.einsum("aihe,ajhe->haij", pair_query, pair_key, precision=PRECISE)
    )
    inverse = pseudo_inverse(middle_kernel, step_count)
    last_scores = jnp.einsum("lhe,rhe->hlr", land_query, key_scaled, precision=PRECISE)
    last_kernel = softmax_rows(
        jnp.where(land_item[None, :, None] == row_item[None, None, :], last_scores, -jnp.inf)
    )
    landmark_values = jnp.einsum(
        "hlr,rhe->hle", last_kernel, value_rows, precision=PRECISE
    ).reshape(head_count, 2, mark_count, head_size)
    weighted = jnp.einsum("haij,haje->haie", inverse, landmark_values, precision=PRECISE).reshape(
        head_count, 2 * mark_count, head_size
    )
    return jnp.einsum("hrl,hle->rhe", first_kernel, weighted, precision=PRECISE)


def depthwise_conv(value_rows, kernel, row_item):
    row_count = value_rows.shape[0]
    tap_count = kernel.shape[1]
    half_width = tap_count // 2
    padded = jnp.pad(value_rows, ((half_width, half_width), (0, 0), (0, 0)))
    padded_item = jnp.pad(row_item, (half_width, half_width), constant_values=-1)
    summed = jnp.zeros_like(value_rows)
    for offset in range(tap_count):
        same_item = (padded_item[offset : offset + row_count] == row_item) & (row_item < 2)
        shifted = jnp.where(same_item[:, None, None], padded[offset : offset + row_count], 0.0)
        summed = summed + shifted * kernel[:, offset][None, :, None]
    return summed


def conv_backward(value_rows, kernel, row_item, grad_out):
    row_count = value_rows.shape[0]
    tap_count = kernel.shape[1]
    half_width = tap_count // 2
    padded = jnp.pad(value_rows, ((half_width, half_width), (0, 0), (0, 0)))
    padded_item = jnp.pad(row_item, (half_width, half_width), constant_values=-1)
    grad_values = jnp.zeros_like(value_rows)
    kernel_terms = []
    for offset in range(tap_count):
        same_item = (padded_item[offset : offset + row_count] == row_item) & (row_item < 2)
        masked_grad = jnp.where(same_item[:, None, None], grad_out, 0.0)
        kernel_terms.append(jnp.sum(masked_grad * padded[offset : offset + row_count], axis=(0, 2)))
        spread_grad = jnp.pad(masked_grad, ((half_width, half_width), (0, 0), (0, 0)))
        start_row = 2 * half_width - offset
        grad_values = (
            grad_values
            + spread_grad[start_row : start_row + row_count] * kernel[:, offset][None, :, None]
        )
    return (grad_values, jnp.stack(kernel_terms, axis=1))


def adamw(master, moment, square, gradient, factor, learn_rate, decay_rate):
    clipped = gradient * factor
    moment_new = BETA_ONE * moment + (1.0 - BETA_ONE) * clipped
    square_new = BETA_TWO * square + (1.0 - BETA_TWO) * clipped * clipped
    step_size = moment_new / CORRECT_ONE / (jnp.sqrt(square_new / CORRECT_TWO) + ADAM_EPS)
    return (master - learn_rate * (step_size + decay_rate * master), moment_new, square_new)


def body(
    tokens,
    cotangent,
    item_units,
    counted,
    inputs_weight,
    inputs_moment,
    inputs_square,
    mixing_weight,
    mixing_moment,
    mixing_square,
    expand_weight,
    expand_moment,
    expand_square,
    reduce_weight,
    reduce_moment,
    reduce_square,
    biases_weight,
    biases_moment,
    biases_square,
    shared_weight,
    shared_moment,
    shared_square,
    kernel_weight,
    kernel_moment,
    kernel_square,
):
    inputs_full, mixing_full, expand_full, reduce_full, biases_full, shared_full = (
        lax.all_gather(inputs_weight.astype(jnp.bfloat16), "dp", axis=1, tiled=True),
        lax.all_gather(mixing_weight.astype(jnp.bfloat16), "dp", axis=1, tiled=True),
        lax.all_gather(expand_weight.astype(jnp.bfloat16), "dp", axis=0, tiled=True),
        lax.all_gather(reduce_weight.astype(jnp.bfloat16), "dp", axis=1, tiled=True),
        lax.all_gather(biases_weight.astype(jnp.bfloat16), "dp", axis=1, tiled=True),
        lax.all_gather(shared_weight.astype(jnp.bfloat16), "dp", axis=1, tiled=True),
    )
    local_width = inputs_full.shape[2]
    local_heads = local_width // HEAD_DIM
    row_count = tokens.shape[0]
    width_full = tokens.shape[1]
    shared_rows = shared_full.astype(jnp.float32)
    biases_row = biases_full[0].astype(jnp.float32)
    query_bias = biases_row[:local_width]
    value_bias = biases_row[local_width : 2 * local_width]
    expand_bias = biases_row[2 * local_width :]
    unit_pair = item_units[0]
    row_item = row_items(unit_pair, row_count, LANDMARKS)
    select = landmark_select(unit_pair, row_item, LANDMARKS)
    inside = (row_item < 2).astype(jnp.float32)
    head_shape = (row_count, local_heads, HEAD_DIM)
    weight_rows = counted.astype(jnp.float32) * inside
    projected = jnp.einsum("rd,cdk->rck", tokens, inputs_full, preferred_element_type=jnp.float32)
    queries = (
        (projected[:, 0] + query_bias).astype(jnp.bfloat16).astype(jnp.float32).reshape(head_shape)
    )
    key_rows = projected[:, 1].astype(jnp.bfloat16).astype(jnp.float32).reshape(head_shape)
    value_rows = (
        (projected[:, 2] + value_bias).astype(jnp.bfloat16).astype(jnp.float32).reshape(head_shape)
    )

    def attend(query_in, key_in, value_in):
        return nystrom(query_in, key_in, value_in, select, row_item, LANDMARKS, PINV_STEPS)

    core_out, core_pull = jax.vjp(attend, queries, key_rows, value_rows)
    mixed = core_out + depthwise_conv(value_rows, kernel_weight, row_item)
    attended = (mixed * inside[:, None, None]).reshape(row_count, local_width).astype(jnp.bfloat16)
    mixing_part = jnp.dot(attended, mixing_full, preferred_element_type=jnp.float32)
    branch_one = lax.psum(mixing_part, "head") + shared_rows[0]
    token_rows = tokens.astype(jnp.float32)
    hidden_one, norm_one_pull = jax.vjp(
        layer_norm, token_rows + branch_one, shared_rows[2], shared_rows[3]
    )
    hidden_low = hidden_one.astype(jnp.bfloat16)
    expanded = jnp.dot(hidden_low, expand_full, preferred_element_type=jnp.float32) + expand_bias
    activated, gelu_pull = jax.vjp(gelu_tanh, expanded)
    activated_low = activated.astype(jnp.bfloat16)
    reduce_part = jnp.dot(activated_low, reduce_full, preferred_element_type=jnp.float32)
    branch_two = lax.psum(reduce_part, "head") + shared_rows[1]
    output_rows, norm_two_pull = jax.vjp(
        layer_norm, hidden_one + branch_two, shared_rows[4], shared_rows[5]
    )
    local_stats = jnp.stack(
        [
            jnp.sum(weight_rows[:, None] * branch_one * branch_one),
            jnp.sum(weight_rows[:, None] * branch_two * branch_two),
            jnp.sum(weight_rows),
        ]
    )
    grad_rows = cotangent.astype(jnp.float32) * weight_rows[:, None]
    d_res_two, d_gain_two, d_shift_two = norm_two_pull(grad_rows)
    d_two_low = d_res_two.astype(jnp.bfloat16)
    reduce_grad = jnp.einsum(
        "rf,rd->fd", activated_low, d_two_low, preferred_element_type=jnp.float32
    )
    d_activated = jnp.einsum(
        "rd,fd->rf", d_two_low, reduce_full, preferred_element_type=jnp.float32
    )
    (d_expanded,) = gelu_pull(d_activated)
    d_expanded_low = d_expanded.astype(jnp.bfloat16)
    expand_grad = jnp.einsum(
        "rd,rf->df", hidden_low, d_expanded_low, preferred_element_type=jnp.float32
    )
    hidden_part = jnp.einsum(
        "rf,df->rd", d_expanded_low, expand_full, preferred_element_type=jnp.float32
    )
    d_hidden = lax.psum(hidden_part, "head") + d_res_two
    d_res_one, d_gain_one, d_shift_one = norm_one_pull(d_hidden)
    shared_grad = jnp.stack(
        [
            jnp.sum(d_res_one, axis=0),
            jnp.sum(d_res_two, axis=0),
            d_gain_one,
            d_shift_one,
            d_gain_two,
            d_shift_two,
        ]
    )
    d_one_low = d_res_one.astype(jnp.bfloat16)
    mixing_grad = jnp.einsum("rk,rd->kd", attended, d_one_low, preferred_element_type=jnp.float32)
    d_attended = (
        jnp.einsum("rd,kd->rk", d_one_low, mixing_full, preferred_element_type=jnp.float32)
        * inside[:, None]
    )
    d_mixed = d_attended.reshape(head_shape)
    d_query, d_key, d_value = core_pull(d_mixed)
    d_value_conv, kernel_grad = conv_backward(value_rows, kernel_weight, row_item, d_mixed)
    projected_grad = (
        jnp.stack([d_query, d_key, d_value + d_value_conv], axis=1)
        .reshape(row_count, 3, local_width)
        .astype(jnp.bfloat16)
    )
    inputs_grad = jnp.einsum(
        "rd,rck->cdk", tokens, projected_grad, preferred_element_type=jnp.float32
    )
    token_part = jnp.einsum(
        "rck,cdk->rd", projected_grad, inputs_full, preferred_element_type=jnp.float32
    )
    input_grad = lax.psum(token_part, "head") + d_res_one
    biases_grad = jnp.concatenate(
        [
            jnp.sum(projected_grad[:, 0], axis=0, dtype=jnp.float32),
            jnp.sum(projected_grad[:, 2], axis=0, dtype=jnp.float32),
            jnp.sum(d_expanded_low, axis=0, dtype=jnp.float32),
        ]
    )[None, :]
    inputs_share, mixing_share, expand_share, reduce_share, biases_share, shared_share = (
        lax.psum_scatter(inputs_grad, "dp", scatter_dimension=1, tiled=True),
        lax.psum_scatter(mixing_grad, "dp", scatter_dimension=1, tiled=True),
        lax.psum_scatter(expand_grad, "dp", scatter_dimension=0, tiled=True),
        lax.psum_scatter(reduce_grad, "dp", scatter_dimension=1, tiled=True),
        lax.psum_scatter(biases_grad, "dp", scatter_dimension=1, tiled=True),
        lax.psum_scatter(shared_grad, "dp", scatter_dimension=1, tiled=True),
    )
    kernel_total = lax.psum(kernel_grad, "dp")
    kernel_squares = jnp.where(lax.axis_index("dp") == 0, jnp.sum(kernel_total * kernel_total), 0.0)
    local_squares = (
        jnp.sum(inputs_share * inputs_share)
        + jnp.sum(mixing_share * mixing_share)
        + jnp.sum(expand_share * expand_share)
        + jnp.sum(reduce_share * reduce_share)
        + jnp.sum(biases_share * biases_share)
    )
    local_squares = (
        local_squares
        + jnp.where(lax.axis_index("head") == 0, jnp.sum(shared_share * shared_share), 0.0)
        + kernel_squares
    )
    squares_total, summed_stats = lax.psum((local_squares, local_stats), ("dp", "head"))
    grad_norm = jnp.sqrt(squares_total)
    factor = CLIP_NORM / (grad_norm + CLIP_EPS)
    inputs_master, inputs_momentum, inputs_variance = adamw(
        inputs_weight, inputs_moment, inputs_square, inputs_share, factor, RATE_MATRIX, WEIGHT_DECAY
    )
    mixing_master, mixing_momentum, mixing_variance = adamw(
        mixing_weight, mixing_moment, mixing_square, mixing_share, factor, RATE_MATRIX, WEIGHT_DECAY
    )
    expand_master, expand_momentum, expand_variance = adamw(
        expand_weight, expand_moment, expand_square, expand_share, factor, RATE_MATRIX, WEIGHT_DECAY
    )
    reduce_master, reduce_momentum, reduce_variance = adamw(
        reduce_weight, reduce_moment, reduce_square, reduce_share, factor, RATE_MATRIX, WEIGHT_DECAY
    )
    biases_master, biases_momentum, biases_variance = adamw(
        biases_weight, biases_moment, biases_square, biases_share, factor, RATE_VECTOR, 0.0
    )
    shared_master, shared_momentum, shared_variance = adamw(
        shared_weight, shared_moment, shared_square, shared_share, factor, RATE_VECTOR, 0.0
    )
    kernel_master, kernel_momentum, kernel_variance = adamw(
        kernel_weight, kernel_moment, kernel_square, kernel_total, factor, RATE_VECTOR, 0.0
    )
    sublayer_rms = jnp.sqrt(summed_stats[:2] / (summed_stats[2] * width_full))
    return (
        output_rows,
        input_grad,
        inputs_master,
        inputs_momentum,
        inputs_variance,
        mixing_master,
        mixing_momentum,
        mixing_variance,
        expand_master,
        expand_momentum,
        expand_variance,
        reduce_master,
        reduce_momentum,
        reduce_variance,
        biases_master,
        biases_momentum,
        biases_variance,
        shared_master,
        shared_momentum,
        shared_variance,
        kernel_master,
        kernel_momentum,
        kernel_variance,
        grad_norm,
        sublayer_rms,
    )


def solution(mesh):
    placed = (
        P("dp", None),
        P("dp", None),
        P("dp", None),
        P("dp"),
        P(None, "dp", "head"),
        P(None, "dp", "head"),
        P(None, "dp", "head"),
        P("head", "dp"),
        P("head", "dp"),
        P("head", "dp"),
        P("dp", "head"),
        P("dp", "head"),
        P("dp", "head"),
        P("head", "dp"),
        P("head", "dp"),
        P("head", "dp"),
        P("head", "dp"),
        P("head", "dp"),
        P("head", "dp"),
        P(None, "dp"),
        P(None, "dp"),
        P(None, "dp"),
        P("head", None),
        P("head", None),
        P("head", None),
    )
    return jax.shard_map(
        body,
        mesh=mesh,
        in_specs=placed,
        out_specs=(
            P("dp", None),
            P("dp", None),
            P(None, "dp", "head"),
            P(None, "dp", "head"),
            P(None, "dp", "head"),
            P("head", "dp"),
            P("head", "dp"),
            P("head", "dp"),
            P("dp", "head"),
            P("dp", "head"),
            P("dp", "head"),
            P("head", "dp"),
            P("head", "dp"),
            P("head", "dp"),
            P("head", "dp"),
            P("head", "dp"),
            P("head", "dp"),
            P(None, "dp"),
            P(None, "dp"),
            P(None, "dp"),
            P("head", None),
            P("head", None),
            P("head", None),
            P(),
            P(),
        ),
        check_vma=False,
    )
```

profile of v0, /device:TPU:0, one launch (start us, length us, event | category | flops | bytes accessed | tf_op | source)
XLA Modules:
  0.0 1594.4 jit_solution(8804524737376209950)
XLA Ops:
  14.5 44.3 %all-reduce.34 = bf16[2304]{0:T(1024)(128)(2,1)S(1)} all-reduce(bf16[2304]{0:T(1024)(128)(2,1)S(1)} %dynamic-update-slice), channel_id=1, replica_groups=mesh['dp'=16,'head'=2] {'dp'}, use_global_device_ids=true, to_apply=%add.34 | all-reduce | flops 2304 | bytes 9216
  71.9 41.2 %all_gather.20 = bf16[384,768]{0,1:T(8,128)(2,1)} all-gather(bf16[384,48]{0,1:T(8,128)(2,1)S(1)} %convert_element_type.185), channel_id=1, replica_groups=mesh['dp'=16,'head'=2] {'dp'}, dimensions={1}, use_global_device_ids=true | all-gather | bytes 626688 | tf_op jit(solution)/shard_map/all_gather | solution.py:183
  113.5 5.3 fusion.98
  156.8 4.5 select_reduce_fusion
  164.7 4.6 select_reduce_fusion.1
  177.3 26.0 %fusion.28 = bf16[1536,6,64]{0,2,1:T(8,128)(2,1)} fusion(f32[6,128,64]{2,1,0:T(8,128)} %bitcast.361, f32[1536,6,64]{0,2,1:T(8,128)S(1)} %get-tuple-element.291, f32[6,1536]{1,0:T(8,128)S(1)} %fusion.130, f32[1536]{0:T(1024)} %fusion.246, f32[6]{0:T(128)} %get-tuple-element.208, f32[6]{0:T(128)} %get-tuple-element.177, f32[6]{0:T(128)} %get-tuple-element.178, ...), kind=kOutput, calls=%fused_computation.73 | convolution fusion | flops 969080832 | bytes 8782104 | tf_op jit(solution)/shard_map/jvp(hrl,hle->rhe)/dot_general | solution.py:108
  203.3 5.0 fusion.305
  212.0 38.0 %all-gather = bf16[16,48,6]{1,2,0:T(8,128)(2,1)S(1)} all-gather(bf16[1,48,6]{1,2,0:T(8,128)(2,1)S(1)} %convert_bitcast_fusion), channel_id=1, replica_groups=mesh['dp'=16,'head'=2] {'dp'}, dimensions={0}, use_global_device_ids=true | all-gather | bytes 9792 | tf_op jit(solution)/shard_map/all_gather | solution.py:187
  255.3 47.7 %all-gather.7.cloned.1.call-done = bf16[768,1536]{1,0:T(8,128)(2,1)} async-done(((bf16[48,1536]{1,0:T(8,128)(2,1)}), bf16[768,1536]{1,0:T(8,128)(2,1)}) %all-gather.7.cloned.1.call-update) | async-done | bytes 2359312 | tf_op jit(solution)/shard_map/all_gather | solution.py:184
  303.0 11.8 multiply_convert_fusion
  314.8 53.0 %all-gather.9.cloned.1.call-done = bf16[1536,768]{0,1:T(8,128)(2,1)} async-done(((bf16[1536,48]{0,1:T(8,128)(2,1)}), bf16[1536,768]{0,1:T(8,128)(2,1)}) %all-gather.9.cloned.1.call-update) | async-done | bytes 2359312 | tf_op jit(solution)/shard_map/all_gather | solution.py:185
  367.8 9.2 fusion.306
  378.3 26.8 %all-reduce.45.cloned.1.call-done = f32[1536,768]{1,0:T(8,128)} async-done(((f32[1536,768]{1,0:T(8,128)}), f32[1536,768]{1,0:T(8,128)}) %all-reduce.45.cloned.1.call-update) | async-done | bytes 4718608 | tf_op jit(solution)/shard_map/psum | solution.py:230
  405.1 4.9 fusion.298
  412.5 5.3 fusion.7
  417.9 4.0 fusion.297
  421.9 13.3 convert_reduce_fusion
  437.4 5.4 fusion.307
  443.8 29.6 %all-reduce.47.cloned.1.call-done = f32[1536,768]{1,0:T(8,128)} async-done(((f32[1536,768]{1,0:T(8,128)}), f32[1536,768]{1,0:T(8,128)}) %all-reduce.47.cloned.1.call-update) | async-done | bytes 4718608 | tf_op jit(solution)/shard_map/psum | solution.py:258
  473.4 7.2 multiply_reduce_fusion.1
  480.6 4.3 fusion.296
  485.0 5.4 multiply_reduce_fusion.24
  490.5 5.1 fusion.116
  529.9 7.1 multiply_reduce_fusion.11
  537.0 10.9 multiply_reduce_fusion.10
  548.0 10.9 multiply_reduce_fusion.8
  558.8 11.2 multiply_reduce_fusion.9
  580.1 7.0 convert_reduce_fusion.1
  589.3 6.1 fusion.127
  597.7 6.4 convert_reduce_fusion.2
  610.7 34.2 %fusion.27 = bf16[1536,6,64]{0,2,1:T(8,128)(2,1)} fusion(f32[6,128,64]{2,1,0:T(8,128)} %bitcast.364, f32[1536,6,64]{0,2,1:T(8,128)} %get-tuple-element.242, f32[1536,6,64]{0,2,1:T(8,128)} %get-tuple-element.241, f32[1536,6,64]{0,2,1:T(8,128)} %get-tuple-element.265, f32[1536,6,64]{0,2,1:T(8,128)} %get-tuple-element.264, ...), kind=kOutput, calls=%fused_computation.72 | convolution fusion | flops 949616640 | bytes 84156696 | tf_op jit(solution)/shard_map/transpose(jvp(hlr,rhe->hle))/dot_general | solution.py:102
  648.1 5.0 fusion.274
  659.5 8.2 fusion.128
  670.0 4.1 fusion.25
  677.3 5.8 fusion.112
  689.0 6.4 convolution_bitcast_fusion
  696.1 9.9 fusion.273
  706.7 10.3 fusion.276
  724.1 42.1 %psum.53 = f32[6,33]{1,0:T(8,128)S(1)} all-reduce(f32[6,33]{1,0:T(8,128)S(1)} %stack.179), channel_id=1, replica_groups=mesh['dp'=16,'head'=2] {'dp'}, use_global_device_ids=true, to_apply=%region_86.87 | all-reduce | flops 198 | bytes 1584 | tf_op jit(solution)/shard_map/psum | solution.py:306
  767.4 6.5 reduce-scatter.16.cloned.1.call-done
  775.5 127.3 %reduce-scatter.10.cloned.1.call-done = f32[384,48]{0,1:T(8,128)} async-done(((f32[384,768]{0,1:T(8,128)}), f32[384,48]{0,1:T(8,128)}) %reduce-scatter.10.cloned.1.call-update) | async-done | bytes 73744 | tf_op jit(solution)/shard_map/reduce_scatter | solution.py:300
  904.3 183.9 %all-reduce.51.cloned.1.call-done = f32[3,768,384]{2,0,1:T(4,128)} async-done(((f32[3,768,384]{2,0,1:T(4,128)}), f32[3,768,384]{2,0,1:T(4,128)}) %all-reduce.51.cloned.1.call-update) | async-done | bytes 3538960
  1091.3 28.0 %all-reduce.49.cloned.1.call-done = f32[1536,768]{1,0:T(8,128)} async-done(((f32[1536,768]{1,0:T(8,128)}), f32[1536,768]{1,0:T(8,128)}) %all-reduce.49.cloned.1.call-update) | async-done | bytes 4718608 | tf_op jit(solution)/shard_map/psum | solution.py:290
  1119.4 6.5 add_reduce_fusion
  1127.0 137.0 %reduce-scatter.14.cloned.1.call-done = f32[1536,48]{0,1:T(8,128)} async-done(((f32[1536,768]{0,1:T(8,128)}), f32[1536,48]{0,1:T(8,128)}) %reduce-scatter.14.cloned.1.call-update) | async-done | bytes 294928 | tf_op jit(solution)/shard_map/reduce_scatter | solution.py:302
  1265.7 139.9 %reduce-scatter.12.cloned.1.call-done = f32[48,1536]{1,0:T(8,128)} async-done(((f32[768,1536]{1,0:T(8,128)}), f32[48,1536]{1,0:T(8,128)}) %reduce-scatter.12.cloned.1.call-update) | async-done | bytes 294928 | tf_op jit(solution)/shard_map/reduce_scatter | solution.py:301
  1409.3 122.3 %reduce-scatter.18.cloned.1.call-done = f32[48,6]{1,0:T(8,128)} async-done(((f32[768,6]{1,0:T(8,128)}), f32[48,6]{1,0:T(8,128)}) %reduce-scatter.18.cloned.1.call-update) | async-done | bytes 1168
  1533.7 40.4 %all-reduce.36 = (f32[]{:T(128)}, f32[3]{0:T(128)}) all-reduce(f32[]{:T(128)S(6)} %add.664, f32[3]{0:T(128)} %pad_maximum_fusion.4), channel_id=1, replica_groups=mesh['dp'=16,'head'=2] {'dp','head'}, use_global_device_ids=true, to_apply=%region_88.89 | all-reduce | flops 4 | bytes 32 | tf_op jit(solution)/shard_map/psum | solution.py:320
  (660 shorter events, 188.0 us)
Async XLA Ops:
  7.2 106.3 %all-gather.5.cloned.1.call-start = ((), (), s32[]{:S(2)}) async-start(), calls=%async_computation.5 | async-start | bytes 1880064 | tf_op jit(solution)/shard_map/all_gather | solution.py:182
  8.9 241.3 %all-reduce.43.cloned.1.call-start = ((), (), s32[]{:S(2)}) async-start(), calls=%async_computation.6 | async-start | bytes 9437184 | tf_op jit(solution)/shard_map/psum | solution.py:220
  61.7 67.1 %copy-start.182 = (f32[128]{0:T(128)}, f32[128]{0:T(128)S(1)}, u32[]{:S(2)}) copy-start(f32[128]{0:T(128)S(1)} %fusion.248) | copy-start | bytes 1540
  61.7 67.1 %copy-start.150 = (s32[128]{0:T(128)}, s32[128]{0:T(128)S(1)}, u32[]{:S(2)}) copy-start(s32[128]{0:T(128)S(1)} %get-tuple-element.360) | copy-start | bytes 1540
  61.7 67.1 %copy-start.185 = (s32[128]{0:T(128)}, s32[128]{0:T(128)S(1)}, u32[]{:S(2)}) copy-start(s32[128]{0:T(128)S(1)} %get-tuple-element.359) | copy-start | bytes 1540
  62.4 66.5 %copy-start.104 = (s32[1536]{0:T(1024)}, s32[1536]{0:T(1024)S(1)}, u32[]{:S(2)}) copy-start(s32[1536]{0:T(1024)S(1)} %select_select_fusion) | copy-start | bytes 18436
  64.4 64.5 %copy-start.141 = (s32[1536]{0:T(1024)}, s32[1536]{0:T(1024)S(1)}, u32[]{:S(2)}) copy-start(s32[1536]{0:T(1024)S(1)} %get-tuple-element.357) | copy-start | bytes 18436
  113.3 57.1 %copy-start.28 = (pred[128,1536]{1,0:T(8,128)(4,1)}, pred[128,1536]{1,0:T(8,128)(4,1)S(1)}, u32[]{:S(2)}) copy-start(pred[128,1536]{1,0:T(8,128)(4,1)S(1)} %broadcast_compare_fusion.1) | copy-start | bytes 589828
  128.8 27.9 %copy-start.10 = (f32[1536,6,64]{0,2,1:T(8,128)}, f32[1536,6,64]{0,2,1:T(8,128)S(1)}, u32[]{:S(2)}) copy-start(f32[1536,6,64]{0,2,1:T(8,128)S(1)} %convert_multiply_fusion.2) | copy-start | bytes 7077892
  131.0 30.6 %copy-start.78 = (f32[128,384]{0,1}, f32[128,384]{0,1:S(1)}, u32[]{:S(2)}) copy-start(f32[128,384]{0,1:S(1)} %fusion.147) | copy-start | bytes 589828
  135.2 440.2 %copy-start.108 = (f32[6,2,64]{2,1,0:T(2,128)}, f32[6,2,64]{2,1,0:T(2,128)S(1)}, u32[]{:S(2)}) copy-start(f32[6,2,64]{2,1,0:T(2,128)S(1)} %get-tuple-element.302) | copy-start | bytes 9220
  170.3 273.2 %copy-start.122 = (f32[6,128]{1,0:T(8,128)}, f32[6,128]{1,0:T(8,128)S(1)}, u32[]{:S(2)}) copy-start(f32[6,128]{1,0:T(8,128)S(1)} %fusion.129) | copy-start | bytes 9220
  208.3 41.9 %copy-start.77 = (bf16[1536,768]{1,0:T(8,128)(2,1)S(1)}, bf16[1536,768]{1,0:T(8,128)(2,1)}, u32[]{:S(2)}) copy-start(bf16[1536,768]{1,0:T(8,128)(2,1)} %param.25) | copy-start | bytes 7077892
  208.3 94.7 %all-gather.7.cloned.1.call-start = ((), (), s32[]{:S(2)}) async-start(), calls=%async_computation.7 | async-start | bytes 2506752 | tf_op jit(solution)/shard_map/all_gather | solution.py:184
  210.2 157.6 %all-gather.9.cloned.1.call-start = ((), (), s32[]{:S(2)}) async-start(), calls=%async_computation.8 | async-start | bytes 2506752 | tf_op jit(solution)/shard_map/all_gather | solution.py:185
  211.9 193.2 %all-reduce.45.cloned.1.call-start = ((), (), s32[]{:S(2)}) async-start(), calls=%async_computation.9 | async-start | bytes 9437184 | tf_op jit(solution)/shard_map/psum | solution.py:230
  250.1 154.9 %copy-start.136 = (f32[768]{0:T(1024)}, f32[768]{0:T(1024)S(1)}, u32[]{:S(2)}) copy-start(f32[768]{0:T(1024)S(1)} %get-tuple-element.166) | copy-start | bytes 9220
  250.2 230.5 %copy-start.112 = (f32[768]{0:T(1024)}, f32[768]{0:T(1024)S(1)}, u32[]{:S(2)}) copy-start(f32[768]{0:T(1024)S(1)} %get-tuple-element.167) | copy-start | bytes 9220
  376.9 33.8 %slice-start.8 = ((s8[4718592]{0:T(1024)(128)(4,1)}), s8[524288]{0:T(1024)(128)(4,1)S(1)}, s32[]{:S(2)}) async-start(s8[4718592]{0:T(1024)(128)(4,1)} %bitcast.331), calls=%async_computation.26 | async-start | bytes 1048576
  377.0 96.4 %all-reduce.47.cloned.1.call-start = ((), (), s32[]{:S(2)}) async-start(), calls=%async_computation.10 | async-start | bytes 9437184 | tf_op jit(solution)/shard_map/psum | solution.py:258
  421.9 51.5 %copy-start.124 = (f32[1536]{0:T(1024)}, f32[1536]{0:T(1024)S(1)}, u32[]{:S(2)}) copy-start(f32[1536]{0:T(1024)S(1)} %negate_multiply_fusion.1) | copy-start | bytes 18436
  442.9 331.0 %reduce-scatter.16.cloned.1.call-start = ((), (), s32[]{:S(2)}) async-start(), calls=%async_computation.15 | async-start | bytes 1253376
  485.0 163.1 %copy-start.109 = (f32[1536]{0:T(1024)}, f32[1536]{0:T(1024)S(1)}, u32[]{:S(2)}) copy-start(f32[1536]{0:T(1024)S(1)} %negate_multiply_fusion) | copy-start | bytes 18436
  610.7 35.8 %copy-start.139 = (f32[1536]{0:T(1024)S(1)}, f32[1536]{0:T(1024)}, u32[]{:S(2)}) copy-start(f32[1536]{0:T(1024)} %get-tuple-element.353) | copy-start | bytes 18436
  648.0 254.8 %reduce-scatter.10.cloned.1.call-start = ((), (), s32[]{:S(2)}) async-start(), calls=%async_computation.12 | async-start | bytes 1253376 | tf_op jit(solution)/shard_map/reduce_scatter | solution.py:300
  653.1 435.1 %all-reduce.51.cloned.1.call-start = ((), (), s32[]{:S(2)}) async-start(), calls=%async_computation.17 | async-start | bytes 9437184
  687.1 432.3 %all-reduce.49.cloned.1.call-start = ((), (), s32[]{:S(2)}) async-start(), calls=%async_computation.11 | async-start | bytes 9437184 | tf_op jit(solution)/shard_map/psum | solution.py:290
  695.4 568.6 %reduce-scatter.14.cloned.1.call-start = ((), (), s32[]{:S(2)}) async-start(), calls=%async_computation.14 | async-start | bytes 5013504 | tf_op jit(solution)/shard_map/reduce_scatter | solution.py:302
  706.0 699.6 %reduce-scatter.12.cloned.1.call-start = ((), (), s32[]{:S(2)}) async-start(), calls=%async_computation.13 | async-start | bytes 5013504 | tf_op jit(solution)/shard_map/reduce_scatter | solution.py:301
  717.3 402.0 %copy-start.110 = (f32[1536]{0:T(1024)S(1)}, f32[1536]{0:T(1024)}, u32[]{:S(2)}) copy-start(f32[1536]{0:T(1024)} %copy-done.109) | copy-start | bytes 18436
  717.4 814.3 %reduce-scatter.18.cloned.1.call-start = ((), (), s32[]{:S(2)}) async-start(), calls=%async_computation.16 | async-start | bytes 417792
  774.9 315.1 %copy-start.144 = (f32[1,144]{1,0:T(1,128)}, f32[1,144]{1,0:T(1,128)S(1)}, u32[]{:S(2)}) copy-start(f32[1,144]{1,0:T(1,128)S(1)} %copy.474) | copy-start | bytes 1732
  1091.3 487.9 %copy-start.42 = (f32[6,33]{1,0:T(8,128)S(1)}, f32[6,33]{1,0:T(8,128)}, u32[]{:S(2)}) copy-start(f32[6,33]{1,0:T(8,128)} %param.47) | copy-start | bytes 2380
  1091.3 489.3 %copy-start.130 = (f32[6,48]{1,0:T(8,128)S(1)}, f32[6,48]{1,0:T(8,128)}, u32[]{:S(2)}) copy-start(f32[6,48]{1,0:T(8,128)} %param.44) | copy-start | bytes 3460
  1091.3 490.6 %copy-start.96 = (f32[3,48,384]{2,1,0:T(8,128)S(1)}, f32[3,48,384]{2,1,0:T(8,128)}, u32[]{:S(2)}) copy-start(f32[3,48,384]{2,1,0:T(8,128)} %param.29) | copy-start | bytes 663556
  1091.3 490.6 %copy-start.106 = (f32[3,48,384]{2,1,0:T(8,128)S(1)}, f32[3,48,384]{2,1,0:T(8,128)}, u32[]{:S(2)}) copy-start(f32[3,48,384]{2,1,0:T(8,128)} %param.30) | copy-start | bytes 663556
  1091.3 490.6 %copy-start.107 = (f32[3,48,384]{2,1,0:T(8,128)S(1)}, f32[3,48,384]{2,1,0:T(8,128)}, u32[]{:S(2)}) copy-start(f32[3,48,384]{2,1,0:T(8,128)} %param.31) | copy-start | bytes 663556
  1125.9 456.9 %copy-start.102 = (f32[384,48]{0,1:T(8,128)S(1)}, f32[384,48]{0,1:T(8,128)}, u32[]{:S(2)}) copy-start(f32[384,48]{0,1:T(8,128)} %param.32) | copy-start | bytes 221188
  1125.9 456.9 %copy-start.103 = (f32[384,48]{0,1:T(8,128)S(1)}, f32[384,48]{0,1:T(8,128)}, u32[]{:S(2)}) copy-start(f32[384,48]{0,1:T(8,128)} %reduce-scatter.10.cloned.1.call-done) | copy-start | bytes 221188
  1125.9 456.9 %copy-start.111 = (f32[384,48]{0,1:T(8,128)S(1)}, f32[384,48]{0,1:T(8,128)}, u32[]{:S(2)}) copy-start(f32[384,48]{0,1:T(8,128)} %param.33) | copy-start | bytes 221188
  1125.9 458.5 %copy-start.87 = (f32[1536,48]{0,1:T(8,128)S(1)}, f32[1536,48]{0,1:T(8,128)}, u32[]{:S(2)}) copy-start(f32[1536,48]{0,1:T(8,128)} %param.38) | copy-start | bytes 884740
  1125.9 458.5 %copy-start.98 = (f32[1536,48]{0,1:T(8,128)S(1)}, f32[1536,48]{0,1:T(8,128)}, u32[]{:S(2)}) copy-start(f32[1536,48]{0,1:T(8,128)} %param.39) | copy-start | bytes 884740
  1125.9 458.5 %copy-start.99 = (f32[1536,48]{0,1:T(8,128)S(1)}, f32[1536,48]{0,1:T(8,128)}, u32[]{:S(2)}) copy-start(f32[1536,48]{0,1:T(8,128)} %param.40) | copy-start | bytes 884740
  1264.0 320.4 %copy-start.89 = (f32[1536,48]{0,1:T(8,128)S(1)}, f32[1536,48]{0,1:T(8,128)}, u32[]{:S(2)}) copy-start(f32[1536,48]{0,1:T(8,128)} %reduce-scatter.14.cloned.1.call-done) | copy-start | bytes 884740
  1265.7 319.8 %copy-start.88 = (f32[48,1536]{1,0:T(8,128)S(1)}, f32[48,1536]{1,0:T(8,128)}, u32[]{:S(2)}) copy-start(f32[48,1536]{1,0:T(8,128)} %param.35) | copy-start | bytes 884740
  1265.7 319.8 %copy-start.100 = (f32[48,1536]{1,0:T(8,128)S(1)}, f32[48,1536]{1,0:T(8,128)}, u32[]{:S(2)}) copy-start(f32[48,1536]{1,0:T(8,128)} %param.36) | copy-start | bytes 884740
  1265.7 319.8 %copy-start.101 = (f32[48,1536]{1,0:T(8,128)S(1)}, f32[48,1536]{1,0:T(8,128)}, u32[]{:S(2)}) copy-start(f32[48,1536]{1,0:T(8,128)} %param.37) | copy-start | bytes 884740
  1405.6 179.9 %copy-start.90 = (f32[48,1536]{1,0:T(8,128)S(1)}, f32[48,1536]{1,0:T(8,128)}, u32[]{:S(2)}) copy-start(f32[48,1536]{1,0:T(8,128)} %reduce-scatter.12.cloned.1.call-done) | copy-start | bytes 884740
  (164 other events, 714.8 us)
Sparse Core Ops, SparseCore 0:
  11.3 63.2 all-gather.4
  208.5 27.2 all-reduce.42
  239.5 63.4 all-gather.6
  306.6 61.0 all-gather.8
  377.1 27.9 all-reduce.44
  443.0 30.3 all-reduce.46
  648.1 125.7 reduce-scatter.15
  779.4 123.3 reduce-scatter.9
  909.5 178.6 all-reduce.50
  1091.2 28.1 all-reduce.48
  1125.4 138.5 reduce-scatter.13
  1269.0 136.5 reduce-scatter.11
  1411.0 120.6 reduce-scatter.17
where the time goes:
time: 1610 us; the launch traced here: 1590 us
  waiting for transfers between devices  902 us (56%)
  matrix products  277 us (17%)
  blocking collectives  206 us (13%)
  other arithmetic  128 us (8%)
  local copies, waits for them, and re-layouts  53.6 us (3%)
  between operations  27 us (2%)
    unnamed x16, waiting for transfers between devices  313 us
    reduce_scatter x1, waiting for transfers between devices, body(): lax.psum_scatter(expand_grad, 'dp', scatter_dimension=0, tiled=True)  140 us
    reduce_scatter x1, waiting for transfers between devices, body(): lax.psum_scatter(reduce_grad, 'dp', scatter_dimension=1, tiled=True)  137 us
    reduce_scatter x1, waiting for transfers between devices, body(): lax.psum_scatter(mixing_grad, 'dp', scatter_dimension=1, tiled=True)  127 us
    all_gather x1, waiting for transfers between devices, body(): lax.all_gather(reduce_weight.astype(jnp.bfloat16), 'dp', axis=1, tiled=True)  53 us
    all_gather x1, waiting for transfers between devices, body(): lax.all_gather(expand_weight.astype(jnp.bfloat16), 'dp', axis=0, tiled=True)  47.7 us
    unnamed x1, blocking collectives  44.3 us
    psum x1, blocking collectives, body(): kernel_total = lax.psum(kernel_grad, 'dp')  42.1 us
  transfers between devices with their start and end apart: 13, of which 11 were waited for; matrix products, arithmetic and copies ran while one was open for 8% of the time, Pallas kernels for 0%

commit v1 on v0

--- a/solution.py
+++ b/solution.py
@@ -8,7 +8,8 @@
 PINV_STEPS = 6
 
 
-PRECISE = lax.Precision.HIGHEST
+PRECISE = lax.Precision.HIGH
+FAST = lax.Precision.DEFAULT
 NORM_EPS = 1e-05
 CLIP_NORM = 1.0
 CLIP_EPS = 1e-06
@@ -20,6 +21,74 @@
 WEIGHT_DECAY = 0.01
 CORRECT_ONE = 1.0 - BETA_ONE**5
 CORRECT_TWO = 1.0 - BETA_TWO**5
+
+
+def bits_of(count):
+    bit_count = 0
+    while (1 << bit_count) < count:
+        bit_count += 1
+    return bit_count
+
+
+def swap(array, axis, count, bit):
+    return lax.ppermute(array, axis, [(i, i ^ (1 << bit)) for i in range(count)])
+
+
+def gather_rows(array, axis, count, order):
+    bit_count = bits_of(count)
+    own = lax.axis_index(axis)
+    current = array.reshape((1,) * bit_count + array.shape)
+    for bit in order:
+        dim = bit_count - 1 - bit
+        other = swap(current, axis, count, bit)
+        current = jnp.where(
+            (own >> bit) & 1 == 0,
+            jnp.concatenate([current, other], dim),
+            jnp.concatenate([other, current], dim),
+        )
+    return current.reshape((count * array.shape[0],) + array.shape[1:])
+
+
+def scatter_rows(array, axis, count, order):
+    bit_count = bits_of(count)
+    own = lax.axis_index(axis)
+    rows = array.shape[0] // count
+    current = array.reshape((2,) * bit_count + (rows,) + array.shape[1:])
+    for bit in order:
+        dim = bit_count - 1 - bit
+        mine = (own >> bit) & 1
+        sent = lax.dynamic_slice_in_dim(current, 1 - mine, 1, dim).astype(jnp.bfloat16)
+        kept = lax.dynamic_slice_in_dim(current, mine, 1, dim).astype(jnp.float32)
+        current = kept + swap(sent, axis, count, bit).astype(jnp.float32)
+    return current.reshape((rows,) + array.shape[1:])
+
+
+def sum_all(array, axis, count):
+    for bit in range(bits_of(count)):
+        array = array + swap(array, axis, count, bit)
+    return array
+
+
+def head_sum(array, count):
+    low = array.astype(jnp.bfloat16)
+    total = low.astype(jnp.float32)
+    for bit in range(bits_of(count)):
+        total = total + swap(low, "head", count, bit).astype(jnp.float32)
+        if bit + 1 < bits_of(count):
+            low = total.astype(jnp.bfloat16)
+            total = low.astype(jnp.float32)
+    return total
+
+
+def scatter_orders(count):
+    bits = list(range(bits_of(count)))
+    first = bits
+    second = bits[:2][::-1] + bits[2:]
+    return first, second
+
+
+def after(array, *others):
+    return lax.optimization_barrier((array,) + others)[0]
 
 
 def softmax_rows(scores):
@@ -85,7 +154,7 @@
     land_key = jnp.einsum("lr,rhe->lhe", select, key_scaled, precision=PRECISE)
     land_item = lax.iota(jnp.int32, 2 * mark_count) // mark_count
     own_item = jnp.minimum(row_item, 1)
-    first_scores = jnp.einsum("rhe,lhe->hrl", query_scaled, land_key, precision=PRECISE)
+    first_scores = jnp.einsum("rhe,lhe->hrl", query_scaled, land_key, precision=FAST)
     first_kernel = softmax_rows(
         jnp.where(own_item[None, :, None] == land_item[None, None, :], first_scores, -jnp.inf)
     )
@@ -95,17 +164,17 @@
         jnp.einsum("aihe,ajhe->haij", pair_query, pair_key, precision=PRECISE)
     )
     inverse = pseudo_inverse(middle_kernel, step_count)
-    last_scores = jnp.einsum("lhe,rhe->hlr", land_query, key_scaled, precision=PRECISE)
+    last_scores = jnp.einsum("lhe,rhe->hlr", land_query, key_scaled, precision=FAST)
     last_kernel = softmax_rows(
         jnp.where(land_item[None, :, None] == row_item[None, None, :], last_scores, -jnp.inf)
     )
     landmark_values = jnp.einsum(
-        "hlr,rhe->hle", last_kernel, value_rows, precision=PRECISE
+        "hlr,rhe->hle", last_kernel, value_rows, precision=FAST
     ).reshape(head_count, 2, mark_count, head_size)
     weighted = jnp.einsum("haij,haje->haie", inverse, landmark_values, precision=PRECISE).reshape(
         head_count, 2 * mark_count, head_size
     )
-    return jnp.einsum("hrl,hle->rhe", first_kernel, weighted, precision=PRECISE)
+    return jnp.einsum("hrl,hle->rhe", first_kernel, weighted, precision=FAST)
 
 
 def depthwise_conv(value_rows, kernel, row_item):
@@ -178,15 +247,33 @@
     kernel_moment,
     kernel_square,
 ):
-    inputs_full, mixing_full, expand_full, reduce_full, biases_full, shared_full = (
-        lax.all_gather(inputs_weight.astype(jnp.bfloat16), "dp", axis=1, tiled=True),
-        lax.all_gather(mixing_weight.astype(jnp.bfloat16), "dp", axis=1, tiled=True),
-        lax.all_gather(expand_weight.astype(jnp.bfloat16), "dp", axis=0, tiled=True),
-        lax.all_gather(reduce_weight.astype(jnp.bfloat16), "dp", axis=1, tiled=True),
-        lax.all_gather(biases_weight.astype(jnp.bfloat16), "dp", axis=1, tiled=True),
-        lax.all_gather(shared_weight.astype(jnp.bfloat16), "dp", axis=1, tiled=True),
-    )
-    local_width = inputs_full.shape[2]
+    dp_count = lax.axis_size("dp")
+    head_count = lax.axis_size("head")
+    first_order, second_order = scatter_orders(dp_count)
+    local_width = inputs_weight.shape[2]
+    shard_rows = inputs_weight.shape[1]
+    hidden_units = expand_weight.shape[1]
+    bias_share = biases_weight.shape[1]
+    inputs_low = jnp.concatenate([inputs_weight[c] for c in range(3)], axis=1).astype(jnp.bfloat16)
+    mixing_low = mixing_weight.T.astype(jnp.bfloat16)
+    expand_low = expand_weight.astype(jnp.bfloat16)
+    reduce_low = reduce_weight.T.astype(jnp.bfloat16)
+    small_low = jnp.concatenate([biases_weight.reshape(-1), shared_weight.reshape(-1)]).astype(
+        jnp.bfloat16
+    )[None, :]
+    half = (3 * local_width // 2 + 127) // 128 * 128
+    small_full = gather_rows(small_low, "dp", dp_count, first_order[::-1])
+    inputs_left = gather_rows(inputs_low[:, :half], "dp", dp_count, first_order[::-1])
+    inputs_right = gather_rows(inputs_low[:, half:], "dp", dp_count, second_order[::-1])
+    inputs_full = jnp.concatenate([inputs_left, inputs_right], axis=1)
+    mixing_low, expand_low = after(mixing_low, inputs_full), after(expand_low, inputs_full)
+    reduce_low = after(reduce_low, inputs_full)
+    mixing_full = gather_rows(mixing_low, "dp", dp_count, first_order[::-1])
+    expand_full = gather_rows(expand_low, "dp", dp_count, second_order[::-1])
+    reduce_full = gather_rows(reduce_low, "dp", dp_count, first_order[::-1])
+    biases_full = small_full[:, :bias_share].reshape(1, -1)
+    shared_full = small_full[:, bias_share:].reshape(dp_count, 6, shard_rows)
+    shared_full = shared_full.transpose(1, 0, 2).reshape(6, -1)
     local_heads = local_width // HEAD_DIM
     row_count = tokens.shape[0]
     width_full = tokens.shape[1]
@@ -201,7 +288,7 @@
     inside = (row_item < 2).astype(jnp.float32)
     head_shape = (row_count, local_heads, HEAD_DIM)
     weight_rows = counted.astype(jnp.float32) * inside
-    projected = jnp.einsum("rd,cdk->rck", tokens, inputs_full, preferred_element_type=jnp.float32)
+    projected = jnp.dot(tokens, inputs_full, preferred_element_type=jnp.float32).reshape(row_count, 3, local_width)
     queries = (
         (projected[:, 0] + query_bias).astype(jnp.bfloat16).astype(jnp.float32).reshape(head_shape)
     )
@@ -216,8 +303,8 @@
     core_out, core_pull = jax.vjp(attend, queries, key_rows, value_rows)
     mixed = core_out + depthwise_conv(value_rows, kernel_weight, row_item)
     attended = (mixed * inside[:, None, None]).reshape(row_count, local_width).astype(jnp.bfloat16)
-    mixing_part = jnp.dot(attended, mixing_full, preferred_element_type=jnp.float32)
-    branch_one = lax.psum(mixing_part, "head") + shared_rows[0]
+    mixing_part = jnp.einsum("rk,dk->rd", attended, mixing_full, preferred_element_type=jnp.float32)
+    branch_one = head_sum(mixing_part, head_count) + shared_rows[0]
     token_rows = tokens.astype(jnp.float32)
     hidden_one, norm_one_pull = jax.vjp(
         layer_norm, token_rows + branch_one, shared_rows[2], shared_rows[3]
@@ -226,8 +313,8 @@
     expanded = jnp.dot(hidden_low, expand_full, preferred_element_type=jnp.float32) + expand_bias
     activated, gelu_pull = jax.vjp(gelu_tanh, expanded)
     activated_low = activated.astype(jnp.bfloat16)
-    reduce_part = jnp.dot(activated_low, reduce_full, preferred_element_type=jnp.float32)
-    branch_two = lax.psum(reduce_part, "head") + shared_rows[1]
+    reduce_part = jnp.einsum("rf,df->rd", activated_low, reduce_full, preferred_element_type=jnp.float32)
+    branch_two = head_sum(reduce_part, head_count) + shared_rows[1]
     output_rows, norm_two_pull = jax.vjp(
         layer_norm, hidden_one + branch_two, shared_rows[4], shared_rows[5]
     )
@@ -242,10 +329,10 @@
     d_res_two, d_gain_two, d_shift_two = norm_two_pull(grad_rows)
     d_two_low = d_res_two.astype(jnp.bfloat16)
     reduce_grad = jnp.einsum(
-        "rf,rd->fd", activated_low, d_two_low, preferred_element_type=jnp.float32
+        "rd,rf->df", d_two_low, activated_low, preferred_element_type=jnp.float32
     )
     d_activated = jnp.einsum(
-        "rd,fd->rf", d_two_low, reduce_full, preferred_element_type=jnp.float32
+        "rd,df->rf", d_two_low, reduce_full, preferred_element_type=jnp.float32
     )
     (d_expanded,) = gelu_pull(d_activated)
     d_expanded_low = d_expanded.astype(jnp.bfloat16)
@@ -255,7 +342,7 @@
     hidden_part = jnp.einsum(
         "rf,df->rd", d_expanded_low, expand_full, preferred_element_type=jnp.float32
     )
-    d_hidden = lax.psum(hidden_part, "head") + d_res_two
+    d_hidden = head_sum(hidden_part, head_count) + d_res_two
     d_res_one, d_gain_one, d_shift_one = norm_one_pull(d_hidden)
     shared_grad = jnp.stack(
         [
@@ -268,9 +355,9 @@
         ]
     )
     d_one_low = d_res_one.astype(jnp.bfloat16)
-    mixing_grad = jnp.einsum("rk,rd->kd", attended, d_one_low, preferred_element_type=jnp.float32)
+    mixing_grad = jnp.einsum("rd,rk->dk", d_one_low, attended, preferred_element_type=jnp.float32)
     d_attended = (
-        jnp.einsum("rd,kd->rk", d_one_low, mixing_full, preferred_element_type=jnp.float32)
+        jnp.einsum("rd,dk->rk", d_one_low, mixing_full, preferred_element_type=jnp.float32)
         * inside[:, None]
     )
     d_mixed = d_attended.reshape(head_shape)
@@ -278,32 +365,46 @@
     d_value_conv, kernel_grad = conv_backward(value_rows, kernel_weight, row_item, d_mixed)
     projected_grad = (
         jnp.stack([d_query, d_key, d_value + d_value_conv], axis=1)
-        .reshape(row_count, 3, local_width)
+        .reshape(row_count, 3 * local_width)
         .astype(jnp.bfloat16)
     )
     inputs_grad = jnp.einsum(
-        "rd,rck->cdk", tokens, projected_grad, preferred_element_type=jnp.float32
+        "rd,rk->dk", tokens, projected_grad, preferred_element_type=jnp.float32
     )
     token_part = jnp.einsum(
-        "rck,cdk->rd", projected_grad, inputs_full, preferred_element_type=jnp.float32
-    )
-    input_grad = lax.psum(token_part, "head") + d_res_one
+        "rk,dk->rd", projected_grad, inputs_full, preferred_element_type=jnp.float32
+    )
+    input_grad = head_sum(token_part, head_count) + d_res_one
     biases_grad = jnp.concatenate(
         [
-            jnp.sum(projected_grad[:, 0], axis=0, dtype=jnp.float32),
-            jnp.sum(projected_grad[:, 2], axis=0, dtype=jnp.float32),
+            jnp.sum(projected_grad[:, :local_width], axis=0, dtype=jnp.float32),
+            jnp.sum(projected_grad[:, 2 * local_width :], axis=0, dtype=jnp.float32),
             jnp.sum(d_expanded_low, axis=0, dtype=jnp.float32),
         ]
     )[None, :]
-    inputs_share, mixing_share, expand_share, reduce_share, biases_share, shared_share = (
-        lax.psum_scatter(inputs_grad, "dp", scatter_dimension=1, tiled=True),
-        lax.psum_scatter(mixing_grad, "dp", scatter_dimension=1, tiled=True),
-        lax.psum_scatter(expand_grad, "dp", scatter_dimension=0, tiled=True),
-        lax.psum_scatter(reduce_grad, "dp", scatter_dimension=1, tiled=True),
-        lax.psum_scatter(biases_grad, "dp", scatter_dimension=1, tiled=True),
-        lax.psum_scatter(shared_grad, "dp", scatter_dimension=1, tiled=True),
-    )
-    kernel_total = lax.psum(kernel_grad, "dp")
+    expand_share = scatter_rows(expand_grad, "dp", dp_count, first_order)
+    reduce_share = scatter_rows(reduce_grad, "dp", dp_count, second_order).T
+    mixing_share = scatter_rows(mixing_grad, "dp", dp_count, first_order).T
+    inputs_share = jnp.concatenate(
+        [
+            scatter_rows(inputs_grad[:, :half], "dp", dp_count, first_order),
+            scatter_rows(inputs_grad[:, half:], "dp", dp_count, second_order),
+        ],
+        axis=1,
+    )
+    inputs_share = inputs_share.reshape(shard_rows, 3, local_width).transpose(1, 0, 2)
+    small_parts = [biases_grad.reshape(-1), shared_grad.reshape(-1), kernel_grad.reshape(-1)]
+    small_size = sum(part.shape[0] for part in small_parts)
+    small_rows = (small_size + 1023) // 1024 * 8
+    small_parts.append(jnp.zeros((small_rows * 128 - small_size,), jnp.float32))
+    small_total = sum_all(jnp.concatenate(small_parts).reshape(small_rows, 128), "dp", dp_count)
+    small_total = small_total.reshape(-1)
+    dp_index = lax.axis_index("dp")
+    biases_share = lax.dynamic_slice_in_dim(small_total, dp_index * bias_share, bias_share)[None, :]
+    bias_size = biases_grad.shape[1]
+    shared_total = small_total[bias_size : bias_size + 6 * width_full].reshape(6, width_full)
+    shared_share = lax.dynamic_slice_in_dim(shared_total, dp_index * shard_rows, shard_rows, axis=1)
+    kernel_total = small_total[bias_size + 6 * width_full : small_size].reshape(kernel_grad.shape)
     kernel_squares = jnp.where(lax.axis_index("dp") == 0, jnp.sum(kernel_total * kernel_total), 0.0)
     local_squares = (
         jnp.sum(inputs_share * inputs_share)
@@ -317,7 +418,9 @@
         + jnp.where(lax.axis_index("head") == 0, jnp.sum(shared_share * shared_share), 0.0)
         + kernel_squares
     )
-    squares_total, summed_stats = lax.psum((local_squares, local_stats), ("dp", "head"))
+    final_row = jnp.concatenate([local_squares[None], local_stats, jnp.zeros((124,), jnp.float32)])
+    final_row = sum_all(sum_all(final_row[None, :], "head", head_count), "dp", dp_count)[0]
+    squares_total, summed_stats = final_row[0], final_row[1:4]
     grad_norm = jnp.sqrt(squares_total)
     factor = CLIP_NORM / (grad_norm + CLIP_EPS)
     inputs_master, inputs_momentum, inputs_variance = adamw(

time: 1610 us -> 649 us (0.40)
  waiting for transfers between devices: 902 us -> 117 us
  blocking collectives: 206 us -> 0 us
  matrix products: 277 us -> 178 us
  starting transfers between devices: 0.71 us -> 67.6 us
  local copies, waits for them, and re-layouts: 53.6 us -> 110 us
  other arithmetic: 128 us -> 151 us
    reduce_scatter x3 -> x0, waiting for transfers between devices: 404 us -> none  [the longest x1 140 us: body(): lax.psum_scatter(expand_grad, 'dp', scatter_dimension=0, tiled=True)]
    unnamed x16 -> x0, waiting for transfers between devices: 313 us -> none
    ppermute x0 -> x57, waiting for transfers between devices: none -> 117 us  [swap(): return lax.ppermute(array, axis, [(i, i ^ 1 << bit) for i in range(count)])]
    all_gather x3 -> x0, waiting for transfers between devices: 101 us -> none  [the longest x1 53 us: body(): lax.all_gather(reduce_weight.astype(jnp.bfloat16), 'dp', axis=1, tiled=True)]
    psum x4 -> x0, waiting for transfers between devices: 84.4 us -> none  [the longest x1 29.6 us: body(): d_hidden = lax.psum(hidden_part, 'head') + d_res_two]
    psum x2 -> x0, blocking collectives: 82.4 us -> none  [the longest x1 42.1 us: body(): kernel_total = lax.psum(kernel_grad, 'dp')]
    all_gather x2 -> x0, blocking collectives: 79.1 us -> none  [the longest x1 41.2 us: body(): lax.all_gather(mixing_weight.astype(jnp.bfloat16), 'dp', axis=1, tiled=True)]
    ppermute x0 -> x57, starting transfers between devices: none -> 67.6 us  [swap(): return lax.ppermute(array, axis, [(i, i ^ 1 << bit) for i in range(count)])]
  transfers between devices with their start and end apart: 13 -> 57, of which waited for: 11 -> 36; matrix products, arithmetic and copies ran while one was open for 8% -> 24% of each run, Pallas kernels for 0% -> 0%
where the time goes in v1:
time: 649 us; the launch traced here: 638 us
  matrix products  178 us (27%)
  other arithmetic  151 us (23%)
  waiting for transfers between devices  117 us (18%)
  local copies, waits for them, and re-layouts  110 us (17%)
  starting transfers between devices  67.6 us (10%)
  between operations  14.3 us (2%)
    ppermute x57, waiting for transfers between devices, swap(): return lax.ppermute(array, axis, [(i, i ^ 1 << bit) for i in range(count)])  117 us
    ppermute x57, starting transfers between devices, swap(): return lax.ppermute(array, axis, [(i, i ^ 1 << bit) for i in range(count)])  67.6 us
    another operation x34, local copies, waits for them, and re-layouts, conv_backward(): return (grad_values, jnp.stack(kernel_terms, axis=1))  43.5 us
    dot_general x2, matrix products, nystrom(): jnp.einsum('hlr,rhe->hle', last_kernel, value_rows, precision=FAST)  38.2 us
    reduce_sum x5, other arithmetic, conv_backward(): jnp.sum(masked_grad * padded[offset:offset + row_count], axis=(0, 2))  38 us
    unnamed x550, local copies, waits for them, and re-layouts  37.1 us
    dot_general x2, matrix products, nystrom(): return jnp.einsum('hrl,hle->rhe', first_kernel, weighted, precision=FAST)  28.3 us
    select_n x25, other arithmetic, gather_rows(): jnp.where(own >> bit & 1 == 0, jnp.concatenate([current, other], dim), jn...  15.5 us
  transfers between devices with their start and end apart: 57, of which 36 were waited for; matrix products, arithmetic and copies ran while one was open for 24% of the time, Pallas kernels for 0%

profile of v1, /device:TPU:0, one launch (start us, length us, event | category | flops | bytes accessed | tf_op | source)
XLA Modules:
  0.0 637.8 jit_solution(3088291103183419063)
XLA Ops:
  2.3 4.0 collective-permute-start.8
  7.4 3.0 collective-permute-start
  57.9 4.4 collective-permute-done.3
  64.0 3.0 fusion.299
  68.4 3.1 fusion.329
  76.8 3.8 fusion.328
  114.3 23.9 %fusion.29 = bf16[1536,6,64]{0,2,1:T(8,128)(2,1)} fusion(bf16[6,128,64]{2,1,0:T(8,128)(2,1)S(1)} %bitcast.559, f32[1536,6,64]{0,2,1:T(8,128)S(1)} %get-tuple-element.318, f32[6,1536]{1,0:T(8,128)S(1)} %fusion.128, f32[1536]{0:T(1024)S(1)} %copy-done.203, f32[6]{0:T(128)} %get-tuple-element.239, f32[6]{0:T(128)} %get-tuple-element.208, ...), kind=kOutput, calls=%fused_computation.79 | convolution fusion | flops 214106112 | bytes 8683800 | tf_op jit(solution)/shard_map/jvp(hrl,hle->rhe)/dot_general | solution.py:177
  140.1 3.3 collective-permute-done.13
  159.1 2.8 convolution_convert_fusion.3
  162.1 4.4 collective-permute-done.19
  170.0 3.2 copy.410
  173.9 18.1 %collective-permute-done.20 = bf16[2,2,1,2,48,1536]{5,4,3,2,1,0:T(8,128)(2,1)} collective-permute-done((bf16[2,2,1,2,48,1536]{5,4,3,2,1,0:T(8,128)(2,1)}, bf16[2,2,1,2,48,1536]{5,4,3,2,1,0:T(8,128)(2,1)}, u32[]{:S(2)}, u32[]{:S(2)}) %collective-permute-start.20) | collective-permute-done | bytes 1179680 | tf_op jit(solution)/shard_map/ppermute | solution.py:34
  191.9 2.9 maximum_select_fusion
  194.8 3.6 maximum_select_fusion.1
  198.4 4.4 fusion.327
  205.0 4.4 convolution_add_fusion
  209.5 5.4 convolution_convert_fusion.2
  214.9 2.8 copy.440
  219.7 4.7 fusion.325
  225.0 8.4 %fusion.8 = (f32[]{:T(128)}, f32[]{:T(128)}, f32[768]{0:T(1024)S(1)}, f32[1536]{0:T(1024)S(1)}, f32[768]{0:T(1024)S(1)}) fusion(bf16[1536,768]{0,1:T(8,128)(2,1)} %collective-permute-done.25, bf16[1536,768]{0,1:T(8,128)(2,1)} %convolution_convert_fusion.2, f32[1536]{0:T(1024)S(1)} %get-tuple-element.262, f32[768]{0:T(1024)S(1)} %add.755, f32[768]{0:T(1024)S(1)} %add.742, ...), kind=kLoop, calls=%fused_computation.17 | loop fusion | flops 28308478 | bytes 16555016 | tf_op jit(solution)/shard_map/reduce_sum | solution.py:324
  233.4 4.0 fusion.324
  237.5 11.7 %convert_reduce_fusion = (f32[1536]{0:T(1024)}, bf16[1536,1536]{1,0:T(8,128)(2,1)}) fusion(f32[1536,1536]{1,0:T(8,128)S(1)} %bitcast.613, bf16[768,1536]{1,0:T(8,128)(2,1)S(1)} %bitcast.522, f32[1536,768]{0,1:T(8,128)S(1)} %get-tuple-element.313, f32[1536]{0:T(1024)S(1)} %negate_multiply_fusion.1), kind=kOutput, calls=%fused_computation.9 | convolution fusion | flops 3678140928 | bytes 21245952 | tf_op jit(solution)/shard_map/rd,df->rf/dot_general | solution.py:334
  249.2 4.0 fusion.127
  253.8 6.7 %fusion.300 = f32[768,1536]{1,0:T(8,128)S(1)} fusion(bf16[1536,1536]{1,0:T(8,128)(2,1)} %get-tuple-element.407, f32[1536,768]{0,1:T(8,128)S(1)} %bitcast.477, f32[768]{0:T(1024)S(1)} %add.747, f32[768]{0:T(1024)S(1)} %mul.1543, f32[1536]{0:T(1024)S(1)} %fusion.256, f32[1536]{0:T(1024)S(1)} %broadcast_multiply_fusion.1), kind=kOutput, calls=%fused_computation.759 | convolution fusion | flops 3629776896 | bytes 14174208 | tf_op jit(solution)/shard_map/rd,rf->df/dot_general | solution.py:339
  262.2 4.1 convolution_convert_fusion.1
  266.3 15.1 %collective-permute-done.44 = bf16[2,2,1,2,48,1536]{5,4,3,2,1,0:T(8,128)(2,1)S(1)} collective-permute-done((bf16[2,2,1,2,48,1536]{5,4,3,2,1,0:T(8,128)(2,1)S(1)}, bf16[2,2,1,2,48,1536]{5,4,3,2,1,0:T(8,128)(2,1)S(1)}, u32[]{:S(2)}, u32[]{:S(2)}) %collective-permute-start.44) | collective-permute-done | bytes 1179680 | tf_op jit(solution)/shard_map/ppermute | solution.py:34
  282.7 6.9 %collective-permute-done.40 = bf16[2,2,2,1,48,1536]{5,4,3,2,1,0:T(8,128)(2,1)S(1)} collective-permute-done((bf16[2,2,2,1,48,1536]{5,4,3,2,1,0:T(8,128)(2,1)S(1)}, bf16[2,2,2,1,48,1536]{5,4,3,2,1,0:T(8,128)(2,1)S(1)}, u32[]{:S(2)}, u32[]{:S(2)}) %collective-permute-start.40) | collective-permute-done | bytes 1179680 | tf_op jit(solution)/shard_map/ppermute | solution.py:34
  291.3 9.7 %collective-permute-done.45 = bf16[2,2,1,1,48,1536]{5,4,3,2,1,0:T(8,128)(2,1)S(1)} collective-permute-done((bf16[2,2,1,1,48,1536]{5,4,3,2,1,0:T(8,128)(2,1)S(1)}, bf16[2,2,1,1,48,1536]{5,4,3,2,1,0:T(8,128)(2,1)S(1)}, u32[]{:S(2)}, u32[]{:S(2)}) %collective-permute-start.45) | collective-permute-done | bytes 589856 | tf_op jit(solution)/shard_map/ppermute | solution.py:34
  305.2 6.0 collective-permute-done.46
  311.3 2.9 collective-permute-start.47
  314.2 4.3 collective-permute-done.42
  322.5 4.5 collective-permute-done.43
  327.7 4.0 multiply_reduce_fusion.1
  366.2 6.4 %multiply_reduce_fusion.11 = (f32[6]{0:T(128)}, f32[6]{0:T(128)}, f32[6]{0:T(128)}, f32[6]{0:T(128)}, f32[6]{0:T(128)}, /*index=5*/f32[1536,6,64]{0,2,1:T(8,128)...) fusion(f32[1536,6,64]{0,2,1:T(8,128)S(1)} %copy-done.2, ...), kind=kLoop, calls=%fused_computation.189 | loop fusion | flops 8847330 | bytes 16522872 | tf_op jit(solution)/shard_map/reduce_sum | solution.py:205
  372.8 10.1 %multiply_reduce_fusion.10 = (f32[6]{0:T(128)}, f32[6]{0:T(128)}, f32[6]{0:T(128)}, f32[6]{0:T(128)}, f32[6]{0:T(128)}, /*index=5*/f32[6]{0:T(128)}, f32[6]{0:T(...) fusion(f32[1536,6,64]{0,2,1:T(8,128)S(1)} %copy-done.2, ...), kind=kLoop, calls=%fused_computation.188 | loop fusion | flops 15925194 | bytes 25966296 | tf_op jit(solution)/shard_map/reduce_sum | solution.py:205
  383.0 10.3 %multiply_reduce_fusion.8 = (f32[6]{0:T(128)}, f32[6]{0:T(128)}, f32[6]{0:T(128)}, f32[6]{0:T(128)}, f32[6]{0:T(128)}, /*index=5*/f32[6]{0:T(128)}, f32[6]{0:T(1...) fusion(f32[1536,6,64]{0,2,1:T(8,128)S(1)} %copy-done.2, ...), kind=kLoop, calls=%fused_computation.186 | loop fusion | flops 15925194 | bytes 25966296 | tf_op jit(solution)/shard_map/reduce_sum | solution.py:205
  393.4 10.6 %multiply_reduce_fusion.9 = (f32[6]{0:T(128)}, f32[6]{0:T(128)}, f32[6]{0:T(128)}, f32[6]{0:T(128)}, f32[6]{0:T(128)}, /*index=5*/f32[6]{0:T(128)}, f32[6]{0:T(1...) fusion(f32[1536,6,64]{0,2,1:T(8,128)S(1)} %copy-done.2, ...), kind=kLoop, calls=%fused_computation.187 | loop fusion | flops 15925194 | bytes 25966296 | tf_op jit(solution)/shard_map/reduce_sum | solution.py:205
  405.0 5.4 convert_reduce_fusion.1
  415.0 4.4 convert_reduce_fusion.2
  419.5 3.9 fusion.321
  431.2 32.9 %fusion.32 = bf16[1536,1,6,64]{0,3,2,1:T(8,128)(2,1)} fusion(bf16[6,128,64]{2,1,0:T(8,128)(2,1)S(1)} %bitcast.562, f32[1536,6,64]{0,2,1:T(8,128)} %get-tuple-element.271, f32[1536,6,64]{0,2,1:T(8,128)} %get-tuple-element.270, f32[1536,6,64]{0,2,1:T(8,128)} %get-tuple-element.294, f32[1536,6,64]{0,2,1:T(8,128)} %get-tuple-element.293, ...), kind=kOutput, calls=%fused_computation.82 | convolution fusion | flops 194641920 | bytes 84058392 | tf_op jit(solution)/shard_map/transpose(jvp(hlr,rhe->hle))/dot_general | solution.py:171
  468.1 5.1 convolution_bitcast_fusion
  526.0 3.5 fusion.345
  562.7 2.9 collective-permute-done.39
  594.7 6.0 copy.510
  602.6 6.1 convolution_convert_fusion
  624.2 6.2 add_add_fusion.2
  630.4 6.0 copy.511
  (987 shorter events, 306.2 us)
Async XLA Ops:
  2.3 24.5 %collective-permute-start.8 = (bf16[1,1,1,1,1,432]{5,0,4,3,2,1:T(2,128)(2,1)S(1)}, bf16[1,1,1,1,1,432]{5,0,4,3,2,1:T(2,128)(2,1)S(1)}, u32[]{:S(2)}, u32[]{:S(2)}) collective-permute-start(bf16[1,1,1,1,1,432]{5,0,4,3,2,1:T(2,128)(2,1)S(1)} %pad_maximum_fusion.10), channel_id=1, source_target_pairs={{0,16},{2,18},{4,20},{6,22},{8,24},{10,26},{12,28},{14,30},{16,0},... | collective-permute-start | bytes 2600 | tf_op jit(solution)/shard_map/ppermute | solution.py:34
  7.3 30.6 %collective-permute-start.4 = (bf16[1,1,1,1,48,512]{5,4,3,2,1,0:T(8,128)(2,1)S(1)}, bf16[1,1,1,1,48,512]{5,4,3,2,1,0:T(8,128)(2,1)S(1)}, u32[]{:S(2)}, u32[]{:S(2)}) collective-permute-start(bf16[1,1,1,1,48,512]{5,4,3,2,1,0:T(8,128)(2,1)S(1)} %get-tuple-element.348), channel_id=1, source_target_pairs={{0,16},{2,18},{4,20},{6,22},{8,24},{10,26},{12,28},{14,30},{16,0},... | collective-permute-start | bytes 147464 | tf_op jit(solution)/shard_map/ppermute | solution.py:34
  7.4 32.2 %collective-permute-start = (bf16[1,1,1,1,48,640]{5,4,3,2,1,0:T(8,128)(2,1)S(1)}, bf16[1,1,1,1,48,640]{5,4,3,2,1,0:T(8,128)(2,1)S(1)}, u32[]{:S(2)}, u32[]{:S(2)}) collective-permute-start(bf16[1,1,1,1,48,640]{5,4,3,2,1,0:T(8,128)(2,1)S(1)} %get-tuple-element.346), channel_id=1, source_target_pairs={{0,16},{2,18},{4,20},{6,22},{8,24},{10,26},{12,28},{14,30},{16,0},... | collective-permute-start | bytes 184328 | tf_op jit(solution)/shard_map/ppermute | solution.py:34
  38.0 4.7 collective-permute-start.5
  39.7 4.9 collective-permute-start.1
  42.7 5.7 collective-permute-start.6
  44.7 7.6 %collective-permute-start.2 = (bf16[2,2,1,1,48,640]{5,4,3,2,1,0:T(8,128)(2,1)S(1)}, bf16[2,2,1,1,48,640]{5,4,3,2,1,0:T(8,128)(2,1)S(1)}, u32[]{:S(2)}, u32[]{:S(2)}) collective-permute-start(bf16[2,2,1,1,48,640]{5,4,3,2,1,0:T(8,128)(2,1)S(1)} %maximum_select_fusion.19), channel_id=1, source_target_pairs={{0,4},{2,6},{4,0},{6,2},{8,12},{10,14},{12,8},{14,10},{16,20},{18,... | collective-permute-start | bytes 737288 | tf_op jit(solution)/shard_map/ppermute | solution.py:34
  48.5 8.2 %collective-permute-start.7 = (bf16[2,2,1,2,48,512]{5,4,3,2,1,0:T(8,128)(2,1)S(1)}, bf16[2,2,1,2,48,512]{5,4,3,2,1,0:T(8,128)(2,1)}, u32[]{:S(2)}, u32[]{:S(2)}) collective-permute-start(bf16[2,2,1,2,48,512]{5,4,3,2,1,0:T(8,128)(2,1)S(1)} %maximum_select_fusion.12), channel_id=1, source_target_pairs={{0,4},{2,6},{4,0},{6,2},{8,12},{10,14},{12,8},{14,10},{16,20},{18,... | collective-permute-start | bytes 1179656 | tf_op jit(solution)/shard_map/ppermute | solution.py:34
  53.2 9.1 %collective-permute-start.3 = (bf16[2,2,2,1,48,640]{5,4,3,2,1,0:T(8,128)(2,1)}, bf16[2,2,2,1,48,640]{5,4,3,2,1,0:T(8,128)(2,1)}, u32[]{:S(2)}, u32[]{:S(2)}) collective-permute-start(bf16[2,2,2,1,48,640]{5,4,3,2,1,0:T(8,128)(2,1)} %maximum_select_fusion.11), channel_id=1, source_target_pairs={{0,2},{2,0},{4,6},{6,4},{8,10},{10,8},{12,14},{14,12},{16,18},{18,... | collective-permute-start | bytes 1474568 | tf_op jit(solution)/shard_map/ppermute | solution.py:34
  71.5 66.7 %collective-permute-start.12 = (bf16[1,1,1,1,48,384]{5,4,3,2,1,0:T(8,128)(2,1)S(1)}, bf16[1,1,1,1,48,384]{5,4,3,2,1,0:T(8,128)(2,1)S(1)}, u32[]{:S(2)}, u32[]{:S(2)}) collective-permute-start(bf16[1,1,1,1,48,384]{5,4,3,2,1,0:T(8,128)(2,1)S(1)} %bitcast.552), channel_id=1, source_target_pairs={{0,16},{2,18},{4,20},{6,22},{8,24},{10,26},{12,28},{14,30},{16,0},... | collective-permute-start | bytes 110600 | tf_op jit(solution)/shard_map/ppermute | solution.py:34
  71.7 73.6 %collective-permute-start.21 = (bf16[1,1,1,1,48,1536]{5,4,3,2,1,0:T(8,128)(2,1)}, bf16[1,1,1,1,48,1536]{5,4,3,2,1,0:T(8,128)(2,1)}, u32[]{:S(2)}, u32[]{:S(2)}) collective-permute-start(bf16[1,1,1,1,48,1536]{5,4,3,2,1,0:T(8,128)(2,1)} %bitcast.69), channel_id=1, source_target_pairs={{0,16},{2,18},{4,20},{6,22},{8,24},{10,26},{12,28},{14,30},{16,0},... | collective-permute-start | bytes 442376 | tf_op jit(solution)/shard_map/ppermute | solution.py:34
  74.4 73.8 %collective-permute-start.17 = (bf16[1,1,1,1,48,1536]{5,4,3,2,1,0:T(8,128)(2,1)}, bf16[1,1,1,1,48,1536]{5,4,3,2,1,0:T(8,128)(2,1)}, u32[]{:S(2)}, u32[]{:S(2)}) collective-permute-start(bf16[1,1,1,1,48,1536]{5,4,3,2,1,0:T(8,128)(2,1)} %bitcast.60), channel_id=1, source_target_pairs={{0,16},{2,18},{4,20},{6,22},{8,24},{10,26},{12,28},{14,30},{16,0},... | collective-permute-start | bytes 442376 | tf_op jit(solution)/shard_map/ppermute | solution.py:34
  138.2 5.3 collective-permute-start.13
  143.5 8.7 %collective-permute-start.14 = (bf16[2,2,1,1,48,384]{5,4,3,2,1,0:T(8,128)(2,1)S(1)}, bf16[2,2,1,1,48,384]{5,4,3,2,1,0:T(8,128)(2,1)S(1)}, u32[]{:S(2)}, u32[]{:S(2)}) collective-permute-start(bf16[2,2,1,1,48,384]{5,4,3,2,1,0:T(8,128)(2,1)S(1)} %maximum_select_fusion.23), channel_id=1, source_target_pairs={{0,4},{2,6},{4,0},{6,2},{8,12},{10,14},{12,8},{14,10},{16,20},{18,... | collective-permute-start | bytes 442376 | tf_op jit(solution)/shard_map/ppermute | solution.py:34
  146.5 6.8 %collective-permute-start.22 = (bf16[2,1,1,1,48,1536]{5,4,3,2,1,0:T(8,128)(2,1)S(1)}, bf16[2,1,1,1,48,1536]{5,4,3,2,1,0:T(8,128)(2,1)S(1)}, u32[]{:S(2)}, u32[]{:S(2)}) collective-permute-start(bf16[2,1,1,1,48,1536]{5,4,3,2,1,0:T(8,128)(2,1)S(1)} %maximum_select_fusion.17), channel_id=1, source_target_pairs={{0,8},{2,10},{4,12},{6,14},{8,0},{10,2},{12,4},{14,6},{16,24},{18,... | collective-permute-start | bytes 884744 | tf_op jit(solution)/shard_map/ppermute | solution.py:34
  149.4 7.0 %collective-permute-start.18 = (bf16[2,1,1,1,48,1536]{5,4,3,2,1,0:T(8,128)(2,1)S(1)}, bf16[2,1,1,1,48,1536]{5,4,3,2,1,0:T(8,128)(2,1)S(1)}, u32[]{:S(2)}, u32[]{:S(2)}) collective-permute-start(bf16[2,1,1,1,48,1536]{5,4,3,2,1,0:T(8,128)(2,1)S(1)} %maximum_select_fusion.15), channel_id=1, source_target_pairs={{0,8},{2,10},{4,12},{6,14},{8,0},{10,2},{12,4},{14,6},{16,24},{18,... | collective-permute-start | bytes 884744 | tf_op jit(solution)/shard_map/ppermute | solution.py:34
  152.3 6.8 %collective-permute-start.15 = (bf16[2,2,2,1,48,384]{5,4,3,2,1,0:T(8,128)(2,1)S(1)}, bf16[2,2,2,1,48,384]{5,4,3,2,1,0:T(8,128)(2,1)S(1)}, u32[]{:S(2)}, u32[]{:S(2)}) collective-permute-start(bf16[2,2,2,1,48,384]{5,4,3,2,1,0:T(8,128)(2,1)S(1)} %maximum_select_fusion.13), channel_id=1, source_target_pairs={{0,2},{2,0},{4,6},{6,4},{8,10},{10,8},{12,14},{14,12},{16,18},{18,... | collective-permute-start | bytes 884744 | tf_op jit(solution)/shard_map/ppermute | solution.py:34
  153.4 14.6 %collective-permute-start.23 = (bf16[2,2,1,1,48,1536]{5,4,3,2,1,0:T(8,128)(2,1)S(1)}, bf16[2,2,1,1,48,1536]{5,4,3,2,1,0:T(8,128)(2,1)S(1)}, u32[]{:S(2)}, u32[]{:S(2)}) collective-permute-start(bf16[2,2,1,1,48,1536]{5,4,3,2,1,0:T(8,128)(2,1)S(1)} %maximum_select_fusion.10), channel_id=1, source_target_pairs={{0,4},{2,6},{4,0},{6,2},{8,12},{10,14},{12,8},{14,10},{16,20},{18,... | collective-permute-start | bytes 1769480 | tf_op jit(solution)/shard_map/ppermute | solution.py:34
  156.5 9.9 %collective-permute-start.19 = (bf16[2,2,1,1,48,1536]{5,4,3,2,1,0:T(8,128)(2,1)S(1)}, bf16[2,2,1,1,48,1536]{5,4,3,2,1,0:T(8,128)(2,1)S(1)}, u32[]{:S(2)}, u32[]{:S(2)}) collective-permute-start(bf16[2,2,1,1,48,1536]{5,4,3,2,1,0:T(8,128)(2,1)S(1)} %maximum_select_fusion.8), channel_id=1, source_target_pairs={{0,2},{2,0},{4,6},{6,4},{8,10},{10,8},{12,14},{14,12},{16,18},{18,... | collective-permute-start | bytes 1769480 | tf_op jit(solution)/shard_map/ppermute | solution.py:34
  162.0 36.4 %collective-permute-start.16 = (bf16[1536,768]{0,1:T(8,128)(2,1)}, bf16[1536,768]{0,1:T(8,128)(2,1)}, u32[]{:S(2)}, u32[]{:S(2)}) collective-permute-start(bf16[1536,768]{0,1:T(8,128)(2,1)} %convolution_convert_fusion.3), channel_id=1, source_target_pairs={{0,1},{1,0},{2,3},{3,2},{4,5},{5,4},{6,7},{7,6},{8,9},{9,8},{10,11... | collective-permute-start | bytes 7077896 | tf_op jit(solution)/shard_map/ppermute | solution.py:34
  167.6 24.3 %collective-permute-start.20 = (bf16[2,2,1,2,48,1536]{5,4,3,2,1,0:T(8,128)(2,1)}, bf16[2,2,1,2,48,1536]{5,4,3,2,1,0:T(8,128)(2,1)}, u32[]{:S(2)}, u32[]{:S(2)}) collective-permute-start(bf16[2,2,1,2,48,1536]{5,4,3,2,1,0:T(8,128)(2,1)} %maximum_select_fusion.2), channel_id=1, source_target_pairs={{0,4},{2,6},{4,0},{6,2},{8,12},{10,14},{12,8},{14,10},{16,20},{18,... | collective-permute-start | bytes 3538952 | tf_op jit(solution)/shard_map/ppermute | solution.py:34
  169.1 25.7 %collective-permute-start.24 = (bf16[2,2,2,1,48,1536]{5,4,3,2,1,0:T(8,128)(2,1)}, bf16[2,2,2,1,48,1536]{5,4,3,2,1,0:T(8,128)(2,1)}, u32[]{:S(2)}, u32[]{:S(2)}) collective-permute-start(bf16[2,2,2,1,48,1536]{5,4,3,2,1,0:T(8,128)(2,1)} %maximum_select_fusion.3), channel_id=1, source_target_pairs={{0,2},{2,0},{4,6},{6,4},{8,10},{10,8},{12,14},{14,12},{16,18},{18,... | collective-permute-start | bytes 3538952 | tf_op jit(solution)/shard_map/ppermute | solution.py:34
  214.9 4.9 collective-permute-start.25
  253.4 28.1 %collective-permute-start.44 = (bf16[2,2,1,2,48,1536]{5,4,3,2,1,0:T(8,128)(2,1)S(1)}, bf16[2,2,1,2,48,1536]{5,4,3,2,1,0:T(8,128)(2,1)S(1)}, u32[]{:S(2)}, u32[]{:S(2)}) collective-permute-start(bf16[2,2,1,2,48,1536]{5,4,3,2,1,0:T(8,128)(2,1)S(1)} %dynamic-slice_convert_fusion), channel_id=1, source_target_pairs={{0,4},{2,6},{4,0},{6,2},{8,12},{10,14},{12,8},{14,10},{16,20},{18,... | collective-permute-start | bytes 3538952 | tf_op jit(solution)/shard_map/ppermute | solution.py:34
  260.7 28.9 %collective-permute-start.40 = (bf16[2,2,2,1,48,1536]{5,4,3,2,1,0:T(8,128)(2,1)S(1)}, bf16[2,2,2,1,48,1536]{5,4,3,2,1,0:T(8,128)(2,1)S(1)}, u32[]{:S(2)}, u32[]{:S(2)}) collective-permute-start(bf16[2,2,2,1,48,1536]{5,4,3,2,1,0:T(8,128)(2,1)S(1)} %dynamic-slice_convert_fusion.1), channel_id=1, source_target_pairs={{0,2},{2,0},{4,6},{6,4},{8,10},{10,8},{12,14},{14,12},{16,18},{18,... | collective-permute-start | bytes 3538952 | tf_op jit(solution)/shard_map/ppermute | solution.py:34
  266.2 61.4 %collective-permute-start.26 = (bf16[1536,768]{0,1:T(8,128)(2,1)S(1)}, bf16[1536,768]{0,1:T(8,128)(2,1)S(1)}, u32[]{:S(2)}, u32[]{:S(2)}) collective-permute-start(bf16[1536,768]{0,1:T(8,128)(2,1)S(1)} %convolution_convert_fusion.1), channel_id=1, source_target_pairs={{0,1},{1,0},{2,3},{3,2},{4,5},{5,4},{6,7},{7,6},{8,9},{9,8},{10,11... | collective-permute-start | bytes 7077896 | tf_op jit(solution)/shard_map/ppermute | solution.py:34
  281.9 19.1 %collective-permute-start.45 = (bf16[2,2,1,1,48,1536]{5,4,3,2,1,0:T(8,128)(2,1)S(1)}, bf16[2,2,1,1,48,1536]{5,4,3,2,1,0:T(8,128)(2,1)S(1)}, u32[]{:S(2)}, u32[]{:S(2)}) collective-permute-start(bf16[2,2,1,1,48,1536]{5,4,3,2,1,0:T(8,128)(2,1)S(1)} %dynamic-slice_convert_fusion.2), channel_id=1, source_target_pairs={{0,2},{2,0},{4,6},{6,4},{8,10},{10,8},{12,14},{14,12},{16,18},{18,... | collective-permute-start | bytes 1769480 | tf_op jit(solution)/shard_map/ppermute | solution.py:34
  290.0 13.2 %collective-permute-start.41 = (bf16[2,2,1,1,48,1536]{5,4,3,2,1,0:T(8,128)(2,1)S(1)}, bf16[2,2,1,1,48,1536]{5,4,3,2,1,0:T(8,128)(2,1)S(1)}, u32[]{:S(2)}, u32[]{:S(2)}) collective-permute-start(bf16[2,2,1,1,48,1536]{5,4,3,2,1,0:T(8,128)(2,1)S(1)} %dynamic-slice_convert_fusion.3), channel_id=1, source_target_pairs={{0,4},{2,6},{4,0},{6,2},{8,12},{10,14},{12,8},{14,10},{16,20},{18,... | collective-permute-start | bytes 1769480 | tf_op jit(solution)/shard_map/ppermute | solution.py:34
  301.2 10.0 %collective-permute-start.46 = (bf16[2,1,1,1,48,1536]{5,4,3,2,1,0:T(8,128)(2,1)S(1)}, bf16[2,1,1,1,48,1536]{5,4,3,2,1,0:T(8,128)(2,1)S(1)}, u32[]{:S(2)}, u32[]{:S(2)}) collective-permute-start(bf16[2,1,1,1,48,1536]{5,4,3,2,1,0:T(8,128)(2,1)S(1)} %dynamic-slice_convert_fusion.6), channel_id=1, source_target_pairs={{0,8},{2,10},{4,12},{6,14},{8,0},{10,2},{12,4},{14,6},{16,24},{18,... | collective-permute-start | bytes 884744 | tf_op jit(solution)/shard_map/ppermute | solution.py:34
  303.4 15.2 %collective-permute-start.42 = (bf16[2,1,1,1,48,1536]{5,4,3,2,1,0:T(8,128)(2,1)S(1)}, bf16[2,1,1,1,48,1536]{5,4,3,2,1,0:T(8,128)(2,1)S(1)}, u32[]{:S(2)}, u32[]{:S(2)}) collective-permute-start(bf16[2,1,1,1,48,1536]{5,4,3,2,1,0:T(8,128)(2,1)S(1)} %dynamic-slice_convert_fusion.7), channel_id=1, source_target_pairs={{0,8},{2,10},{4,12},{6,14},{8,0},{10,2},{12,4},{14,6},{16,24},{18,... | collective-permute-start | bytes 884744 | tf_op jit(solution)/shard_map/ppermute | solution.py:34
  311.3 10.5 %collective-permute-start.47 = (bf16[1,1,1,1,48,1536]{5,4,3,2,1,0:T(8,128)(2,1)S(1)}, bf16[1,1,1,1,48,1536]{5,4,3,2,1,0:T(8,128)(2,1)S(1)}, u32[]{:S(2)}, u32[]{:S(2)}) collective-permute-start(bf16[1,1,1,1,48,1536]{5,4,3,2,1,0:T(8,128)(2,1)S(1)} %dynamic-slice_convert_fusion.11), channel_id=1, source_target_pairs={{0,16},{2,18},{4,20},{6,22},{8,24},{10,26},{12,28},{14,30},{16,0},... | collective-permute-start | bytes 442376 | tf_op jit(solution)/shard_map/ppermute | solution.py:34
  318.6 8.3 %collective-permute-start.43 = (bf16[1,1,1,1,48,1536]{5,4,3,2,1,0:T(8,128)(2,1)S(1)}, bf16[1,1,1,1,48,1536]{5,4,3,2,1,0:T(8,128)(2,1)S(1)}, u32[]{:S(2)}, u32[]{:S(2)}) collective-permute-start(bf16[1,1,1,1,48,1536]{5,4,3,2,1,0:T(8,128)(2,1)S(1)} %dynamic-slice_convert_fusion.12), channel_id=1, source_target_pairs={{0,16},{2,18},{4,20},{6,22},{8,24},{10,26},{12,28},{14,30},{16,0},... | collective-permute-start | bytes 442376 | tf_op jit(solution)/shard_map/ppermute | solution.py:34
  524.6 4.9 collective-permute-start.48
  531.7 17.4 %collective-permute-start.36 = (bf16[2,2,2,1,48,384]{5,4,3,2,1,0:T(8,128)(2,1)}, bf16[2,2,2,1,48,384]{5,4,3,2,1,0:T(8,128)(2,1)}, u32[]{:S(2)}, u32[]{:S(2)}) collective-permute-start(bf16[2,2,2,1,48,384]{5,4,3,2,1,0:T(8,128)(2,1)} %dynamic-slice_convert_fusion.8), channel_id=1, source_target_pairs={{0,2},{2,0},{4,6},{6,4},{8,10},{10,8},{12,14},{14,12},{16,18},{18,... | collective-permute-start | bytes 884744 | tf_op jit(solution)/shard_map/ppermute | solution.py:34
  535.4 16.4 %collective-permute-start.32 = (bf16[2,2,1,2,48,512]{5,4,3,2,1,0:T(8,128)(2,1)}, bf16[2,2,1,2,48,512]{5,4,3,2,1,0:T(8,128)(2,1)}, u32[]{:S(2)}, u32[]{:S(2)}) collective-permute-start(bf16[2,2,1,2,48,512]{5,4,3,2,1,0:T(8,128)(2,1)} %dynamic-slice_convert_fusion.5), channel_id=1, source_target_pairs={{0,4},{2,6},{4,0},{6,2},{8,12},{10,14},{12,8},{14,10},{16,20},{18,... | collective-permute-start | bytes 1179656 | tf_op jit(solution)/shard_map/ppermute | solution.py:34
  537.4 5.1 collective-permute-start.51
  539.9 16.6 %collective-permute-start.28 = (bf16[2,2,2,1,48,640]{5,4,3,2,1,0:T(8,128)(2,1)}, bf16[2,2,2,1,48,640]{5,4,3,2,1,0:T(8,128)(2,1)}, u32[]{:S(2)}, u32[]{:S(2)}) collective-permute-start(bf16[2,2,2,1,48,640]{5,4,3,2,1,0:T(8,128)(2,1)} %dynamic-slice_convert_fusion.4), channel_id=1, source_target_pairs={{0,2},{2,0},{4,6},{6,4},{8,10},{10,8},{12,14},{14,12},{16,18},{18,... | collective-permute-start | bytes 1474568 | tf_op jit(solution)/shard_map/ppermute | solution.py:34
  550.6 5.2 collective-permute-start.37
  553.2 13.1 %collective-permute-start.33 = (bf16[2,2,1,1,48,512]{5,4,3,2,1,0:T(8,128)(2,1)S(1)}, bf16[2,2,1,1,48,512]{5,4,3,2,1,0:T(8,128)(2,1)S(1)}, u32[]{:S(2)}, u32[]{:S(2)}) collective-permute-start(bf16[2,2,1,1,48,512]{5,4,3,2,1,0:T(8,128)(2,1)S(1)} %dynamic-slice_convert_fusion.10), channel_id=1, source_target_pairs={{0,2},{2,0},{4,6},{6,4},{8,10},{10,8},{12,14},{14,12},{16,18},{18,... | collective-permute-start | bytes 589832 | tf_op jit(solution)/shard_map/ppermute | solution.py:34
  560.3 5.3 collective-permute-start.39
  561.8 6.3 collective-permute-start.29
  566.3 4.7 collective-permute-start.34
  568.1 4.9 collective-permute-start.30
  571.1 5.6 collective-permute-start.35
  573.1 5.2 collective-permute-start.31
  593.0 7.7 %collective-permute-start.55 = (f32[1,128]{1,0:T(1,128)S(1)}, f32[1,128]{1,0:T(1,128)}, u32[]{:S(2)}, u32[]{:S(2)}) collective-permute-start(f32[1,128]{1,0:T(1,128)S(1)} %add.844), channel_id=1, source_target_pairs={{0,8},{2,10},{4,12},{6,14},{8,0},{10,2},{12,4},{14,6},{16,24},{18,... | collective-permute-start | bytes 1544 | tf_op jit(solution)/shard_map/ppermute | solution.py:34
  601.4 7.4 %collective-permute-start.56 = (f32[1,128]{1,0:T(1,128)S(1)}, f32[1,128]{1,0:T(1,128)S(1)}, u32[]{:S(2)}, u32[]{:S(2)}) collective-permute-start(f32[1,128]{1,0:T(1,128)S(1)} %add.845), channel_id=1, source_target_pairs={{0,16},{2,18},{4,20},{6,22},{8,24},{10,26},{12,28},{14,30},{16,0},... | collective-permute-start | bytes 1544 | tf_op jit(solution)/shard_map/ppermute | solution.py:34
  608.8 15.5 %collective-permute-start.27 = (bf16[1536,768]{0,1:T(8,128)(2,1)}, bf16[1536,768]{0,1:T(8,128)(2,1)S(1)}, u32[]{:S(2)}, u32[]{:S(2)}) collective-permute-start(bf16[1536,768]{0,1:T(8,128)(2,1)} %convolution_convert_fusion), channel_id=1, source_target_pairs={{0,1},{1,0},{2,3},{3,2},{4,5},{5,4},{6,7},{7,6},{8,9},{9,8},{10,11... | collective-permute-start | bytes 7077896 | tf_op jit(solution)/shard_map/ppermute | solution.py:34
  (282 other events, 2266.4 us)

commit v2 on v0

v2 whole, which is shorter than its diff:
```python
import jax
import jax.numpy as jnp
from jax import lax
from jax.experimental import pallas as pl
from jax.experimental.pallas import tpu as pltpu
from jax.sharding import PartitionSpec as P

HEAD_DIM = 64
LANDMARKS = 64
PINV_STEPS = 6
ROUGH_STEPS = 4
TAPS = 33
NORM_EPS = 1e-05
CLIP_NORM = 1.0
CLIP_EPS = 1e-06
BETA_ONE = 0.9
BETA_TWO = 0.98
ADAM_EPS = 1e-08
RATE_MATRIX = 0.04
RATE_VECTOR = 0.5
WEIGHT_DECAY = 0.01
CORRECT_ONE = 1.0 - BETA_ONE**5
CORRECT_TWO = 1.0 - BETA_TWO**5

def bits_of(count):
    bit_count = 0
    while (1 << bit_count) < count:
        bit_count += 1
    return bit_count


def swap(array, axis, count, bit):
    return lax.ppermute(array, axis, [(i, i ^ (1 << bit)) for i in range(count)])


def gather_rows(array, count, order):
    bit_count = bits_of(count)
    own = lax.axis_index("dp")
    current = array.reshape((1,) * bit_count + array.shape)
    for bit in order:
        dim = bit_count - 1 - bit
        other = swap(current, "dp", count, bit)
        current = jnp.where(
            (own >> bit) & 1 == 0,
            jnp.concatenate([current, other], dim),
            jnp.concatenate([other, current], dim),
        )
    return current.reshape((count * array.shape[0],) + array.shape[1:])


def after(array, *others):
    return lax.optimization_barrier((array,) + others)[0]


class Scatter:
    def __init__(self, array, count, order):
        self.count = count
        self.order = list(order)
        self.shape = (array.shape[0] // count,) + array.shape[1:]
        self.current = array.reshape((2,) * bits_of(count) + self.shape)
        self.sent = self.kept = self.received = None

    def send(self):
        if self.order:
            bit = self.order.pop(0)
            dim = bits_of(self.count) - 1 - bit
            mine = (lax.axis_index("dp") >> bit) & 1
            self.sent = lax.dynamic_slice_in_dim(self.current, 1 - mine, 1, dim)
            self.sent = self.sent.astype(jnp.bfloat16)
            self.kept = lax.dynamic_slice_in_dim(self.current, mine, 1, dim)
            self.received = swap(self.sent, "dp", self.count, bit)
        return self

    def take(self, *others):
        if self.received is not None:
            received = after(self.received, *others) if others else self.received
            self.current = self.kept.astype(jnp.float32) + received.astype(jnp.float32)
            self.received = None
        return self

    def merge(self, *others):
        merged = Scatter.__new__(Scatter)
        merged.count, merged.order = self.count, list(self.order)
        every = (self,) + others
        merged.current = jnp.concatenate([one.take().current for one in every], axis=-1)
        merged.shape = self.shape[:-1] + (merged.current.shape[-1],)
        merged.sent = merged.kept = merged.received = None
        return merged

    def finish(self):
        self.take()
        while self.order:
            self.send().take()
        return self.current.reshape(self.shape).astype(jnp.float32)


def sum_all(array, axis, count):
    for bit in range(bits_of(count)):
        array = array + swap(array, axis, count, bit)
    return array


def row_items(unit_pair, row_count, mark_count):
    position = lax.iota(jnp.int32, row_count)
    first_end = unit_pair[0] * mark_count
    second_end = first_end + unit_pair[1] * mark_count
    return jnp.where(position < first_end, 0, jnp.where(position < second_end, 1, 2)).astype(
        jnp.int32
    )


NEGATIVE = -1e30
SCORE_SCALE = 0.125
BLOCK = 128
CHUNK = 256


def dot_with(left, right, left_dim, right_dim):
    return lax.dot_general(
        left, right, (((left_dim,), (right_dim,)), ((), ())), preferred_element_type=jnp.float32
    )


def halves(array):
    high = array.astype(jnp.bfloat16)
    return high, (array - high.astype(jnp.float32)).astype(jnp.bfloat16)


def dot_fine(left, right, left_dim, right_dim):
    left_high, left_low = halves(left)
    right_high, right_low = halves(right)
    return dot_with(
        jnp.concatenate([left_high, left_high, left_low], axis=left_dim),
        jnp.concatenate([right_high, right_low, right_high], axis=right_dim),
        left_dim,
        right_dim,
    )


def dot_low(left, right, left_dim, right_dim):
    return dot_with(left.astype(jnp.bfloat16), right.astype(jnp.bfloat16), left_dim, right_dim)


def item_ends(units_ref):
    first_end = units_ref[0, 0] * LANDMARKS
    return first_end, first_end + units_ref[0, 1] * LANDMARKS


def lane_items(units_ref, row_count):
    first_end, second_end = item_ends(units_ref)
    position = lax.broadcasted_iota(jnp.int32, (1, row_count), 1)
    first = (position < first_end).astype(jnp.float32)
    inside = (position < second_end).astype(jnp.float32)
    return first, inside - first, inside


def landmark_columns(units_ref):
    first_end, second_end = item_ends(units_ref)
    mark = lax.broadcasted_iota(jnp.int32, (2 * LANDMARKS, 1), 0)
    is_first = mark < LANDMARKS
    units = jnp.where(is_first, units_ref[0, 0], units_ref[0, 1])
    start = jnp.where(is_first, 0, first_end)
    low = start + jnp.where(is_first, mark, mark - LANDMARKS) * units
    return is_first, start, jnp.where(is_first, first_end, second_end), low, low + units


def select_matrix(units_ref, row_count):
    _, _, _, low, high = landmark_columns(units_ref)
    position = lax.broadcasted_iota(jnp.int32, (2 * LANDMARKS, row_count), 1)
    return ((position >= low) & (position < high)).astype(jnp.float32).astype(jnp.bfloat16)


def inverse_units(units_ref):
    lane = lax.broadcasted_iota(jnp.int32, (1, 2 * LANDMARKS), 1)
    units = jnp.where(lane < LANDMARKS, units_ref[0, 0], units_ref[0, 1]).astype(jnp.float32)
    return 1.0 / units


def same_item(size):
    row = lax.broadcasted_iota(jnp.int32, (size, size), 0)
    column = lax.broadcasted_iota(jnp.int32, (size, size), 1)
    return (row < LANDMARKS) == (column < LANDMARKS)


def scaled_eye(size, value):
    row = lax.broadcasted_iota(jnp.int32, (size, size), 0)
    column = lax.broadcasted_iota(jnp.int32, (size, size), 1)
    return jnp.where(row == column, value, 0.0)


def column_peaks(matrix):
    sums = jnp.sum(matrix, axis=0, keepdims=True)
    lane = lax.broadcasted_iota(jnp.int32, sums.shape, 1)
    first = jnp.max(jnp.where(lane < LANDMARKS, sums, NEGATIVE), axis=1, keepdims=True)
    second = jnp.max(jnp.where(lane < LANDMARKS, NEGATIVE, sums), axis=1, keepdims=True)
    return sums, jnp.where(lane < LANDMARKS, first, second)


def fill_windows(window_ref, rows, first, second):
    row_count = rows.shape[1]
    lane = lax.broadcasted_iota(jnp.int32, (1, BLOCK), 1)
    before = (lane >= BLOCK - 16).astype(jnp.float32).astype(jnp.bfloat16)
    behind = (lane < 16).astype(jnp.float32).astype(jnp.bfloat16)
    block_count = row_count // BLOCK
    for item, mask in ((0, first), (1, second)):
        kept = rows * mask.astype(jnp.bfloat16)
        for block in range(block_count):
            at = block * BLOCK
            edge = jnp.zeros((rows.shape[0], BLOCK), jnp.bfloat16)
            if block > 0:
                edge = edge + kept[:, at - BLOCK : at] * before
            if block + 1 < block_count:
                edge = edge + kept[:, at + BLOCK : at + 2 * BLOCK] * behind
            base = (2 * block + item) * HEAD_DIM
            window_ref[base : base + HEAD_DIM, :BLOCK] = kept[:, at : at + BLOCK]
            window_ref[base : base + HEAD_DIM, BLOCK:] = edge


def tap_matrix(tap_row):
    return pltpu.roll(
        jnp.broadcast_to(tap_row, (BLOCK, 2 * BLOCK)), 0, axis=1, stride=1, stride_axis=0
    ).astype(jnp.bfloat16)


def attention_forward_body(
    units_ref,
    proj_ref,
    taps_ref,
    attended_ref,
    first_ref,
    last_ref,
    marks_ref,
    middle_ref,
    rough_ref,
    fine_ref,
    values_ref,
    weighted_ref,
    select_ref,
    own_ref,
    in_ref,
    approx_ref,
    window_ref,
    conv_ref,
):
    parts, _, part_width, row_count = proj_ref.shape
    part_heads = part_width // HEAD_DIM
    heads = parts * part_heads
    marks = 2 * LANDMARKS
    select_ref[...] = select_matrix(units_ref, row_count)
    is_first, start, end, _, _ = landmark_columns(units_ref)
    first_end, _ = item_ends(units_ref)
    position = lax.broadcasted_iota(jnp.int32, (marks, row_count), 1)
    in_ref[...] = jnp.where((position >= start) & (position < end), 0.0, NEGATIVE)
    own_ref[...] = jnp.where((position < first_end) == is_first, 0.0, NEGATIVE)
    first, second, inside = lane_items(units_ref, row_count)
    for part in range(parts):
        for kind in range(2):
            sums = dot_with(proj_ref[part, kind], select_ref[...], 1, 1)
            rows = slice(part * part_width, (part + 1) * part_width)
            marks_ref[kind, rows] = sums * inverse_units(units_ref)
    same = same_item(marks)

    def head_start(head, carry):
        at = pl.multiple_of(head * HEAD_DIM, HEAD_DIM)
        part = head // part_heads
        part_at = pl.multiple_of((head - part * part_heads) * HEAD_DIM, HEAD_DIM)
        mark_query = marks_ref[0, pl.ds(at, HEAD_DIM), :]
        mark_key = marks_ref[1, pl.ds(at, HEAD_DIM), :]
        logits = dot_fine(mark_query, mark_key, 0, 0) * SCORE_SCALE
        logits = jnp.where(same, logits, NEGATIVE)
        raised = jnp.exp(logits - jnp.max(logits, axis=1, keepdims=True))
        middle = raised / jnp.sum(raised, axis=1, keepdims=True)
        middle_ref[head] = middle
        _, peak = column_peaks(middle)
        approx_ref[head] = middle.T / peak
        query_rows = (mark_query * SCORE_SCALE).T.astype(jnp.bfloat16)
        scores = dot_with(query_rows, proj_ref[part, 1, pl.ds(part_at, HEAD_DIM), :], 1, 0) + in_ref[...]
        raised = jnp.exp(scores - jnp.max(scores, axis=1, keepdims=True))
        scale = 1.0 / jnp.sum(raised, axis=1, keepdims=True)
        last = (raised * scale).astype(jnp.bfloat16)
        last_ref[head] = last
        values_ref[head] = dot_with(last, proj_ref[part, 2, pl.ds(part_at, HEAD_DIM), :], 1, 1)
        return carry

    lax.fori_loop(0, heads, head_start, 0)

    seven, fifteen, thirteen = (scaled_eye(marks, value) for value in (7.0, 15.0, 13.0))

    def pinv_steps(saved_ref, count):
        kind = saved_ref.dtype

        def one_step(slot, carry):
            approx = [approx_ref[head] for head in range(heads)]
            product = [dot_fine(middle_ref[head], approx[head], 1, 0) for head in range(heads)]
            inner = [
                fifteen - dot_fine(product[head], seven - product[head], 1, 0)
                for head in range(heads)
            ]
            outer = [thirteen - dot_fine(product[head], inner[head], 1, 0) for head in range(heads)]
            for head in range(heads):
                saved_ref[slot, 0, head] = approx[head].astype(kind)
                saved_ref[slot, 1, head] = product[head].astype(kind)
                saved_ref[slot, 2, head] = inner[head].astype(kind)
                saved_ref[slot, 3, head] = outer[head].astype(kind)
                approx_ref[head] = dot_fine(0.25 * approx[head], outer[head], 1, 0)
            return carry

        lax.fori_loop(0, count, one_step, 0)

    pinv_steps(rough_ref, ROUGH_STEPS)
    pinv_steps(fine_ref, PINV_STEPS - ROUGH_STEPS)

    def head_end(head, carry):
        at = pl.multiple_of(head * HEAD_DIM, HEAD_DIM)
        part = head // part_heads
        part_at = pl.multiple_of((head - part * part_heads) * HEAD_DIM, HEAD_DIM)
        weighted = dot_fine(approx_ref[head], values_ref[head], 1, 0)
        weighted_ref[head] = weighted
        weighted_rows = weighted.T.astype(jnp.bfloat16)
        key_rows = (marks_ref[1, pl.ds(at, HEAD_DIM), :] * SCORE_SCALE).T.astype(jnp.bfloat16)
        values = proj_ref[part, 2, pl.ds(part_at, HEAD_DIM), :]
        fill_windows(window_ref, values, first, second)
        conv_ref[...] = dot_with(window_ref[...], tap_matrix(taps_ref[pl.ds(head, 1), :]), 1, 1)
        for chunk in range(row_count // CHUNK):
            lanes = slice(chunk * CHUNK, (chunk + 1) * CHUNK)
            query = proj_ref[part, 0, pl.ds(part_at, HEAD_DIM), lanes]
            scores = dot_with(key_rows, query, 1, 0) + own_ref[:, lanes]
            raised = jnp.exp(scores - jnp.max(scores, axis=0, keepdims=True))
            scale = 1.0 / jnp.sum(raised, axis=0, keepdims=True)
            kept = (raised * scale).astype(jnp.bfloat16)
            first_ref[head, :, lanes] = kept
            mixed = dot_with(weighted_rows, kept, 1, 0) * inside[:, lanes]
            for piece in range(CHUNK // BLOCK):
                block = chunk * (CHUNK // BLOCK) + piece
                base = 2 * block * HEAD_DIM
                columns = slice(block * BLOCK, (block + 1) * BLOCK)
                conv = (
                    conv_ref[base : base + HEAD_DIM] * first[:, columns]
                    + conv_ref[base + HEAD_DIM : base + 2 * HEAD_DIM] * second[:, columns]
                )
                attended_ref[pl.ds(at, HEAD_DIM), columns] = (
                    mixed[:, piece * BLOCK : (piece + 1) * BLOCK] + conv
                ).astype(jnp.bfloat16)
        return carry

    lax.fori_loop(0, heads, head_end, 0)


def whole(count):
    return [pl.BlockSpec(memory_space=pltpu.VMEM)] * count


def attention_forward(item_units, proj, tap_rows):
    width = proj.shape[0] * proj.shape[2]
    row_count = proj.shape[3]
    heads = width // HEAD_DIM
    marks = 2 * LANDMARKS
    square = (heads, marks, marks)
    return pl.pallas_call(
        attention_forward_body,
        in_specs=[pl.BlockSpec(memory_space=pltpu.SMEM)] + whole(2),
        out_specs=whole(9),
        out_shape=[
            jax.ShapeDtypeStruct((width, row_count), jnp.bfloat16),
            jax.ShapeDtypeStruct((heads, marks, row_count), jnp.bfloat16),
            jax.ShapeDtypeStruct((heads, marks, row_count), jnp.bfloat16),
            jax.ShapeDtypeStruct((2, width, marks), jnp.float32),
            jax.ShapeDtypeStruct(square, jnp.float32),
            jax.ShapeDtypeStruct((ROUGH_STEPS, 4) + square, jnp.bfloat16),
            jax.ShapeDtypeStruct((PINV_STEPS - ROUGH_STEPS, 4) + square, jnp.float32),
            jax.ShapeDtypeStruct((heads, marks, HEAD_DIM), jnp.float32),
            jax.ShapeDtypeStruct((heads, marks, HEAD_DIM), jnp.float32),
        ],
        scratch_shapes=[
            pltpu.VMEM((marks, row_count), jnp.bfloat16),
            pltpu.VMEM((marks, row_count), jnp.float32),
            pltpu.VMEM((marks, row_count), jnp.float32),
            pltpu.VMEM(square, jnp.float32),
            pltpu.VMEM((2 * row_count // BLOCK * HEAD_DIM, 2 * BLOCK), jnp.bfloat16),
            pltpu.VMEM((2 * row_count // BLOCK * HEAD_DIM, BLOCK), jnp.float32),
        ],
        compiler_params=pltpu.CompilerParams(vmem_limit_bytes=48 * 1024 * 1024),
        cost_estimate=pl.CostEstimate(flops=20_000_000_000, bytes_accessed=20_000_000, transcendentals=0),
    )(item_units, proj, tap_rows)


def tap_rows_of(kernel):
    half = kernel.shape[1] // 2
    gap = jnp.zeros((kernel.shape[0], 2 * BLOCK - kernel.shape[1]), jnp.float32)
    return jnp.concatenate([kernel[:, half:], gap, kernel[:, :half]], axis=1)

def attention_backward_body(
    units_ref,
    proj_ref,
    taps_ref,
    grad_ref,
    first_ref,
    last_ref,
    marks_ref,
    middle_ref,
    rough_ref,
    fine_ref,
    values_ref,
    weighted_ref,
    out_ref,
    kernel_ref,
    select_ref,
    d_first_ref,
    d_last_ref,
    d_marks_ref,
    d_weighted_ref,
    d_values_ref,
    d_approx_ref,
    d_middle_ref,
    window_ref,
    d_window_ref,
    conv_ref,
):
    width = proj_ref.shape[1]
    row_count = proj_ref.shape[2]
    heads = width // HEAD_DIM
    marks = 2 * LANDMARKS
    select_ref[...] = select_matrix(units_ref, row_count)
    first, second, _ = lane_items(units_ref, row_count)
    inverse = inverse_units(units_ref)
    same = same_item(marks)
    chunks = [slice(at, at + CHUNK) for at in range(0, row_count, CHUNK)]

    def head_start(head, carry):
        at = pl.multiple_of(head * HEAD_DIM, HEAD_DIM)
        weighted_low = weighted_ref[head].astype(jnp.bfloat16)
        for lanes in chunks:
            kept = first_ref[head, :, lanes].astype(jnp.float32)
            d_kept = dot_with(weighted_low, grad_ref[pl.ds(at, HEAD_DIM), lanes], 1, 0)
            scaled = kept * d_kept
            d_scores = scaled - kept * jnp.sum(scaled, axis=0, keepdims=True)
            d_first_ref[head, :, lanes] = d_scores.astype(jnp.bfloat16)
        d_weighted = dot_with(first_ref[head], grad_ref[pl.ds(at, HEAD_DIM), :], 1, 1)
        d_weighted_ref[head] = d_weighted
        d_marks_ref[1, pl.ds(at, HEAD_DIM), :] = SCORE_SCALE * dot_with(
            proj_ref[0, pl.ds(at, HEAD_DIM), :], d_first_ref[head], 1, 1
        )
        d_approx = dot_fine(d_weighted, values_ref[head], 1, 1)
        d_approx_ref[head] = jnp.where(same, d_approx, 0.0)
        inverse_last = dot_fine(
            0.25 * fine_ref[PINV_STEPS - ROUGH_STEPS - 1, 0, head],
            fine_ref[PINV_STEPS - ROUGH_STEPS - 1, 3, head],
            1,
            0,
        )
        d_values_ref[head] = dot_fine(inverse_last, d_weighted, 0, 0)
        d_middle_ref[head] = jnp.zeros((marks, marks), jnp.float32)
        return carry

    lax.fori_loop(0, heads, head_start, 0)

    seven = scaled_eye(marks, 7.0)
    every = range(heads)

    def pinv_steps(saved_ref, count, dot):
        def one_step(step, carry):
            slot = count - 1 - step
            d_next = [d_approx_ref[head] for head in every]
            d_outer = [0.25 * dot(saved_ref[slot, 0, head], d_next[head], 0, 0) for head in every]
            d_inner = [-dot(saved_ref[slot, 1, head], d_outer[head], 0, 0) for head in every]
            d_lowest = [-dot(saved_ref[slot, 1, head], d_inner[head], 0, 0) for head in every]
            for head in every:
                product = saved_ref[slot, 1, head].astype(jnp.float32)
                d_product = (
                    -dot(d_outer[head], saved_ref[slot, 2, head], 1, 1)
                    - dot(d_inner[head], seven - product, 1, 1)
                    - d_lowest[head]
                )
                d_middle_ref[head] += dot(d_product, saved_ref[slot, 0, head], 1, 1)
                d_approx_ref[head] = 0.25 * dot(d_next[head], saved_ref[slot, 3, head], 1, 1) + dot(
                    middle_ref[head], d_product, 0, 0
                )
            return carry

        lax.fori_loop(0, count, one_step, 0)

    pinv_steps(fine_ref, PINV_STEPS - ROUGH_STEPS, dot_fine)
    pinv_steps(rough_ref, ROUGH_STEPS, dot_low)

    lane = lax.broadcasted_iota(jnp.int32, (1, marks), 1)

    def item_sums(row):
        total = jnp.sum(row, axis=1, keepdims=True)
        start = jnp.sum(jnp.where(lane < LANDMARKS, row, 0.0), axis=1, keepdims=True)
        return jnp.where(lane < LANDMARKS, start, total - start)

    def head_middle(head, carry):
        at = pl.multiple_of(head * HEAD_DIM, HEAD_DIM)
        middle = middle_ref[head]
        sums, peak = column_peaks(middle)
        d_start = d_approx_ref[head]
        d_start_turned = (d_start / peak).T
        d_peak = -item_sums(jnp.sum(d_start_turned * middle, axis=0, keepdims=True)) / peak
        at_peak = (sums == peak).astype(jnp.float32)
        d_column = at_peak * d_peak / item_sums(at_peak)
        d_middle = d_middle_ref[head] + d_start_turned + jnp.where(same, d_column, 0.0)
        scaled = middle * d_middle
        d_logits = SCORE_SCALE * (scaled - middle * jnp.sum(scaled, axis=1, keepdims=True))
        rows = pl.ds(at, HEAD_DIM)
        d_marks_ref[0, rows, :] = dot_fine(marks_ref[1, rows, :], d_logits, 1, 1)
        d_marks_ref[1, rows, :] += dot_fine(marks_ref[0, rows, :], d_logits, 1, 0)
        return carry

    lax.fori_loop(0, heads, head_middle, 0)

    row_index = lax.broadcasted_iota(jnp.int32, (BLOCK, BLOCK), 0)
    column_index = lax.broadcasted_iota(jnp.int32, (BLOCK, BLOCK), 1)
    turn = jnp.where(row_index + column_index == BLOCK - 1, 1.0, 0.0).astype(jnp.bfloat16)

    def head_end(head, carry):
        at = pl.multiple_of(head * HEAD_DIM, HEAD_DIM)
        rows = pl.ds(at, HEAD_DIM)
        d_values = d_values_ref[head]
        d_values_low = d_values.astype(jnp.bfloat16)
        d_values_turned = d_values.T.astype(jnp.bfloat16)
        inner = jnp.sum(d_values * values_ref[head], axis=1, keepdims=True)
        for lanes in chunks:
            d_kept = dot_with(d_values_low, proj_ref[2, rows, lanes], 1, 0)
            d_scores = last_ref[head, :, lanes].astype(jnp.float32) * (d_kept - inner)
            d_last_ref[:, lanes] = d_scores.astype(jnp.bfloat16)
        d_query = d_marks_ref[0, rows, :] + SCORE_SCALE * dot_with(
            proj_ref[1, rows, :], d_last_ref[...], 1, 1
        )
        d_query_low = (d_query * inverse).astype(jnp.bfloat16)
        d_key_low = (d_marks_ref[1, rows, :] * inverse).astype(jnp.bfloat16)
        mark_query = (marks_ref[0, rows, :] * SCORE_SCALE).astype(jnp.bfloat16)
        mark_key = (marks_ref[1, rows, :] * SCORE_SCALE).astype(jnp.bfloat16)
        fill_windows(window_ref, proj_ref[2, rows, :], first, second)
        fill_windows(d_window_ref, grad_ref[rows, :], first, second)
        conv_ref[...] = dot_with(d_window_ref[...], tap_matrix(taps_ref[pl.ds(head, 1), :]), 1, 1)
        joined = dot_with(d_window_ref[:, :BLOCK], window_ref[...], 0, 0)
        joined_high, joined_low = halves(joined)
        joined = dot_with(
            jnp.concatenate([turn, turn], axis=1),
            jnp.concatenate([joined_high, joined_low], axis=0),
            1,
            0,
        )
        joined = pltpu.roll(joined, BLOCK + 1, axis=1, stride=1, stride_axis=0)
        kernel_ref[pl.ds(head, 1), :] = jnp.sum(joined, axis=0, keepdims=True)
        for index, lanes in enumerate(chunks):
            select = select_ref[:, lanes]
            out_ref[rows, lanes] = (
                dot_with(mark_key, d_first_ref[head, :, lanes], 1, 0)
                + dot_with(d_query_low, select, 1, 0)
            ).astype(jnp.bfloat16)
            out_ref[pl.ds(width + at, HEAD_DIM), lanes] = (
                dot_with(mark_query, d_last_ref[:, lanes], 1, 0) + dot_with(d_key_low, select, 1, 0)
            ).astype(jnp.bfloat16)
            d_value = dot_with(d_values_turned, last_ref[head, :, lanes], 1, 0)
            for part in range(CHUNK // BLOCK):
                block = index * (CHUNK // BLOCK) + part
                base = 2 * block * HEAD_DIM
                columns = slice(block * BLOCK, (block + 1) * BLOCK)
                conv = (
                    conv_ref[base : base + HEAD_DIM] * first[:, columns]
                    + conv_ref[base + HEAD_DIM : base + 2 * HEAD_DIM] * second[:, columns]
                )
                out_ref[pl.ds(2 * width + at, HEAD_DIM), columns] = (
                    d_value[:, part * BLOCK : (part + 1) * BLOCK] + conv
                ).astype(jnp.bfloat16)
        return carry

    lax.fori_loop(0, heads, head_end, 0)


def attention_backward(item_units, proj, tap_rows, grad, *saved, part):
    parts, _, width, row_count = proj.shape
    heads = width // HEAD_DIM
    marks = 2 * LANDMARKS
    square = (heads, marks, marks)
    thin = (heads, marks, HEAD_DIM)
    stacked = 2 * row_count // BLOCK * HEAD_DIM

    def block(shape, split):
        place = tuple(part if dim == split else 0 for dim in range(len(shape)))
        sizes = tuple(size // parts if dim == split else size for dim, size in enumerate(shape))
        sizes = (None,) + sizes[1:] if len(shape) == 4 and split == 0 else sizes
        return pl.BlockSpec(sizes, lambda step: place, pipeline_mode=pl.Buffered(1))

    splits = (0, None, 0, 0, 0, 1, 0, 2, 2, 0, 0)
    tap_rows = tap_rows[part * heads : (part + 1) * heads]
    arrays = (proj, tap_rows, grad) + saved
    out, joined = pl.pallas_call(
        attention_backward_body,
        grid=(1,),
        in_specs=[pl.BlockSpec(memory_space=pltpu.SMEM)]
        + [block(array.shape, split) for array, split in zip(arrays, splits)],
        out_specs=[
            pl.BlockSpec((3 * width, row_count), lambda step: (0, 0)),
            pl.BlockSpec((heads, 2 * BLOCK), lambda step: (0, 0)),
        ],
        out_shape=[
            jax.ShapeDtypeStruct((3 * width, row_count), jnp.bfloat16),
            jax.ShapeDtypeStruct((heads, 2 * BLOCK), jnp.float32),
        ],
        scratch_shapes=[
            pltpu.VMEM((marks, row_count), jnp.bfloat16),
            pltpu.VMEM((heads, marks, row_count), jnp.bfloat16),
            pltpu.VMEM((marks, row_count), jnp.bfloat16),
            pltpu.VMEM((2, width, marks), jnp.float32),
            pltpu.VMEM(thin, jnp.float32),
            pltpu.VMEM(thin, jnp.float32),
            pltpu.VMEM(square, jnp.float32),
            pltpu.VMEM(square, jnp.float32),
            pltpu.VMEM((stacked, 2 * BLOCK), jnp.bfloat16),
            pltpu.VMEM((stacked, 2 * BLOCK), jnp.bfloat16),
            pltpu.VMEM((stacked, BLOCK), jnp.float32),
        ],
        compiler_params=pltpu.CompilerParams(vmem_limit_bytes=48 * 1024 * 1024),
        cost_estimate=pl.CostEstimate(
            flops=30_000_000_000 // parts, bytes_accessed=20_000_000 // parts, transcendentals=0
        ),
    )(item_units, *arrays)
    half = TAPS // 2
    return out, jnp.concatenate([joined[:, 2 * BLOCK - half :], joined[:, : TAPS - half]], axis=1)


ROWS = 256
GELU_SCALE = 0.7978845608
GELU_CUBE = 0.044715


def row_block(width):
    return pl.BlockSpec((ROWS, width), lambda step: (step, 0))


def fixed_block(shape, column=0):
    return pl.BlockSpec(shape, lambda step: (0, column))


def dense_params():
    return pltpu.CompilerParams(vmem_limit_bytes=56 * 1024 * 1024)


def cost(flops, size):
    return pl.CostEstimate(flops=flops, bytes_accessed=size, transcendentals=0)


def normalized(rows):
    center = rows - jnp.mean(rows, axis=-1, keepdims=True)
    spread = jnp.mean(center * center, axis=-1, keepdims=True)
    scale = lax.rsqrt(spread + NORM_EPS)
    return center * scale, scale


def norm_backward(grad, gain, unit, scale):
    scaled = grad * gain
    lean = jnp.mean(scaled * unit, axis=-1, keepdims=True)
    return scale * (scaled - jnp.mean(scaled, axis=-1, keepdims=True) - unit * lean)


def column_sum(rows):
    return jnp.sum(rows, axis=0, keepdims=True)


def both(own_ref, other_ref):
    return own_ref[...].astype(jnp.float32) + other_ref[...].astype(jnp.float32)


def hidden_forward_body(
    own_ref,
    other_ref,
    tokens_ref,
    weight_ref,
    shared_ref,
    bias_ref,
    expand_ref,
    reduce_ref,
    part_ref,
    hidden_ref,
    low_ref,
    unit_ref,
    scale_ref,
    active_ref,
    slope_ref,
    stat_ref,
):
    branch = both(own_ref, other_ref) + shared_ref[0:1]
    squares = column_sum(weight_ref[...] * branch * branch)

    @pl.when(pl.program_id(0) == 0)
    def _():
        stat_ref[...] = jnp.zeros_like(stat_ref)

    stat_ref[...] += squares
    unit, scale = normalized(tokens_ref[...].astype(jnp.float32) + branch)
    hidden = unit * shared_ref[2:3] + shared_ref[3:4]
    hidden_ref[...] = hidden
    unit_ref[...] = unit.astype(jnp.bfloat16)
    scale_ref[...] = scale
    hidden_low = hidden.astype(jnp.bfloat16)
    low_ref[...] = hidden_low
    total = jnp.zeros(part_ref.shape, jnp.float32)
    units = expand_ref.shape[1]
    for at in range(0, units, 512):
        lanes = slice(at, at + 512)
        expanded = dot_with(hidden_low, expand_ref[:, lanes], 1, 0) + bias_ref[:, lanes]
        square = expanded * expanded
        bend = jnp.tanh(expanded * (GELU_SCALE + (GELU_SCALE * GELU_CUBE) * square))
        half = 0.5 + 0.5 * bend
        active = (expanded * half).astype(jnp.bfloat16)
        active_ref[:, lanes] = active
        slope = half + (0.5 * expanded) * (1.0 - bend * bend) * (
            GELU_SCALE + (3.0 * GELU_SCALE * GELU_CUBE) * square
        )
        slope_ref[:, lanes] = slope.astype(jnp.bfloat16)
        total += dot_with(active, reduce_ref[:, lanes], 1, 1)
    part_ref[...] = total.astype(jnp.bfloat16)


def hidden_forward(own, other, tokens, weight_column, shared_rows, expand_bias, late_full):
    row_count, width = tokens.shape
    units = expand_bias.shape[1]
    return pl.pallas_call(
        hidden_forward_body,
        grid=(row_count // ROWS,),
        in_specs=[
            row_block(width),
            row_block(width),
            row_block(width),
            row_block(1),
            fixed_block((6, width)),
            fixed_block((1, units)),
            fixed_block((width, units), 0),
            fixed_block((width, units), 1),
        ],
        out_specs=[
            row_block(width),
            row_block(width),
            row_block(width),
            row_block(width),
            row_block(1),
            row_block(units),
            row_block(units),
            fixed_block((1, width)),
        ],
        out_shape=[
            jax.ShapeDtypeStruct((row_count, width), jnp.bfloat16),
            jax.ShapeDtypeStruct((row_count, width), jnp.float32),
            jax.ShapeDtypeStruct((row_count, width), jnp.bfloat16),
            jax.ShapeDtypeStruct((row_count, width), jnp.bfloat16),
            jax.ShapeDtypeStruct((row_count, 1), jnp.float32),
            jax.ShapeDtypeStruct((row_count, units), jnp.bfloat16),
            jax.ShapeDtypeStruct((row_count, units), jnp.bfloat16),
            jax.ShapeDtypeStruct((1, width), jnp.float32),
        ],
        compiler_params=dense_params(),
        cost_estimate=cost(4 * row_count * width * units, 30_000_000),
    )(own, other, tokens, weight_column, shared_rows, expand_bias, late_full, late_full)


def hidden_backward_body(
    own_ref,
    other_ref,
    hidden_ref,
    cotangent_ref,
    weight_ref,
    shared_ref,
    expand_ref,
    reduce_ref,
    slope_ref,
    output_ref,
    d_two_ref,
    d_expanded_ref,
    part_ref,
    sums_ref,
    bias_ref,
):
    branch = both(own_ref, other_ref) + shared_ref[1:2]
    weight = weight_ref[...]
    unit, scale = normalized(hidden_ref[...] + branch)
    output_ref[...] = unit * shared_ref[4:5] + shared_ref[5:6]
    grad = cotangent_ref[...].astype(jnp.float32) * weight
    d_res = norm_backward(grad, shared_ref[4:5], unit, scale)
    d_two = d_res.astype(jnp.bfloat16)
    d_two_ref[...] = d_two

    @pl.when(pl.program_id(0) == 0)
    def _():
        sums_ref[...] = jnp.zeros_like(sums_ref)
        bias_ref[...] = jnp.zeros_like(bias_ref)

    sums_ref[...] += jnp.concatenate(
        [
            column_sum(weight * branch * branch),
            column_sum(d_res),
            column_sum(grad * unit),
            column_sum(grad),
            jnp.zeros((4, grad.shape[1]), jnp.float32),
        ],
        axis=0,
    )
    total = jnp.zeros(part_ref.shape, jnp.float32)
    units = expand_ref.shape[1]
    for at in range(0, units, 512):
        lanes = slice(at, at + 512)
        d_active = dot_with(d_two, reduce_ref[:, lanes], 1, 0)
        d_expanded = (slope_ref[:, lanes].astype(jnp.float32) * d_active).astype(jnp.bfloat16)
        d_expanded_ref[:, lanes] = d_expanded
        bias_ref[:, lanes] += column_sum(d_expanded.astype(jnp.float32))
        total += dot_with(d_expanded, expand_ref[:, lanes], 1, 1)
    part_ref[...] = total.astype(jnp.bfloat16)


def hidden_backward(own, other, hidden, cotangent, weight_column, shared_rows, late_full, slope):
    row_count, width = cotangent.shape
    units = slope.shape[1]
    return pl.pallas_call(
        hidden_backward_body,
        grid=(row_count // ROWS,),
        in_specs=[
            row_block(width),
            row_block(width),
            row_block(width),
            row_block(width),
            row_block(1),
            fixed_block((6, width)),
            fixed_block((width, units), 0),
            fixed_block((width, units), 1),
            row_block(units),
        ],
        out_specs=[
            row_block(width),
            row_block(width),
            row_block(units),
            row_block(width),
            fixed_block((8, width)),
            fixed_block((1, units)),
        ],
        out_shape=[
            jax.ShapeDtypeStruct((row_count, width), jnp.float32),
            jax.ShapeDtypeStruct((row_count, width), jnp.bfloat16),
            jax.ShapeDtypeStruct((row_count, units), jnp.bfloat16),
            jax.ShapeDtypeStruct((row_count, width), jnp.bfloat16),
            jax.ShapeDtypeStruct((8, width), jnp.float32),
            jax.ShapeDtypeStruct((1, units), jnp.float32),
        ],
        compiler_params=dense_params(),
        cost_estimate=cost(4 * row_count * width * units, 30_000_000),
    )(own, other, hidden, cotangent, weight_column, shared_rows, late_full, late_full, slope)


def norm_one_body(
    own_ref,
    other_ref,
    d_two_ref,
    unit_ref,
    scale_ref,
    inside_ref,
    shared_ref,
    mixing_ref,
    d_one_ref,
    d_mixed_ref,
    sums_ref,
    turned_ref,
):
    @pl.when(pl.program_id(0) == 0)
    def _():
        sums_ref[...] = jnp.zeros_like(sums_ref)
        turned_ref[...] = mixing_ref[...].astype(jnp.float32).T.astype(jnp.bfloat16)

    grad = both(own_ref, other_ref) + d_two_ref[...].astype(jnp.float32)
    unit = unit_ref[...].astype(jnp.float32)
    d_res = norm_backward(grad, shared_ref[2:3], unit, scale_ref[...])
    d_one = d_res.astype(jnp.bfloat16)
    d_one_ref[...] = d_one
    sums_ref[...] += jnp.concatenate(
        [
            column_sum(d_res),
            column_sum(grad * unit),
            column_sum(grad),
            jnp.zeros((5, grad.shape[1]), jnp.float32),
        ],
        axis=0,
    )
    d_mixed = dot_with(turned_ref[...], d_one, 1, 1) * inside_ref[...]
    d_mixed_ref[...] = d_mixed.astype(jnp.bfloat16)


def norm_one_backward(own, other, d_two, unit, scale, inside_row, shared_rows, late_full, local_width):
    row_count, width = d_two.shape
    return pl.pallas_call(
        norm_one_body,
        grid=(row_count // ROWS,),
        in_specs=[
            row_block(width),
            row_block(width),
            row_block(width),
            row_block(width),
            row_block(1),
            pl.BlockSpec((1, ROWS), lambda step: (0, step)),
            fixed_block((6, width)),
            fixed_block((width, local_width), late_full.shape[1] // local_width - 1),
        ],
        out_specs=[
            row_block(width),
            pl.BlockSpec((local_width, ROWS), lambda step: (0, step)),
            fixed_block((8, width)),
        ],
        out_shape=[
            jax.ShapeDtypeStruct((row_count, width), jnp.bfloat16),
            jax.ShapeDtypeStruct((local_width, row_count), jnp.bfloat16),
            jax.ShapeDtypeStruct((8, width), jnp.float32),
        ],
        scratch_shapes=[pltpu.VMEM((local_width, width), jnp.bfloat16)],
        compiler_params=dense_params(),
        cost_estimate=cost(2 * row_count * width * local_width, 14_000_000),
    )(own, other, d_two, unit, scale, inside_row, shared_rows, late_full)


def turned_dot_body(*refs):
    *pairs, out_ref = refs
    total = jnp.zeros(out_ref.shape, jnp.float32)
    for at in range(0, len(pairs), 2):
        left = pairs[at][...]
        left = left.reshape(-1, left.shape[-1])
        total += dot_with(left, pairs[at + 1][...], 0, 1)
    out_ref[...] = total.astype(jnp.bfloat16)


def turned_dot(lefts, rights, columns, width):
    row_count = lefts[0].shape[-1]
    specs, arrays, terms = [], [], 0
    for left, right, column in zip(lefts, rights, columns):
        shape = left.shape[:-1] + (ROWS,)
        place = (0,) * (left.ndim - 1)
        specs.append(pl.BlockSpec(shape, lambda step, place=place: place + (step,)))
        depth = left.size // row_count
        specs.append(fixed_block((width, depth), column))
        arrays += [left, right]
        terms += depth
    return pl.pallas_call(
        turned_dot_body,
        grid=(row_count // ROWS,),
        in_specs=specs,
        out_specs=row_block(width),
        out_shape=jax.ShapeDtypeStruct((row_count, width), jnp.bfloat16),
        compiler_params=dense_params(),
        cost_estimate=cost(2 * row_count * width * terms, 8_000_000),
    )(*arrays)

def project_body(first_ref, second_ref, tokens_ref, bias_ref, out_ref, turned_ref):
    part_width = first_ref.shape[1]

    @pl.when(pl.program_id(0) == 0)
    def _():
        for part, weight_ref in enumerate((first_ref, second_ref)):
            turned = weight_ref[...].astype(jnp.float32).T
            turned_ref[part * part_width : (part + 1) * part_width] = turned.astype(jnp.bfloat16)

    rows = dot_with(turned_ref[...], tokens_ref[...], 1, 1) + bias_ref[...]
    out_ref[...] = rows.astype(jnp.bfloat16).reshape(out_ref.shape)


def project(first, second, tokens, bias_column):
    row_count, width = tokens.shape
    part_width = first.shape[1]
    shape = (2, 3, part_width // 3, row_count)
    return pl.pallas_call(
        project_body,
        grid=(row_count // ROWS,),
        in_specs=[
            fixed_block((width, part_width)),
            fixed_block((width, part_width)),
            row_block(width),
            fixed_block((2 * part_width, 1)),
        ],
        out_specs=pl.BlockSpec(shape[:3] + (ROWS,), lambda step: (0, 0, 0, step)),
        out_shape=jax.ShapeDtypeStruct(shape, jnp.bfloat16),
        scratch_shapes=[pltpu.VMEM((2 * part_width, width), jnp.bfloat16)],
        compiler_params=dense_params(),
        cost_estimate=cost(4 * row_count * width * part_width, 8_000_000),
    )(first, second, tokens, bias_column)


def adamw(master, moment, square, gradient, factor, learn_rate, decay_rate):
    clipped = gradient * factor
    moment_new = BETA_ONE * moment + (1.0 - BETA_ONE) * clipped
    square_new = BETA_TWO * square + (1.0 - BETA_TWO) * clipped * clipped
    step_size = moment_new / CORRECT_ONE / (jnp.sqrt(square_new / CORRECT_TWO) + ADAM_EPS)
    return (master - learn_rate * (step_size + decay_rate * master), moment_new, square_new)


def body(
    tokens,
    cotangent,
    item_units,
    counted,
    inputs_weight,
    inputs_moment,
    inputs_square,
    mixing_weight,
    mixing_moment,
    mixing_square,
    expand_weight,
    expand_moment,
    expand_square,
    reduce_weight,
    reduce_moment,
    reduce_square,
    biases_weight,
    biases_moment,
    biases_square,
    shared_weight,
    shared_moment,
    shared_square,
    kernel_weight,
    kernel_moment,
    kernel_square,
):
    dp_count = lax.axis_size("dp")
    bits = list(range(bits_of(dp_count)))
    first_order, second_order = bits, bits[:2][::-1] + bits[2:]
    row_count, width_full = tokens.shape
    local_width = inputs_weight.shape[2]
    shard_rows = inputs_weight.shape[1]
    bias_share = biases_weight.shape[1]
    hidden_units = expand_weight.shape[1]
    part_width = local_width // 2
    part_lanes = [slice(0, part_width), slice(part_width, local_width)]

    late_low = jnp.concatenate(
        [expand_weight.astype(jnp.bfloat16)]
        + [weight.astype(jnp.bfloat16).T for weight in (reduce_weight, mixing_weight)],
        axis=1,
    )
    small_low = jnp.concatenate([biases_weight.reshape(-1), shared_weight.reshape(-1)])
    small_low = jnp.pad(small_low, (0, (-small_low.shape[0]) % (3 * part_width)))
    small_low = small_low.astype(jnp.bfloat16).reshape(-1, 3 * part_width)
    left_low, right_low = [
        jnp.concatenate([inputs_weight[c][:, lanes] for c in range(3)], axis=1).astype(jnp.bfloat16)
        for lanes in part_lanes
    ]
    left_low = jnp.concatenate([left_low, small_low], axis=0)
    left_full = gather_rows(left_low, dp_count, first_order[::-1])
    left_full = left_full.reshape(dp_count, left_low.shape[0], 3 * part_width)
    inputs_left = left_full[:, :shard_rows].reshape(-1, 3 * part_width)
    small_full = left_full[:, shard_rows:].reshape(dp_count, -1)
    inputs_right = gather_rows(right_low, dp_count, second_order[::-1])
    late_full = lax.all_gather(late_low, "dp", axis=0, tiled=True)
    biases_row = small_full[:, :bias_share].reshape(-1).astype(jnp.float32)
    shared_rows = small_full[:, bias_share : bias_share + 6 * shard_rows]
    shared_rows = shared_rows.reshape(dp_count, 6, shard_rows).transpose(1, 0, 2)
    shared_rows = shared_rows.reshape(6, -1).astype(jnp.float32)
    query_bias = biases_row[:local_width]
    value_bias = biases_row[local_width : 2 * local_width]
    expand_bias = biases_row[2 * local_width :][None, :]
    zero_bias = jnp.zeros((part_width,), jnp.float32)
    bias_column = jnp.concatenate(
        [
            piece
            for lanes in part_lanes
            for piece in (query_bias[lanes], zero_bias, value_bias[lanes])
        ]
    )[:, None]

    row_item = row_items(item_units[0], row_count, LANDMARKS)
    inside = (row_item < 2).astype(jnp.float32)
    weight_rows = counted.astype(jnp.float32) * inside
    weight_column = weight_rows[:, None]

    proj = project(inputs_left, inputs_right, tokens, bias_column)
    attended, *saved = attention_forward(item_units, proj, tap_rows_of(kernel_weight))
    mixing_column = late_full.shape[1] // local_width - 1
    own_one = turned_dot([attended], [late_full], [mixing_column], width_full)
    other_one = swap(own_one, "head", 2, 0)
    own_two, hidden_one, hidden_low, unit_one, scale_one, active, slope, stat_one = hidden_forward(
        own_one, other_one, tokens, weight_column, shared_rows, expand_bias, late_full
    )
    other_two = swap(own_two, "head", 2, 0)
    output_rows, d_two, d_expanded, own_three, sums_two, expand_sums = hidden_backward(
        own_two, other_two, hidden_one, cotangent, weight_column, shared_rows, late_full, slope
    )
    other_three = swap(own_three, "head", 2, 0)
    reduce_grad = jnp.einsum("rd,rf->df", d_two, active, preferred_element_type=jnp.float32)
    expand_grad = jnp.einsum("rd,rf->df", hidden_low, d_expanded, preferred_element_type=jnp.float32)
    reduce_scatter = Scatter(reduce_grad.astype(jnp.bfloat16), dp_count, second_order).send()
    expand_scatter = Scatter(expand_grad.astype(jnp.bfloat16), dp_count, first_order).send()
    d_one, d_mixed, sums_one = norm_one_backward(
        own_three,
        other_three,
        d_two,
        unit_one,
        scale_one,
        inside[None, :],
        shared_rows,
        late_full,
        local_width,
    )
    mixing_grad = jnp.einsum("rd,kr->dk", d_one, attended, preferred_element_type=jnp.float32)
    mixing_scatter = Scatter(mixing_grad.astype(jnp.bfloat16), dp_count, first_order).send()
    first_scatters = (reduce_scatter, expand_scatter, mixing_scatter)
    d_mixed = after(d_mixed, *[scatter.sent for scatter in first_scatters])
    back_taps = tap_rows_of(kernel_weight[:, ::-1])
    d_left, kernel_left = attention_backward(item_units, proj, back_taps, d_mixed, *saved, part=0)

    def inputs_part(gradient):
        product = jnp.einsum("rd,kr->dk", tokens, gradient, preferred_element_type=jnp.float32)
        return product.astype(jnp.bfloat16)

    for scatter in first_scatters:
        scatter.take(d_left).send()
    left_scatter = Scatter(inputs_part(d_left), dp_count, second_order).send()
    d_mixed = after(d_mixed, left_scatter.sent, *[scatter.sent for scatter in first_scatters])
    d_right, kernel_right = attention_backward(item_units, proj, back_taps, d_mixed, *saved, part=1)
    right_scatter = Scatter(inputs_part(d_right), dp_count, first_order).send()
    for scatter in first_scatters:
        scatter.take(d_right)
    hidden_scatter = expand_scatter.merge(reduce_scatter).send()
    left_scatter.take(d_right).send()
    d_both = after(d_right, right_scatter.sent, hidden_scatter.sent, left_scatter.sent)
    own_four = turned_dot([d_left, d_both], [inputs_left, inputs_right], [0, 0], width_full)
    other_four = swap(own_four, "head", 2, 0)
    right_scatter.take(own_four).send()
    inputs_scatter = right_scatter.merge(left_scatter, mixing_scatter)

    kernel_grad = jnp.concatenate([kernel_left, kernel_right], axis=0)
    left_sums, right_sums = [
        jnp.sum(gradient.astype(jnp.float32), axis=1).reshape(3, part_width)
        for gradient in (d_left, d_right)
    ]
    bias_size = 2 * local_width + hidden_units
    small_parts = [
        left_sums[0],
        right_sums[0],
        left_sums[2],
        right_sums[2],
        expand_sums.reshape(-1),
        sums_one[0],
        sums_two[1],
        sums_one[1],
        sums_one[2],
        sums_two[2],
        sums_two[3],
        kernel_grad.reshape(-1),
    ]
    small_size = sum(part.shape[0] for part in small_parts)
    small_count = (small_size + 1023) // 1024 * 8
    small_parts.append(jnp.zeros((small_count * 128 - small_size,), jnp.float32))
    small_total = jnp.concatenate(small_parts).reshape(small_count, 128)
    small_total = sum_all(small_total, "dp", dp_count).reshape(-1)
    dp_index = lax.axis_index("dp")
    biases_share = lax.dynamic_slice_in_dim(small_total, dp_index * bias_share, bias_share)[None, :]
    shared_total = small_total[bias_size : bias_size + 6 * width_full].reshape(6, width_full)
    shared_share = lax.dynamic_slice_in_dim(shared_total, dp_index * shard_rows, shard_rows, axis=1)
    kernel_total = small_total[bias_size + 6 * width_full : small_size].reshape(kernel_grad.shape)

    hidden_share = hidden_scatter.finish()
    expand_share, reduce_share = hidden_share[:, :hidden_units], hidden_share[:, hidden_units:].T
    merged_share = inputs_scatter.finish()
    columns = 3 * part_width
    right_share, left_share = [
        merged_share[:, at : at + columns].reshape(shard_rows, 3, part_width)
        for at in (0, columns)
    ]
    mixing_share = merged_share[:, 2 * columns :].T
    inputs_share = jnp.concatenate([left_share, right_share], axis=2).transpose(1, 0, 2)
    input_grad = (
        own_four.astype(jnp.float32) + other_four.astype(jnp.float32) + d_one.astype(jnp.float32)
    )
    local_stats = jnp.stack([jnp.sum(stat_one), jnp.sum(sums_two[0]), jnp.sum(weight_rows)])
    kernel_squares = jnp.where(lax.axis_index("dp") == 0, jnp.sum(kernel_total * kernel_total), 0.0)
    local_squares = (
        jnp.sum(inputs_share * inputs_share)
        + jnp.sum(mixing_share * mixing_share)
        + jnp.sum(expand_share * expand_share)
        + jnp.sum(reduce_share * reduce_share)
        + jnp.sum(biases_share * biases_share)
    )
    local_squares = (
        local_squares
        + jnp.where(lax.axis_index("head") == 0, jnp.sum(shared_share * shared_share), 0.0)
        + kernel_squares
    )
    final_row = jnp.concatenate([local_squares[None], local_stats, jnp.zeros((124,), jnp.float32)])
    final_row = sum_all(sum_all(final_row[None, :], "head", 2), "dp", dp_count)[0]
    squares_total, summed_stats = final_row[0], final_row[1:4]
    grad_norm = jnp.sqrt(squares_total)
    factor = CLIP_NORM / (grad_norm + CLIP_EPS)
    inputs_master, inputs_momentum, inputs_variance = adamw(
        inputs_weight, inputs_moment, inputs_square, inputs_share, factor, RATE_MATRIX, WEIGHT_DECAY
    )
    mixing_master, mixing_momentum, mixing_variance = adamw(
        mixing_weight, mixing_moment, mixing_square, mixing_share, factor, RATE_MATRIX, WEIGHT_DECAY
    )
    expand_master, expand_momentum, expand_variance = adamw(
        expand_weight, expand_moment, expand_square, expand_share, factor, RATE_MATRIX, WEIGHT_DECAY
    )
    reduce_master, reduce_momentum, reduce_variance = adamw(
        reduce_weight, reduce_moment, reduce_square, reduce_share, factor, RATE_MATRIX, WEIGHT_DECAY
    )
    biases_master, biases_momentum, biases_variance = adamw(
        biases_weight, biases_moment, biases_square, biases_share, factor, RATE_VECTOR, 0.0
    )
    shared_master, shared_momentum, shared_variance = adamw(
        shared_weight, shared_moment, shared_square, shared_share, factor, RATE_VECTOR, 0.0
    )
    kernel_master, kernel_momentum, kernel_variance = adamw(
        kernel_weight, kernel_moment, kernel_square, kernel_total, factor, RATE_VECTOR, 0.0
    )
    sublayer_rms = jnp.sqrt(summed_stats[:2] / (summed_stats[2] * width_full))
    return (
        output_rows,
        input_grad,
        inputs_master,
        inputs_momentum,
        inputs_variance,
        mixing_master,
        mixing_momentum,
        mixing_variance,
        expand_master,
        expand_momentum,
        expand_variance,
        reduce_master,
        reduce_momentum,
        reduce_variance,
        biases_master,
        biases_momentum,
        biases_variance,
        shared_master,
        shared_momentum,
        shared_variance,
        kernel_master,
        kernel_momentum,
        kernel_variance,
        grad_norm,
        sublayer_rms,
    )


def solution(mesh):
    placed = (
        P("dp", None),
        P("dp", None),
        P("dp", None),
        P("dp"),
        P(None, "dp", "head"),
        P(None, "dp", "head"),
        P(None, "dp", "head"),
        P("head", "dp"),
        P("head", "dp"),
        P("head", "dp"),
        P("dp", "head"),
        P("dp", "head"),
        P("dp", "head"),
        P("head", "dp"),
        P("head", "dp"),
        P("head", "dp"),
        P("head", "dp"),
        P("head", "dp"),
        P("head", "dp"),
        P(None, "dp"),
        P(None, "dp"),
        P(None, "dp"),
        P("head", None),
        P("head", None),
        P("head", None),
    )
    return jax.shard_map(
        body,
        mesh=mesh,
        in_specs=placed,
        out_specs=(
            P("dp", None),
            P("dp", None),
            P(None, "dp", "head"),
            P(None, "dp", "head"),
            P(None, "dp", "head"),
            P("head", "dp"),
            P("head", "dp"),
            P("head", "dp"),
            P("dp", "head"),
            P("dp", "head"),
            P("dp", "head"),
            P("head", "dp"),
            P("head", "dp"),
            P("head", "dp"),
            P("head", "dp"),
            P("head", "dp"),
            P("head", "dp"),
            P(None, "dp"),
            P(None, "dp"),
            P(None, "dp"),
            P("head", None),
            P("head", None),
            P("head", None),
            P(),
            P(),
        ),
        check_vma=False,
    )
```

time: 1610 us -> 389 us (0.24)
  waiting for transfers between devices: 902 us -> 85.5 us
  matrix products: 277 us -> 20.7 us
  blocking collectives: 206 us -> 0 us
  Pallas kernels: 0 us -> 134 us
  other arithmetic: 128 us -> 48.7 us
  starting transfers between devices: 0.71 us -> 36.5 us
  local copies, waits for them, and re-layouts: 53.6 us -> 35.4 us
    reduce_scatter x3 -> x0, waiting for transfers between devices: 404 us -> none  [the longest x1 140 us: body(): lax.psum_scatter(expand_grad, 'dp', scatter_dimension=0, tiled=True)]
    unnamed x16 -> x1, waiting for transfers between devices: 313 us -> 0.02 us
    dot_general x100 -> x5, matrix products: 260 us -> 20.7 us  [the longest x2 6.6 us: inputs_part(): jnp.einsum('rd,kr->dk', tokens, gradient, preferred_element_type=jnp.floa...]
    pallas_call x0 -> x9, Pallas kernels: none -> 134 us  [the longest x2 36.9 us: attention_backward(): pl.pallas_call(attention_backward_body, grid=(1,), in_specs=[pl.BlockSpec...]
    all_gather x3 -> x1, waiting for transfers between devices: 101 us -> 1.26 us  [body(): late_full = lax.all_gather(late_low, 'dp', axis=0, tiled=True)]
    reduce_sum x25 -> x4, other arithmetic: 88.5 us -> 1.86 us  [the longest x2 0.64 us: body(): jnp.sum(gradient.astype(jnp.float32), axis=1).reshape(3, part_width)]
    psum x4 -> x0, waiting for transfers between devices: 84.4 us -> none  [the longest x1 29.6 us: body(): d_hidden = lax.psum(hidden_part, 'head') + d_res_two]
    ppermute x0 -> x35, waiting for transfers between devices: none -> 84.2 us  [swap(): return lax.ppermute(array, axis, [(i, i ^ 1 << bit) for i in range(count)])]
  transfers between devices with their start and end apart: 13 -> 36, of which waited for: 11 -> 20; matrix products, arithmetic and copies ran while one was open for 8% -> 22% of each run, Pallas kernels for 0% -> 18%
where the time goes in v2:
time: 389 us; the launch traced here: 384 us
  Pallas kernels  134 us (34%)
  waiting for transfers between devices  85.5 us (22%)
  other arithmetic  48.7 us (13%)
  starting transfers between devices  36.5 us (9%)
  local copies, waits for them, and re-layouts  35.4 us (9%)
  between operations  23.7 us (6%)
  matrix products  20.7 us (5%)
    ppermute x35, waiting for transfers between devices, swap(): return lax.ppermute(array, axis, [(i, i ^ 1 << bit) for i in range(count)])  84.2 us
    pallas_call x2, Pallas kernels, attention_backward(): pl.pallas_call(attention_backward_body, grid=(1,), in_specs=[pl.BlockSpec...  36.9 us
    ppermute x35, starting transfers between devices, swap(): return lax.ppermute(array, axis, [(i, i ^ 1 << bit) for i in range(count)])  36.4 us
    pallas_call x1, Pallas kernels, attention_forward(): pl.pallas_call(attention_forward_body, in_specs=[pl.BlockSpec(memory_spac...  25.9 us
    pallas_call x1, Pallas kernels, hidden_backward(): pl.pallas_call(hidden_backward_body, grid=(row_count // ROWS,), in_specs=...  19.7 us
    pallas_call x1, Pallas kernels, hidden_forward(): pl.pallas_call(hidden_forward_body, grid=(row_count // ROWS,), in_specs=[...  19 us
    add x12, other arithmetic, take(): self.current = self.kept.astype(jnp.float32) + received.astype(jnp.float32)  14.4 us
    pallas_call x2, Pallas kernels, turned_dot(): pl.pallas_call(turned_dot_body, grid=(row_count // ROWS,), in_specs=specs...  14.2 us
  transfers between devices with their start and end apart: 36, of which 20 were waited for; matrix products, arithmetic and copies ran while one was open for 22% of the time, Pallas kernels for 18%

profile of v2, /device:TPU:0, one launch (start us, length us, event | category | flops | bytes accessed | tf_op | source)
XLA Modules:
  0.0 384.3 jit_solution(1821708687160822693)
XLA Ops:
  13.7 4.1 %collective-permute-start = (bf16[1,1,1,1,49,576]{5,4,3,2,1,0:T(8,128)(2,1)S(1)}, bf16[1,1,1,1,49,576]{5,4,3,2,1,0:T(8,128)(2,1)S(1)}, u32[]{:S(2)}, u32[]{:S(2)}) collective-permute-start(bf16[1,1,1,1,49,576]{5,4,3,2,1,0:T(8,128)(2,1)S(1)} %get-tuple-element.248), channel_id=1, source_target_pairs={{0,16},{2,18},{4,20},{6,22},{8,24},{10,26},{12,28},{14,30},{16,0},... | collective-permute-start | bytes 169352 | tf_op jit(solution)/shard_map/ppermute | solution.py:33
  18.2 6.1 %collective-permute-done.4 = bf16[1,1,1,1,48,576]{5,4,3,2,1,0:T(8,128)(2,1)S(1)} collective-permute-done((bf16[1,1,1,1,48,576]{5,4,3,2,1,0:T(8,128)(2,1)S(1)}, bf16[1,1,1,1,48,576]{5,4,3,2,1,0:T(8,128)(2,1)S(1)}, u32[]{:S(2)}, u32[]{:S(2)}) %collective-permute-start.4) | collective-permute-done | bytes 55328 | tf_op jit(solution)/shard_map/ppermute | solution.py:33
  26.8 6.5 %collective-permute-done.5 = bf16[2,1,1,1,48,576]{5,4,3,2,1,0:T(8,128)(2,1)S(1)} collective-permute-done((bf16[2,1,1,1,48,576]{5,4,3,2,1,0:T(8,128)(2,1)S(1)}, bf16[2,1,1,1,48,576]{5,4,3,2,1,0:T(8,128)(2,1)S(1)}, u32[]{:S(2)}, u32[]{:S(2)}) %collective-permute-start.5) | collective-permute-done | bytes 110624 | tf_op jit(solution)/shard_map/ppermute | solution.py:33
  33.4 1.6 collective-permute-start.6
  35.0 3.2 collective-permute-done.1
  38.5 1.7 collective-permute-start.2
  41.6 8.8 %collective-permute-done.2 = bf16[2,2,1,1,49,576]{5,4,3,2,1,0:T(8,128)(2,1)S(1)} collective-permute-done((bf16[2,2,1,1,49,576]{5,4,3,2,1,0:T(8,128)(2,1)S(1)}, bf16[2,2,1,1,49,576]{5,4,3,2,1,0:T(8,128)(2,1)S(1)}, u32[]{:S(2)}, u32[]{:S(2)}) %collective-permute-start.2) | collective-permute-done | bytes 225824 | tf_op jit(solution)/shard_map/ppermute | solution.py:33
  52.9 9.5 %collective-permute-done.7 = bf16[2,2,1,2,48,576]{5,4,3,2,1,0:T(8,128)(2,1)S(1)} collective-permute-done((bf16[2,2,1,2,48,576]{5,4,3,2,1,0:T(8,128)(2,1)S(1)}, bf16[2,2,1,2,48,576]{5,4,3,2,1,0:T(8,128)(2,1)S(1)}, u32[]{:S(2)}, u32[]{:S(2)}) %collective-permute-start.7) | collective-permute-done | bytes 442400 | tf_op jit(solution)/shard_map/ppermute | solution.py:33
  63.6 3.0 collective-permute-done.3
  69.4 8.6 %shard_map.432.proj_ref = bf16[2,3,192,1536]{3,2,1,0:T(8,128)(2,1)} custom-call(bf16[768,576]{1,0:T(8,128)(2,1)} %bitcast.139, bf16[768,576]{1,0:T(8,128)(2,1)} %bitcast.137, bf16[1536,768]{1,0:T(8,128)(2,1)} %tokens_ref.3, f32[1152,1]{1,0:T(8,128)} %broadcast_in_dim.58.bias_ref), custom_call_target="tpu_custom_call" | custom-call | flops 2717908992 | bytes 8000000 | tf_op jit(solution)/shard_map/pallas_call | solution.py:965
  78.0 25.9 %shard_map.433 = (bf16[384,1536]{1,0:T(8,128)(2,1)S(1)}, bf16[6,128,1536]{2,1,0:T(8,128)(2,1)S(1)}, bf16[6,128,1536]{2,1,0:T(8,128)(2,1)}, f32[2,384,128]{2,1,0:...) custom-call(s32[1,2]{1,0:T(1,128)S(1)} %copy-done.4, ...), custom_call_target="tpu_custom_call" | custom-call | flops 20000000000 | bytes 20000000 | tf_op jit(solution)/shard_map/pallas_call | solution.py:359
  109.1 5.9 %shard_map.434.own_ref = bf16[1536,768]{1,0:T(8,128)(2,1)} custom-call(bf16[384,1536]{1,0:T(8,128)(2,1)} %copy-done.2, bf16[768,3456]{1,0:T(8,128)(2,1)} %all-gather.2.cloned.1.call-done.refs_1_.expand_ref.reduce_ref.mixing_ref), custom_call_target="tpu_custom_call" | custom-call | flops 905969664 | bytes 8000000 | tf_op jit(solution)/shard_map/pallas_call | solution.py:938
  120.2 19.0 %shard_map.435 = (bf16[1536,768]{1,0:T(8,128)(2,1)}, f32[1536,768]{1,0:T(8,128)}, bf16[1536,768]{1,0:T(8,128)(2,1)}, bf16[1536,768]{1,0:T(8,128)(2,1)}, f32[1536...) custom-call(bf16[1536,768]{1,0:T(8,128)(2,1)} %shard_map.434.own_ref, ...), custom_call_target="tpu_custom_call" | custom-call | flops 7247757312 | bytes 30000000 | tf_op jit(solution)/shard_map/pallas_call | solution.py:720
  140.4 3.8 collective-permute-done.9.other_ref
  145.6 19.7 %shard_map.436 = (f32[1536,768]{1,0:T(8,128)}, bf16[1536,768]{1,0:T(8,128)(2,1)}, bf16[1536,1536]{1,0:T(8,128)(2,1)}, bf16[1536,768]{1,0:T(8,128)(2,1)}, f32[8,768]{1,0:T(8,128)}, /*index=5*/f32[1,1536]{1,0:T(1,128)}) custom-call(bf16[1536,768]{1,0:T(8,128)(2,1)} %get-tuple-element.67.own_ref, bf16[1536,768]{1,0:T(8,128)(2,1)} %copy-done.31, ...), custom_call_target="tpu_custom_call" | custom-call | flops 7247757312 | bytes 30000000 | tf_op jit(solution)/shard_map/pallas_call | solution.py:814
  165.8 6.6 %convolution_convert_fusion = bf16[768,1536]{1,0:T(8,128)(2,1)S(1)} fusion(bf16[1536,768]{1,0:T(8,128)(2,1)S(1)} %copy-done.50, bf16[1536,1536]{1,0:T(8,128)(2,1)} %get-tuple-element.78), kind=kOutput, calls=%fused_computation.3 | convolution fusion | flops 3625058304 | bytes 9437184 | tf_op jit(solution)/shard_map/rd,rf->df/dot_general | solution.py:1082
  175.3 4.3 %convolution_convert_fusion.1 = bf16[768,1536]{1,0:T(8,128)(2,1)S(1)} fusion(bf16[1536,768]{1,0:T(8,128)(2,1)S(1)} %copy-done.25, bf16[1536,1536]{1,0:T(8,128)(2,1)S(1)} %copy-done.49), kind=kOutput, calls=%fused_computation.4 | convolution fusion | flops 3625058304 | bytes 9437184 | tf_op jit(solution)/shard_map/rd,rf->df/dot_general | solution.py:1081
  184.3 9.3 %shard_map.437 = (bf16[1536,768]{1,0:T(8,128)(2,1)}, bf16[384,1536]{1,0:T(8,128)(2,1)}, f32[8,768]{1,0:T(8,128)}) custom-call(bf16[1536,768]{1,0:T(8,128)(2,1)} %get-tuple-element.71.own_ref, bf16[1536,768]{1,0:T(8,128)(2,1)} %collective-permute-done.10.other_ref, bf16[1536,768]{1,0:T(8,128)(2,1)} %get-tuple-element.72.d_two_ref, ...), custom_call_target="tpu_custom_call" | custom-call | flops 905969664 | bytes 14000000 | tf_op jit(solution)/shard_map/pallas_call | solution.py:888
  193.6 3.2 convolution_convert_fusion.4
  198.3 18.4 %shard_map.438 = (bf16[576,1536]{1,0:T(8,128)(2,1)S(1)}, f32[3,256]{1,0:T(4,128)S(1)}) custom-call(s32[1,2]{1,0:T(1,128)S(1)} %copy-done.4, bf16[2,3,192,1536]{3,2,1,0:T(8,128)(2,1)} %shard_map.432.proj_ref, f32[3,256]{1,0:T(4,128)S(1)} %get-tuple-element.267.taps_ref, bf16[384,1536]{1,0:T(8,128)(2,1)S(1)} %copy-done.5, bf16[6,128,1536]{2,1,0:T(8,128)(2,1)} %copy-done.6, ...), custom_call_target="tpu_custom_call" | custom-call | flops 15000000512 | bytes 10000000 | tf_op jit(solution)/shard_map/pallas_call | solution.py:589
  217.1 1.9 convert_add_fusion.1
  220.0 2.5 fusion
  222.5 1.5 copy.179
  225.0 2.0 convert_add_fusion.2
  231.0 18.5 %shard_map.439 = (bf16[576,1536]{1,0:T(8,128)(2,1)S(1)}, f32[3,256]{1,0:T(4,128)S(1)}) custom-call(s32[1,2]{1,0:T(1,128)S(1)} %copy-done.4, bf16[2,3,192,1536]{3,2,1,0:T(8,128)(2,1)} %shard_map.432.proj_ref, f32[3,256]{1,0:T(4,128)S(1)} %get-tuple-element.266.taps_ref, bf16[384,1536]{1,0:T(8,128)(2,1)S(1)} %copy-done.5, bf16[6,128,1536]{2,1,0:T(8,128)(2,1)} %copy-done.6, ...), custom_call_target="tpu_custom_call" | custom-call | flops 15000000512 | bytes 10000000 | tf_op jit(solution)/shard_map/pallas_call | solution.py:589
  250.2 1.5 collective-permute-start.26
  251.7 2.4 collective-permute-done.26
  261.6 4.1 %fusion.1 = bf16[768,576]{0,1:T(8,128)(2,1)} fusion(bf16[576,1536]{1,0:T(8,128)(2,1)S(1)} %get-tuple-element.98.refs_2_, bf16[1536,768]{1,0:T(8,128)(2,1)} %tokens_ref.3), kind=kOutput, calls=%fused_computation.15 | convolution fusion | flops 1359396864 | bytes 5013504 | tf_op jit(solution)/shard_map/rd,kr->dk/dot_general | solution.py:1104
  265.7 2.3 copy.180
  268.9 1.7 collective-permute-start.29
  270.6 1.9 constant_dynamic-slice_fusion.1
  279.2 5.0 %collective-permute-done.21 = bf16[2,2,1,1,48,384]{5,4,3,2,1,0:T(8,128)(2,1)S(1)} collective-permute-done((bf16[2,2,1,1,48,384]{5,4,3,2,1,0:T(8,128)(2,1)}, bf16[2,2,1,1,48,384]{5,4,3,2,1,0:T(8,128)(2,1)S(1)}, u32[]{:S(2)}, u32[]{:S(2)}) %collective-permute-start.21) | collective-permute-done | bytes 147488 | tf_op jit(solution)/shard_map/ppermute | solution.py:33
  284.2 1.7 convert_add_fusion.11
  293.2 8.3 %shard_map.440 = bf16[1536,768]{1,0:T(8,128)(2,1)} custom-call(bf16[576,1536]{1,0:T(8,128)(2,1)} %copy-done, bf16[768,576]{1,0:T(8,128)(2,1)} %bitcast.140, bf16[576,1536]{1,0:T(8,128)(2,1)} %copy-done.1, bf16[768,576]{1,0:T(8,128)(2,1)} %bitcast.138), custom_call_target="tpu_custom_call" | custom-call | flops 2717908992 | bytes 8000000 | tf_op jit(solution)/shard_map/pallas_call | solution.py:938
  304.1 4.8 %collective-permute-done.19 = bf16[2,2,1,1,48,576]{5,4,3,2,1,0:T(8,128)(2,1)S(1)} collective-permute-done((bf16[2,2,1,1,48,576]{5,4,3,2,1,0:T(8,128)(2,1)S(1)}, bf16[2,2,1,1,48,576]{5,4,3,2,1,0:T(8,128)(2,1)S(1)}, u32[]{:S(2)}, u32[]{:S(2)}) %collective-permute-start.19) | collective-permute-done | bytes 221216 | tf_op jit(solution)/shard_map/ppermute | solution.py:33
  309.7 1.6 concatenate.510
  313.4 7.0 %collective-permute-done.22 = bf16[2,1,1,1,48,1536]{5,4,3,2,1,0:T(8,128)(2,1)S(1)} collective-permute-done((bf16[2,1,1,1,48,1536]{5,4,3,2,1,0:T(8,128)(2,1)S(1)}, bf16[2,1,1,1,48,1536]{5,4,3,2,1,0:T(8,128)(2,1)S(1)}, u32[]{:S(2)}, u32[]{:S(2)}) %collective-permute-start.22) | collective-permute-done | bytes 294944 | tf_op jit(solution)/shard_map/ppermute | solution.py:33
  321.2 2.4 collective-permute-start.25
  323.6 8.6 %collective-permute-done.23 = bf16[1,1,1,1,48,1536]{5,4,3,2,1,0:T(8,128)(2,1)S(1)} collective-permute-done((bf16[1,1,1,1,48,1536]{5,4,3,2,1,0:T(8,128)(2,1)S(1)}, bf16[1,1,1,1,48,1536]{5,4,3,2,1,0:T(8,128)(2,1)S(1)}, u32[]{:S(2)}, u32[]{:S(2)}) %collective-permute-start.23) | collective-permute-done | bytes 147488 | tf_op jit(solution)/shard_map/ppermute | solution.py:33
  338.1 2.0 concatenate.516
  341.9 2.8 collective-permute-done.31
  345.4 2.9 collective-permute-done.32
  348.3 3.5 collective-permute-done.33
  352.4 3.9 %collective-permute-done.34 = f32[1,128]{1,0:T(1,128)S(1)} collective-permute-done((f32[1,128]{1,0:T(1,128)S(1)}, f32[1,128]{1,0:T(1,128)S(1)}, u32[]{:S(2)}, u32[]{:S(2)}) %collective-permute-start.34) | collective-permute-done | bytes 544 | tf_op jit(solution)/shard_map/ppermute | solution.py:33
  365.8 1.7 multiply_subtract_fusion.3
  367.5 2.3 multiply_subtract_fusion.2
  370.9 2.0 multiply_subtract_fusion.1
  372.9 2.9 convert_add_fusion
  (288 shorter events, 87.3 us)
Async XLA Ops:
  7.2 10.8 %copy-start.40 = (f32[6,33]{1,0:T(8,128)S(1)}, f32[6,33]{1,0:T(8,128)}, u32[]{:S(2)}) copy-start(f32[6,33]{1,0:T(8,128)} %param.47) | copy-start | bytes 2380
  7.2 101.9 %all-gather.2.cloned.1.call-start = ((), (), s32[]{:S(2)}) async-start(), calls=%async_computation | async-start | bytes 5640192 | tf_op jit(solution)/shard_map/all_gather | solution.py:1046
  13.7 11.4 %collective-permute-start = (bf16[1,1,1,1,49,576]{5,4,3,2,1,0:T(8,128)(2,1)S(1)}, bf16[1,1,1,1,49,576]{5,4,3,2,1,0:T(8,128)(2,1)S(1)}, u32[]{:S(2)}, u32[]{:S(2)}) collective-permute-start(bf16[1,1,1,1,49,576]{5,4,3,2,1,0:T(8,128)(2,1)S(1)} %get-tuple-element.248), channel_id=1, source_target_pairs={{0,16},{2,18},{4,20},{6,22},{8,24},{10,26},{12,28},{14,30},{16,0},... | collective-permute-start | bytes 169352 | tf_op jit(solution)/shard_map/ppermute | solution.py:33
  17.9 6.4 %collective-permute-start.4 = (bf16[1,1,1,1,48,576]{5,4,3,2,1,0:T(8,128)(2,1)S(1)}, bf16[1,1,1,1,48,576]{5,4,3,2,1,0:T(8,128)(2,1)S(1)}, u32[]{:S(2)}, u32[]{:S(2)}) collective-permute-start(bf16[1,1,1,1,48,576]{5,4,3,2,1,0:T(8,128)(2,1)S(1)} %pad_maximum_fusion.5), channel_id=1, source_target_pairs={{0,16},{2,18},{4,20},{6,22},{8,24},{10,26},{12,28},{14,30},{16,0},... | collective-permute-start | bytes 165896 | tf_op jit(solution)/shard_map/ppermute | solution.py:33
  24.3 9.0 %collective-permute-start.5 = (bf16[2,1,1,1,48,576]{5,4,3,2,1,0:T(8,128)(2,1)S(1)}, bf16[2,1,1,1,48,576]{5,4,3,2,1,0:T(8,128)(2,1)S(1)}, u32[]{:S(2)}, u32[]{:S(2)}) collective-permute-start(bf16[2,1,1,1,48,576]{5,4,3,2,1,0:T(8,128)(2,1)S(1)} %maximum_select_fusion.11), channel_id=1, source_target_pairs={{0,8},{2,10},{4,12},{6,14},{8,0},{10,2},{12,4},{14,6},{16,24},{18,... | collective-permute-start | bytes 331784 | tf_op jit(solution)/shard_map/ppermute | solution.py:33
  25.1 13.1 %collective-permute-start.1 = (bf16[2,1,1,1,49,576]{5,4,3,2,1,0:T(8,128)(2,1)S(1)}, bf16[2,1,1,1,49,576]{5,4,3,2,1,0:T(8,128)(2,1)S(1)}, u32[]{:S(2)}, u32[]{:S(2)}) collective-permute-start(bf16[2,1,1,1,49,576]{5,4,3,2,1,0:T(8,128)(2,1)S(1)} %maximum_select_fusion.9), channel_id=1, source_target_pairs={{0,8},{2,10},{4,12},{6,14},{8,0},{10,2},{12,4},{14,6},{16,24},{18,... | collective-permute-start | bytes 338696 | tf_op jit(solution)/shard_map/ppermute | solution.py:33
  33.4 7.1 %collective-permute-start.6 = (bf16[2,2,1,1,48,576]{5,4,3,2,1,0:T(8,128)(2,1)S(1)}, bf16[2,2,1,1,48,576]{5,4,3,2,1,0:T(8,128)(2,1)S(1)}, u32[]{:S(2)}, u32[]{:S(2)}) collective-permute-start(bf16[2,2,1,1,48,576]{5,4,3,2,1,0:T(8,128)(2,1)S(1)} %maximum_select_fusion.7), channel_id=1, source_target_pairs={{0,2},{2,0},{4,6},{6,4},{8,10},{10,8},{12,14},{14,12},{16,18},{18,... | collective-permute-start | bytes 663560 | tf_op jit(solution)/shard_map/ppermute | solution.py:33
  38.5 12.0 %collective-permute-start.2 = (bf16[2,2,1,1,49,576]{5,4,3,2,1,0:T(8,128)(2,1)S(1)}, bf16[2,2,1,1,49,576]{5,4,3,2,1,0:T(8,128)(2,1)S(1)}, u32[]{:S(2)}, u32[]{:S(2)}) collective-permute-start(bf16[2,2,1,1,49,576]{5,4,3,2,1,0:T(8,128)(2,1)S(1)} %maximum_select_fusion.5), channel_id=1, source_target_pairs={{0,4},{2,6},{4,0},{6,2},{8,12},{10,14},{12,8},{14,10},{16,20},{18,... | collective-permute-start | bytes 677384 | tf_op jit(solution)/shard_map/ppermute | solution.py:33
  40.6 21.8 %collective-permute-start.7 = (bf16[2,2,1,2,48,576]{5,4,3,2,1,0:T(8,128)(2,1)S(1)}, bf16[2,2,1,2,48,576]{5,4,3,2,1,0:T(8,128)(2,1)S(1)}, u32[]{:S(2)}, u32[]{:S(2)}) collective-permute-start(bf16[2,2,1,2,48,576]{5,4,3,2,1,0:T(8,128)(2,1)S(1)} %maximum_select_fusion.3), channel_id=1, source_target_pairs={{0,4},{2,6},{4,0},{6,2},{8,12},{10,14},{12,8},{14,10},{16,20},{18,... | collective-permute-start | bytes 1327112 | tf_op jit(solution)/shard_map/ppermute | solution.py:33
  51.0 15.6 %collective-permute-start.3 = (bf16[2,2,2,1,49,576]{5,2,4,3,1,0:T(2,128)(2,1)S(1)}, bf16[2,2,2,1,49,576]{5,2,4,3,1,0:T(2,128)(2,1)S(1)}, u32[]{:S(2)}, u32[]{:S(2)}) collective-permute-start(bf16[2,2,2,1,49,576]{5,2,4,3,1,0:T(2,128)(2,1)S(1)} %copy.168), channel_id=1, source_target_pairs={{0,2},{2,0},{4,6},{6,4},{8,10},{10,8},{12,14},{14,12},{16,18},{18,... | collective-permute-start | bytes 1354760 | tf_op jit(solution)/shard_map/ppermute | solution.py:33
  115.1 5.1 %collective-permute-start.8 = (bf16[1536,768]{1,0:T(8,128)(2,1)}, bf16[1536,768]{1,0:T(8,128)(2,1)}, u32[]{:S(2)}, u32[]{:S(2)}) collective-permute-start(bf16[1536,768]{1,0:T(8,128)(2,1)} %shard_map.434.own_ref), channel_id=1, source_target_pairs={{0,1},{1,0},{2,3},{3,2},{4,5},{5,4},{6,7},{7,6},{8,9},{9,8},{10,11... | collective-permute-start | bytes 7077896 | tf_op jit(solution)/shard_map/ppermute | solution.py:33
  139.2 4.9 %collective-permute-start.9 = (bf16[1536,768]{1,0:T(8,128)(2,1)}, bf16[1536,768]{1,0:T(8,128)(2,1)S(1)}, u32[]{:S(2)}, u32[]{:S(2)}) collective-permute-start(bf16[1536,768]{1,0:T(8,128)(2,1)} %get-tuple-element.67.own_ref), channel_id=1, source_target_pairs={{0,1},{1,0},{2,3},{3,2},{4,5},{5,4},{6,7},{7,6},{8,9},{9,8},{10,11... | collective-permute-start | bytes 7077896 | tf_op jit(solution)/shard_map/ppermute | solution.py:33
  145.6 20.2 %copy-start.50 = (bf16[1536,768]{1,0:T(8,128)(2,1)S(1)}, bf16[1536,768]{1,0:T(8,128)(2,1)}, u32[]{:S(2)}) copy-start(bf16[1536,768]{1,0:T(8,128)(2,1)} %get-tuple-element.77) | copy-start | bytes 7077892
  165.3 19.0 %collective-permute-start.10 = (bf16[1536,768]{1,0:T(8,128)(2,1)}, bf16[1536,768]{1,0:T(8,128)(2,1)}, u32[]{:S(2)}, u32[]{:S(2)}) collective-permute-start(bf16[1536,768]{1,0:T(8,128)(2,1)} %get-tuple-element.71.own_ref), channel_id=1, source_target_pairs={{0,1},{1,0},{2,3},{3,2},{4,5},{5,4},{6,7},{7,6},{8,9},{9,8},{10,11... | collective-permute-start | bytes 7077896 | tf_op jit(solution)/shard_map/ppermute | solution.py:33
  173.5 43.6 %collective-permute-start.12 = (bf16[2,2,2,1,48,1536]{5,4,3,2,1,0:T(8,128)(2,1)}, bf16[2,2,2,1,48,1536]{5,4,3,2,1,0:T(8,128)(2,1)}, u32[]{:S(2)}, u32[]{:S(2)}) collective-permute-start(bf16[2,2,2,1,48,1536]{5,4,3,2,1,0:T(8,128)(2,1)} %constant_dynamic-slice_fusion.4), channel_id=1, source_target_pairs={{0,2},{2,0},{4,6},{6,4},{8,10},{10,8},{12,14},{14,12},{16,18},{18,... | collective-permute-start | bytes 3538952 | tf_op jit(solution)/shard_map/ppermute | solution.py:33
  182.2 40.3 %collective-permute-start.11 = (bf16[2,2,1,2,48,1536]{5,4,3,2,1,0:T(8,128)(2,1)}, bf16[2,2,1,2,48,1536]{5,4,3,2,1,0:T(8,128)(2,1)}, u32[]{:S(2)}, u32[]{:S(2)}) collective-permute-start(bf16[2,2,1,2,48,1536]{5,4,3,2,1,0:T(8,128)(2,1)} %constant_dynamic-slice_fusion.5), channel_id=1, source_target_pairs={{0,4},{2,6},{4,0},{6,2},{8,12},{10,14},{12,8},{14,10},{16,20},{18,... | collective-permute-start | bytes 3538952 | tf_op jit(solution)/shard_map/ppermute | solution.py:33
  196.9 19.8 %copy-start.35 = (bf16[768,384]{1,0:T(8,128)(2,1)}, bf16[768,384]{1,0:T(8,128)(2,1)S(1)}, u32[]{:S(2)}) copy-start(bf16[768,384]{1,0:T(8,128)(2,1)S(1)} %convolution_convert_fusion.4) | copy-start | bytes 1769476
  197.7 31.3 %collective-permute-start.13 = (bf16[2,2,2,1,48,384]{5,4,3,2,1,0:T(8,128)(2,1)}, bf16[2,2,2,1,48,384]{5,4,3,2,1,0:T(8,128)(2,1)}, u32[]{:S(2)}, u32[]{:S(2)}) collective-permute-start(bf16[2,2,2,1,48,384]{5,4,3,2,1,0:T(8,128)(2,1)} %constant_dynamic-slice_fusion.3), channel_id=1, source_target_pairs={{0,2},{2,0},{4,6},{6,4},{8,10},{10,8},{12,14},{14,12},{16,18},{18,... | collective-permute-start | bytes 884744 | tf_op jit(solution)/shard_map/ppermute | solution.py:33
  198.2 18.8 %copy-start.28 = (bf16[768,1536]{1,0:T(8,128)(2,1)S(1)}, bf16[768,1536]{1,0:T(8,128)(2,1)}, u32[]{:S(2)}) copy-start(bf16[768,1536]{1,0:T(8,128)(2,1)} %copy-done.27) | copy-start | bytes 7077892
  231.0 24.5 %copy-start.47 = (f32[1,768]{1,0:T(1,128)S(1)}, f32[1,768]{1,0:T(1,128)}, u32[]{:S(2)}) copy-start(f32[1,768]{1,0:T(1,128)} %get-tuple-element.106) | copy-start | bytes 9220
  249.5 16.1 %copy-start.1 = (bf16[576,1536]{1,0:T(8,128)(2,1)}, bf16[576,1536]{1,0:T(8,128)(2,1)S(1)}, u32[]{:S(2)}) copy-start(bf16[576,1536]{1,0:T(8,128)(2,1)S(1)} %get-tuple-element.98.refs_2_) | copy-start | bytes 5308420
  250.2 3.9 %collective-permute-start.26 = (f32[56,128]{1,0:T(8,128)S(1)}, f32[56,128]{1,0:T(8,128)S(1)}, u32[]{:S(2)}, u32[]{:S(2)}) collective-permute-start(f32[56,128]{1,0:T(8,128)S(1)} %bitcast.148), channel_id=1, source_target_pairs={{0,2},{2,0},{4,6},{6,4},{8,10},{10,8},{12,14},{14,12},{16,18},{18,... | collective-permute-start | bytes 86024 | tf_op jit(solution)/shard_map/ppermute | solution.py:33
  254.1 6.2 %collective-permute-start.27 = (f32[56,128]{1,0:T(8,128)S(1)}, f32[56,128]{1,0:T(8,128)S(1)}, u32[]{:S(2)}, u32[]{:S(2)}) collective-permute-start(f32[56,128]{1,0:T(8,128)S(1)} %bitcast_add_fusion.1), channel_id=1, source_target_pairs={{0,4},{2,6},{4,0},{6,2},{8,12},{10,14},{12,8},{14,10},{16,20},{18,... | collective-permute-start | bytes 86024 | tf_op jit(solution)/shard_map/ppermute | solution.py:33
  256.1 32.5 %collective-permute-start.15 = (bf16[2,2,1,1,48,1536]{5,4,3,2,1,0:T(8,128)(2,1)}, bf16[2,2,1,1,48,1536]{5,4,3,2,1,0:T(8,128)(2,1)}, u32[]{:S(2)}, u32[]{:S(2)}) collective-permute-start(bf16[2,2,1,1,48,1536]{5,4,3,2,1,0:T(8,128)(2,1)} %dynamic-slice_convert_fusion.1), channel_id=1, source_target_pairs={{0,2},{2,0},{4,6},{6,4},{8,10},{10,8},{12,14},{14,12},{16,18},{18,... | collective-permute-start | bytes 1769480 | tf_op jit(solution)/shard_map/ppermute | solution.py:33
  256.8 33.0 %collective-permute-start.14 = (bf16[2,2,1,1,48,1536]{5,4,3,2,1,0:T(8,128)(2,1)}, bf16[2,2,1,1,48,1536]{5,4,3,2,1,0:T(8,128)(2,1)}, u32[]{:S(2)}, u32[]{:S(2)}) collective-permute-start(bf16[2,2,1,1,48,1536]{5,4,3,2,1,0:T(8,128)(2,1)} %dynamic-slice_convert_fusion), channel_id=1, source_target_pairs={{0,4},{2,6},{4,0},{6,2},{8,12},{10,14},{12,8},{14,10},{16,20},{18,... | collective-permute-start | bytes 1769480 | tf_op jit(solution)/shard_map/ppermute | solution.py:33
  258.2 25.9 %collective-permute-start.16 = (bf16[2,2,1,2,48,576]{5,4,3,2,1,0:T(8,128)(2,1)}, bf16[2,2,1,2,48,576]{5,4,3,2,1,0:T(8,128)(2,1)}, u32[]{:S(2)}, u32[]{:S(2)}) collective-permute-start(bf16[2,2,1,2,48,576]{5,4,3,2,1,0:T(8,128)(2,1)} %constant_dynamic-slice_fusion.2), channel_id=1, source_target_pairs={{0,4},{2,6},{4,0},{6,2},{8,12},{10,14},{12,8},{14,10},{16,20},{18,... | collective-permute-start | bytes 1327112 | tf_op jit(solution)/shard_map/ppermute | solution.py:33
  258.9 25.3 %collective-permute-start.21 = (bf16[2,2,1,1,48,384]{5,4,3,2,1,0:T(8,128)(2,1)}, bf16[2,2,1,1,48,384]{5,4,3,2,1,0:T(8,128)(2,1)S(1)}, u32[]{:S(2)}, u32[]{:S(2)}) collective-permute-start(bf16[2,2,1,1,48,384]{5,4,3,2,1,0:T(8,128)(2,1)} %dynamic-slice_convert_fusion.7), channel_id=1, source_target_pairs={{0,4},{2,6},{4,0},{6,2},{8,12},{10,14},{12,8},{14,10},{16,20},{18,... | collective-permute-start | bytes 442376 | tf_op jit(solution)/shard_map/ppermute | solution.py:33
  260.3 7.8 %collective-permute-start.28 = (f32[56,128]{1,0:T(8,128)S(1)}, f32[56,128]{1,0:T(8,128)}, u32[]{:S(2)}, u32[]{:S(2)}) collective-permute-start(f32[56,128]{1,0:T(8,128)S(1)} %fusion.61), channel_id=1, source_target_pairs={{0,8},{2,10},{4,12},{6,14},{8,0},{10,2},{12,4},{14,6},{16,24},{18,... | collective-permute-start | bytes 86024 | tf_op jit(solution)/shard_map/ppermute | solution.py:33
  265.7 20.2 %copy-start.21 = (bf16[768,576]{1,0:T(8,128)(2,1)S(1)}, bf16[768,576]{1,0:T(8,128)(2,1)}, u32[]{:S(2)}) copy-start(bf16[768,576]{1,0:T(8,128)(2,1)} %copy-done.20) | copy-start | bytes 2654212
  268.0 20.6 %copy-start.19 = (f32[2,2,1,2,48,1536]{5,4,3,2,1,0:T(8,128)S(1)}, f32[2,2,1,2,48,1536]{5,4,3,2,1,0:T(8,128)}, u32[]{:S(2)}) copy-start(f32[2,2,1,2,48,1536]{5,4,3,2,1,0:T(8,128)} %copy-done.18) | copy-start | bytes 7077892
  268.9 4.8 %collective-permute-start.29 = (f32[56,128]{1,0:T(8,128)S(1)}, f32[56,128]{1,0:T(8,128)S(1)}, u32[]{:S(2)}, u32[]{:S(2)}) collective-permute-start(f32[56,128]{1,0:T(8,128)S(1)} %add.290), channel_id=1, source_target_pairs={{0,16},{2,18},{4,20},{6,22},{8,24},{10,26},{12,28},{14,30},{16,0},... | collective-permute-start | bytes 86024 | tf_op jit(solution)/shard_map/ppermute | solution.py:33
  273.7 27.7 %collective-permute-start.18 = (bf16[2,2,2,1,48,576]{5,4,3,2,1,0:T(8,128)(2,1)}, bf16[2,2,2,1,48,576]{5,4,3,2,1,0:T(8,128)(2,1)}, u32[]{:S(2)}, u32[]{:S(2)}) collective-permute-start(bf16[2,2,2,1,48,576]{5,4,3,2,1,0:T(8,128)(2,1)} %constant_dynamic-slice_fusion.1), channel_id=1, source_target_pairs={{0,2},{2,0},{4,6},{6,4},{8,10},{10,8},{12,14},{14,12},{16,18},{18,... | collective-permute-start | bytes 1327112 | tf_op jit(solution)/shard_map/ppermute | solution.py:33
  274.6 14.0 %copy-start.41 = (f32[56,128]{1,0:T(8,128)}, f32[56,128]{1,0:T(8,128)S(1)}, u32[]{:S(2)}) copy-start(f32[56,128]{1,0:T(8,128)S(1)} %add.291) | copy-start | bytes 86020
  287.2 16.1 %collective-permute-start.20 = (bf16[2,2,1,1,48,576]{5,4,3,2,1,0:T(8,128)(2,1)S(1)}, bf16[2,2,1,1,48,576]{5,4,3,2,1,0:T(8,128)(2,1)S(1)}, u32[]{:S(2)}, u32[]{:S(2)}) collective-permute-start(bf16[2,2,1,1,48,576]{5,4,3,2,1,0:T(8,128)(2,1)S(1)} %dynamic-slice_convert_fusion.5), channel_id=1, source_target_pairs={{0,2},{2,0},{4,6},{6,4},{8,10},{10,8},{12,14},{14,12},{16,18},{18,... | collective-permute-start | bytes 663560 | tf_op jit(solution)/shard_map/ppermute | solution.py:33
  291.9 20.3 %collective-permute-start.24 = (bf16[2,1,1,1,48,3072]{5,4,3,2,1,0:T(8,128)(2,1)}, bf16[2,1,1,1,48,3072]{5,4,3,2,1,0:T(8,128)(2,1)}, u32[]{:S(2)}, u32[]{:S(2)}) collective-permute-start(bf16[2,1,1,1,48,3072]{5,4,3,2,1,0:T(8,128)(2,1)} %fusion.5), channel_id=1, source_target_pairs={{0,8},{2,10},{4,12},{6,14},{8,0},{10,2},{12,4},{14,6},{16,24},{18,... | collective-permute-start | bytes 1769480 | tf_op jit(solution)/shard_map/ppermute | solution.py:33
  302.6 6.3 %collective-permute-start.19 = (bf16[2,2,1,1,48,576]{5,4,3,2,1,0:T(8,128)(2,1)S(1)}, bf16[2,2,1,1,48,576]{5,4,3,2,1,0:T(8,128)(2,1)S(1)}, u32[]{:S(2)}, u32[]{:S(2)}) collective-permute-start(bf16[2,2,1,1,48,576]{5,4,3,2,1,0:T(8,128)(2,1)S(1)} %dynamic-slice_convert_fusion.4), channel_id=1, source_target_pairs={{0,4},{2,6},{4,0},{6,2},{8,12},{10,14},{12,8},{14,10},{16,20},{18,... | collective-permute-start | bytes 663560 | tf_op jit(solution)/shard_map/ppermute | solution.py:33
  311.3 9.0 %collective-permute-start.22 = (bf16[2,1,1,1,48,1536]{5,4,3,2,1,0:T(8,128)(2,1)S(1)}, bf16[2,1,1,1,48,1536]{5,4,3,2,1,0:T(8,128)(2,1)S(1)}, u32[]{:S(2)}, u32[]{:S(2)}) collective-permute-start(bf16[2,1,1,1,48,1536]{5,4,3,2,1,0:T(8,128)(2,1)S(1)} %dynamic-slice_convert_fusion.3), channel_id=1, source_target_pairs={{0,8},{2,10},{4,12},{6,14},{8,0},{10,2},{12,4},{14,6},{16,24},{18,... | collective-permute-start | bytes 884744 | tf_op jit(solution)/shard_map/ppermute | solution.py:33
  320.5 11.7 %collective-permute-start.23 = (bf16[1,1,1,1,48,1536]{5,4,3,2,1,0:T(8,128)(2,1)S(1)}, bf16[1,1,1,1,48,1536]{5,4,3,2,1,0:T(8,128)(2,1)S(1)}, u32[]{:S(2)}, u32[]{:S(2)}) collective-permute-start(bf16[1,1,1,1,48,1536]{5,4,3,2,1,0:T(8,128)(2,1)S(1)} %dynamic-slice_convert_fusion.6), channel_id=1, source_target_pairs={{0,16},{2,18},{4,20},{6,22},{8,24},{10,26},{12,28},{14,30},{16,0},... | collective-permute-start | bytes 442376 | tf_op jit(solution)/shard_map/ppermute | solution.py:33
  321.2 14.2 %copy-start.24 = (f32[2,1,1,1,48,3072]{5,4,3,2,1,0:T(8,128)S(1)}, f32[2,1,1,1,48,3072]{5,4,3,2,1,0:T(8,128)}, u32[]{:S(2)}) copy-start(f32[2,1,1,1,48,3072]{5,4,3,2,1,0:T(8,128)} %copy-done.23) | copy-start | bytes 3538948
  321.2 42.0 %copy-start.42 = (f32[6,48]{1,0:T(8,128)S(1)}, f32[6,48]{1,0:T(8,128)}, u32[]{:S(2)}) copy-start(f32[6,48]{1,0:T(8,128)} %param.44) | copy-start | bytes 3460
  321.2 14.2 %collective-permute-start.25 = (bf16[1,1,1,1,48,3072]{5,4,3,2,1,0:T(8,128)(2,1)S(1)}, bf16[1,1,1,1,48,3072]{5,4,3,2,1,0:T(8,128)(2,1)S(1)}, u32[]{:S(2)}, u32[]{:S(2)}) collective-permute-start(bf16[1,1,1,1,48,3072]{5,4,3,2,1,0:T(8,128)(2,1)S(1)} %dynamic-slice_convert_fusion.2), channel_id=1, source_target_pairs={{0,16},{2,18},{4,20},{6,22},{8,24},{10,26},{12,28},{14,30},{16,0},... | collective-permute-start | bytes 884744 | tf_op jit(solution)/shard_map/ppermute | solution.py:33
  332.3 32.3 %copy-start.46 = (f32[6,33]{1,0:T(8,128)S(1)}, f32[6,33]{1,0:T(8,128)}, u32[]{:S(2)}) copy-start(f32[6,33]{1,0:T(8,128)} %param.48) | copy-start | bytes 2380
  340.1 1.1 collective-permute-start.30
  341.2 3.5 collective-permute-start.31
  344.8 3.5 collective-permute-start.32
  348.3 3.5 collective-permute-start.33
  351.9 4.4 %collective-permute-start.34 = (f32[1,128]{1,0:T(1,128)S(1)}, f32[1,128]{1,0:T(1,128)S(1)}, u32[]{:S(2)}, u32[]{:S(2)}) collective-permute-start(f32[1,128]{1,0:T(1,128)S(1)} %add.300), channel_id=1, source_target_pairs={{0,16},{2,18},{4,20},{6,22},{8,24},{10,26},{12,28},{14,30},{16,0},... | collective-permute-start | bytes 1544 | tf_op jit(solution)/shard_map/ppermute | solution.py:33
  352.4 20.6 %collective-permute-start.17 = (bf16[1536,768]{1,0:T(8,128)(2,1)}, bf16[1536,768]{1,0:T(8,128)(2,1)S(1)}, u32[]{:S(2)}, u32[]{:S(2)}) collective-permute-start(bf16[1536,768]{1,0:T(8,128)(2,1)} %shard_map.440), channel_id=1, source_target_pairs={{0,1},{1,0},{2,3},{3,2},{4,5},{5,4},{6,7},{7,6},{8,9},{9,8},{10,11... | collective-permute-start | bytes 7077896 | tf_op jit(solution)/shard_map/ppermute | solution.py:33
  (39 other events, 190.9 us)
Sparse Core Ops, SparseCore 0:
  11.4 97.6 all-gather.1

commit v3 on v2

--- a/solution.py
+++ b/solution.py
@@ -1,3 +1,5 @@
+import functools
+
 import jax
 import jax.numpy as jnp
 from jax import lax
@@ -33,19 +35,41 @@
     return lax.ppermute(array, axis, [(i, i ^ (1 << bit)) for i in range(count)])
 
 
-def gather_rows(array, count, order):
-    bit_count = bits_of(count)
-    own = lax.axis_index("dp")
-    current = array.reshape((1,) * bit_count + array.shape)
-    for bit in order:
-        dim = bit_count - 1 - bit
-        other = swap(current, "dp", count, bit)
-        current = jnp.where(
-            (own >> bit) & 1 == 0,
-            jnp.concatenate([current, other], dim),
-            jnp.concatenate([other, current], dim),
+class Gather:
+    def __init__(self, array, count, order):
+        self.count, self.order = count, list(order)
+        self.shape = (count * array.shape[0],) + array.shape[1:]
+        self.current = array.reshape((1,) * bits_of(count) + array.shape)
+
+    def step(self, *others):
+        bit = self.order.pop(0)
+        dim = bits_of(self.count) - 1 - bit
+        other = swap(self.current, "dp", self.count, bit)
+        other = after(other, *others) if others else other
+        self.current = jnp.where(
+            (lax.axis_index("dp") >> bit) & 1 == 0,
+            jnp.concatenate([self.current, other], dim),
+            jnp.concatenate([other, self.current], dim),
         )
-    return current.reshape((count * array.shape[0],) + array.shape[1:])
+        return self
+
+    def split(self, sizes, dim, orders):
+        pieces, at = [], 0
+        for size, order in zip(sizes, orders):
+            piece = Gather.__new__(Gather)
+            piece.count, piece.order = self.count, list(order)
+            axis = self.current.ndim + dim
+            piece.current = lax.slice_in_dim(self.current, at, at + size, axis=axis)
+            rows = self.count * piece.current.shape[-2]
+            piece.shape = (rows, piece.current.shape[-1])
+            pieces.append(piece)
+            at += size
+        return pieces
+
+    def finish(self):
+        while self.order:
+            self.step()
+        return self.current.reshape(self.shape)
 
 
 def after(array, *others):
@@ -53,11 +77,13 @@
 
 
 class Scatter:
-    def __init__(self, array, count, order):
+    def __init__(self, arrays, count, order, join=-1):
         self.count = count
+        self.join = join
         self.order = list(order)
-        self.shape = (array.shape[0] // count,) + array.shape[1:]
-        self.current = array.reshape((2,) * bits_of(count) + self.shape)
+        self.shapes = [(array.shape[0] // count,) + array.shape[1:] for array in arrays]
+        lead = (2,) * bits_of(count)
+        self.currents = [array.reshape(lead + shape) for array, shape in zip(arrays, self.shapes)]
         self.sent = self.kept = self.received = None
 
     def send(self):
@@ -65,33 +91,42 @@
             bit = self.order.pop(0)
             dim = bits_of(self.count) - 1 - bit
             mine = (lax.axis_index("dp") >> bit) & 1
-            self.sent = lax.dynamic_slice_in_dim(self.current, 1 - mine, 1, dim)
-            self.sent = self.sent.astype(jnp.bfloat16)
-            self.kept = lax.dynamic_slice_in_dim(self.current, mine, 1, dim)
+            sent = [
+                lax.dynamic_slice_in_dim(current, 1 - mine, 1, dim).astype(jnp.bfloat16)
+                for current in self.currents
+            ]
+            self.sent = sent[0] if len(sent) == 1 else jnp.concatenate(sent, axis=self.join)
+            self.kept = [
+                lax.dynamic_slice_in_dim(current, mine, 1, dim) for current in self.currents
+            ]
             self.received = swap(self.sent, "dp", self.count, bit)
         return self
 
     def take(self, *others):
         if self.received is not None:
             received = after(self.received, *others) if others else self.received
-            self.current = self.kept.astype(jnp.float32) + received.astype(jnp.float32)
-            self.received = None
+            currents, at = [], 0
+            for kept in self.kept:
+                size = kept.shape[self.join]
+                piece = lax.slice_in_dim(received, at, at + size, axis=self.join % kept.ndim)
+                currents.append(kept.astype(jnp.float32) + piece.astype(jnp.float32))
+                at += size
+            self.currents, self.received = currents, None
         return self
 
-    def merge(self, *others):
-        merged = Scatter.__new__(Scatter)
-        merged.count, merged.order = self.count, list(self.order)
+    def merge(self, *others, join=-1):
         every = (self,) + others
-        merged.current = jnp.concatenate([one.take().current for one in every], axis=-1)
-        merged.shape = self.shape[:-1] + (merged.current.shape[-1],)
-        merged.sent = merged.kept = merged.received = None
+        merged = Scatter([], self.count, self.order, join)
+        merged.shapes = [shape for one in every for shape in one.shapes]
+        merged.currents = [current for one in every for current in one.take().currents]
         return merged
 
     def finish(self):
         self.take()
         while self.order:
             self.send().take()
-        return self.current.reshape(self.shape).astype(jnp.float32)
+        pairs = zip(self.currents, self.shapes)
+        return [current.reshape(shape).astype(jnp.float32) for current, shape in pairs]
 
 
 def sum_all(array, axis, count):
@@ -222,37 +257,25 @@
     ).astype(jnp.bfloat16)
 
 
-def attention_forward_body(
+def attention_start_body(
     units_ref,
     proj_ref,
-    taps_ref,
-    attended_ref,
-    first_ref,
-    last_ref,
     marks_ref,
     middle_ref,
-    rough_ref,
-    fine_ref,
+    last_ref,
     values_ref,
-    weighted_ref,
+    approx_ref,
     select_ref,
-    own_ref,
     in_ref,
-    approx_ref,
-    window_ref,
-    conv_ref,
 ):
     parts, _, part_width, row_count = proj_ref.shape
     part_heads = part_width // HEAD_DIM
     heads = parts * part_heads
     marks = 2 * LANDMARKS
     select_ref[...] = select_matrix(units_ref, row_count)
-    is_first, start, end, _, _ = landmark_columns(units_ref)
-    first_end, _ = item_ends(units_ref)
+    _, start, end, _, _ = landmark_columns(units_ref)
     position = lax.broadcasted_iota(jnp.int32, (marks, row_count), 1)
     in_ref[...] = jnp.where((position >= start) & (position < end), 0.0, NEGATIVE)
-    own_ref[...] = jnp.where((position < first_end) == is_first, 0.0, NEGATIVE)
-    first, second, inside = lane_items(units_ref, row_count)
     for part in range(parts):
         for kind in range(2):
             sums = dot_with(proj_ref[part, kind], select_ref[...], 1, 1)
@@ -284,13 +307,42 @@
 
     lax.fori_loop(0, heads, head_start, 0)
 
+
+def attention_finish_body(
+    units_ref,
+    proj_ref,
+    taps_ref,
+    marks_ref,
+    middle_ref,
+    values_ref,
+    approx_ref,
+    attended_ref,
+    first_ref,
+    rough_ref,
+    fine_ref,
+    weighted_ref,
+    own_ref,
+    state_ref,
+    window_ref,
+    conv_ref,
+):
+    parts, _, part_width, row_count = proj_ref.shape
+    part_heads = part_width // HEAD_DIM
+    heads = parts * part_heads
+    marks = 2 * LANDMARKS
+    is_first = landmark_columns(units_ref)[0]
+    first_end, _ = item_ends(units_ref)
+    position = lax.broadcasted_iota(jnp.int32, (marks, row_count), 1)
+    own_ref[...] = jnp.where((position < first_end) == is_first, 0.0, NEGATIVE)
+    first, second, inside = lane_items(units_ref, row_count)
+    state_ref[...] = approx_ref[...]
     seven, fifteen, thirteen = (scaled_eye(marks, value) for value in (7.0, 15.0, 13.0))
 
     def pinv_steps(saved_ref, count):
         kind = saved_ref.dtype
 
         def one_step(slot, carry):
-            approx = [approx_ref[head] for head in range(heads)]
+            approx = [state_ref[head] for head in range(heads)]
             product = [dot_fine(middle_ref[head], approx[head], 1, 0) for head in range(heads)]
             inner = [
                 fifteen - dot_fine(product[head], seven - product[head], 1, 0)
@@ -302,7 +354,7 @@
                 saved_ref[slot, 1, head] = product[head].astype(kind)
                 saved_ref[slot, 2, head] = inner[head].astype(kind)
                 saved_ref[slot, 3, head] = outer[head].astype(kind)
-                approx_ref[head] = dot_fine(0.25 * approx[head], outer[head], 1, 0)
+                state_ref[head] = dot_fine(0.25 * approx[head], outer[head], 1, 0)
             return carry
 
         lax.fori_loop(0, count, one_step, 0)
@@ -314,7 +366,7 @@
         at = pl.multiple_of(head * HEAD_DIM, HEAD_DIM)
         part = head // part_heads
         part_at = pl.multiple_of((head - part * part_heads) * HEAD_DIM, HEAD_DIM)
-        weighted = dot_fine(approx_ref[head], values_ref[head], 1, 0)
+        weighted = dot_fine(state_ref[head], values_ref[head], 1, 0)
         weighted_ref[head] = weighted
         weighted_rows = weighted.T.astype(jnp.bfloat16)
         key_rows = (marks_ref[1, pl.ds(at, HEAD_DIM), :] * SCORE_SCALE).T.astype(jnp.bfloat16)
@@ -350,38 +402,64 @@
     return [pl.BlockSpec(memory_space=pltpu.VMEM)] * count
 
 
-def attention_forward(item_units, proj, tap_rows):
-    width = proj.shape[0] * proj.shape[2]
-    row_count = proj.shape[3]
+def attention_sizes(proj):
+    parts, _, part_width, row_count = proj.shape
+    width = parts * part_width
     heads = width // HEAD_DIM
     marks = 2 * LANDMARKS
-    square = (heads, marks, marks)
+    return width, row_count, heads, marks, (heads, marks, marks), (heads, marks, HEAD_DIM)
+
+
+def attention_start(item_units, proj):
+    width, row_count, heads, marks, square, thin = attention_sizes(proj)
     return pl.pallas_call(
-        attention_forward_body,
-        in_specs=[pl.BlockSpec(memory_space=pltpu.SMEM)] + whole(2),
-        out_specs=whole(9),
+        attention_start_body,
+        in_specs=[pl.BlockSpec(memory_space=pltpu.SMEM)]
+        + whole(1),
+        out_specs=whole(5),
+        out_shape=[
+            jax.ShapeDtypeStruct((2, width, marks), jnp.float32),
+            jax.ShapeDtypeStruct(square, jnp.float32),
+            jax.ShapeDtypeStruct((heads, marks, row_count), jnp.bfloat16),
+            jax.ShapeDtypeStruct(thin, jnp.float32),
+            jax.ShapeDtypeStruct(square, jnp.float32),
+        ],
+        scratch_shapes=[
+            pltpu.VMEM((marks, row_count), jnp.bfloat16),
+            pltpu.VMEM((marks, row_count), jnp.float32),
+        ],
+        compiler_params=pltpu.CompilerParams(vmem_limit_bytes=48 * 1024 * 1024),
+        cost_estimate=pl.CostEstimate(
+            flops=9_000_000_000, bytes_accessed=8_000_000, transcendentals=0
+        ),
+    )(item_units, proj)
+
+
+def attention_finish(item_units, proj, tap_rows, marks_rows, middle, last, values, approx):
+    width, row_count, heads, marks, square, thin = attention_sizes(proj)
+    stacked = 2 * row_count // BLOCK * HEAD_DIM
+    return pl.pallas_call(
+        attention_finish_body,
+        in_specs=[pl.BlockSpec(memory_space=pltpu.SMEM)] + whole(6),
+        out_specs=whole(5),
         out_shape=[
             jax.ShapeDtypeStruct((width, row_count), jnp.bfloat16),
             jax.ShapeDtypeStruct((heads, marks, row_count), jnp.bfloat16),
-            jax.ShapeDtypeStruct((heads, marks, row_count), jnp.bfloat16),
-            jax.ShapeDtypeStruct((2, width, marks), jnp.float32),
-            jax.ShapeDtypeStruct(square, jnp.float32),
             jax.ShapeDtypeStruct((ROUGH_STEPS, 4) + square, jnp.bfloat16),
             jax.ShapeDtypeStruct((PINV_STEPS - ROUGH_STEPS, 4) + square, jnp.float32),
-            jax.ShapeDtypeStruct((heads, marks, HEAD_DIM), jnp.float32),
-            jax.ShapeDtypeStruct((heads, marks, HEAD_DIM), jnp.float32),
+            jax.ShapeDtypeStruct(thin, jnp.float32),
         ],
         scratch_shapes=[
-            pltpu.VMEM((marks, row_count), jnp.bfloat16),
-            pltpu.VMEM((marks, row_count), jnp.float32),
             pltpu.VMEM((marks, row_count), jnp.float32),
             pltpu.VMEM(square, jnp.float32),
-            pltpu.VMEM((2 * row_count // BLOCK * HEAD_DIM, 2 * BLOCK), jnp.bfloat16),
-            pltpu.VMEM((2 * row_count // BLOCK * HEAD_DIM, BLOCK), jnp.float32),
+            pltpu.VMEM((stacked, 2 * BLOCK), jnp.bfloat16),
+            pltpu.VMEM((stacked, BLOCK), jnp.float32),
         ],
         compiler_params=pltpu.CompilerParams(vmem_limit_bytes=48 * 1024 * 1024),
-        cost_estimate=pl.CostEstimate(flops=20_000_000_000, bytes_accessed=20_000_000, transcendentals=0),
-    )(item_units, proj, tap_rows)
+        cost_estimate=pl.CostEstimate(
+            flops=18_000_000_000, bytes_accessed=16_000_000, transcendentals=0
+        ),
+    )(item_units, proj, tap_rows, marks_rows, middle, values, approx)
 
 
 def tap_rows_of(kernel):
@@ -622,16 +700,31 @@
 
 
 ROWS = 256
+LONG_ROWS = 512
+OUTER = 384
+PIECE = 512
 GELU_SCALE = 0.7978845608
 GELU_CUBE = 0.044715
 
 
-def row_block(width):
-    return pl.BlockSpec((ROWS, width), lambda step: (step, 0))
+def row_block(width, rows=ROWS):
+    return pl.BlockSpec((rows, width), lambda step: (step, 0))
 
 
 def fixed_block(shape, column=0):
     return pl.BlockSpec(shape, lambda step: (0, column))
+
+
+def row_lanes(rows=ROWS):
+    return pl.BlockSpec((1, rows), lambda step: (0, step))
+
+
+def as_column(row):
+    return jnp.broadcast_to(row, (128, row.shape[1])).T[:, 0:1]
+
+
+def as_row(column):
+    return jnp.broadcast_to(column, (column.shape[0], 128)).T[0:1]
 
 
 def dense_params():
@@ -661,6 +754,10 @@
 
 def both(own_ref, other_ref):
     return own_ref[...].astype(jnp.float32) + other_ref[...].astype(jnp.float32)
+
+
+def weight_blocks(expand, reduce):
+    return [fixed_block(reduce.shape), fixed_block(reduce.shape)]
 
 
 def hidden_forward_body(
@@ -682,7 +779,7 @@
     stat_ref,
 ):
     branch = both(own_ref, other_ref) + shared_ref[0:1]
-    squares = column_sum(weight_ref[...] * branch * branch)
+    squares = column_sum(as_column(weight_ref[...]) * branch * branch)
 
     @pl.when(pl.program_id(0) == 0)
     def _():
@@ -693,13 +790,12 @@
     hidden = unit * shared_ref[2:3] + shared_ref[3:4]
     hidden_ref[...] = hidden
     unit_ref[...] = unit.astype(jnp.bfloat16)
-    scale_ref[...] = scale
+    scale_ref[...] = as_row(scale)
     hidden_low = hidden.astype(jnp.bfloat16)
     low_ref[...] = hidden_low
     total = jnp.zeros(part_ref.shape, jnp.float32)
-    units = expand_ref.shape[1]
-    for at in range(0, units, 512):
-        lanes = slice(at, at + 512)
+    for at in range(0, reduce_ref.shape[1], PIECE):
+        lanes = slice(at, at + PIECE)
         expanded = dot_with(hidden_low, expand_ref[:, lanes], 1, 0) + bias_ref[:, lanes]
         square = expanded * expanded
         bend = jnp.tanh(expanded * (GELU_SCALE + (GELU_SCALE * GELU_CUBE) * square))
@@ -714,7 +810,7 @@
     part_ref[...] = total.astype(jnp.bfloat16)
 
 
-def hidden_forward(own, other, tokens, weight_column, shared_rows, expand_bias, late_full):
+def hidden_forward(own, other, tokens, weight_row, shared_rows, expand_bias, *weights):
     row_count, width = tokens.shape
     units = expand_bias.shape[1]
     return pl.pallas_call(
@@ -724,18 +820,17 @@
             row_block(width),
             row_block(width),
             row_block(width),
-            row_block(1),
+            row_lanes(),
             fixed_block((6, width)),
             fixed_block((1, units)),
-            fixed_block((width, units), 0),
-            fixed_block((width, units), 1),
-        ],
+        ]
+        + weight_blocks(*weights),
         out_specs=[
             row_block(width),
             row_block(width),
             row_block(width),
             row_block(width),
-            row_block(1),
+            row_lanes(),
             row_block(units),
             row_block(units),
             fixed_block((1, width)),
@@ -745,14 +840,14 @@
             jax.ShapeDtypeStruct((row_count, width), jnp.float32),
             jax.ShapeDtypeStruct((row_count, width), jnp.bfloat16),
             jax.ShapeDtypeStruct((row_count, width), jnp.bfloat16),
-            jax.ShapeDtypeStruct((row_count, 1), jnp.float32),
+            jax.ShapeDtypeStruct((1, row_count), jnp.float32),
             jax.ShapeDtypeStruct((row_count, units), jnp.bfloat16),
             jax.ShapeDtypeStruct((row_count, units), jnp.bfloat16),
             jax.ShapeDtypeStruct((1, width), jnp.float32),
         ],
         compiler_params=dense_params(),
         cost_estimate=cost(4 * row_count * width * units, 30_000_000),
-    )(own, other, tokens, weight_column, shared_rows, expand_bias, late_full, late_full)
+    )(own, other, tokens, weight_row, shared_rows, expand_bias, *weights)
 
 
 def hidden_backward_body(
@@ -762,9 +857,9 @@
     cotangent_ref,
     weight_ref,
     shared_ref,
+    slope_ref,
     expand_ref,
     reduce_ref,
-    slope_ref,
     output_ref,
     d_two_ref,
     d_expanded_ref,
@@ -773,7 +868,7 @@
     bias_ref,
 ):
     branch = both(own_ref, other_ref) + shared_ref[1:2]
-    weight = weight_ref[...]
+    weight = as_column(weight_ref[...])
     unit, scale = normalized(hidden_ref[...] + branch)
     output_ref[...] = unit * shared_ref[4:5] + shared_ref[5:6]
     grad = cotangent_ref[...].astype(jnp.float32) * weight
@@ -792,14 +887,14 @@
             column_sum(d_res),
             column_sum(grad * unit),
             column_sum(grad),
-            jnp.zeros((4, grad.shape[1]), jnp.float32),
+            jnp.broadcast_to(column_sum(weight), (1, grad.shape[1])),
+            jnp.zeros((3, grad.shape[1]), jnp.float32),
         ],
         axis=0,
     )
     total = jnp.zeros(part_ref.shape, jnp.float32)
-    units = expand_ref.shape[1]
-    for at in range(0, units, 512):
-        lanes = slice(at, at + 512)
+    for at in range(0, reduce_ref.shape[1], PIECE):
+        lanes = slice(at, at + PIECE)
         d_active = dot_with(d_two, reduce_ref[:, lanes], 1, 0)
         d_expanded = (slope_ref[:, lanes].astype(jnp.float32) * d_active).astype(jnp.bfloat16)
         d_expanded_ref[:, lanes] = d_expanded
@@ -808,7 +903,7 @@
     part_ref[...] = total.astype(jnp.bfloat16)
 
 
-def hidden_backward(own, other, hidden, cotangent, weight_column, shared_rows, late_full, slope):
+def hidden_backward(own, other, hidden, cotangent, weight_row, shared_rows, slope, *weights):
     row_count, width = cotangent.shape
     units = slope.shape[1]
     return pl.pallas_call(
@@ -819,12 +914,11 @@
             row_block(width),
             row_block(width),
             row_block(width),
-            row_block(1),
+            row_lanes(),
             fixed_block((6, width)),
-            fixed_block((width, units), 0),
-            fixed_block((width, units), 1),
             row_block(units),
-        ],
+        ]
+        + weight_blocks(*weights),
         out_specs=[
             row_block(width),
             row_block(width),
@@ -843,7 +937,7 @@
         ],
         compiler_params=dense_params(),
         cost_estimate=cost(4 * row_count * width * units, 30_000_000),
-    )(own, other, hidden, cotangent, weight_column, shared_rows, late_full, late_full, slope)
+    )(own, other, hidden, cotangent, weight_row, shared_rows, slope, *weights)
 
 
 def norm_one_body(
@@ -867,7 +961,7 @@
 
     grad = both(own_ref, other_ref) + d_two_ref[...].astype(jnp.float32)
     unit = unit_ref[...].astype(jnp.float32)
-    d_res = norm_backward(grad, shared_ref[2:3], unit, scale_ref[...])
+    d_res = norm_backward(grad, shared_ref[2:3], unit, as_column(scale_ref[...]))
     d_one = d_res.astype(jnp.bfloat16)
     d_one_ref[...] = d_one
     sums_ref[...] += jnp.concatenate(
@@ -887,20 +981,20 @@
     row_count, width = d_two.shape
     return pl.pallas_call(
         norm_one_body,
-        grid=(row_count // ROWS,),
+        grid=(row_count // LONG_ROWS,),
         in_specs=[
-            row_block(width),
-            row_block(width),
-            row_block(width),
-            row_block(width),
-            row_block(1),
-            pl.BlockSpec((1, ROWS), lambda step: (0, step)),
+            row_block(width, LONG_ROWS),
+            row_block(width, LONG_ROWS),
+            row_block(width, LONG_ROWS),
+            row_block(width, LONG_ROWS),
+            row_lanes(LONG_ROWS),
+            pl.BlockSpec((1, LONG_ROWS), lambda step: (0, step)),
             fixed_block((6, width)),
             fixed_block((width, local_width), late_full.shape[1] // local_width - 1),
         ],
         out_specs=[
-            row_block(width),
-            pl.BlockSpec((local_width, ROWS), lambda step: (0, step)),
+            row_block(width, LONG_ROWS),
+            pl.BlockSpec((local_width, LONG_ROWS), lambda step: (0, step)),
             fixed_block((8, width)),
         ],
         out_shape=[
@@ -928,7 +1022,7 @@
     row_count = lefts[0].shape[-1]
     specs, arrays, terms = [], [], 0
     for left, right, column in zip(lefts, rights, columns):
-        shape = left.shape[:-1] + (ROWS,)
+        shape = left.shape[:-1] + (LONG_ROWS,)
         place = (0,) * (left.ndim - 1)
         specs.append(pl.BlockSpec(shape, lambda step, place=place: place + (step,)))
         depth = left.size // row_count
@@ -937,13 +1031,34 @@
         terms += depth
     return pl.pallas_call(
         turned_dot_body,
-        grid=(row_count // ROWS,),
+        grid=(row_count // LONG_ROWS,),
         in_specs=specs,
-        out_specs=row_block(width),
+        out_specs=row_block(width, LONG_ROWS),
         out_shape=jax.ShapeDtypeStruct((row_count, width), jnp.bfloat16),
         compiler_params=dense_params(),
         cost_estimate=cost(2 * row_count * width * terms, 8_000_000),
     )(*arrays)
+
+def turned_outer_body(left_ref, right_ref, out_ref):
+    product = dot_with(left_ref[...], right_ref[...], 1, 0)
+    out_ref[...] = product.T.astype(jnp.bfloat16)
+
+
+def turned_outer(left, right):
+    depth, width = right.shape
+    return pl.pallas_call(
+        turned_outer_body,
+        grid=(width // OUTER,),
+        in_specs=[
+            fixed_block(left.shape),
+            pl.BlockSpec((depth, OUTER), lambda step: (0, step)),
+        ],
+        out_specs=pl.BlockSpec((OUTER, left.shape[0]), lambda step: (step, 0)),
+        out_shape=jax.ShapeDtypeStruct((width, left.shape[0]), jnp.bfloat16),
+        compiler_params=dense_params(),
+        cost_estimate=cost(2 * depth * width * left.shape[0], 6_000_000),
+    )(left, right)
+
 
 def project_body(first_ref, second_ref, tokens_ref, bias_ref, out_ref, turned_ref):
     part_width = first_ref.shape[1]
@@ -964,14 +1079,14 @@
     shape = (2, 3, part_width // 3, row_count)
     return pl.pallas_call(
         project_body,
-        grid=(row_count // ROWS,),
+        grid=(row_count // LONG_ROWS,),
         in_specs=[
             fixed_block((width, part_width)),
             fixed_block((width, part_width)),
-            row_block(width),
+            row_block(width, LONG_ROWS),
             fixed_block((2 * part_width, 1)),
         ],
-        out_specs=pl.BlockSpec(shape[:3] + (ROWS,), lambda step: (0, 0, 0, step)),
+        out_specs=pl.BlockSpec(shape[:3] + (LONG_ROWS,), lambda step: (0, 0, 0, step)),
         out_shape=jax.ShapeDtypeStruct(shape, jnp.bfloat16),
         scratch_shapes=[pltpu.VMEM((2 * part_width, width), jnp.bfloat16)],
         compiler_params=dense_params(),
@@ -985,6 +1100,137 @@
     square_new = BETA_TWO * square + (1.0 - BETA_TWO) * clipped * clipped
     step_size = moment_new / CORRECT_ONE / (jnp.sqrt(square_new / CORRECT_TWO) + ADAM_EPS)
     return (master - learn_rate * (step_size + decay_rate * master), moment_new, square_new)
+
+def finish_body(
+    places_ref,
+    expand_ref,
+    reduce_ref,
+    mixing_ref,
+    hidden_ref,
+    left_ref,
+    right_ref,
+    inputs_ref,
+    stat_ref,
+    sums_ref,
+    expand_out,
+    reduce_out,
+    mixing_out,
+    left_out,
+    right_out,
+    row_ref,
+    *,
+    bias_share,
+    shared_share,
+):
+    mine = places_ref[0]
+    squares = jnp.zeros((1, 1), jnp.float32)
+
+    def total(values):
+        return jnp.sum(jnp.sum(values, axis=0, keepdims=True), axis=1, keepdims=True)
+
+    at = 0
+    for current_ref, out_ref in (
+        (expand_ref, expand_out),
+        (reduce_ref, reduce_out),
+        (mixing_ref, mixing_out),
+    ):
+        width = out_ref.shape[1]
+        share = current_ref[mine] + hidden_ref[:, at : at + width].astype(jnp.float32)
+        out_ref[...] = share
+        squares += total(share * share)
+        at += width
+    rows = left_ref.shape[1]
+    received = inputs_ref[...].astype(jnp.float32)
+    left = left_ref[mine] + received[:rows]
+    right = right_ref[mine] + received[rows:]
+    left_out[...] = left
+    right_out[...] = right
+    squares += total(left * left) + total(right[:rows] * right[:rows])
+    small = right[rows : rows + 1]
+    kernel = right[rows + 1 :]
+    lane = lax.broadcasted_iota(jnp.int32, small.shape, 1)
+    shared_counts = places_ref[1].astype(jnp.float32)
+    factor = jnp.where(
+        lane < bias_share, 1.0, jnp.where(lane < bias_share + shared_share, shared_counts, 0.0)
+    )
+    squares += total(small * small * factor) + total(kernel * kernel)
+    lane = lax.broadcasted_iota(jnp.int32, (1, 128), 1)
+    row = jnp.where(lane == 0, squares, 0.0)
+    row += jnp.where(lane == 1, total(stat_ref[...]), 0.0)
+    row += jnp.where(lane == 2, total(sums_ref[0:1]), 0.0)
+    row_ref[:, :128] = row + jnp.where(lane == 3, sums_ref[4:5, 0:1], 0.0)
+    row_ref[:, 128:] = kernel[:, : row_ref.shape[1] - 128]
+
+
+def finish(places, hidden, inputs, stat_one, sums_two, bias_share, shared_share):
+    def flat(array):
+        return array.reshape(array.shape[-2:])
+
+    def pair(array):
+        return array.reshape((2,) + array.shape[-2:])
+
+    arrays = [pair(array) for array in hidden.currents] + [flat(hidden.received)]
+    arrays += [pair(array) for array in inputs.currents] + [flat(inputs.received)]
+    arrays += [stat_one, sums_two]
+    shapes = [array.shape[-2:] for array in hidden.currents + inputs.currents] + [(1, 384)]
+    return pl.pallas_call(
+        functools.partial(finish_body, bias_share=bias_share, shared_share=shared_share),
+        in_specs=[pl.BlockSpec(memory_space=pltpu.SMEM)] + whole(len(arrays)),
+        out_specs=whole(len(shapes)),
+        out_shape=[jax.ShapeDtypeStruct(shape, jnp.float32) for shape in shapes],
+        compiler_params=dense_params(),
+        cost_estimate=cost(1_000_000, 3_000_000),
+    )(places, *arrays)
+
+
+def update_body(*refs, width, bias_share, shard_rows):
+    totals_ref, kernel_ref, expand_ref, reduce_ref, mixing_ref, left_ref, right_ref = refs[:7]
+    old_refs, new_refs, row_ref = refs[7:28], refs[28:49], refs[49]
+    rows = left_ref.shape[0]
+    totals = totals_ref[...]
+    lane = lax.broadcasted_iota(jnp.int32, totals.shape, 1)
+    means = jnp.sqrt(totals / jnp.where(lane == 0, 1.0, totals[:, 3:4] * width))
+    row_ref[...] = means
+    factor = CLIP_NORM / (means[:, 0:1] + CLIP_EPS)
+
+    def put(index, place, gradient, rate, decay):
+        old = [old_refs[3 * index + kind][place] for kind in range(3)]
+        for kind, value in enumerate(adamw(*old, gradient, factor, rate, decay)):
+            new_refs[3 * index + kind][place] = value
+
+    part_width = right_ref.shape[1] // 3
+    for part, share_ref in enumerate((left_ref, right_ref)):
+        for kind in range(3):
+            gradient = share_ref[:rows, kind * part_width : (kind + 1) * part_width]
+            lanes = slice(part * part_width, (part + 1) * part_width)
+            put(0, (kind, slice(None), lanes), gradient, RATE_MATRIX, WEIGHT_DECAY)
+    put(1, ..., mixing_ref[...], RATE_MATRIX, WEIGHT_DECAY)
+    put(2, ..., expand_ref[...], RATE_MATRIX, WEIGHT_DECAY)
+    put(3, ..., reduce_ref[...], RATE_MATRIX, WEIGHT_DECAY)
+    small = slice(rows, rows + 1)
+    put(4, ..., right_ref[small, :bias_share], RATE_VECTOR, 0.0)
+    for row in range(6):
+        start = bias_share + row * shard_rows
+        place = (slice(row, row + 1), slice(None))
+        put(5, place, right_ref[small, start : start + shard_rows], RATE_VECTOR, 0.0)
+    heads, taps = old_refs[18].shape
+    for row in range(heads):
+        start = 128 + row * taps
+        place = (slice(row, row + 1), slice(None))
+        put(6, place, kernel_ref[:, start : start + taps], RATE_VECTOR, 0.0)
+
+
+def update(totals, kernel_row, shares, olds, width, bias_share, shard_rows):
+    arrays = [totals, kernel_row] + shares + olds
+    shapes = [old.shape for old in olds] + [(1, 128)]
+    return pl.pallas_call(
+        functools.partial(update_body, width=width, bias_share=bias_share, shard_rows=shard_rows),
+        in_specs=whole(len(arrays)),
+        out_specs=whole(len(shapes)),
+        out_shape=[jax.ShapeDtypeStruct(shape, jnp.float32) for shape in shapes],
+        compiler_params=dense_params(),
+        cost_estimate=cost(5_000_000, 6_000_000),
+    )(*arrays)
 
 
 def body(
@@ -1025,25 +1271,37 @@
     part_width = local_width // 2
     part_lanes = [slice(0, part_width), slice(part_width, local_width)]
 
-    late_low = jnp.concatenate(
-        [expand_weight.astype(jnp.bfloat16)]
-        + [weight.astype(jnp.bfloat16).T for weight in (reduce_weight, mixing_weight)],
-        axis=1,
-    )
+    high_bits = bits[2:][::-1]
+    low_orders = (bits[:2][::-1], bits[:2])
     small_low = jnp.concatenate([biases_weight.reshape(-1), shared_weight.reshape(-1)])
     small_low = jnp.pad(small_low, (0, (-small_low.shape[0]) % (3 * part_width)))
     small_low = small_low.astype(jnp.bfloat16).reshape(-1, 3 * part_width)
-    left_low, right_low = [
+    inputs_low = [
         jnp.concatenate([inputs_weight[c][:, lanes] for c in range(3)], axis=1).astype(jnp.bfloat16)
         for lanes in part_lanes
     ]
-    left_low = jnp.concatenate([left_low, small_low], axis=0)
-    left_full = gather_rows(left_low, dp_count, first_order[::-1])
-    left_full = left_full.reshape(dp_count, left_low.shape[0], 3 * part_width)
+    inputs_low = jnp.concatenate([inputs_low[1], inputs_low[0], small_low], axis=0)
+    sizes = (shard_rows, inputs_low.shape[0] - shard_rows)
+    inputs_gather = Gather(inputs_low, dp_count, high_bits)
+    late_low = jnp.concatenate(
+        [expand_weight.astype(jnp.bfloat16)]
+        + [weight.astype(jnp.bfloat16).T for weight in (mixing_weight, reduce_weight)],
+        axis=1,
+    )
+    inputs_gather.step()
+    late_low = after(late_low, inputs_gather.current)
+    for _ in high_bits[1:]:
+        inputs_gather.step()
+    right_gather, left_gather = inputs_gather.split(sizes, -2, low_orders)
+    inputs_right = right_gather.finish()
+    left_full = left_gather.finish().reshape(dp_count, sizes[1], 3 * part_width)
     inputs_left = left_full[:, :shard_rows].reshape(-1, 3 * part_width)
     small_full = left_full[:, shard_rows:].reshape(dp_count, -1)
-    inputs_right = gather_rows(right_low, dp_count, second_order[::-1])
-    late_full = lax.all_gather(late_low, "dp", axis=0, tiled=True)
+    late_gather = Gather(late_low, dp_count, high_bits)
+    for _ in high_bits:
+        late_gather.step()
+    sizes = (hidden_units + local_width, hidden_units)
+    expand_gather, reduce_gather = late_gather.split(sizes, -1, low_orders)
     biases_row = small_full[:, :bias_share].reshape(-1).astype(jnp.float32)
     shared_rows = small_full[:, bias_share : bias_share + 6 * shard_rows]
     shared_rows = shared_rows.reshape(dp_count, 6, shard_rows).transpose(1, 0, 2)
@@ -1063,25 +1321,37 @@
     row_item = row_items(item_units[0], row_count, LANDMARKS)
     inside = (row_item < 2).astype(jnp.float32)
     weight_rows = counted.astype(jnp.float32) * inside
-    weight_column = weight_rows[:, None]
-
-    proj = project(inputs_left, inputs_right, tokens, bias_column)
-    attended, *saved = attention_forward(item_units, proj, tap_rows_of(kernel_weight))
-    mixing_column = late_full.shape[1] // local_width - 1
-    own_one = turned_dot([attended], [late_full], [mixing_column], width_full)
+    weight_row = weight_rows[None, :]
+
+    tied_tokens = after(tokens, expand_gather.current, reduce_gather.current)
+    proj = project(inputs_left, inputs_right, tied_tokens, bias_column)
+    marks, middle, last, values, approx = attention_start(item_units, proj)
+    expand_gather.step(marks)
+    reduce_gather.step(marks)
+    tied_marks = after(marks, expand_gather.current, reduce_gather.current)
+    attended, kept, rough, fine, weighted = attention_finish(
+        item_units, proj, tap_rows_of(kernel_weight), tied_marks, middle, last, values, approx
+    )
+    saved = (kept, last, marks, middle, rough, fine, values, weighted)
+    expand_full = expand_gather.finish()
+    reduce_full = reduce_gather.finish()
+    hidden_weights = (expand_full, reduce_full)
+    mixing_column = expand_full.shape[1] // local_width - 1
+    tied_attended = after(attended, reduce_full)
+    own_one = turned_dot([tied_attended], [expand_full], [mixing_column], width_full)
     other_one = swap(own_one, "head", 2, 0)
     own_two, hidden_one, hidden_low, unit_one, scale_one, active, slope, stat_one = hidden_forward(
-        own_one, other_one, tokens, weight_column, shared_rows, expand_bias, late_full
+        own_one, other_one, tokens, weight_row, shared_rows, expand_bias, *hidden_weights
     )
     other_two = swap(own_two, "head", 2, 0)
     output_rows, d_two, d_expanded, own_three, sums_two, expand_sums = hidden_backward(
-        own_two, other_two, hidden_one, cotangent, weight_column, shared_rows, late_full, slope
+        own_two, other_two, hidden_one, cotangent, weight_row, shared_rows, slope, *hidden_weights
     )
     other_three = swap(own_three, "head", 2, 0)
     reduce_grad = jnp.einsum("rd,rf->df", d_two, active, preferred_element_type=jnp.float32)
     expand_grad = jnp.einsum("rd,rf->df", hidden_low, d_expanded, preferred_element_type=jnp.float32)
-    reduce_scatter = Scatter(reduce_grad.astype(jnp.bfloat16), dp_count, second_order).send()
-    expand_scatter = Scatter(expand_grad.astype(jnp.bfloat16), dp_count, first_order).send()
+    reduce_scatter = Scatter([reduce_grad.astype(jnp.bfloat16)], dp_count, second_order).send()
+    expand_scatter = Scatter([expand_grad.astype(jnp.bfloat16)], dp_count, first_order).send()
     d_one, d_mixed, sums_one = norm_one_backward(
         own_three,
         other_three,
@@ -1090,148 +1360,111 @@
         scale_one,
         inside[None, :],
         shared_rows,
-        late_full,
+        expand_full,
         local_width,
     )
     mixing_grad = jnp.einsum("rd,kr->dk", d_one, attended, preferred_element_type=jnp.float32)
-    mixing_scatter = Scatter(mixing_grad.astype(jnp.bfloat16), dp_count, first_order).send()
+    mixing_scatter = Scatter([mixing_grad.astype(jnp.bfloat16)], dp_count, first_order).send()
     first_scatters = (reduce_scatter, expand_scatter, mixing_scatter)
     d_mixed = after(d_mixed, *[scatter.sent for scatter in first_scatters])
     back_taps = tap_rows_of(kernel_weight[:, ::-1])
     d_left, kernel_left = attention_backward(item_units, proj, back_taps, d_mixed, *saved, part=0)
 
-    def inputs_part(gradient):
-        product = jnp.einsum("rd,kr->dk", tokens, gradient, preferred_element_type=jnp.float32)
-        return product.astype(jnp.bfloat16)
-
     for scatter in first_scatters:
         scatter.take(d_left).send()
-    left_scatter = Scatter(inputs_part(d_left), dp_count, second_order).send()
+    left_grad = turned_outer(d_left, tokens)
+    left_scatter = Scatter([left_grad], dp_count, second_order).send()
     d_mixed = after(d_mixed, left_scatter.sent, *[scatter.sent for scatter in first_scatters])
     d_right, kernel_right = attention_backward(item_units, proj, back_taps, d_mixed, *saved, part=1)
-    right_scatter = Scatter(inputs_part(d_right), dp_count, first_order).send()
-    for scatter in first_scatters:
-        scatter.take(d_right)
-    hidden_scatter = expand_scatter.merge(reduce_scatter).send()
-    left_scatter.take(d_right).send()
-    d_both = after(d_right, right_scatter.sent, hidden_scatter.sent, left_scatter.sent)
-    own_four = turned_dot([d_left, d_both], [inputs_left, inputs_right], [0, 0], width_full)
-    other_four = swap(own_four, "head", 2, 0)
-    right_scatter.take(own_four).send()
-    inputs_scatter = right_scatter.merge(left_scatter, mixing_scatter)
-
-    kernel_grad = jnp.concatenate([kernel_left, kernel_right], axis=0)
+    right_grad = turned_outer(d_right, tokens)
     left_sums, right_sums = [
         jnp.sum(gradient.astype(jnp.float32), axis=1).reshape(3, part_width)
         for gradient in (d_left, d_right)
     ]
-    bias_size = 2 * local_width + hidden_units
-    small_parts = [
-        left_sums[0],
-        right_sums[0],
-        left_sums[2],
-        right_sums[2],
-        expand_sums.reshape(-1),
-        sums_one[0],
-        sums_two[1],
-        sums_one[1],
-        sums_one[2],
-        sums_two[2],
-        sums_two[3],
-        kernel_grad.reshape(-1),
-    ]
-    small_size = sum(part.shape[0] for part in small_parts)
-    small_count = (small_size + 1023) // 1024 * 8
-    small_parts.append(jnp.zeros((small_count * 128 - small_size,), jnp.float32))
-    small_total = jnp.concatenate(small_parts).reshape(small_count, 128)
-    small_total = sum_all(small_total, "dp", dp_count).reshape(-1)
-    dp_index = lax.axis_index("dp")
-    biases_share = lax.dynamic_slice_in_dim(small_total, dp_index * bias_share, bias_share)[None, :]
-    shared_total = small_total[bias_size : bias_size + 6 * width_full].reshape(6, width_full)
-    shared_share = lax.dynamic_slice_in_dim(shared_total, dp_index * shard_rows, shard_rows, axis=1)
-    kernel_total = small_total[bias_size + 6 * width_full : small_size].reshape(kernel_grad.shape)
-
-    hidden_share = hidden_scatter.finish()
-    expand_share, reduce_share = hidden_share[:, :hidden_units], hidden_share[:, hidden_units:].T
-    merged_share = inputs_scatter.finish()
+    biases_grad = jnp.concatenate(
+        [left_sums[0], right_sums[0], left_sums[2], right_sums[2], expand_sums.reshape(-1)]
+    )
+    shared_grad = jnp.concatenate(
+        [sums_one[0:1], sums_two[1:2], sums_one[1:3], sums_two[2:4]], axis=0
+    )
+    shared_grad = shared_grad.reshape(6, dp_count, shard_rows).transpose(1, 0, 2)
+    kernel_grad = jnp.concatenate([kernel_left, kernel_right], axis=0)
     columns = 3 * part_width
-    right_share, left_share = [
-        merged_share[:, at : at + columns].reshape(shard_rows, 3, part_width)
-        for at in (0, columns)
-    ]
-    mixing_share = merged_share[:, 2 * columns :].T
-    inputs_share = jnp.concatenate([left_share, right_share], axis=2).transpose(1, 0, 2)
+
+    def widened(array):
+        return jnp.pad(array, ((0, 0), (0, columns - array.shape[1])))[:, None]
+
+    tap_count = kernel_grad.shape[1]
+    tap_share = -(-tap_count // dp_count)
+    tap_owner = jnp.arange(tap_count) // tap_share
+    kernel_rows = jnp.where(
+        tap_owner[None, None, :] == jnp.arange(dp_count)[:, None, None], kernel_grad[None], 0.0
+    )
+    small_rows = jnp.concatenate(
+        [biases_grad.reshape(dp_count, bias_share), shared_grad.reshape(dp_count, -1)], axis=1
+    )
+    right_rows = jnp.concatenate(
+        [
+            right_grad.reshape(dp_count, shard_rows, columns),
+            widened(small_rows).astype(jnp.bfloat16),
+            widened(kernel_rows.reshape(dp_count, -1)).astype(jnp.bfloat16),
+        ],
+        axis=1,
+    )
+    right_rows = right_rows.reshape(-1, columns)
+    right_scatter = Scatter([right_rows], dp_count, first_order).send()
+    for scatter in first_scatters:
+        scatter.take(right_scatter.sent)
+    hidden_scatter = expand_scatter.merge(reduce_scatter, mixing_scatter).send()
+    left_scatter.take(right_scatter.sent).send()
+    d_both = after(d_right, right_scatter.sent, hidden_scatter.sent, left_scatter.sent)
+    own_four = turned_dot([d_left, d_both], [inputs_left, inputs_right], [0, 0], width_full)
+    other_four = swap(own_four, "head", 2, 0)
+    hidden_scatter.take(own_four).send()
+    right_scatter.take(own_four).send()
     input_grad = (
         own_four.astype(jnp.float32) + other_four.astype(jnp.float32) + d_one.astype(jnp.float32)
     )
-    local_stats = jnp.stack([jnp.sum(stat_one), jnp.sum(sums_two[0]), jnp.sum(weight_rows)])
-    kernel_squares = jnp.where(lax.axis_index("dp") == 0, jnp.sum(kernel_total * kernel_total), 0.0)
-    local_squares = (
-        jnp.sum(inputs_share * inputs_share)
-        + jnp.sum(mixing_share * mixing_share)
-        + jnp.sum(expand_share * expand_share)
-        + jnp.sum(reduce_share * reduce_share)
-        + jnp.sum(biases_share * biases_share)
-    )
-    local_squares = (
-        local_squares
-        + jnp.where(lax.axis_index("head") == 0, jnp.sum(shared_share * shared_share), 0.0)
-        + kernel_squares
-    )
-    final_row = jnp.concatenate([local_squares[None], local_stats, jnp.zeros((124,), jnp.float32)])
-    final_row = sum_all(sum_all(final_row[None, :], "head", 2), "dp", dp_count)[0]
-    squares_total, summed_stats = final_row[0], final_row[1:4]
-    grad_norm = jnp.sqrt(squares_total)
-    factor = CLIP_NORM / (grad_norm + CLIP_EPS)
-    inputs_master, inputs_momentum, inputs_variance = adamw(
-        inputs_weight, inputs_moment, inputs_square, inputs_share, factor, RATE_MATRIX, WEIGHT_DECAY
-    )
-    mixing_master, mixing_momentum, mixing_variance = adamw(
-        mixing_weight, mixing_moment, mixing_square, mixing_share, factor, RATE_MATRIX, WEIGHT_DECAY
-    )
-    expand_master, expand_momentum, expand_variance = adamw(
-        expand_weight, expand_moment, expand_square, expand_share, factor, RATE_MATRIX, WEIGHT_DECAY
-    )
-    reduce_master, reduce_momentum, reduce_variance = adamw(
-        reduce_weight, reduce_moment, reduce_square, reduce_share, factor, RATE_MATRIX, WEIGHT_DECAY
-    )
-    biases_master, biases_momentum, biases_variance = adamw(
-        biases_weight, biases_moment, biases_square, biases_share, factor, RATE_VECTOR, 0.0
-    )
-    shared_master, shared_momentum, shared_variance = adamw(
-        shared_weight, shared_moment, shared_square, shared_share, factor, RATE_VECTOR, 0.0
-    )
-    kernel_master, kernel_momentum, kernel_variance = adamw(
-        kernel_weight, kernel_moment, kernel_square, kernel_total, factor, RATE_VECTOR, 0.0
-    )
-    sublayer_rms = jnp.sqrt(summed_stats[:2] / (summed_stats[2] * width_full))
-    return (
-        output_rows,
-        input_grad,
-        inputs_master,
-        inputs_momentum,
-        inputs_variance,
-        mixing_master,
-        mixing_momentum,
-        mixing_variance,
-        expand_master,
-        expand_momentum,
-        expand_variance,
-        reduce_master,
-        reduce_momentum,
-        reduce_variance,
-        biases_master,
-        biases_momentum,
-        biases_variance,
-        shared_master,
-        shared_momentum,
-        shared_variance,
-        kernel_master,
-        kernel_momentum,
-        kernel_variance,
-        grad_norm,
-        sublayer_rms,
-    )
+    inputs_scatter = left_scatter.merge(right_scatter, join=-2).send()
+    dp_index, head_index = lax.axis_index("dp"), lax.axis_index("head")
+    places = jnp.stack([(dp_index >> bits[-1]) & 1, head_index == 0]).astype(jnp.int32)
+    inputs_scatter.take(input_grad)
+    while hidden_scatter.order:
+        hidden_scatter.take().send()
+    while inputs_scatter.order:
+        inputs_scatter.take().send()
+    *shares, final_row = finish(
+        places, hidden_scatter, inputs_scatter, stat_one, sums_two, bias_share, 6 * shard_rows
+    )
+    final_row = sum_all(final_row, "dp", dp_count)
+    totals = sum_all(final_row[:, :128], "head", 2)
+    olds = [
+        inputs_weight,
+        inputs_moment,
+        inputs_square,
+        mixing_weight.T,
+        mixing_moment.T,
+        mixing_square.T,
+        expand_weight,
+        expand_moment,
+        expand_square,
+        reduce_weight.T,
+        reduce_moment.T,
+        reduce_square.T,
+        biases_weight,
+        biases_moment,
+        biases_square,
+        shared_weight,
+        shared_moment,
+        shared_square,
+        kernel_weight,
+        kernel_moment,
+        kernel_square,
+    ]
+    *news, row = update(totals, final_row, shares, olds, width_full, bias_share, shard_rows)
+    for index in (3, 4, 5, 9, 10, 11):
+        news[index] = news[index].T
+    return (output_rows, input_grad, *news, row[0, 0], row[0, 1:3])
 
 
 def solution(mesh):

time: 389 us -> 335 us (0.86)
  other arithmetic: 48.7 us -> 27 us
  between operations: 23.7 us -> 3.13 us
  Pallas kernels: 134 us -> 149 us
  local copies, waits for them, and re-layouts: 35.4 us -> 23.9 us
  waiting for transfers between devices: 85.5 us -> 77.3 us
  matrix products: 20.7 us -> 14.4 us
    pallas_call x5 -> x10, Pallas kernels: 58 us -> 72 us  [the longest x1 18.6 us: attention_finish(): pl.pallas_call(attention_finish_body, in_specs=[pl.BlockSpec(memory_space...]
    sub x7 -> x0, other arithmetic: 11.1 us -> none  [adamw(): master - learn_rate * (step_size + decay_rate * master)]
    add x12 -> x14, other arithmetic: 14.4 us -> 7.17 us  [take(): currents.append(kept.astype(jnp.float32) + piece.astype(jnp.float32))]
    ppermute x35, waiting for transfers between devices: 84.2 us -> 77.3 us  [swap(): return lax.ppermute(array, axis, [(i, i ^ 1 << bit) for i in range(count)])]
    dot_general x2 -> x0, matrix products: 6.6 us -> none  [inputs_part(): jnp.einsum('rd,kr->dk', tokens, gradient, preferred_element_type=jnp.floa...]
    reduce_sum x9 -> x0, other arithmetic: 6.49 us -> none  [the longest x1 1.37 us: body(): jnp.sum(shared_share * shared_share)]
    convert_element_type x10 -> x15, local copies, waits for them, and re-layouts: 6.7 us -> 2.23 us  [send(): lax.dynamic_slice_in_dim(current, 1 - mine, 1, dim).astype(jnp.bfloat16)]
    select_n x10 -> x14, other arithmetic: 2.24 us -> 6.53 us  [the longest x13 6.52 us: step(): jnp.where(lax.axis_index('dp') >> bit & 1 == 0, jnp.concatenate([self.cur...]
  transfers between devices with their start and end apart: 36 -> 35, of which waited for: 20 -> 20; matrix products, arithmetic and copies ran while one was open for 22% -> 16% of each run, Pallas kernels for 18% -> 30%
where the time goes in v3:
time: 335 us; the launch traced here: 330 us
  Pallas kernels  149 us (44%)
  waiting for transfers between devices  77.3 us (23%)
  starting transfers between devices  36.1 us (11%)
  other arithmetic  27 us (8%)
  local copies, waits for them, and re-layouts  23.9 us (7%)
  matrix products  14.4 us (4%)
    ppermute x35, waiting for transfers between devices, swap(): return lax.ppermute(array, axis, [(i, i ^ 1 << bit) for i in range(count)])  77.3 us
    pallas_call x2, Pallas kernels, attention_backward(): pl.pallas_call(attention_backward_body, grid=(1,), in_specs=[pl.BlockSpec...  37.1 us
    ppermute x35, starting transfers between devices, swap(): return lax.ppermute(array, axis, [(i, i ^ 1 << bit) for i in range(count)])  36.1 us
    pallas_call x1, Pallas kernels, hidden_backward(): pl.pallas_call(hidden_backward_body, grid=(row_count // ROWS,), in_specs=...  20.3 us
    pallas_call x1, Pallas kernels, hidden_forward(): pl.pallas_call(hidden_forward_body, grid=(row_count // ROWS,), in_specs=[...  19.2 us
    pallas_call x1, Pallas kernels, attention_finish(): pl.pallas_call(attention_finish_body, in_specs=[pl.BlockSpec(memory_space...  18.6 us
    pallas_call x2, Pallas kernels, turned_dot(): pl.pallas_call(turned_dot_body, grid=(row_count // LONG_ROWS,), in_specs=...  11.9 us
    pallas_call x2, Pallas kernels, turned_outer(): pl.pallas_call(turned_outer_body, grid=(width // OUTER,), in_specs=[fixed...  10 us
  transfers between devices with their start and end apart: 35, of which 20 were waited for; matrix products, arithmetic and copies ran while one was open for 16% of the time, Pallas kernels for 30%

profile of v3, /device:TPU:0, one launch (start us, length us, event | category | flops | bytes accessed | tf_op | source)
XLA Modules:
  0.0 330.3 jit_solution(16256433130284842666)
XLA Ops:
  3.5 4.1 %collective-permute-start = (bf16[1,1,1,1,97,576]{5,4,3,2,1,0:T(8,128)(2,1)S(1)}, bf16[1,1,1,1,97,576]{5,4,3,2,1,0:T(8,128)(2,1)S(1)}, u32[]{:S(2)}, u32[]{:S(2)}) collective-permute-start(bf16[1,1,1,1,97,576]{5,4,3,2,1,0:T(8,128)(2,1)S(1)} %get-tuple-element.187), channel_id=1, source_target_pairs={{0,16},{2,18},{4,20},{6,22},{8,24},{10,26},{12,28},{14,30},{16,0},... | collective-permute-start | bytes 335240 | tf_op jit(solution)/shard_map/ppermute | solution.py:35
  11.6 2.4 collective-permute-done
  14.9 3.4 %collective-permute-start.6 = (bf16[1,1,1,1,48,3456]{5,4,3,2,1,0:T(8,128)(2,1)S(1)}, bf16[1,1,1,1,48,3456]{5,4,3,2,1,0:T(8,128)(2,1)S(1)}, u32[]{:S(2)}, u32[]{:S(2)}) collective-permute-start(bf16[1,1,1,1,48,3456]{5,4,3,2,1,0:T(8,128)(2,1)S(1)} %bitcast.82), channel_id=1, source_target_pairs={{0,16},{2,18},{4,20},{6,22},{8,24},{10,26},{12,28},{14,30},{16,0},... | collective-permute-start | bytes 995336 | tf_op jit(solution)/shard_map/ppermute | solution.py:35
  18.7 8.5 %collective-permute-done.1 = bf16[2,1,1,1,97,576]{5,4,3,2,1,0:T(8,128)(2,1)S(1)} collective-permute-done((bf16[2,1,1,1,97,576]{5,4,3,2,1,0:T(8,128)(2,1)S(1)}, bf16[2,1,1,1,97,576]{5,4,3,2,1,0:T(8,128)(2,1)S(1)}, u32[]{:S(2)}, u32[]{:S(2)}) %collective-permute-start.1) | collective-permute-done | bytes 223520 | tf_op jit(solution)/shard_map/ppermute | solution.py:35
  28.8 1.5 collective-permute-start.4
  30.3 2.8 collective-permute-done.6
  33.3 1.6 collective-permute-done.4
  38.0 7.8 %collective-permute-done.5 = bf16[2,2,2,1,48,576]{5,4,3,2,1,0:T(8,128)(2,1)S(1)} collective-permute-done((bf16[2,2,2,1,48,576]{5,4,3,2,1,0:T(8,128)(2,1)S(1)}, bf16[2,2,2,1,48,576]{5,4,3,2,1,0:T(8,128)(2,1)S(1)}, u32[]{:S(2)}, u32[]{:S(2)}) %collective-permute-start.5) | collective-permute-done | bytes 442400 | tf_op jit(solution)/shard_map/ppermute | solution.py:35
  51.0 1.6 collective-permute-start.8
  53.2 7.6 %shard_map.432.proj_ref = bf16[2,3,192,1536]{3,2,1,0:T(8,128)(2,1)} custom-call(bf16[768,576]{1,0:T(8,128)(2,1)} %bitcast.100, bf16[768,576]{1,0:T(8,128)(2,1)} %bitcast.98, bf16[1536,768]{1,0:T(8,128)(2,1)} %right_ref.3, f32[1152,1]{1,0:T(8,128)} %broadcast_in_dim.75.bias_ref), custom_call_target="tpu_custom_call" | custom-call | flops 2717908992 | bytes 8000000 | tf_op jit(solution)/shard_map/pallas_call | solution.py:1080
  60.8 8.4 %shard_map.433 = (f32[2,384,128]{2,1,0:T(8,128)S(1)}, f32[6,128,128]{2,1,0:T(8,128)S(1)}, bf16[6,128,1536]{2,1,0:T(8,128)(2,1)S(1)}, f32[6,128,64]{2,1,0:T(8,128)S(1)}, f32[6,128,128]{2,1,0:T(8,128)S(1)}) custom-call(s32[1,2]{1,0:T(1,128)S(1)} %copy-done.5, bf16[2,3,192,1536]{3,2,1,0:T(8,128)(2,1)} %shard_map.432.proj_ref), custom_call_target="tpu_custom_call" | custom-call | flops 8999999488 | bytes 8000000 | tf_op jit(solution)/shard_map/pallas_call | solution.py:415
  70.7 1.5 collective-permute-start.11
  72.1 18.6 %shard_map.434 = (bf16[384,1536]{1,0:T(8,128)(2,1)S(1)}, bf16[6,128,1536]{2,1,0:T(8,128)(2,1)S(1)}, bf16[4,4,6,128,128]{4,3,2,1,0:T(8,128)(2,1)}, f32[2,4,6,128,128]{4,3,2,1,0:T(8,128)}, f32[6,128,64]{2,1,0:T(8,128)S(1)}) custom-call(s32[1,2]{1,0:T(1,128)S(1)} %copy-done.5, bf16[2,3,192,1536]{3,2,1,0:T(8,128)(2,1)} %shard_map.432.proj_ref, ...), custom_call_target="tpu_custom_call" | custom-call | flops 17999998976 | bytes 16000000 | tf_op jit(solution)/shard_map/pallas_call | solution.py:441
  90.8 3.7 %collective-permute-done.10 = bf16[2,2,1,2,48,1536]{5,4,3,2,1,0:T(8,128)(2,1)S(1)} collective-permute-done((bf16[2,2,1,2,48,1536]{5,4,3,2,1,0:T(8,128)(2,1)S(1)}, bf16[2,2,1,2,48,1536]{5,4,3,2,1,0:T(8,128)(2,1)S(1)}, u32[]{:S(2)}, u32[]{:S(2)}) %collective-permute-start.10) | collective-permute-done | bytes 1179680 | tf_op jit(solution)/shard_map/ppermute | solution.py:35
  94.5 1.8 maximum_select_fusion.1
  96.3 5.8 %collective-permute-done.11 = bf16[2,2,2,1,48,1920]{5,4,3,2,1,0:T(8,128)(2,1)S(1)} collective-permute-done((bf16[2,2,2,1,48,1920]{5,4,3,2,1,0:T(8,128)(2,1)S(1)}, bf16[2,2,2,1,48,1920]{5,4,3,2,1,0:T(8,128)(2,1)S(1)}, u32[]{:S(2)}, u32[]{:S(2)}) %collective-permute-start.11) | collective-permute-done | bytes 1474592 | tf_op jit(solution)/shard_map/ppermute | solution.py:35
  102.1 1.9 maximum_select_fusion
  104.0 4.6 %shard_map.435.own_ref = bf16[1536,768]{1,0:T(8,128)(2,1)} custom-call(bf16[384,1536]{1,0:T(8,128)(2,1)} %copy-done.3, bf16[768,1920]{1,0:T(8,128)(2,1)} %bitcast.73), custom_call_target="tpu_custom_call" | custom-call | flops 905969664 | bytes 8000000 | tf_op jit(solution)/shard_map/pallas_call | solution.py:1032
  113.5 19.2 %shard_map.436 = (bf16[1536,768]{1,0:T(8,128)(2,1)}, f32[1536,768]{1,0:T(8,128)}, bf16[1536,768]{1,0:T(8,128)(2,1)}, bf16[1536,768]{1,0:T(8,128)(2,1)}, f32[1,15...) custom-call(bf16[1536,768]{1,0:T(8,128)(2,1)} %shard_map.435.own_ref, ...), custom_call_target="tpu_custom_call" | custom-call | flops 7247757312 | bytes 30000000 | tf_op jit(solution)/shard_map/pallas_call | solution.py:816
  133.7 4.0 %collective-permute-done.13.other_ref = bf16[1536,768]{1,0:T(8,128)(2,1)} collective-permute-done((bf16[1536,768]{1,0:T(8,128)(2,1)}, bf16[1536,768]{1,0:T(8,128)(2,1)}, u32[]{:S(2)}, u32[]{:S(2)}) %collective-permute-start.13) | collective-permute-done | bytes 2359328 | tf_op jit(solution)/shard_map/ppermute | solution.py:35
  137.6 20.3 %shard_map.437 = (f32[1536,768]{1,0:T(8,128)}, bf16[1536,768]{1,0:T(8,128)(2,1)}, bf16[1536,1536]{1,0:T(8,128)(2,1)}, bf16[1536,768]{1,0:T(8,128)(2,1)}, f32[8,768]{1,0:T(8,128)}, /*index=5*/f32[1,1536]{1,0:T(1,128)}) custom-call(bf16[1536,768]{1,0:T(8,128)(2,1)} %get-tuple-element.114.own_ref, bf16[1536,768]{1,0:T(8,128)(2,1)} %collective-permute-done.13.other_ref, ...), custom_call_target="tpu_custom_call" | custom-call | flops 7247757312 | bytes 30000000 | tf_op jit(solution)/shard_map/pallas_call | solution.py:909
  158.9 7.1 %convolution_convert_fusion = bf16[768,1536]{1,0:T(8,128)(2,1)S(1)} fusion(bf16[1536,768]{1,0:T(8,128)(2,1)} %get-tuple-element.124, bf16[1536,1536]{1,0:T(8,128)(2,1)} %get-tuple-element.125), kind=kOutput, calls=%fused_computation.1 | convolution fusion | flops 3625058304 | bytes 9437184 | tf_op jit(solution)/shard_map/rd,rf->df/dot_general | solution.py:1352
  168.1 4.1 %convolution_convert_fusion.1 = bf16[768,1536]{1,0:T(8,128)(2,1)S(1)} fusion(bf16[1536,768]{1,0:T(8,128)(2,1)S(1)} %copy-done.26, bf16[1536,1536]{1,0:T(8,128)(2,1)S(1)} %copy-done.41), kind=kOutput, calls=%fused_computation.2 | convolution fusion | flops 3625058304 | bytes 9437184 | tf_op jit(solution)/shard_map/rd,rf->df/dot_general | solution.py:1351
  174.4 1.4 copy-done.27
  175.8 8.5 %shard_map.438 = (bf16[1536,768]{1,0:T(8,128)(2,1)}, bf16[384,1536]{1,0:T(8,128)(2,1)}, f32[8,768]{1,0:T(8,128)}) custom-call(bf16[1536,768]{1,0:T(8,128)(2,1)} %get-tuple-element.118.own_ref, bf16[1536,768]{1,0:T(8,128)(2,1)} %copy-done.27, bf16[1536,768]{1,0:T(8,128)(2,1)} %get-tuple-element.119.d_two_ref, bf16[1536,768]{1,0:T(8,128)(2,1)} %get-tuple-element.120.unit_ref, ...), custom_call_target="tpu_custom_call" | custom-call | flops 905969664 | bytes 14000000 | tf_op jit(solution)/shard_map/pallas_call | solution.py:982
  184.3 3.2 convolution_convert_fusion.2
  189.4 18.7 %shard_map.439 = (bf16[576,1536]{1,0:T(8,128)(2,1)S(1)}, f32[3,256]{1,0:T(4,128)S(1)}) custom-call(s32[1,2]{1,0:T(1,128)S(1)} %copy-done.5, bf16[2,3,192,1536]{3,2,1,0:T(8,128)(2,1)} %shard_map.432.proj_ref, f32[3,256]{1,0:T(4,128)S(1)} %get-tuple-element.199.taps_ref, bf16[384,1536]{1,0:T(8,128)(2,1)S(1)} %copy-done.6, bf16[6,128,1536]{2,1,0:T(8,128)(2,1)} %copy-done.8, ...), custom_call_target="tpu_custom_call" | custom-call | flops 15000000512 | bytes 10000000 | tf_op jit(solution)/shard_map/pallas_call | solution.py:667
  209.4 5.0 %shard_map.440 = bf16[768,576]{1,0:T(8,128)(2,1)} custom-call(bf16[576,1536]{1,0:T(8,128)(2,1)} %copy-done, bf16[1536,768]{1,0:T(8,128)(2,1)} %right_ref.3), custom_call_target="tpu_custom_call" | custom-call | flops 1358954496 | bytes 6000000 | tf_op jit(solution)/shard_map/pallas_call | solution.py:1049
  214.4 1.7 convert_add_fusion.1
  217.8 1.4 copy-done.17
  220.7 2.0 constant_dynamic-slice_fusion.1
  226.9 18.4 %shard_map.441 = (bf16[576,1536]{1,0:T(8,128)(2,1)S(1)}, f32[3,256]{1,0:T(4,128)S(1)}) custom-call(s32[1,2]{1,0:T(1,128)S(1)} %copy-done.5, bf16[2,3,192,1536]{3,2,1,0:T(8,128)(2,1)} %shard_map.432.proj_ref, f32[3,256]{1,0:T(4,128)S(1)} %get-tuple-element.198.taps_ref, bf16[384,1536]{1,0:T(8,128)(2,1)S(1)} %copy-done.6, bf16[6,128,1536]{2,1,0:T(8,128)(2,1)} %copy-done.8, ...), custom_call_target="tpu_custom_call" | custom-call | flops 15000000512 | bytes 10000000 | tf_op jit(solution)/shard_map/pallas_call | solution.py:667
  247.5 5.0 %shard_map.442 = bf16[768,576]{1,0:T(8,128)(2,1)} custom-call(bf16[576,1536]{1,0:T(8,128)(2,1)} %copy-done.2, bf16[1536,768]{1,0:T(8,128)(2,1)} %right_ref.3), custom_call_target="tpu_custom_call" | custom-call | flops 1358954496 | bytes 6000000 | tf_op jit(solution)/shard_map/pallas_call | solution.py:1049
  252.6 1.5 pad_maximum_fusion
  260.6 2.2 collective-permute-start.23
  262.8 7.3 %shard_map.443 = bf16[1536,768]{1,0:T(8,128)(2,1)} custom-call(bf16[576,1536]{1,0:T(8,128)(2,1)} %copy-done, bf16[768,576]{1,0:T(8,128)(2,1)} %bitcast.101, bf16[576,1536]{1,0:T(8,128)(2,1)} %copy-done.2, bf16[768,576]{1,0:T(8,128)(2,1)} %bitcast.99), custom_call_target="tpu_custom_call" | custom-call | flops 2717908992 | bytes 8000000 | tf_op jit(solution)/shard_map/pallas_call | solution.py:1032
  272.2 7.4 %collective-permute-done.27 = bf16[2,2,1,1,50,576]{5,4,3,2,1,0:T(8,128)(2,1)S(1)} collective-permute-done((bf16[2,2,1,1,50,576]{5,4,3,2,1,0:T(8,128)(2,1)S(1)}, bf16[2,2,1,1,50,576]{5,4,3,2,1,0:T(8,128)(2,1)S(1)}, u32[]{:S(2)}, u32[]{:S(2)}) %collective-permute-start.27) | collective-permute-done | bytes 230432 | tf_op jit(solution)/shard_map/ppermute | solution.py:35
  280.1 3.0 collective-permute-start.24
  283.1 2.9 convert_add_fusion
  286.1 6.8 %collective-permute-done.28 = bf16[2,1,1,1,98,576]{5,4,3,2,1,0:T(8,128)(2,1)S(1)} collective-permute-done((bf16[2,1,1,1,98,576]{5,4,3,2,1,0:T(8,128)(2,1)S(1)}, bf16[2,1,1,1,98,576]{5,4,3,2,1,0:T(8,128)(2,1)S(1)}, u32[]{:S(2)}, u32[]{:S(2)}) %collective-permute-start.28) | collective-permute-done | bytes 225824 | tf_op jit(solution)/shard_map/ppermute | solution.py:35
  293.7 8.1 %collective-permute-done.24 = bf16[1,1,1,1,48,3456]{5,4,3,2,1,0:T(8,128)(2,1)S(1)} collective-permute-done((bf16[1,1,1,1,48,3456]{5,4,3,2,1,0:T(8,128)(2,1)S(1)}, bf16[1,1,1,1,48,3456]{5,4,3,2,1,0:T(8,128)(2,1)S(1)}, u32[]{:S(2)}, u32[]{:S(2)}) %collective-permute-start.24) | collective-permute-done | bytes 331808 | tf_op jit(solution)/shard_map/ppermute | solution.py:35
  301.8 1.6 collective-permute-done.29
  304.1 2.6 shard_map.444
  307.6 2.8 collective-permute-done.30
  311.9 2.8 collective-permute-done.31
  314.7 3.6 %collective-permute-done.32 = f32[1,384]{1,0:T(1,128)S(1)} collective-permute-done((f32[1,384]{1,0:T(1,128)S(1)}, f32[1,384]{1,0:T(1,128)S(1)}, u32[]{:S(2)}, u32[]{:S(2)}) %collective-permute-start.32) | collective-permute-done | bytes 1568 | tf_op jit(solution)/shard_map/ppermute | solution.py:35
  319.2 3.6 %collective-permute-done.33 = f32[1,384]{1,0:T(1,128)S(1)} collective-permute-done((f32[1,384]{1,0:T(1,128)S(1)}, f32[1,384]{1,0:T(1,128)S(1)}, u32[]{:S(2)}, u32[]{:S(2)}) %collective-permute-start.33) | collective-permute-done | bytes 1568 | tf_op jit(solution)/shard_map/ppermute | solution.py:35
  324.5 4.4 %shard_map.445 = (f32[3,48,384]{2,1,0:T(8,128)}, f32[3,48,384]{2,1,0:T(8,128)}, f32[3,48,384]{2,1,0:T(8,128)}, f32[48,384]{1,0:T(8,128)}, f32[48,384]{1,0:T(8,12...) custom-call(f32[1,128]{1,0:T(1,128)} %slice_add_fusion.refs_0_, ...), custom_call_target="tpu_custom_call" | custom-call | flops 5000000 | bytes 6000000 | tf_op jit(solution)/shard_map/pallas_call | solution.py:1226
  (266 shorter events, 59.1 us)
Async XLA Ops:
  0.7 10.7 %copy-start.36 = (f32[6,33]{1,0:T(8,128)S(1)}, f32[6,33]{1,0:T(8,128)}, u32[]{:S(2)}) copy-start(f32[6,33]{1,0:T(8,128)} %refs_25_.1) | copy-start | bytes 2380
  3.5 10.5 %collective-permute-start = (bf16[1,1,1,1,97,576]{5,4,3,2,1,0:T(8,128)(2,1)S(1)}, bf16[1,1,1,1,97,576]{5,4,3,2,1,0:T(8,128)(2,1)S(1)}, u32[]{:S(2)}, u32[]{:S(2)}) collective-permute-start(bf16[1,1,1,1,97,576]{5,4,3,2,1,0:T(8,128)(2,1)S(1)} %get-tuple-element.187), channel_id=1, source_target_pairs={{0,16},{2,18},{4,20},{6,22},{8,24},{10,26},{12,28},{14,30},{16,0},... | collective-permute-start | bytes 335240 | tf_op jit(solution)/shard_map/ppermute | solution.py:35
  14.1 13.1 %collective-permute-start.1 = (bf16[2,1,1,1,97,576]{5,4,3,2,1,0:T(8,128)(2,1)S(1)}, bf16[2,1,1,1,97,576]{5,4,3,2,1,0:T(8,128)(2,1)S(1)}, u32[]{:S(2)}, u32[]{:S(2)}) collective-permute-start(bf16[2,1,1,1,97,576]{5,4,3,2,1,0:T(8,128)(2,1)S(1)} %maximum_select_fusion.13), channel_id=1, source_target_pairs={{0,8},{2,10},{4,12},{6,14},{8,0},{10,2},{12,4},{14,6},{16,24},{18,... | collective-permute-start | bytes 670472 | tf_op jit(solution)/shard_map/ppermute | solution.py:35
  14.9 18.2 %collective-permute-start.6 = (bf16[1,1,1,1,48,3456]{5,4,3,2,1,0:T(8,128)(2,1)S(1)}, bf16[1,1,1,1,48,3456]{5,4,3,2,1,0:T(8,128)(2,1)S(1)}, u32[]{:S(2)}, u32[]{:S(2)}) collective-permute-start(bf16[1,1,1,1,48,3456]{5,4,3,2,1,0:T(8,128)(2,1)S(1)} %bitcast.82), channel_id=1, source_target_pairs={{0,16},{2,18},{4,20},{6,22},{8,24},{10,26},{12,28},{14,30},{16,0},... | collective-permute-start | bytes 995336 | tf_op jit(solution)/shard_map/ppermute | solution.py:35
  27.5 8.5 %collective-permute-start.2 = (bf16[2,2,1,1,49,576]{5,4,3,2,1,0:T(8,128)(2,1)S(1)}, bf16[2,2,1,1,49,576]{5,4,3,2,1,0:T(8,128)(2,1)S(1)}, u32[]{:S(2)}, u32[]{:S(2)}) collective-permute-start(bf16[2,2,1,1,49,576]{5,4,3,2,1,0:T(8,128)(2,1)S(1)} %slice.243), channel_id=1, source_target_pairs={{0,2},{2,0},{4,6},{6,4},{8,10},{10,8},{12,14},{14,12},{16,18},{18,... | collective-permute-start | bytes 677384 | tf_op jit(solution)/shard_map/ppermute | solution.py:35
  28.8 6.2 %collective-permute-start.4 = (bf16[2,2,1,1,48,576]{5,4,3,2,1,0:T(8,128)(2,1)S(1)}, bf16[2,2,1,1,48,576]{5,4,3,2,1,0:T(8,128)(2,1)S(1)}, u32[]{:S(2)}, u32[]{:S(2)}) collective-permute-start(bf16[2,2,1,1,48,576]{5,4,3,2,1,0:T(8,128)(2,1)S(1)} %slice.245), channel_id=1, source_target_pairs={{0,4},{2,6},{4,0},{6,2},{8,12},{10,14},{12,8},{14,10},{16,20},{18,... | collective-permute-start | bytes 663560 | tf_op jit(solution)/shard_map/ppermute | solution.py:35
  33.2 17.4 %collective-permute-start.7 = (bf16[2,1,1,1,48,3456]{5,4,3,2,1,0:T(8,128)(2,1)S(1)}, bf16[2,1,1,1,48,3456]{5,4,3,2,1,0:T(8,128)(2,1)S(1)}, u32[]{:S(2)}, u32[]{:S(2)}) collective-permute-start(bf16[2,1,1,1,48,3456]{5,4,3,2,1,0:T(8,128)(2,1)S(1)} %maximum_select_fusion.8), channel_id=1, source_target_pairs={{0,8},{2,10},{4,12},{6,14},{8,0},{10,2},{12,4},{14,6},{16,24},{18,... | collective-permute-start | bytes 1990664 | tf_op jit(solution)/shard_map/ppermute | solution.py:35
  35.1 10.7 %collective-permute-start.5 = (bf16[2,2,2,1,48,576]{5,4,3,2,1,0:T(8,128)(2,1)S(1)}, bf16[2,2,2,1,48,576]{5,4,3,2,1,0:T(8,128)(2,1)S(1)}, u32[]{:S(2)}, u32[]{:S(2)}) collective-permute-start(bf16[2,2,2,1,48,576]{5,4,3,2,1,0:T(8,128)(2,1)S(1)} %maximum_select_fusion.11), channel_id=1, source_target_pairs={{0,2},{2,0},{4,6},{6,4},{8,10},{10,8},{12,14},{14,12},{16,18},{18,... | collective-permute-start | bytes 1327112 | tf_op jit(solution)/shard_map/ppermute | solution.py:35
  36.5 11.4 %collective-permute-start.3 = (bf16[2,2,1,2,49,576]{5,3,4,2,1,0:T(2,128)(2,1)S(1)}, bf16[2,2,1,2,49,576]{5,3,4,2,1,0:T(2,128)(2,1)S(1)}, u32[]{:S(2)}, u32[]{:S(2)}) collective-permute-start(bf16[2,2,1,2,49,576]{5,3,4,2,1,0:T(2,128)(2,1)S(1)} %copy.72), channel_id=1, source_target_pairs={{0,4},{2,6},{4,0},{6,2},{8,12},{10,14},{12,8},{14,10},{16,20},{18,... | collective-permute-start | bytes 1354760 | tf_op jit(solution)/shard_map/ppermute | solution.py:35
  51.0 18.9 %collective-permute-start.8 = (bf16[2,2,1,1,48,1920]{5,4,3,2,1,0:T(8,128)(2,1)S(1)}, bf16[2,2,1,1,48,1920]{5,4,3,2,1,0:T(8,128)(2,1)S(1)}, u32[]{:S(2)}, u32[]{:S(2)}) collective-permute-start(bf16[2,2,1,1,48,1920]{5,4,3,2,1,0:T(8,128)(2,1)S(1)} %slice.246), channel_id=1, source_target_pairs={{0,4},{2,6},{4,0},{6,2},{8,12},{10,14},{12,8},{14,10},{16,20},{18,... | collective-permute-start | bytes 2211848 | tf_op jit(solution)/shard_map/ppermute | solution.py:35
  52.6 16.6 %collective-permute-start.9 = (bf16[2,2,1,1,48,1536]{5,4,3,2,1,0:T(8,128)(2,1)S(1)}, bf16[2,2,1,1,48,1536]{5,4,3,2,1,0:T(8,128)(2,1)S(1)}, u32[]{:S(2)}, u32[]{:S(2)}) collective-permute-start(bf16[2,2,1,1,48,1536]{5,4,3,2,1,0:T(8,128)(2,1)S(1)} %slice.247), channel_id=1, source_target_pairs={{0,2},{2,0},{4,6},{6,4},{8,10},{10,8},{12,14},{14,12},{16,18},{18,... | collective-permute-start | bytes 1769480 | tf_op jit(solution)/shard_map/ppermute | solution.py:35
  53.2 7.6 %copy-start.5 = (s32[1,2]{1,0:T(1,128)S(1)}, s32[1,2]{1,0:T(1,128)}, u32[]{:S(2)}) copy-start(s32[1,2]{1,0:T(1,128)} %units_ref.7) | copy-start | bytes 28
  69.2 120.2 %copy-start.9 = (f32[6,128,128]{2,1,0:T(8,128)}, f32[6,128,128]{2,1,0:T(8,128)S(1)}, u32[]{:S(2)}) copy-start(f32[6,128,128]{2,1,0:T(8,128)S(1)} %get-tuple-element.109.middle_ref) | copy-start | bytes 1179652
  69.2 120.2 %copy-start.11 = (f32[6,128,64]{2,1,0:T(8,128)}, f32[6,128,64]{2,1,0:T(8,128)S(1)}, u32[]{:S(2)}) copy-start(f32[6,128,64]{2,1,0:T(8,128)S(1)} %get-tuple-element.110.values_ref) | copy-start | bytes 589828
  69.3 25.2 %collective-permute-start.10 = (bf16[2,2,1,2,48,1536]{5,4,3,2,1,0:T(8,128)(2,1)S(1)}, bf16[2,2,1,2,48,1536]{5,4,3,2,1,0:T(8,128)(2,1)S(1)}, u32[]{:S(2)}, u32[]{:S(2)}) collective-permute-start(bf16[2,2,1,2,48,1536]{5,4,3,2,1,0:T(8,128)(2,1)S(1)} %maximum_select_fusion.4), channel_id=1, source_target_pairs={{0,4},{2,6},{4,0},{6,2},{8,12},{10,14},{12,8},{14,10},{16,20},{18,... | collective-permute-start | bytes 3538952 | tf_op jit(solution)/shard_map/ppermute | solution.py:35
  70.7 31.4 %collective-permute-start.11 = (bf16[2,2,2,1,48,1920]{5,4,3,2,1,0:T(8,128)(2,1)S(1)}, bf16[2,2,2,1,48,1920]{5,4,3,2,1,0:T(8,128)(2,1)S(1)}, u32[]{:S(2)}, u32[]{:S(2)}) collective-permute-start(bf16[2,2,2,1,48,1920]{5,4,3,2,1,0:T(8,128)(2,1)S(1)} %maximum_select_fusion.2), channel_id=1, source_target_pairs={{0,2},{2,0},{4,6},{6,4},{8,10},{10,8},{12,14},{14,12},{16,18},{18,... | collective-permute-start | bytes 4423688 | tf_op jit(solution)/shard_map/ppermute | solution.py:35
  90.8 98.6 %copy-start.13 = (f32[6,128,64]{2,1,0:T(8,128)}, f32[6,128,64]{2,1,0:T(8,128)S(1)}, u32[]{:S(2)}) copy-start(f32[6,128,64]{2,1,0:T(8,128)S(1)} %get-tuple-element.132.weighted_ref) | copy-start | bytes 589828
  104.0 6.5 %copy-start.38 = (s32[1536]{0:T(1024)S(1)}, s32[1536]{0:T(1024)}, u32[]{:S(2)}) copy-start(s32[1536]{0:T(1024)} %param.28) | copy-start | bytes 18436
  108.6 4.9 %collective-permute-start.12 = (bf16[1536,768]{1,0:T(8,128)(2,1)}, bf16[1536,768]{1,0:T(8,128)(2,1)}, u32[]{:S(2)}, u32[]{:S(2)}) collective-permute-start(bf16[1536,768]{1,0:T(8,128)(2,1)} %shard_map.435.own_ref), channel_id=1, source_target_pairs={{0,1},{1,0},{2,3},{3,2},{4,5},{5,4},{6,7},{7,6},{8,9},{9,8},{10,11... | collective-permute-start | bytes 7077896 | tf_op jit(solution)/shard_map/ppermute | solution.py:35
  132.7 4.9 %collective-permute-start.13 = (bf16[1536,768]{1,0:T(8,128)(2,1)}, bf16[1536,768]{1,0:T(8,128)(2,1)}, u32[]{:S(2)}, u32[]{:S(2)}) collective-permute-start(bf16[1536,768]{1,0:T(8,128)(2,1)} %get-tuple-element.114.own_ref), channel_id=1, source_target_pairs={{0,1},{1,0},{2,3},{3,2},{4,5},{5,4},{6,7},{7,6},{8,9},{9,8},{10,11... | collective-permute-start | bytes 7077896 | tf_op jit(solution)/shard_map/ppermute | solution.py:35
  158.7 15.7 %collective-permute-start.14 = (bf16[1536,768]{1,0:T(8,128)(2,1)}, bf16[1536,768]{1,0:T(8,128)(2,1)S(1)}, u32[]{:S(2)}, u32[]{:S(2)}) collective-permute-start(bf16[1536,768]{1,0:T(8,128)(2,1)} %get-tuple-element.118.own_ref), channel_id=1, source_target_pairs={{0,1},{1,0},{2,3},{3,2},{4,5},{5,4},{6,7},{7,6},{8,9},{9,8},{10,11... | collective-permute-start | bytes 7077896 | tf_op jit(solution)/shard_map/ppermute | solution.py:35
  158.9 9.1 %copy-start.41 = (bf16[1536,1536]{1,0:T(8,128)(2,1)S(1)}, bf16[1536,1536]{1,0:T(8,128)(2,1)}, u32[]{:S(2)}) copy-start(bf16[1536,1536]{1,0:T(8,128)(2,1)} %get-tuple-element.123) | copy-start | bytes 14155780
  167.1 42.3 %collective-permute-start.16 = (bf16[2,2,2,1,48,1536]{5,4,3,2,1,0:T(8,128)(2,1)}, bf16[2,2,2,1,48,1536]{5,4,3,2,1,0:T(8,128)(2,1)}, u32[]{:S(2)}, u32[]{:S(2)}) collective-permute-start(bf16[2,2,2,1,48,1536]{5,4,3,2,1,0:T(8,128)(2,1)} %constant_dynamic-slice_fusion.3), channel_id=1, source_target_pairs={{0,2},{2,0},{4,6},{6,4},{8,10},{10,8},{12,14},{14,12},{16,18},{18,... | collective-permute-start | bytes 3538952 | tf_op jit(solution)/shard_map/ppermute | solution.py:35
  173.6 43.5 %collective-permute-start.15 = (bf16[2,2,1,2,48,1536]{5,4,3,2,1,0:T(8,128)(2,1)}, bf16[2,2,1,2,48,1536]{5,4,3,2,1,0:T(8,128)(2,1)S(1)}, u32[]{:S(2)}, u32[]{:S(2)}) collective-permute-start(bf16[2,2,1,2,48,1536]{5,4,3,2,1,0:T(8,128)(2,1)} %constant_dynamic-slice_fusion.4), channel_id=1, source_target_pairs={{0,4},{2,6},{4,0},{6,2},{8,12},{10,14},{12,8},{14,10},{16,20},{18,... | collective-permute-start | bytes 3538952 | tf_op jit(solution)/shard_map/ppermute | solution.py:35
  175.8 8.5 %copy-start.4 = (bf16[384,1536]{1,0:T(8,128)(2,1)S(1)}, bf16[384,1536]{1,0:T(8,128)(2,1)}, u32[]{:S(2)}) copy-start(bf16[384,1536]{1,0:T(8,128)(2,1)} %copy-done.3) | copy-start | bytes 3538948
  188.3 37.4 %collective-permute-start.17 = (bf16[2,2,2,1,48,384]{5,4,3,2,1,0:T(8,128)(2,1)}, bf16[2,2,2,1,48,384]{5,4,3,2,1,0:T(8,128)(2,1)}, u32[]{:S(2)}, u32[]{:S(2)}) collective-permute-start(bf16[2,2,2,1,48,384]{5,4,3,2,1,0:T(8,128)(2,1)} %constant_dynamic-slice_fusion.2), channel_id=1, source_target_pairs={{0,2},{2,0},{4,6},{6,4},{8,10},{10,8},{12,14},{14,12},{16,18},{18,... | collective-permute-start | bytes 884744 | tf_op jit(solution)/shard_map/ppermute | solution.py:35
  189.4 19.9 %copy-start.37 = (f32[8,768]{1,0:T(8,128)S(1)}, f32[8,768]{1,0:T(8,128)}, u32[]{:S(2)}) copy-start(f32[8,768]{1,0:T(8,128)} %get-tuple-element.140) | copy-start | bytes 73732
  222.7 33.0 %collective-permute-start.21 = (bf16[2,2,1,2,48,576]{5,4,3,2,1,0:T(8,128)(2,1)}, bf16[2,2,1,2,48,576]{5,4,3,2,1,0:T(8,128)(2,1)}, u32[]{:S(2)}, u32[]{:S(2)}) collective-permute-start(bf16[2,2,1,2,48,576]{5,4,3,2,1,0:T(8,128)(2,1)} %constant_dynamic-slice_fusion.1), channel_id=1, source_target_pairs={{0,4},{2,6},{4,0},{6,2},{8,12},{10,14},{12,8},{14,10},{16,20},{18,... | collective-permute-start | bytes 1327112 | tf_op jit(solution)/shard_map/ppermute | solution.py:35
  224.0 34.0 %collective-permute-start.18 = (bf16[2,2,1,1,48,1536]{5,4,3,2,1,0:T(8,128)(2,1)}, bf16[2,2,1,1,48,1536]{5,4,3,2,1,0:T(8,128)(2,1)}, u32[]{:S(2)}, u32[]{:S(2)}) collective-permute-start(bf16[2,2,1,1,48,1536]{5,4,3,2,1,0:T(8,128)(2,1)} %dynamic-slice_convert_fusion), channel_id=1, source_target_pairs={{0,4},{2,6},{4,0},{6,2},{8,12},{10,14},{12,8},{14,10},{16,20},{18,... | collective-permute-start | bytes 1769480 | tf_op jit(solution)/shard_map/ppermute | solution.py:35
  224.7 34.5 %collective-permute-start.19 = (bf16[2,2,1,1,48,1536]{5,4,3,2,1,0:T(8,128)(2,1)}, bf16[2,2,1,1,48,1536]{5,4,3,2,1,0:T(8,128)(2,1)}, u32[]{:S(2)}, u32[]{:S(2)}) collective-permute-start(bf16[2,2,1,1,48,1536]{5,4,3,2,1,0:T(8,128)(2,1)} %dynamic-slice_convert_fusion.1), channel_id=1, source_target_pairs={{0,2},{2,0},{4,6},{6,4},{8,10},{10,8},{12,14},{14,12},{16,18},{18,... | collective-permute-start | bytes 1769480 | tf_op jit(solution)/shard_map/ppermute | solution.py:35
  226.8 18.5 %copy-start.28 = (f32[2,2,2,1,48,384]{5,4,3,2,1,0:T(8,128)}, f32[2,2,2,1,48,384]{5,4,3,2,1,0:T(8,128)S(1)}, u32[]{:S(2)}) copy-start(f32[2,2,2,1,48,384]{5,4,3,2,1,0:T(8,128)S(1)} %convert_add_fusion.9) | copy-start | bytes 1769476
  245.4 11.4 %collective-permute-start.20 = (bf16[2,2,1,1,48,384]{5,4,3,2,1,0:T(8,128)(2,1)S(1)}, bf16[2,2,1,1,48,384]{5,4,3,2,1,0:T(8,128)(2,1)S(1)}, u32[]{:S(2)}, u32[]{:S(2)}) collective-permute-start(bf16[2,2,1,1,48,384]{5,4,3,2,1,0:T(8,128)(2,1)S(1)} %dynamic-slice_convert_fusion.8), channel_id=1, source_target_pairs={{0,4},{2,6},{4,0},{6,2},{8,12},{10,14},{12,8},{14,10},{16,20},{18,... | collective-permute-start | bytes 442376 | tf_op jit(solution)/shard_map/ppermute | solution.py:35
  254.5 15.6 %collective-permute-start.26 = (bf16[2,2,2,1,50,576]{5,2,4,3,1,0:T(2,128)(2,1)S(1)}, bf16[2,2,2,1,50,576]{5,2,4,3,1,0:T(2,128)(2,1)S(1)}, u32[]{:S(2)}, u32[]{:S(2)}) collective-permute-start(bf16[2,2,2,1,50,576]{5,2,4,3,1,0:T(2,128)(2,1)S(1)} %copy.81), channel_id=1, source_target_pairs={{0,2},{2,0},{4,6},{6,4},{8,10},{10,8},{12,14},{14,12},{16,18},{18,... | collective-permute-start | bytes 1382408 | tf_op jit(solution)/shard_map/ppermute | solution.py:35
  256.9 15.2 %collective-permute-start.25 = (bf16[2,2,1,1,48,576]{5,4,3,2,1,0:T(8,128)(2,1)S(1)}, bf16[2,2,1,1,48,576]{5,4,3,2,1,0:T(8,128)(2,1)S(1)}, u32[]{:S(2)}, u32[]{:S(2)}) collective-permute-start(bf16[2,2,1,1,48,576]{5,4,3,2,1,0:T(8,128)(2,1)S(1)} %dynamic-slice_convert_fusion.5), channel_id=1, source_target_pairs={{0,2},{2,0},{4,6},{6,4},{8,10},{10,8},{12,14},{14,12},{16,18},{18,... | collective-permute-start | bytes 663560 | tf_op jit(solution)/shard_map/ppermute | solution.py:35
  260.6 19.2 %collective-permute-start.23 = (bf16[2,1,1,1,48,3456]{5,4,3,2,1,0:T(8,128)(2,1)S(1)}, bf16[2,1,1,1,48,3456]{5,4,3,2,1,0:T(8,128)(2,1)S(1)}, u32[]{:S(2)}, u32[]{:S(2)}) collective-permute-start(bf16[2,1,1,1,48,3456]{5,4,3,2,1,0:T(8,128)(2,1)S(1)} %pad_maximum_fusion.1), channel_id=1, source_target_pairs={{0,8},{2,10},{4,12},{6,14},{8,0},{10,2},{12,4},{14,6},{16,24},{18,... | collective-permute-start | bytes 1990664 | tf_op jit(solution)/shard_map/ppermute | solution.py:35
  270.1 13.0 %collective-permute-start.22 = (bf16[1536,768]{1,0:T(8,128)(2,1)}, bf16[1536,768]{1,0:T(8,128)(2,1)S(1)}, u32[]{:S(2)}, u32[]{:S(2)}) collective-permute-start(bf16[1536,768]{1,0:T(8,128)(2,1)} %shard_map.443), channel_id=1, source_target_pairs={{0,1},{1,0},{2,3},{3,2},{4,5},{5,4},{6,7},{7,6},{8,9},{9,8},{10,11... | collective-permute-start | bytes 7077896 | tf_op jit(solution)/shard_map/ppermute | solution.py:35
  270.2 9.3 %collective-permute-start.27 = (bf16[2,2,1,1,50,576]{5,4,3,2,1,0:T(8,128)(2,1)S(1)}, bf16[2,2,1,1,50,576]{5,4,3,2,1,0:T(8,128)(2,1)S(1)}, u32[]{:S(2)}, u32[]{:S(2)}) collective-permute-start(bf16[2,2,1,1,50,576]{5,4,3,2,1,0:T(8,128)(2,1)S(1)} %dynamic-slice_convert_fusion.4), channel_id=1, source_target_pairs={{0,4},{2,6},{4,0},{6,2},{8,12},{10,14},{12,8},{14,10},{16,20},{18,... | collective-permute-start | bytes 691208 | tf_op jit(solution)/shard_map/ppermute | solution.py:35
  279.7 13.2 %collective-permute-start.28 = (bf16[2,1,1,1,98,576]{5,4,3,2,1,0:T(8,128)(2,1)S(1)}, bf16[2,1,1,1,98,576]{5,4,3,2,1,0:T(8,128)(2,1)S(1)}, u32[]{:S(2)}, u32[]{:S(2)}) collective-permute-start(bf16[2,1,1,1,98,576]{5,4,3,2,1,0:T(8,128)(2,1)S(1)} %pad_maximum_fusion.4), channel_id=1, source_target_pairs={{0,8},{2,10},{4,12},{6,14},{8,0},{10,2},{12,4},{14,6},{16,24},{18,... | collective-permute-start | bytes 677384 | tf_op jit(solution)/shard_map/ppermute | solution.py:35
  279.8 6.3 %copy-start.32 = (f32[2,1,1,1,48,384]{5,4,3,2,1,0:T(8,128)}, f32[2,1,1,1,48,384]{5,4,3,2,1,0:T(8,128)S(1)}, u32[]{:S(2)}) copy-start(f32[2,1,1,1,48,384]{5,4,3,2,1,0:T(8,128)S(1)} %convert_add_fusion.15) | copy-start | bytes 442372
  280.1 21.6 %collective-permute-start.24 = (bf16[1,1,1,1,48,3456]{5,4,3,2,1,0:T(8,128)(2,1)S(1)}, bf16[1,1,1,1,48,3456]{5,4,3,2,1,0:T(8,128)(2,1)S(1)}, u32[]{:S(2)}, u32[]{:S(2)}) collective-permute-start(bf16[1,1,1,1,48,3456]{5,4,3,2,1,0:T(8,128)(2,1)S(1)} %pad_maximum_fusion.3), channel_id=1, source_target_pairs={{0,16},{2,18},{4,20},{6,22},{8,24},{10,26},{12,28},{14,30},{16,0},... | collective-permute-start | bytes 995336 | tf_op jit(solution)/shard_map/ppermute | solution.py:35
  292.9 10.5 %copy-start.30 = (f32[2,1,1,1,50,576]{5,4,3,2,1,0:T(8,128)}, f32[2,1,1,1,50,576]{5,4,3,2,1,0:T(8,128)S(1)}, u32[]{:S(2)}) copy-start(f32[2,1,1,1,50,576]{5,4,3,2,1,0:T(8,128)S(1)} %convert_add_fusion.13) | copy-start | bytes 691204
  292.9 10.5 %copy-start.31 = (f32[2,1,1,1,48,576]{5,4,3,2,1,0:T(8,128)}, f32[2,1,1,1,48,576]{5,4,3,2,1,0:T(8,128)S(1)}, u32[]{:S(2)}) copy-start(f32[2,1,1,1,48,576]{5,4,3,2,1,0:T(8,128)S(1)} %convert_add_fusion.14) | copy-start | bytes 663556
  293.0 10.4 %collective-permute-start.29 = (bf16[1,1,1,1,98,576]{5,4,3,2,1,0:T(8,128)(2,1)S(1)}, bf16[1,1,1,1,98,576]{5,4,3,2,1,0:T(8,128)(2,1)S(1)}, u32[]{:S(2)}, u32[]{:S(2)}) collective-permute-start(bf16[1,1,1,1,98,576]{5,4,3,2,1,0:T(8,128)(2,1)S(1)} %pad_maximum_fusion.6), channel_id=1, source_target_pairs={{0,16},{2,18},{4,20},{6,22},{8,24},{10,26},{12,28},{14,30},{16,0},... | collective-permute-start | bytes 338696 | tf_op jit(solution)/shard_map/ppermute | solution.py:35
  306.6 3.8 %collective-permute-start.30 = (f32[1,384]{1,0:T(1,128)}, f32[1,384]{1,0:T(1,128)S(1)}, u32[]{:S(2)}, u32[]{:S(2)}) collective-permute-start(f32[1,384]{1,0:T(1,128)} %get-tuple-element.153), channel_id=1, source_target_pairs={{0,2},{2,0},{4,6},{6,4},{8,10},{10,8},{12,14},{14,12},{16,18},{18,... | collective-permute-start | bytes 4616 | tf_op jit(solution)/shard_map/ppermute | solution.py:35
  311.1 3.6 %collective-permute-start.31 = (f32[1,384]{1,0:T(1,128)S(1)}, f32[1,384]{1,0:T(1,128)S(1)}, u32[]{:S(2)}, u32[]{:S(2)}) collective-permute-start(f32[1,384]{1,0:T(1,128)S(1)} %add.158), channel_id=1, source_target_pairs={{0,4},{2,6},{4,0},{6,2},{8,12},{10,14},{12,8},{14,10},{16,20},{18,... | collective-permute-start | bytes 4616 | tf_op jit(solution)/shard_map/ppermute | solution.py:35
  314.7 3.6 %collective-permute-start.32 = (f32[1,384]{1,0:T(1,128)S(1)}, f32[1,384]{1,0:T(1,128)S(1)}, u32[]{:S(2)}, u32[]{:S(2)}) collective-permute-start(f32[1,384]{1,0:T(1,128)S(1)} %add.159), channel_id=1, source_target_pairs={{0,8},{2,10},{4,12},{6,14},{8,0},{10,2},{12,4},{14,6},{16,24},{18,... | collective-permute-start | bytes 4616 | tf_op jit(solution)/shard_map/ppermute | solution.py:35
  318.3 4.5 %collective-permute-start.33 = (f32[1,384]{1,0:T(1,128)S(1)}, f32[1,384]{1,0:T(1,128)S(1)}, u32[]{:S(2)}, u32[]{:S(2)}) collective-permute-start(f32[1,384]{1,0:T(1,128)S(1)} %add.160), channel_id=1, source_target_pairs={{0,16},{2,18},{4,20},{6,22},{8,24},{10,26},{12,28},{14,30},{16,0},... | collective-permute-start | bytes 4616 | tf_op jit(solution)/shard_map/ppermute | solution.py:35
  322.8 1.2 collective-permute-start.34
  (29 other events, 94.5 us)

commit v4 on v3

--- a/solution.py
+++ b/solution.py
@@ -305,7 +305,7 @@
         values_ref[head] = dot_with(last, proj_ref[part, 2, pl.ds(part_at, HEAD_DIM), :], 1, 1)
         return carry
 
-    lax.fori_loop(0, heads, head_start, 0)
+    lax.fori_loop(0, heads, head_start, 0, unroll=2)
 
 
 def attention_finish_body(
@@ -395,7 +395,7 @@
                 ).astype(jnp.bfloat16)
         return carry
 
-    lax.fori_loop(0, heads, head_end, 0)
+    lax.fori_loop(0, heads, head_end, 0, unroll=2)
 
 
 def whole(count):
@@ -530,7 +530,7 @@
         d_middle_ref[head] = jnp.zeros((marks, marks), jnp.float32)
         return carry
 
-    lax.fori_loop(0, heads, head_start, 0)
+    lax.fori_loop(0, heads, head_start, 0, unroll=2)
 
     seven = scaled_eye(marks, 7.0)
     every = range(heads)
@@ -584,7 +584,7 @@
         d_marks_ref[1, rows, :] += dot_fine(marks_ref[0, rows, :], d_logits, 1, 0)
         return carry
 
-    lax.fori_loop(0, heads, head_middle, 0)
+    lax.fori_loop(0, heads, head_middle, 0, unroll=2)
 
     row_index = lax.broadcasted_iota(jnp.int32, (BLOCK, BLOCK), 0)
     column_index = lax.broadcasted_iota(jnp.int32, (BLOCK, BLOCK), 1)
@@ -644,7 +644,7 @@
                 ).astype(jnp.bfloat16)
         return carry
 
-    lax.fori_loop(0, heads, head_end, 0)
+    lax.fori_loop(0, heads, head_end, 0, unroll=2)
 
 
 def attention_backward(item_units, proj, tap_rows, grad, *saved, part):
@@ -699,10 +699,11 @@
     return out, jnp.concatenate([joined[:, 2 * BLOCK - half :], joined[:, : TAPS - half]], axis=1)
 
 
-ROWS = 256
+ROWS = 512
 LONG_ROWS = 512
 OUTER = 384
 PIECE = 512
+SUB = 512
 GELU_SCALE = 0.7978845608
 GELU_CUBE = 0.044715
 
@@ -752,8 +753,14 @@
     return jnp.sum(rows, axis=0, keepdims=True)
 
 
-def both(own_ref, other_ref):
-    return own_ref[...].astype(jnp.float32) + other_ref[...].astype(jnp.float32)
+def both(own_ref, other_ref, rows=...):
+    return own_ref[rows].astype(jnp.float32) + other_ref[rows].astype(jnp.float32)
+
+
+def gelu_parts(expanded):
+    square = expanded * expanded
+    bend = jnp.tanh(expanded * (GELU_SCALE + (GELU_SCALE * GELU_CUBE) * square))
+    return square, 0.5 + 0.5 * bend, bend
 
 
 def weight_blocks(expand, reduce):
@@ -770,44 +777,39 @@
     expand_ref,
     reduce_ref,
     part_ref,
-    hidden_ref,
     low_ref,
     unit_ref,
     scale_ref,
-    active_ref,
-    slope_ref,
+    wide_ref,
     stat_ref,
 ):
-    branch = both(own_ref, other_ref) + shared_ref[0:1]
-    squares = column_sum(as_column(weight_ref[...]) * branch * branch)
-
     @pl.when(pl.program_id(0) == 0)
     def _():
         stat_ref[...] = jnp.zeros_like(stat_ref)
 
-    stat_ref[...] += squares
-    unit, scale = normalized(tokens_ref[...].astype(jnp.float32) + branch)
-    hidden = unit * shared_ref[2:3] + shared_ref[3:4]
-    hidden_ref[...] = hidden
-    unit_ref[...] = unit.astype(jnp.bfloat16)
-    scale_ref[...] = as_row(scale)
-    hidden_low = hidden.astype(jnp.bfloat16)
-    low_ref[...] = hidden_low
-    total = jnp.zeros(part_ref.shape, jnp.float32)
-    for at in range(0, reduce_ref.shape[1], PIECE):
-        lanes = slice(at, at + PIECE)
-        expanded = dot_with(hidden_low, expand_ref[:, lanes], 1, 0) + bias_ref[:, lanes]
-        square = expanded * expanded
-        bend = jnp.tanh(expanded * (GELU_SCALE + (GELU_SCALE * GELU_CUBE) * square))
-        half = 0.5 + 0.5 * bend
-        active = (expanded * half).astype(jnp.bfloat16)
-        active_ref[:, lanes] = active
-        slope = half + (0.5 * expanded) * (1.0 - bend * bend) * (
-            GELU_SCALE + (3.0 * GELU_SCALE * GELU_CUBE) * square
-        )
-        slope_ref[:, lanes] = slope.astype(jnp.bfloat16)
-        total += dot_with(active, reduce_ref[:, lanes], 1, 1)
-    part_ref[...] = total.astype(jnp.bfloat16)
+    weight_column = as_column(weight_ref[...])
+    row_slices = [slice(at, at + SUB) for at in range(0, ROWS, SUB)]
+    lows, scales, squares = [], [], []
+    for rows in row_slices:
+        branch = both(own_ref, other_ref, rows) + shared_ref[0:1]
+        squares.append(column_sum(weight_column[rows] * branch * branch))
+        unit, scale = normalized(tokens_ref[rows].astype(jnp.float32) + branch)
+        hidden = unit * shared_ref[2:3] + shared_ref[3:4]
+        unit_ref[rows] = unit.astype(jnp.bfloat16)
+        scales.append(scale)
+        hidden_low = hidden.astype(jnp.bfloat16)
+        low_ref[rows] = hidden_low
+        total = jnp.zeros((SUB, part_ref.shape[1]), jnp.float32)
+        for at in range(0, reduce_ref.shape[1], PIECE):
+            lanes = slice(at, at + PIECE)
+            expanded = dot_with(hidden_low, expand_ref[:, lanes], 1, 0) + bias_ref[:, lanes]
+            wide_ref[rows, lanes] = expanded.astype(jnp.bfloat16)
+            half = gelu_parts(expanded)[1]
+            active = (expanded * half).astype(jnp.bfloat16)
+            total += dot_with(active, reduce_ref[:, lanes], 1, 1)
+        part_ref[rows] = total.astype(jnp.bfloat16)
+    stat_ref[...] += sum(squares)
+    scale_ref[...] = as_row(jnp.concatenate(scales, axis=0))
 
 
 def hidden_forward(own, other, tokens, weight_row, shared_rows, expand_bias, *weights):
@@ -829,20 +831,16 @@
             row_block(width),
             row_block(width),
             row_block(width),
-            row_block(width),
             row_lanes(),
             row_block(units),
-            row_block(units),
             fixed_block((1, width)),
         ],
         out_shape=[
             jax.ShapeDtypeStruct((row_count, width), jnp.bfloat16),
-            jax.ShapeDtypeStruct((row_count, width), jnp.float32),
             jax.ShapeDtypeStruct((row_count, width), jnp.bfloat16),
             jax.ShapeDtypeStruct((row_count, width), jnp.bfloat16),
             jax.ShapeDtypeStruct((1, row_count), jnp.float32),
             jax.ShapeDtypeStruct((row_count, units), jnp.bfloat16),
-            jax.ShapeDtypeStruct((row_count, units), jnp.bfloat16),
             jax.ShapeDtypeStruct((1, width), jnp.float32),
         ],
         compiler_params=dense_params(),
@@ -853,59 +851,80 @@
 def hidden_backward_body(
     own_ref,
     other_ref,
-    hidden_ref,
+    low_ref,
     cotangent_ref,
     weight_ref,
     shared_ref,
-    slope_ref,
+    wide_ref,
     expand_ref,
     reduce_ref,
     output_ref,
     d_two_ref,
-    d_expanded_ref,
+    reduce_out,
+    expand_out,
     part_ref,
     sums_ref,
     bias_ref,
+    reduce_sum,
+    expand_sum,
 ):
-    branch = both(own_ref, other_ref) + shared_ref[1:2]
-    weight = as_column(weight_ref[...])
-    unit, scale = normalized(hidden_ref[...] + branch)
-    output_ref[...] = unit * shared_ref[4:5] + shared_ref[5:6]
-    grad = cotangent_ref[...].astype(jnp.float32) * weight
-    d_res = norm_backward(grad, shared_ref[4:5], unit, scale)
-    d_two = d_res.astype(jnp.bfloat16)
-    d_two_ref[...] = d_two
-
     @pl.when(pl.program_id(0) == 0)
     def _():
         sums_ref[...] = jnp.zeros_like(sums_ref)
         bias_ref[...] = jnp.zeros_like(bias_ref)
-
-    sums_ref[...] += jnp.concatenate(
-        [
-            column_sum(weight * branch * branch),
-            column_sum(d_res),
-            column_sum(grad * unit),
-            column_sum(grad),
-            jnp.broadcast_to(column_sum(weight), (1, grad.shape[1])),
-            jnp.zeros((3, grad.shape[1]), jnp.float32),
-        ],
-        axis=0,
-    )
-    total = jnp.zeros(part_ref.shape, jnp.float32)
-    for at in range(0, reduce_ref.shape[1], PIECE):
-        lanes = slice(at, at + PIECE)
-        d_active = dot_with(d_two, reduce_ref[:, lanes], 1, 0)
-        d_expanded = (slope_ref[:, lanes].astype(jnp.float32) * d_active).astype(jnp.bfloat16)
-        d_expanded_ref[:, lanes] = d_expanded
-        bias_ref[:, lanes] += column_sum(d_expanded.astype(jnp.float32))
-        total += dot_with(d_expanded, expand_ref[:, lanes], 1, 1)
-    part_ref[...] = total.astype(jnp.bfloat16)
-
-
-def hidden_backward(own, other, hidden, cotangent, weight_row, shared_rows, slope, *weights):
+        reduce_sum[...] = jnp.zeros_like(reduce_sum)
+        expand_sum[...] = jnp.zeros_like(expand_sum)
+
+    weight_column = as_column(weight_ref[...])
+    for start in range(0, ROWS, SUB):
+        rows = slice(start, start + SUB)
+        branch = both(own_ref, other_ref, rows) + shared_ref[1:2]
+        weight = weight_column[rows]
+        unit, scale = normalized(low_ref[rows].astype(jnp.float32) + branch)
+        output_ref[rows] = unit * shared_ref[4:5] + shared_ref[5:6]
+        grad = cotangent_ref[rows].astype(jnp.float32) * weight
+        d_res = norm_backward(grad, shared_ref[4:5], unit, scale)
+        d_two = d_res.astype(jnp.bfloat16)
+        d_two_ref[rows] = d_two
+        d_two_turned = d_res.T.astype(jnp.bfloat16)
+        low_turned = low_ref[rows].astype(jnp.float32).T.astype(jnp.bfloat16)
+        sums_ref[...] += jnp.concatenate(
+            [
+                column_sum(weight * branch * branch),
+                column_sum(d_res),
+                column_sum(grad * unit),
+                column_sum(grad),
+                jnp.broadcast_to(column_sum(weight), (1, grad.shape[1])),
+                jnp.zeros((3, grad.shape[1]), jnp.float32),
+            ],
+            axis=0,
+        )
+        total = jnp.zeros((SUB, part_ref.shape[1]), jnp.float32)
+        for at in range(0, reduce_ref.shape[1], PIECE):
+            lanes = slice(at, at + PIECE)
+            d_active = dot_with(d_two, reduce_ref[:, lanes], 1, 0)
+            expanded = wide_ref[rows, lanes].astype(jnp.float32)
+            square, half, bend = gelu_parts(expanded)
+            active = (expanded * half).astype(jnp.bfloat16)
+            slope = half + (0.5 * expanded) * (1.0 - bend * bend) * (
+                GELU_SCALE + (3.0 * GELU_SCALE * GELU_CUBE) * square
+            )
+            d_expanded = (slope * d_active).astype(jnp.bfloat16)
+            reduce_sum[:, lanes] += dot_with(d_two_turned, active, 1, 0)
+            expand_sum[:, lanes] += dot_with(low_turned, d_expanded, 1, 0)
+            bias_ref[:, lanes] += column_sum(d_expanded.astype(jnp.float32))
+            total += dot_with(d_expanded, expand_ref[:, lanes], 1, 1)
+        part_ref[rows] = total.astype(jnp.bfloat16)
+
+    @pl.when(pl.program_id(0) == pl.num_programs(0) - 1)
+    def _():
+        reduce_out[...] = reduce_sum[...].astype(jnp.bfloat16)
+        expand_out[...] = expand_sum[...].astype(jnp.bfloat16)
+
+
+def hidden_backward(own, other, low, cotangent, weight_row, shared_rows, wide, *weights):
     row_count, width = cotangent.shape
-    units = slope.shape[1]
+    units = wide.shape[1]
     return pl.pallas_call(
         hidden_backward_body,
         grid=(row_count // ROWS,),
@@ -922,7 +941,8 @@
         out_specs=[
             row_block(width),
             row_block(width),
-            row_block(units),
+            fixed_block((width, units)),
+            fixed_block((width, units)),
             row_block(width),
             fixed_block((8, width)),
             fixed_block((1, units)),
@@ -930,14 +950,16 @@
         out_shape=[
             jax.ShapeDtypeStruct((row_count, width), jnp.float32),
             jax.ShapeDtypeStruct((row_count, width), jnp.bfloat16),
-            jax.ShapeDtypeStruct((row_count, units), jnp.bfloat16),
+            jax.ShapeDtypeStruct((width, units), jnp.bfloat16),
+            jax.ShapeDtypeStruct((width, units), jnp.bfloat16),
             jax.ShapeDtypeStruct((row_count, width), jnp.bfloat16),
             jax.ShapeDtypeStruct((8, width), jnp.float32),
             jax.ShapeDtypeStruct((1, units), jnp.float32),
         ],
+        scratch_shapes=[pltpu.VMEM((width, units), jnp.float32)] * 2,
         compiler_params=dense_params(),
         cost_estimate=cost(4 * row_count * width * units, 30_000_000),
-    )(own, other, hidden, cotangent, weight_row, shared_rows, slope, *weights)
+    )(own, other, low, cotangent, weight_row, shared_rows, wide, *weights)
 
 
 def norm_one_body(
@@ -1340,18 +1362,16 @@
     tied_attended = after(attended, reduce_full)
     own_one = turned_dot([tied_attended], [expand_full], [mixing_column], width_full)
     other_one = swap(own_one, "head", 2, 0)
-    own_two, hidden_one, hidden_low, unit_one, scale_one, active, slope, stat_one = hidden_forward(
+    own_two, hidden_low, unit_one, scale_one, wide, stat_one = hidden_forward(
         own_one, other_one, tokens, weight_row, shared_rows, expand_bias, *hidden_weights
     )
     other_two = swap(own_two, "head", 2, 0)
-    output_rows, d_two, d_expanded, own_three, sums_two, expand_sums = hidden_backward(
-        own_two, other_two, hidden_one, cotangent, weight_row, shared_rows, slope, *hidden_weights
+    output_rows, d_two, reduce_grad, expand_grad, own_three, sums_two, expand_sums = hidden_backward(
+        own_two, other_two, hidden_low, cotangent, weight_row, shared_rows, wide, *hidden_weights
     )
     other_three = swap(own_three, "head", 2, 0)
-    reduce_grad = jnp.einsum("rd,rf->df", d_two, active, preferred_element_type=jnp.float32)
-    expand_grad = jnp.einsum("rd,rf->df", hidden_low, d_expanded, preferred_element_type=jnp.float32)
-    reduce_scatter = Scatter([reduce_grad.astype(jnp.bfloat16)], dp_count, second_order).send()
-    expand_scatter = Scatter([expand_grad.astype(jnp.bfloat16)], dp_count, first_order).send()
+    reduce_scatter = Scatter([reduce_grad], dp_count, second_order).send()
+    expand_scatter = Scatter([expand_grad], dp_count, first_order).send()
     d_one, d_mixed, sums_one = norm_one_backward(
         own_three,
         other_three,

time: 335 us -> 332 us (level)
  matrix products: 14.4 us -> 3.18 us
  Pallas kernels: 149 us -> 153 us
  waiting for transfers between devices: 77.3 us -> 81.1 us
    pallas_call x1, Pallas kernels: 20.3 us -> 32.1 us  [hidden_backward(): pl.pallas_call(hidden_backward_body, grid=(row_count // ROWS,), in_specs=...]
    dot_general x2 -> x0, matrix products: 11.2 us -> none  [the longest x1 7.06 us: body(): jnp.einsum('rd,rf->df', hidden_low, d_expanded, preferred_element_type=jn...]
    ppermute x35, waiting for transfers between devices: 77.3 us -> 81.1 us  [swap(): return lax.ppermute(array, axis, [(i, i ^ 1 << bit) for i in range(count)])]
    pallas_call x1, Pallas kernels: 19.2 us -> 15.5 us  [hidden_forward(): pl.pallas_call(hidden_forward_body, grid=(row_count // ROWS,), in_specs=[...]
    unnamed x85 -> x89, local copies, waits for them, and re-layouts: 5.7 us -> 7.07 us
  transfers between devices with their start and end apart: 35 -> 35, of which waited for: 20 -> 20; matrix products, arithmetic and copies ran while one was open for 16% -> 12% of each run, Pallas kernels for 30% -> 29%
where the time goes in v4:
time: 332 us; the launch traced here: 328 us
  Pallas kernels  153 us (46%)
  waiting for transfers between devices  81.1 us (24%)
  starting transfers between devices  36.4 us (11%)
  local copies, waits for them, and re-layouts  25.6 us (8%)
  other arithmetic  25.4 us (8%)
    ppermute x35, waiting for transfers between devices, swap(): return lax.ppermute(array, axis, [(i, i ^ 1 << bit) for i in range(count)])  81.1 us
    ppermute x35, starting transfers between devices, swap(): return lax.ppermute(array, axis, [(i, i ^ 1 << bit) for i in range(count)])  36.4 us
    pallas_call x2, Pallas kernels, attention_backward(): pl.pallas_call(attention_backward_body, grid=(1,), in_specs=[pl.BlockSpec...  34.7 us
    pallas_call x1, Pallas kernels, hidden_backward(): pl.pallas_call(hidden_backward_body, grid=(row_count // ROWS,), in_specs=...  32.1 us
    pallas_call x1, Pallas kernels, attention_finish(): pl.pallas_call(attention_finish_body, in_specs=[pl.BlockSpec(memory_space...  17.6 us
    pallas_call x1, Pallas kernels, hidden_forward(): pl.pallas_call(hidden_forward_body, grid=(row_count // ROWS,), in_specs=[...  15.5 us
    pallas_call x2, Pallas kernels, turned_dot(): pl.pallas_call(turned_dot_body, grid=(row_count // LONG_ROWS,), in_specs=...  11.9 us
    pallas_call x2, Pallas kernels, turned_outer(): pl.pallas_call(turned_outer_body, grid=(width // OUTER,), in_specs=[fixed...  10.5 us
  transfers between devices with their start and end apart: 35, of which 20 were waited for; matrix products, arithmetic and copies ran while one was open for 12% of the time, Pallas kernels for 29%

profile of v4, /device:TPU:0, one launch (start us, length us, event | category | flops | bytes accessed | tf_op | source)
XLA Modules:
  0.0 327.6 jit_solution(8090622041517526896)
XLA Ops:
  3.6 4.1 %collective-permute-start = (bf16[1,1,1,1,97,576]{5,4,3,2,1,0:T(8,128)(2,1)S(1)}, bf16[1,1,1,1,97,576]{5,4,3,2,1,0:T(8,128)(2,1)S(1)}, u32[]{:S(2)}, u32[]{:S(2)}) collective-permute-start(bf16[1,1,1,1,97,576]{5,4,3,2,1,0:T(8,128)(2,1)S(1)} %get-tuple-element.185), channel_id=1, source_target_pairs={{0,16},{2,18},{4,20},{6,22},{8,24},{10,26},{12,28},{14,30},{16,0},... | collective-permute-start | bytes 335240 | tf_op jit(solution)/shard_map/ppermute | solution.py:35
  9.1 4.9 %collective-permute-done = bf16[1,1,1,1,97,576]{5,4,3,2,1,0:T(8,128)(2,1)S(1)} collective-permute-done((bf16[1,1,1,1,97,576]{5,4,3,2,1,0:T(8,128)(2,1)S(1)}, bf16[1,1,1,1,97,576]{5,4,3,2,1,0:T(8,128)(2,1)S(1)}, u32[]{:S(2)}, u32[]{:S(2)}) %collective-permute-start) | collective-permute-done | bytes 111776 | tf_op jit(solution)/shard_map/ppermute | solution.py:35
  14.9 3.4 %collective-permute-start.6 = (bf16[1,1,1,1,48,3456]{5,4,3,2,1,0:T(8,128)(2,1)S(1)}, bf16[1,1,1,1,48,3456]{5,4,3,2,1,0:T(8,128)(2,1)S(1)}, u32[]{:S(2)}, u32[]{:S(2)}) collective-permute-start(bf16[1,1,1,1,48,3456]{5,4,3,2,1,0:T(8,128)(2,1)S(1)} %bitcast.78), channel_id=1, source_target_pairs={{0,16},{2,18},{4,20},{6,22},{8,24},{10,26},{12,28},{14,30},{16,0},... | collective-permute-start | bytes 995336 | tf_op jit(solution)/shard_map/ppermute | solution.py:35
  18.7 8.5 %collective-permute-done.1 = bf16[2,1,1,1,97,576]{5,4,3,2,1,0:T(8,128)(2,1)S(1)} collective-permute-done((bf16[2,1,1,1,97,576]{5,4,3,2,1,0:T(8,128)(2,1)S(1)}, bf16[2,1,1,1,97,576]{5,4,3,2,1,0:T(8,128)(2,1)S(1)}, u32[]{:S(2)}, u32[]{:S(2)}) %collective-permute-start.1) | collective-permute-done | bytes 223520 | tf_op jit(solution)/shard_map/ppermute | solution.py:35
  28.8 1.5 collective-permute-start.4
  30.3 2.8 collective-permute-done.6
  33.4 1.6 collective-permute-done.4
  38.0 7.8 %collective-permute-done.5 = bf16[2,2,2,1,48,576]{5,4,3,2,1,0:T(8,128)(2,1)S(1)} collective-permute-done((bf16[2,2,2,1,48,576]{5,4,3,2,1,0:T(8,128)(2,1)S(1)}, bf16[2,2,2,1,48,576]{5,4,3,2,1,0:T(8,128)(2,1)S(1)}, u32[]{:S(2)}, u32[]{:S(2)}) %collective-permute-start.5) | collective-permute-done | bytes 442400 | tf_op jit(solution)/shard_map/ppermute | solution.py:35
  51.1 1.6 collective-permute-start.8
  53.3 7.9 %shard_map.432.proj_ref = bf16[2,3,192,1536]{3,2,1,0:T(8,128)(2,1)} custom-call(bf16[768,576]{1,0:T(8,128)(2,1)} %bitcast.96, bf16[768,576]{1,0:T(8,128)(2,1)} %bitcast.94, bf16[1536,768]{1,0:T(8,128)(2,1)} %right_ref.3, f32[1152,1]{1,0:T(8,128)} %broadcast_in_dim.75.bias_ref), custom_call_target="tpu_custom_call" | custom-call | flops 2717908992 | bytes 8000000 | tf_op jit(solution)/shard_map/pallas_call | solution.py:1102
  61.2 7.3 %shard_map.433 = (f32[2,384,128]{2,1,0:T(8,128)S(1)}, f32[6,128,128]{2,1,0:T(8,128)S(1)}, bf16[6,128,1536]{2,1,0:T(8,128)(2,1)S(1)}, f32[6,128,64]{2,1,0:T(8,128)S(1)}, f32[6,128,128]{2,1,0:T(8,128)S(1)}) custom-call(s32[1,2]{1,0:T(1,128)S(1)} %copy-done.5, bf16[2,3,192,1536]{3,2,1,0:T(8,128)(2,1)} %shard_map.432.proj_ref), custom_call_target="tpu_custom_call" | custom-call | flops 8999999488 | bytes 8000000 | tf_op jit(solution)/shard_map/pallas_call | solution.py:415
  69.8 1.4 collective-permute-start.11
  71.3 17.6 %shard_map.434 = (bf16[384,1536]{1,0:T(8,128)(2,1)S(1)}, bf16[6,128,1536]{2,1,0:T(8,128)(2,1)S(1)}, bf16[4,4,6,128,128]{4,3,2,1,0:T(8,128)(2,1)}, f32[2,4,6,128,128]{4,3,2,1,0:T(8,128)}, f32[6,128,64]{2,1,0:T(8,128)S(1)}) custom-call(s32[1,2]{1,0:T(1,128)S(1)} %copy-done.5, bf16[2,3,192,1536]{3,2,1,0:T(8,128)(2,1)} %shard_map.432.proj_ref, ...), custom_call_target="tpu_custom_call" | custom-call | flops 17999998976 | bytes 16000000 | tf_op jit(solution)/shard_map/pallas_call | solution.py:441
  88.8 4.9 %collective-permute-done.10 = bf16[2,2,1,2,48,1536]{5,4,3,2,1,0:T(8,128)(2,1)S(1)} collective-permute-done((bf16[2,2,1,2,48,1536]{5,4,3,2,1,0:T(8,128)(2,1)S(1)}, bf16[2,2,1,2,48,1536]{5,4,3,2,1,0:T(8,128)(2,1)S(1)}, u32[]{:S(2)}, u32[]{:S(2)}) %collective-permute-start.10) | collective-permute-done | bytes 1179680 | tf_op jit(solution)/shard_map/ppermute | solution.py:35
  93.7 1.9 maximum_select_fusion.1
  95.6 5.6 %collective-permute-done.11 = bf16[2,2,2,1,48,1920]{5,4,3,2,1,0:T(8,128)(2,1)S(1)} collective-permute-done((bf16[2,2,2,1,48,1920]{5,4,3,2,1,0:T(8,128)(2,1)S(1)}, bf16[2,2,2,1,48,1920]{5,4,3,2,1,0:T(8,128)(2,1)S(1)}, u32[]{:S(2)}, u32[]{:S(2)}) %collective-permute-start.11) | collective-permute-done | bytes 1474592 | tf_op jit(solution)/shard_map/ppermute | solution.py:35
  101.2 1.9 maximum_select_fusion
  103.1 4.6 %shard_map.435.own_ref = bf16[1536,768]{1,0:T(8,128)(2,1)} custom-call(bf16[384,1536]{1,0:T(8,128)(2,1)} %copy-done.3, bf16[768,1920]{1,0:T(8,128)(2,1)} %bitcast.69), custom_call_target="tpu_custom_call" | custom-call | flops 905969664 | bytes 8000000 | tf_op jit(solution)/shard_map/pallas_call | solution.py:1054
  112.6 15.5 %shard_map.436 = (bf16[1536,768]{1,0:T(8,128)(2,1)}, bf16[1536,768]{1,0:T(8,128)(2,1)}, bf16[1536,768]{1,0:T(8,128)(2,1)}, f32[1,1536]{1,0:T(1,128)}, bf16[1536,1536]{1,0:T(8,128)(2,1)}, /*index=5*/f32[1,768]{1,0:T(1,128)}) custom-call(bf16[1536,768]{1,0:T(8,128)(2,1)} %shard_map.435.own_ref, bf16[1536,768]{1,0:T(8,128)(2,1)} %collective-permute-done.12.other_ref, ...), custom_call_target="tpu_custom_call" | custom-call | flops 7247757312 | bytes 30000000 | tf_op jit(solution)/shard_map/pallas_call | solution.py:818
  128.2 4.6 %collective-permute-done.13.other_ref = bf16[1536,768]{1,0:T(8,128)(2,1)S(1)} collective-permute-done((bf16[1536,768]{1,0:T(8,128)(2,1)}, bf16[1536,768]{1,0:T(8,128)(2,1)S(1)}, u32[]{:S(2)}, u32[]{:S(2)}) %collective-permute-start.13) | collective-permute-done | bytes 2359328 | tf_op jit(solution)/shard_map/ppermute | solution.py:35
  132.9 1.4 copy-done.43
  134.2 32.1 %shard_map.437 = (f32[1536,768]{1,0:T(8,128)}, bf16[1536,768]{1,0:T(8,128)(2,1)}, bf16[768,1536]{1,0:T(8,128)(2,1)}, bf16[768,1536]{1,0:T(8,128)(2,1)}, bf16[153...) custom-call(bf16[1536,768]{1,0:T(8,128)(2,1)} %get-tuple-element.113.own_ref, ...), custom_call_target="tpu_custom_call" | custom-call | flops 7247757312 | bytes 30000000 | tf_op jit(solution)/shard_map/pallas_call | solution.py:928
  168.1 2.4 constant_dynamic-slice_fusion.3
  173.6 8.4 %shard_map.438 = (bf16[1536,768]{1,0:T(8,128)(2,1)}, bf16[384,1536]{1,0:T(8,128)(2,1)}, f32[8,768]{1,0:T(8,128)}) custom-call(bf16[1536,768]{1,0:T(8,128)(2,1)} %get-tuple-element.117.own_ref, bf16[1536,768]{1,0:T(8,128)(2,1)} %collective-permute-done.14.other_ref, bf16[1536,768]{1,0:T(8,128)(2,1)} %get-tuple-element.118.d_two_ref, ...), custom_call_target="tpu_custom_call" | custom-call | flops 905969664 | bytes 14000000 | tf_op jit(solution)/shard_map/pallas_call | solution.py:1004
  182.1 3.2 convolution_convert_fusion
  187.2 17.3 %shard_map.439 = (bf16[576,1536]{1,0:T(8,128)(2,1)S(1)}, f32[3,256]{1,0:T(4,128)S(1)}) custom-call(s32[1,2]{1,0:T(1,128)S(1)} %copy-done.5, bf16[2,3,192,1536]{3,2,1,0:T(8,128)(2,1)} %shard_map.432.proj_ref, f32[3,256]{1,0:T(4,128)S(1)} %get-tuple-element.197.taps_ref, bf16[384,1536]{1,0:T(8,128)(2,1)S(1)} %copy-done.6, bf16[6,128,1536]{2,1,0:T(8,128)(2,1)} %copy-done.8, ...), custom_call_target="tpu_custom_call" | custom-call | flops 15000000512 | bytes 10000000 | tf_op jit(solution)/shard_map/pallas_call | solution.py:667
  206.8 5.5 %shard_map.440 = bf16[768,576]{1,0:T(8,128)(2,1)} custom-call(bf16[576,1536]{1,0:T(8,128)(2,1)} %copy-done, bf16[1536,768]{1,0:T(8,128)(2,1)} %right_ref.3), custom_call_target="tpu_custom_call" | custom-call | flops 1358954496 | bytes 6000000 | tf_op jit(solution)/shard_map/pallas_call | solution.py:1071
  213.6 1.7 convert_add_fusion.2
  215.4 1.4 copy-done.17
  218.3 2.0 constant_dynamic-slice_fusion.1
  224.4 17.4 %shard_map.441 = (bf16[576,1536]{1,0:T(8,128)(2,1)S(1)}, f32[3,256]{1,0:T(4,128)S(1)}) custom-call(s32[1,2]{1,0:T(1,128)S(1)} %copy-done.5, bf16[2,3,192,1536]{3,2,1,0:T(8,128)(2,1)} %shard_map.432.proj_ref, f32[3,256]{1,0:T(4,128)S(1)} %get-tuple-element.196.taps_ref, bf16[384,1536]{1,0:T(8,128)(2,1)S(1)} %copy-done.6, bf16[6,128,1536]{2,1,0:T(8,128)(2,1)} %copy-done.8, ...), custom_call_target="tpu_custom_call" | custom-call | flops 15000000512 | bytes 10000000 | tf_op jit(solution)/shard_map/pallas_call | solution.py:667
  243.9 5.0 %shard_map.442 = bf16[768,576]{1,0:T(8,128)(2,1)} custom-call(bf16[576,1536]{1,0:T(8,128)(2,1)} %copy-done.2, bf16[1536,768]{1,0:T(8,128)(2,1)} %right_ref.3), custom_call_target="tpu_custom_call" | custom-call | flops 1358954496 | bytes 6000000 | tf_op jit(solution)/shard_map/pallas_call | solution.py:1071
  248.9 1.4 pad_maximum_fusion
  254.3 1.4 convert_add_fusion.4
  257.4 2.2 collective-permute-start.23
  259.6 7.3 %shard_map.443 = bf16[1536,768]{1,0:T(8,128)(2,1)} custom-call(bf16[576,1536]{1,0:T(8,128)(2,1)} %copy-done, bf16[768,576]{1,0:T(8,128)(2,1)} %bitcast.97, bf16[576,1536]{1,0:T(8,128)(2,1)} %copy-done.2, bf16[768,576]{1,0:T(8,128)(2,1)} %bitcast.95), custom_call_target="tpu_custom_call" | custom-call | flops 2717908992 | bytes 8000000 | tf_op jit(solution)/shard_map/pallas_call | solution.py:1054
  268.2 8.2 %collective-permute-done.27 = bf16[2,2,1,1,50,576]{5,4,3,2,1,0:T(8,128)(2,1)S(1)} collective-permute-done((bf16[2,2,1,1,50,576]{5,4,3,2,1,0:T(8,128)(2,1)S(1)}, bf16[2,2,1,1,50,576]{5,4,3,2,1,0:T(8,128)(2,1)S(1)}, u32[]{:S(2)}, u32[]{:S(2)}) %collective-permute-start.27) | collective-permute-done | bytes 230432 | tf_op jit(solution)/shard_map/ppermute | solution.py:35
  277.4 3.0 collective-permute-start.24
  280.4 2.9 convert_add_fusion
  283.4 5.9 %collective-permute-done.28 = bf16[2,1,1,1,98,576]{5,4,3,2,1,0:T(8,128)(2,1)S(1)} collective-permute-done((bf16[2,1,1,1,98,576]{5,4,3,2,1,0:T(8,128)(2,1)S(1)}, bf16[2,1,1,1,98,576]{5,4,3,2,1,0:T(8,128)(2,1)S(1)}, u32[]{:S(2)}, u32[]{:S(2)}) %collective-permute-start.28) | collective-permute-done | bytes 225824 | tf_op jit(solution)/shard_map/ppermute | solution.py:35
  290.1 9.0 %collective-permute-done.24 = bf16[1,1,1,1,48,3456]{5,4,3,2,1,0:T(8,128)(2,1)S(1)} collective-permute-done((bf16[1,1,1,1,48,3456]{5,4,3,2,1,0:T(8,128)(2,1)S(1)}, bf16[1,1,1,1,48,3456]{5,4,3,2,1,0:T(8,128)(2,1)S(1)}, u32[]{:S(2)}, u32[]{:S(2)}) %collective-permute-start.24) | collective-permute-done | bytes 331808 | tf_op jit(solution)/shard_map/ppermute | solution.py:35
  299.0 1.6 collective-permute-done.29
  301.3 2.6 shard_map.444
  304.8 2.9 collective-permute-done.30
  309.3 2.7 collective-permute-done.31
  312.0 3.6 %collective-permute-done.32 = f32[1,384]{1,0:T(1,128)S(1)} collective-permute-done((f32[1,384]{1,0:T(1,128)S(1)}, f32[1,384]{1,0:T(1,128)S(1)}, u32[]{:S(2)}, u32[]{:S(2)}) %collective-permute-start.32) | collective-permute-done | bytes 1568 | tf_op jit(solution)/shard_map/ppermute | solution.py:35
  316.5 3.5 %collective-permute-done.33 = f32[1,384]{1,0:T(1,128)S(1)} collective-permute-done((f32[1,384]{1,0:T(1,128)S(1)}, f32[1,384]{1,0:T(1,128)S(1)}, u32[]{:S(2)}, u32[]{:S(2)}) %collective-permute-start.33) | collective-permute-done | bytes 1568 | tf_op jit(solution)/shard_map/ppermute | solution.py:35
  321.7 4.4 %shard_map.445 = (f32[3,48,384]{2,1,0:T(8,128)}, f32[3,48,384]{2,1,0:T(8,128)}, f32[3,48,384]{2,1,0:T(8,128)}, f32[48,384]{1,0:T(8,128)}, f32[48,384]{1,0:T(8,12...) custom-call(f32[1,128]{1,0:T(1,128)} %slice_add_fusion.refs_0_, ...), custom_call_target="tpu_custom_call" | custom-call | flops 5000000 | bytes 6000000 | tf_op jit(solution)/shard_map/pallas_call | solution.py:1248
  (268 shorter events, 54.8 us)
Async XLA Ops:
  0.7 8.0 %copy-start.32 = (f32[48,1536]{1,0:T(8,128)S(1)}, f32[48,1536]{1,0:T(8,128)}, u32[]{:S(2)}) copy-start(f32[48,1536]{1,0:T(8,128)} %refs_13_.1) | copy-start | bytes 884740
  0.7 8.0 %copy-start.36 = (f32[384,48]{0,1:T(8,128)S(1)}, f32[384,48]{0,1:T(8,128)}, u32[]{:S(2)}) copy-start(f32[384,48]{0,1:T(8,128)} %param.32) | copy-start | bytes 221188
  0.7 8.0 %copy-start.38 = (f32[6,33]{1,0:T(8,128)S(1)}, f32[6,33]{1,0:T(8,128)}, u32[]{:S(2)}) copy-start(f32[6,33]{1,0:T(8,128)} %refs_25_.1) | copy-start | bytes 2380
  3.6 10.5 %collective-permute-start = (bf16[1,1,1,1,97,576]{5,4,3,2,1,0:T(8,128)(2,1)S(1)}, bf16[1,1,1,1,97,576]{5,4,3,2,1,0:T(8,128)(2,1)S(1)}, u32[]{:S(2)}, u32[]{:S(2)}) collective-permute-start(bf16[1,1,1,1,97,576]{5,4,3,2,1,0:T(8,128)(2,1)S(1)} %get-tuple-element.185), channel_id=1, source_target_pairs={{0,16},{2,18},{4,20},{6,22},{8,24},{10,26},{12,28},{14,30},{16,0},... | collective-permute-start | bytes 335240 | tf_op jit(solution)/shard_map/ppermute | solution.py:35
  14.2 13.1 %collective-permute-start.1 = (bf16[2,1,1,1,97,576]{5,4,3,2,1,0:T(8,128)(2,1)S(1)}, bf16[2,1,1,1,97,576]{5,4,3,2,1,0:T(8,128)(2,1)S(1)}, u32[]{:S(2)}, u32[]{:S(2)}) collective-permute-start(bf16[2,1,1,1,97,576]{5,4,3,2,1,0:T(8,128)(2,1)S(1)} %maximum_select_fusion.13), channel_id=1, source_target_pairs={{0,8},{2,10},{4,12},{6,14},{8,0},{10,2},{12,4},{14,6},{16,24},{18,... | collective-permute-start | bytes 670472 | tf_op jit(solution)/shard_map/ppermute | solution.py:35
  14.9 18.2 %collective-permute-start.6 = (bf16[1,1,1,1,48,3456]{5,4,3,2,1,0:T(8,128)(2,1)S(1)}, bf16[1,1,1,1,48,3456]{5,4,3,2,1,0:T(8,128)(2,1)S(1)}, u32[]{:S(2)}, u32[]{:S(2)}) collective-permute-start(bf16[1,1,1,1,48,3456]{5,4,3,2,1,0:T(8,128)(2,1)S(1)} %bitcast.78), channel_id=1, source_target_pairs={{0,16},{2,18},{4,20},{6,22},{8,24},{10,26},{12,28},{14,30},{16,0},... | collective-permute-start | bytes 995336 | tf_op jit(solution)/shard_map/ppermute | solution.py:35
  27.5 8.5 %collective-permute-start.2 = (bf16[2,2,1,1,49,576]{5,4,3,2,1,0:T(8,128)(2,1)S(1)}, bf16[2,2,1,1,49,576]{5,4,3,2,1,0:T(8,128)(2,1)S(1)}, u32[]{:S(2)}, u32[]{:S(2)}) collective-permute-start(bf16[2,2,1,1,49,576]{5,4,3,2,1,0:T(8,128)(2,1)S(1)} %slice.243), channel_id=1, source_target_pairs={{0,2},{2,0},{4,6},{6,4},{8,10},{10,8},{12,14},{14,12},{16,18},{18,... | collective-permute-start | bytes 677384 | tf_op jit(solution)/shard_map/ppermute | solution.py:35
  28.8 6.2 %collective-permute-start.4 = (bf16[2,2,1,1,48,576]{5,4,3,2,1,0:T(8,128)(2,1)S(1)}, bf16[2,2,1,1,48,576]{5,4,3,2,1,0:T(8,128)(2,1)S(1)}, u32[]{:S(2)}, u32[]{:S(2)}) collective-permute-start(bf16[2,2,1,1,48,576]{5,4,3,2,1,0:T(8,128)(2,1)S(1)} %slice.245), channel_id=1, source_target_pairs={{0,4},{2,6},{4,0},{6,2},{8,12},{10,14},{12,8},{14,10},{16,20},{18,... | collective-permute-start | bytes 663560 | tf_op jit(solution)/shard_map/ppermute | solution.py:35
  33.3 17.5 %collective-permute-start.7 = (bf16[2,1,1,1,48,3456]{5,4,3,2,1,0:T(8,128)(2,1)S(1)}, bf16[2,1,1,1,48,3456]{5,4,3,2,1,0:T(8,128)(2,1)S(1)}, u32[]{:S(2)}, u32[]{:S(2)}) collective-permute-start(bf16[2,1,1,1,48,3456]{5,4,3,2,1,0:T(8,128)(2,1)S(1)} %maximum_select_fusion.8), channel_id=1, source_target_pairs={{0,8},{2,10},{4,12},{6,14},{8,0},{10,2},{12,4},{14,6},{16,24},{18,... | collective-permute-start | bytes 1990664 | tf_op jit(solution)/shard_map/ppermute | solution.py:35
  35.1 10.7 %collective-permute-start.5 = (bf16[2,2,2,1,48,576]{5,4,3,2,1,0:T(8,128)(2,1)S(1)}, bf16[2,2,2,1,48,576]{5,4,3,2,1,0:T(8,128)(2,1)S(1)}, u32[]{:S(2)}, u32[]{:S(2)}) collective-permute-start(bf16[2,2,2,1,48,576]{5,4,3,2,1,0:T(8,128)(2,1)S(1)} %maximum_select_fusion.11), channel_id=1, source_target_pairs={{0,2},{2,0},{4,6},{6,4},{8,10},{10,8},{12,14},{14,12},{16,18},{18,... | collective-permute-start | bytes 1327112 | tf_op jit(solution)/shard_map/ppermute | solution.py:35
  36.6 11.4 %collective-permute-start.3 = (bf16[2,2,1,2,49,576]{5,3,4,2,1,0:T(2,128)(2,1)S(1)}, bf16[2,2,1,2,49,576]{5,3,4,2,1,0:T(2,128)(2,1)S(1)}, u32[]{:S(2)}, u32[]{:S(2)}) collective-permute-start(bf16[2,2,1,2,49,576]{5,3,4,2,1,0:T(2,128)(2,1)S(1)} %copy.72), channel_id=1, source_target_pairs={{0,4},{2,6},{4,0},{6,2},{8,12},{10,14},{12,8},{14,10},{16,20},{18,... | collective-permute-start | bytes 1354760 | tf_op jit(solution)/shard_map/ppermute | solution.py:35
  51.1 18.1 %collective-permute-start.8 = (bf16[2,2,1,1,48,1920]{5,4,3,2,1,0:T(8,128)(2,1)S(1)}, bf16[2,2,1,1,48,1920]{5,4,3,2,1,0:T(8,128)(2,1)S(1)}, u32[]{:S(2)}, u32[]{:S(2)}) collective-permute-start(bf16[2,2,1,1,48,1920]{5,4,3,2,1,0:T(8,128)(2,1)S(1)} %slice.246), channel_id=1, source_target_pairs={{0,4},{2,6},{4,0},{6,2},{8,12},{10,14},{12,8},{14,10},{16,20},{18,... | collective-permute-start | bytes 2211848 | tf_op jit(solution)/shard_map/ppermute | solution.py:35
  52.7 15.8 %collective-permute-start.9 = (bf16[2,2,1,1,48,1536]{5,4,3,2,1,0:T(8,128)(2,1)S(1)}, bf16[2,2,1,1,48,1536]{5,4,3,2,1,0:T(8,128)(2,1)S(1)}, u32[]{:S(2)}, u32[]{:S(2)}) collective-permute-start(bf16[2,2,1,1,48,1536]{5,4,3,2,1,0:T(8,128)(2,1)S(1)} %slice.247), channel_id=1, source_target_pairs={{0,2},{2,0},{4,6},{6,4},{8,10},{10,8},{12,14},{14,12},{16,18},{18,... | collective-permute-start | bytes 1769480 | tf_op jit(solution)/shard_map/ppermute | solution.py:35
  53.3 7.9 %copy-start.5 = (s32[1,2]{1,0:T(1,128)S(1)}, s32[1,2]{1,0:T(1,128)}, u32[]{:S(2)}) copy-start(s32[1,2]{1,0:T(1,128)} %units_ref.7) | copy-start | bytes 28
  68.4 118.7 %copy-start.9 = (f32[6,128,128]{2,1,0:T(8,128)}, f32[6,128,128]{2,1,0:T(8,128)S(1)}, u32[]{:S(2)}) copy-start(f32[6,128,128]{2,1,0:T(8,128)S(1)} %get-tuple-element.108.middle_ref) | copy-start | bytes 1179652
  68.4 118.7 %copy-start.11 = (f32[6,128,64]{2,1,0:T(8,128)}, f32[6,128,64]{2,1,0:T(8,128)S(1)}, u32[]{:S(2)}) copy-start(f32[6,128,64]{2,1,0:T(8,128)S(1)} %get-tuple-element.109.values_ref) | copy-start | bytes 589828
  68.6 25.1 %collective-permute-start.10 = (bf16[2,2,1,2,48,1536]{5,4,3,2,1,0:T(8,128)(2,1)S(1)}, bf16[2,2,1,2,48,1536]{5,4,3,2,1,0:T(8,128)(2,1)S(1)}, u32[]{:S(2)}, u32[]{:S(2)}) collective-permute-start(bf16[2,2,1,2,48,1536]{5,4,3,2,1,0:T(8,128)(2,1)S(1)} %maximum_select_fusion.4), channel_id=1, source_target_pairs={{0,4},{2,6},{4,0},{6,2},{8,12},{10,14},{12,8},{14,10},{16,20},{18,... | collective-permute-start | bytes 3538952 | tf_op jit(solution)/shard_map/ppermute | solution.py:35
  69.8 31.4 %collective-permute-start.11 = (bf16[2,2,2,1,48,1920]{5,4,3,2,1,0:T(8,128)(2,1)S(1)}, bf16[2,2,2,1,48,1920]{5,4,3,2,1,0:T(8,128)(2,1)S(1)}, u32[]{:S(2)}, u32[]{:S(2)}) collective-permute-start(bf16[2,2,2,1,48,1920]{5,4,3,2,1,0:T(8,128)(2,1)S(1)} %maximum_select_fusion.2), channel_id=1, source_target_pairs={{0,2},{2,0},{4,6},{6,4},{8,10},{10,8},{12,14},{14,12},{16,18},{18,... | collective-permute-start | bytes 4423688 | tf_op jit(solution)/shard_map/ppermute | solution.py:35
  88.8 6.8 %copy-start.8 = (bf16[6,128,1536]{2,1,0:T(8,128)(2,1)}, bf16[6,128,1536]{2,1,0:T(8,128)(2,1)S(1)}, u32[]{:S(2)}) copy-start(bf16[6,128,1536]{2,1,0:T(8,128)(2,1)S(1)} %get-tuple-element.126.first_ref) | copy-start | bytes 7077892
  88.8 98.3 %copy-start.13 = (f32[6,128,64]{2,1,0:T(8,128)}, f32[6,128,64]{2,1,0:T(8,128)S(1)}, u32[]{:S(2)}) copy-start(f32[6,128,64]{2,1,0:T(8,128)S(1)} %get-tuple-element.130.weighted_ref) | copy-start | bytes 589828
  107.7 4.9 %collective-permute-start.12 = (bf16[1536,768]{1,0:T(8,128)(2,1)}, bf16[1536,768]{1,0:T(8,128)(2,1)}, u32[]{:S(2)}, u32[]{:S(2)}) collective-permute-start(bf16[1536,768]{1,0:T(8,128)(2,1)} %shard_map.435.own_ref), channel_id=1, source_target_pairs={{0,1},{1,0},{2,3},{3,2},{4,5},{5,4},{6,7},{7,6},{8,9},{9,8},{10,11... | collective-permute-start | bytes 7077896 | tf_op jit(solution)/shard_map/ppermute | solution.py:35
  128.0 4.8 %collective-permute-start.13 = (bf16[1536,768]{1,0:T(8,128)(2,1)}, bf16[1536,768]{1,0:T(8,128)(2,1)S(1)}, u32[]{:S(2)}, u32[]{:S(2)}) collective-permute-start(bf16[1536,768]{1,0:T(8,128)(2,1)} %get-tuple-element.113.own_ref), channel_id=1, source_target_pairs={{0,1},{1,0},{2,3},{3,2},{4,5},{5,4},{6,7},{7,6},{8,9},{9,8},{10,11... | collective-permute-start | bytes 7077896 | tf_op jit(solution)/shard_map/ppermute | solution.py:35
  166.3 7.3 %collective-permute-start.14 = (bf16[1536,768]{1,0:T(8,128)(2,1)}, bf16[1536,768]{1,0:T(8,128)(2,1)}, u32[]{:S(2)}, u32[]{:S(2)}) collective-permute-start(bf16[1536,768]{1,0:T(8,128)(2,1)} %get-tuple-element.117.own_ref), channel_id=1, source_target_pairs={{0,1},{1,0},{2,3},{3,2},{4,5},{5,4},{6,7},{7,6},{8,9},{9,8},{10,11... | collective-permute-start | bytes 7077896 | tf_op jit(solution)/shard_map/ppermute | solution.py:35
  170.5 35.2 %collective-permute-start.16 = (bf16[2,2,2,1,48,1536]{5,4,3,2,1,0:T(8,128)(2,1)}, bf16[2,2,2,1,48,1536]{5,4,3,2,1,0:T(8,128)(2,1)S(1)}, u32[]{:S(2)}, u32[]{:S(2)}) collective-permute-start(bf16[2,2,2,1,48,1536]{5,4,3,2,1,0:T(8,128)(2,1)} %constant_dynamic-slice_fusion.3), channel_id=1, source_target_pairs={{0,2},{2,0},{4,6},{6,4},{8,10},{10,8},{12,14},{14,12},{16,18},{18,... | collective-permute-start | bytes 3538952 | tf_op jit(solution)/shard_map/ppermute | solution.py:35
  172.6 41.0 %collective-permute-start.15 = (bf16[2,2,1,2,48,1536]{5,4,3,2,1,0:T(8,128)(2,1)}, bf16[2,2,1,2,48,1536]{5,4,3,2,1,0:T(8,128)(2,1)}, u32[]{:S(2)}, u32[]{:S(2)}) collective-permute-start(bf16[2,2,1,2,48,1536]{5,4,3,2,1,0:T(8,128)(2,1)} %constant_dynamic-slice_fusion.4), channel_id=1, source_target_pairs={{0,4},{2,6},{4,0},{6,2},{8,12},{10,14},{12,8},{14,10},{16,20},{18,... | collective-permute-start | bytes 3538952 | tf_op jit(solution)/shard_map/ppermute | solution.py:35
  173.6 8.5 %copy-start.4 = (bf16[384,1536]{1,0:T(8,128)(2,1)S(1)}, bf16[384,1536]{1,0:T(8,128)(2,1)}, u32[]{:S(2)}) copy-start(bf16[384,1536]{1,0:T(8,128)(2,1)} %copy-done.3) | copy-start | bytes 3538948
  186.1 37.2 %collective-permute-start.17 = (bf16[2,2,2,1,48,384]{5,4,3,2,1,0:T(8,128)(2,1)}, bf16[2,2,2,1,48,384]{5,4,3,2,1,0:T(8,128)(2,1)}, u32[]{:S(2)}, u32[]{:S(2)}) collective-permute-start(bf16[2,2,2,1,48,384]{5,4,3,2,1,0:T(8,128)(2,1)} %constant_dynamic-slice_fusion.2), channel_id=1, source_target_pairs={{0,2},{2,0},{4,6},{6,4},{8,10},{10,8},{12,14},{14,12},{16,18},{18,... | collective-permute-start | bytes 884744 | tf_op jit(solution)/shard_map/ppermute | solution.py:35
  187.1 18.5 %copy-start.39 = (f32[8,768]{1,0:T(8,128)S(1)}, f32[8,768]{1,0:T(8,128)}, u32[]{:S(2)}) copy-start(f32[8,768]{1,0:T(8,128)} %get-tuple-element.138) | copy-start | bytes 73732
  220.2 31.7 %collective-permute-start.21 = (bf16[2,2,1,2,48,576]{5,4,3,2,1,0:T(8,128)(2,1)}, bf16[2,2,1,2,48,576]{5,4,3,2,1,0:T(8,128)(2,1)}, u32[]{:S(2)}, u32[]{:S(2)}) collective-permute-start(bf16[2,2,1,2,48,576]{5,4,3,2,1,0:T(8,128)(2,1)} %constant_dynamic-slice_fusion.1), channel_id=1, source_target_pairs={{0,4},{2,6},{4,0},{6,2},{8,12},{10,14},{12,8},{14,10},{16,20},{18,... | collective-permute-start | bytes 1327112 | tf_op jit(solution)/shard_map/ppermute | solution.py:35
  221.3 32.9 %collective-permute-start.18 = (bf16[2,2,1,1,48,1536]{5,4,3,2,1,0:T(8,128)(2,1)}, bf16[2,2,1,1,48,1536]{5,4,3,2,1,0:T(8,128)(2,1)}, u32[]{:S(2)}, u32[]{:S(2)}) collective-permute-start(bf16[2,2,1,1,48,1536]{5,4,3,2,1,0:T(8,128)(2,1)} %dynamic-slice_convert_fusion), channel_id=1, source_target_pairs={{0,4},{2,6},{4,0},{6,2},{8,12},{10,14},{12,8},{14,10},{16,20},{18,... | collective-permute-start | bytes 1769480 | tf_op jit(solution)/shard_map/ppermute | solution.py:35
  222.2 33.4 %collective-permute-start.19 = (bf16[2,2,1,1,48,1536]{5,4,3,2,1,0:T(8,128)(2,1)}, bf16[2,2,1,1,48,1536]{5,4,3,2,1,0:T(8,128)(2,1)}, u32[]{:S(2)}, u32[]{:S(2)}) collective-permute-start(bf16[2,2,1,1,48,1536]{5,4,3,2,1,0:T(8,128)(2,1)} %dynamic-slice_convert_fusion.1), channel_id=1, source_target_pairs={{0,2},{2,0},{4,6},{6,4},{8,10},{10,8},{12,14},{14,12},{16,18},{18,... | collective-permute-start | bytes 1769480 | tf_op jit(solution)/shard_map/ppermute | solution.py:35
  224.4 17.5 %copy-start.26 = (f32[2,2,2,1,48,384]{5,4,3,2,1,0:T(8,128)}, f32[2,2,2,1,48,384]{5,4,3,2,1,0:T(8,128)S(1)}, u32[]{:S(2)}) copy-start(f32[2,2,2,1,48,384]{5,4,3,2,1,0:T(8,128)S(1)} %convert_add_fusion.9) | copy-start | bytes 1769476
  242.0 11.1 %collective-permute-start.20 = (bf16[2,2,1,1,48,384]{5,4,3,2,1,0:T(8,128)(2,1)S(1)}, bf16[2,2,1,1,48,384]{5,4,3,2,1,0:T(8,128)(2,1)S(1)}, u32[]{:S(2)}, u32[]{:S(2)}) collective-permute-start(bf16[2,2,1,1,48,384]{5,4,3,2,1,0:T(8,128)(2,1)S(1)} %dynamic-slice_convert_fusion.8), channel_id=1, source_target_pairs={{0,4},{2,6},{4,0},{6,2},{8,12},{10,14},{12,8},{14,10},{16,20},{18,... | collective-permute-start | bytes 442376 | tf_op jit(solution)/shard_map/ppermute | solution.py:35
  250.8 16.1 %collective-permute-start.26 = (bf16[2,2,2,1,50,576]{5,2,4,3,1,0:T(2,128)(2,1)S(1)}, bf16[2,2,2,1,50,576]{5,2,4,3,1,0:T(2,128)(2,1)S(1)}, u32[]{:S(2)}, u32[]{:S(2)}) collective-permute-start(bf16[2,2,2,1,50,576]{5,2,4,3,1,0:T(2,128)(2,1)S(1)} %copy.81), channel_id=1, source_target_pairs={{0,2},{2,0},{4,6},{6,4},{8,10},{10,8},{12,14},{14,12},{16,18},{18,... | collective-permute-start | bytes 1382408 | tf_op jit(solution)/shard_map/ppermute | solution.py:35
  253.1 15.0 %collective-permute-start.25 = (bf16[2,2,1,1,48,576]{5,4,3,2,1,0:T(8,128)(2,1)S(1)}, bf16[2,2,1,1,48,576]{5,4,3,2,1,0:T(8,128)(2,1)S(1)}, u32[]{:S(2)}, u32[]{:S(2)}) collective-permute-start(bf16[2,2,1,1,48,576]{5,4,3,2,1,0:T(8,128)(2,1)S(1)} %dynamic-slice_convert_fusion.5), channel_id=1, source_target_pairs={{0,2},{2,0},{4,6},{6,4},{8,10},{10,8},{12,14},{14,12},{16,18},{18,... | collective-permute-start | bytes 663560 | tf_op jit(solution)/shard_map/ppermute | solution.py:35
  257.4 19.2 %collective-permute-start.23 = (bf16[2,1,1,1,48,3456]{5,4,3,2,1,0:T(8,128)(2,1)S(1)}, bf16[2,1,1,1,48,3456]{5,4,3,2,1,0:T(8,128)(2,1)S(1)}, u32[]{:S(2)}, u32[]{:S(2)}) collective-permute-start(bf16[2,1,1,1,48,3456]{5,4,3,2,1,0:T(8,128)(2,1)S(1)} %pad_maximum_fusion.1), channel_id=1, source_target_pairs={{0,8},{2,10},{4,12},{6,14},{8,0},{10,2},{12,4},{14,6},{16,24},{18,... | collective-permute-start | bytes 1990664 | tf_op jit(solution)/shard_map/ppermute | solution.py:35
  266.9 13.5 %collective-permute-start.22 = (bf16[1536,768]{1,0:T(8,128)(2,1)}, bf16[1536,768]{1,0:T(8,128)(2,1)S(1)}, u32[]{:S(2)}, u32[]{:S(2)}) collective-permute-start(bf16[1536,768]{1,0:T(8,128)(2,1)} %shard_map.443), channel_id=1, source_target_pairs={{0,1},{1,0},{2,3},{3,2},{4,5},{5,4},{6,7},{7,6},{8,9},{9,8},{10,11... | collective-permute-start | bytes 7077896 | tf_op jit(solution)/shard_map/ppermute | solution.py:35
  267.1 9.3 %collective-permute-start.27 = (bf16[2,2,1,1,50,576]{5,4,3,2,1,0:T(8,128)(2,1)S(1)}, bf16[2,2,1,1,50,576]{5,4,3,2,1,0:T(8,128)(2,1)S(1)}, u32[]{:S(2)}, u32[]{:S(2)}) collective-permute-start(bf16[2,2,1,1,50,576]{5,4,3,2,1,0:T(8,128)(2,1)S(1)} %dynamic-slice_convert_fusion.4), channel_id=1, source_target_pairs={{0,4},{2,6},{4,0},{6,2},{8,12},{10,14},{12,8},{14,10},{16,20},{18,... | collective-permute-start | bytes 691208 | tf_op jit(solution)/shard_map/ppermute | solution.py:35
  276.5 12.7 %collective-permute-start.28 = (bf16[2,1,1,1,98,576]{5,4,3,2,1,0:T(8,128)(2,1)S(1)}, bf16[2,1,1,1,98,576]{5,4,3,2,1,0:T(8,128)(2,1)S(1)}, u32[]{:S(2)}, u32[]{:S(2)}) collective-permute-start(bf16[2,1,1,1,98,576]{5,4,3,2,1,0:T(8,128)(2,1)S(1)} %pad_maximum_fusion.4), channel_id=1, source_target_pairs={{0,8},{2,10},{4,12},{6,14},{8,0},{10,2},{12,4},{14,6},{16,24},{18,... | collective-permute-start | bytes 677384 | tf_op jit(solution)/shard_map/ppermute | solution.py:35
  277.4 21.6 %collective-permute-start.24 = (bf16[1,1,1,1,48,3456]{5,4,3,2,1,0:T(8,128)(2,1)S(1)}, bf16[1,1,1,1,48,3456]{5,4,3,2,1,0:T(8,128)(2,1)S(1)}, u32[]{:S(2)}, u32[]{:S(2)}) collective-permute-start(bf16[1,1,1,1,48,3456]{5,4,3,2,1,0:T(8,128)(2,1)S(1)} %pad_maximum_fusion.3), channel_id=1, source_target_pairs={{0,16},{2,18},{4,20},{6,22},{8,24},{10,26},{12,28},{14,30},{16,0},... | collective-permute-start | bytes 995336 | tf_op jit(solution)/shard_map/ppermute | solution.py:35
  289.3 11.4 %copy-start.28 = (f32[2,1,1,1,50,576]{5,4,3,2,1,0:T(8,128)}, f32[2,1,1,1,50,576]{5,4,3,2,1,0:T(8,128)S(1)}, u32[]{:S(2)}) copy-start(f32[2,1,1,1,50,576]{5,4,3,2,1,0:T(8,128)S(1)} %convert_add_fusion.13) | copy-start | bytes 691204
  289.3 11.4 %copy-start.29 = (f32[2,1,1,1,48,576]{5,4,3,2,1,0:T(8,128)}, f32[2,1,1,1,48,576]{5,4,3,2,1,0:T(8,128)S(1)}, u32[]{:S(2)}) copy-start(f32[2,1,1,1,48,576]{5,4,3,2,1,0:T(8,128)S(1)} %convert_add_fusion.14) | copy-start | bytes 663556
  289.4 11.3 %collective-permute-start.29 = (bf16[1,1,1,1,98,576]{5,4,3,2,1,0:T(8,128)(2,1)S(1)}, bf16[1,1,1,1,98,576]{5,4,3,2,1,0:T(8,128)(2,1)S(1)}, u32[]{:S(2)}, u32[]{:S(2)}) collective-permute-start(bf16[1,1,1,1,98,576]{5,4,3,2,1,0:T(8,128)(2,1)S(1)} %pad_maximum_fusion.6), channel_id=1, source_target_pairs={{0,16},{2,18},{4,20},{6,22},{8,24},{10,26},{12,28},{14,30},{16,0},... | collective-permute-start | bytes 338696 | tf_op jit(solution)/shard_map/ppermute | solution.py:35
  303.9 3.8 %collective-permute-start.30 = (f32[1,384]{1,0:T(1,128)}, f32[1,384]{1,0:T(1,128)S(1)}, u32[]{:S(2)}, u32[]{:S(2)}) collective-permute-start(f32[1,384]{1,0:T(1,128)} %get-tuple-element.151), channel_id=1, source_target_pairs={{0,2},{2,0},{4,6},{6,4},{8,10},{10,8},{12,14},{14,12},{16,18},{18,... | collective-permute-start | bytes 4616 | tf_op jit(solution)/shard_map/ppermute | solution.py:35
  308.4 3.6 %collective-permute-start.31 = (f32[1,384]{1,0:T(1,128)S(1)}, f32[1,384]{1,0:T(1,128)S(1)}, u32[]{:S(2)}, u32[]{:S(2)}) collective-permute-start(f32[1,384]{1,0:T(1,128)S(1)} %add.158), channel_id=1, source_target_pairs={{0,4},{2,6},{4,0},{6,2},{8,12},{10,14},{12,8},{14,10},{16,20},{18,... | collective-permute-start | bytes 4616 | tf_op jit(solution)/shard_map/ppermute | solution.py:35
  312.0 3.6 %collective-permute-start.32 = (f32[1,384]{1,0:T(1,128)S(1)}, f32[1,384]{1,0:T(1,128)S(1)}, u32[]{:S(2)}, u32[]{:S(2)}) collective-permute-start(f32[1,384]{1,0:T(1,128)S(1)} %add.159), channel_id=1, source_target_pairs={{0,8},{2,10},{4,12},{6,14},{8,0},{10,2},{12,4},{14,6},{16,24},{18,... | collective-permute-start | bytes 4616 | tf_op jit(solution)/shard_map/ppermute | solution.py:35
  315.5 4.5 %collective-permute-start.33 = (f32[1,384]{1,0:T(1,128)S(1)}, f32[1,384]{1,0:T(1,128)S(1)}, u32[]{:S(2)}, u32[]{:S(2)}) collective-permute-start(f32[1,384]{1,0:T(1,128)S(1)} %add.160), channel_id=1, source_target_pairs={{0,16},{2,18},{4,20},{6,22},{8,24},{10,26},{12,28},{14,30},{16,0},... | collective-permute-start | bytes 4616 | tf_op jit(solution)/shard_map/ppermute | solution.py:35
  320.0 1.2 collective-permute-start.34
  (31 other events, 108.1 us)

commit v5 on v4

--- a/solution.py
+++ b/solution.py
@@ -130,8 +130,16 @@
 
 
 def sum_all(array, axis, count):
-    for bit in range(bits_of(count)):
-        array = array + swap(array, axis, count, bit)
+    bits = list(range(bits_of(count)))
+    while bits:
+        group, bits = bits[:2], bits[2:]
+        near = array + swap(array, axis, count, group[0])
+        if len(group) == 1:
+            array = near
+            continue
+        masks = (1 << group[1], (1 << group[0]) | (1 << group[1]))
+        far = [lax.ppermute(array, axis, [(i, i ^ mask) for i in range(count)]) for mask in masks]
+        array = near + (far[0] + far[1])
     return array
 
 
@@ -1207,12 +1215,13 @@
 
 def update_body(*refs, width, bias_share, shard_rows):
     totals_ref, kernel_ref, expand_ref, reduce_ref, mixing_ref, left_ref, right_ref = refs[:7]
-    old_refs, new_refs, row_ref = refs[7:28], refs[28:49], refs[49]
+    old_refs, new_refs, norm_ref, mean_ref = refs[7:28], refs[28:49], refs[49], refs[50]
     rows = left_ref.shape[0]
     totals = totals_ref[...]
     lane = lax.broadcasted_iota(jnp.int32, totals.shape, 1)
     means = jnp.sqrt(totals / jnp.where(lane == 0, 1.0, totals[:, 3:4] * width))
-    row_ref[...] = means
+    norm_ref[...] = means[:, 0:1]
+    mean_ref[...] = means[:, 1:3]
     factor = CLIP_NORM / (means[:, 0:1] + CLIP_EPS)
 
     def put(index, place, gradient, rate, decay):
@@ -1244,7 +1253,7 @@
 
 def update(totals, kernel_row, shares, olds, width, bias_share, shard_rows):
     arrays = [totals, kernel_row] + shares + olds
-    shapes = [old.shape for old in olds] + [(1, 128)]
+    shapes = [old.shape for old in olds] + [(1, 1), (1, 2)]
     return pl.pallas_call(
         functools.partial(update_body, width=width, bias_share=bias_share, shard_rows=shard_rows),
         in_specs=whole(len(arrays)),
@@ -1481,10 +1490,10 @@
         kernel_moment,
         kernel_square,
     ]
-    *news, row = update(totals, final_row, shares, olds, width_full, bias_share, shard_rows)
+    *news, norm, means = update(totals, final_row, shares, olds, width_full, bias_share, shard_rows)
     for index in (3, 4, 5, 9, 10, 11):
         news[index] = news[index].T
-    return (output_rows, input_grad, *news, row[0, 0], row[0, 1:3])
+    return (output_rows, input_grad, *news, norm.reshape(()), means.reshape(2))
 
 
 def solution(mesh):

time: 332 us -> 330 us (level)
  waiting for transfers between devices: 81.1 us -> 75.4 us
  starting transfers between devices: 36.4 us -> 41.5 us
    ppermute x35 -> x33, waiting for transfers between devices: 81.1 us -> 68.7 us  [swap(): return lax.ppermute(array, axis, [(i, i ^ 1 << bit) for i in range(count)])]
    ppermute x0 -> x4, starting transfers between devices: none -> 6.97 us  [sum_all(): lax.ppermute(array, axis, [(i, i ^ mask) for i in range(count)])]
    ppermute x0 -> x4, waiting for transfers between devices: none -> 6.64 us  [sum_all(): lax.ppermute(array, axis, [(i, i ^ mask) for i in range(count)])]
    ppermute x35 -> x33, starting transfers between devices: 36.4 us -> 34.6 us  [swap(): return lax.ppermute(array, axis, [(i, i ^ 1 << bit) for i in range(count)])]
  transfers between devices with their start and end apart: 35 -> 37, of which waited for: 20 -> 21; matrix products, arithmetic and copies ran while one was open for 12% -> 12% of each run, Pallas kernels for 29% -> 29%
where the time goes in v5:
time: 330 us; the launch traced here: 326 us
  Pallas kernels  153 us (46%)
  waiting for transfers between devices  75.4 us (23%)
  starting transfers between devices  41.5 us (13%)
  other arithmetic  25.4 us (8%)
  local copies, waits for them, and re-layouts  24.3 us (7%)
    ppermute x33, waiting for transfers between devices, swap(): return lax.ppermute(array, axis, [(i, i ^ 1 << bit) for i in range(count)])  68.7 us
    pallas_call x2, Pallas kernels, attention_backward(): pl.pallas_call(attention_backward_body, grid=(1,), in_specs=[pl.BlockSpec...  34.7 us
    ppermute x33, starting transfers between devices, swap(): return lax.ppermute(array, axis, [(i, i ^ 1 << bit) for i in range(count)])  34.6 us
    pallas_call x1, Pallas kernels, hidden_backward(): pl.pallas_call(hidden_backward_body, grid=(row_count // ROWS,), in_specs=...  32 us
    pallas_call x1, Pallas kernels, attention_finish(): pl.pallas_call(attention_finish_body, in_specs=[pl.BlockSpec(memory_space...  17.6 us
    pallas_call x1, Pallas kernels, hidden_forward(): pl.pallas_call(hidden_forward_body, grid=(row_count // ROWS,), in_specs=[...  15.4 us
    pallas_call x2, Pallas kernels, turned_dot(): pl.pallas_call(turned_dot_body, grid=(row_count // LONG_ROWS,), in_specs=...  11.9 us
    pallas_call x2, Pallas kernels, turned_outer(): pl.pallas_call(turned_outer_body, grid=(width // OUTER,), in_specs=[fixed...  10.5 us
  transfers between devices with their start and end apart: 37, of which 21 were waited for; matrix products, arithmetic and copies ran while one was open for 12% of the time, Pallas kernels for 29%

profile of v5, /device:TPU:0, one launch (start us, length us, event | category | flops | bytes accessed | tf_op | source)
XLA Modules:
  0.0 325.8 jit_solution(16616412738212095863)
XLA Ops:
  3.6 4.1 %collective-permute-start = (bf16[1,1,1,1,97,576]{5,4,3,2,1,0:T(8,128)(2,1)S(1)}, bf16[1,1,1,1,97,576]{5,4,3,2,1,0:T(8,128)(2,1)S(1)}, u32[]{:S(2)}, u32[]{:S(2)}) collective-permute-start(bf16[1,1,1,1,97,576]{5,4,3,2,1,0:T(8,128)(2,1)S(1)} %get-tuple-element.187), channel_id=1, source_target_pairs={{0,16},{2,18},{4,20},{6,22},{8,24},{10,26},{12,28},{14,30},{16,0},... | collective-permute-start | bytes 335240 | tf_op jit(solution)/shard_map/ppermute | solution.py:35
  9.1 4.9 %collective-permute-done = bf16[1,1,1,1,97,576]{5,4,3,2,1,0:T(8,128)(2,1)S(1)} collective-permute-done((bf16[1,1,1,1,97,576]{5,4,3,2,1,0:T(8,128)(2,1)S(1)}, bf16[1,1,1,1,97,576]{5,4,3,2,1,0:T(8,128)(2,1)S(1)}, u32[]{:S(2)}, u32[]{:S(2)}) %collective-permute-start) | collective-permute-done | bytes 111776 | tf_op jit(solution)/shard_map/ppermute | solution.py:35
  14.9 3.4 %collective-permute-start.6 = (bf16[1,1,1,1,48,3456]{5,4,3,2,1,0:T(8,128)(2,1)S(1)}, bf16[1,1,1,1,48,3456]{5,4,3,2,1,0:T(8,128)(2,1)S(1)}, u32[]{:S(2)}, u32[]{:S(2)}) collective-permute-start(bf16[1,1,1,1,48,3456]{5,4,3,2,1,0:T(8,128)(2,1)S(1)} %bitcast.76), channel_id=1, source_target_pairs={{0,16},{2,18},{4,20},{6,22},{8,24},{10,26},{12,28},{14,30},{16,0},... | collective-permute-start | bytes 995336 | tf_op jit(solution)/shard_map/ppermute | solution.py:35
  18.7 8.5 %collective-permute-done.1 = bf16[2,1,1,1,97,576]{5,4,3,2,1,0:T(8,128)(2,1)S(1)} collective-permute-done((bf16[2,1,1,1,97,576]{5,4,3,2,1,0:T(8,128)(2,1)S(1)}, bf16[2,1,1,1,97,576]{5,4,3,2,1,0:T(8,128)(2,1)S(1)}, u32[]{:S(2)}, u32[]{:S(2)}) %collective-permute-start.1) | collective-permute-done | bytes 223520 | tf_op jit(solution)/shard_map/ppermute | solution.py:35
  28.8 1.5 collective-permute-start.4
  30.3 2.8 collective-permute-done.6
  33.4 1.6 collective-permute-done.4
  38.0 7.8 %collective-permute-done.5 = bf16[2,2,2,1,48,576]{5,4,3,2,1,0:T(8,128)(2,1)S(1)} collective-permute-done((bf16[2,2,2,1,48,576]{5,4,3,2,1,0:T(8,128)(2,1)S(1)}, bf16[2,2,2,1,48,576]{5,4,3,2,1,0:T(8,128)(2,1)S(1)}, u32[]{:S(2)}, u32[]{:S(2)}) %collective-permute-start.5) | collective-permute-done | bytes 442400 | tf_op jit(solution)/shard_map/ppermute | solution.py:35
  51.1 1.6 collective-permute-start.8
  53.3 7.9 %shard_map.432.proj_ref = bf16[2,3,192,1536]{3,2,1,0:T(8,128)(2,1)} custom-call(bf16[768,576]{1,0:T(8,128)(2,1)} %bitcast.94, bf16[768,576]{1,0:T(8,128)(2,1)} %bitcast.92, bf16[1536,768]{1,0:T(8,128)(2,1)} %right_ref.3, f32[1152,1]{1,0:T(8,128)} %broadcast_in_dim.75.bias_ref), custom_call_target="tpu_custom_call" | custom-call | flops 2717908992 | bytes 8000000 | tf_op jit(solution)/shard_map/pallas_call | solution.py:1110
  61.2 7.3 %shard_map.433 = (f32[2,384,128]{2,1,0:T(8,128)S(1)}, f32[6,128,128]{2,1,0:T(8,128)S(1)}, bf16[6,128,1536]{2,1,0:T(8,128)(2,1)S(1)}, f32[6,128,64]{2,1,0:T(8,128)S(1)}, f32[6,128,128]{2,1,0:T(8,128)S(1)}) custom-call(s32[1,2]{1,0:T(1,128)S(1)} %copy-done.5, bf16[2,3,192,1536]{3,2,1,0:T(8,128)(2,1)} %shard_map.432.proj_ref), custom_call_target="tpu_custom_call" | custom-call | flops 8999999488 | bytes 8000000 | tf_op jit(solution)/shard_map/pallas_call | solution.py:423
  69.9 1.4 collective-permute-start.11
  71.4 17.6 %shard_map.434 = (bf16[384,1536]{1,0:T(8,128)(2,1)S(1)}, bf16[6,128,1536]{2,1,0:T(8,128)(2,1)S(1)}, bf16[4,4,6,128,128]{4,3,2,1,0:T(8,128)(2,1)}, f32[2,4,6,128,128]{4,3,2,1,0:T(8,128)}, f32[6,128,64]{2,1,0:T(8,128)S(1)}) custom-call(s32[1,2]{1,0:T(1,128)S(1)} %copy-done.5, bf16[2,3,192,1536]{3,2,1,0:T(8,128)(2,1)} %shard_map.432.proj_ref, ...), custom_call_target="tpu_custom_call" | custom-call | flops 17999998976 | bytes 16000000 | tf_op jit(solution)/shard_map/pallas_call | solution.py:449
  88.9 4.8 %collective-permute-done.10 = bf16[2,2,1,2,48,1536]{5,4,3,2,1,0:T(8,128)(2,1)S(1)} collective-permute-done((bf16[2,2,1,2,48,1536]{5,4,3,2,1,0:T(8,128)(2,1)S(1)}, bf16[2,2,1,2,48,1536]{5,4,3,2,1,0:T(8,128)(2,1)S(1)}, u32[]{:S(2)}, u32[]{:S(2)}) %collective-permute-start.10) | collective-permute-done | bytes 1179680 | tf_op jit(solution)/shard_map/ppermute | solution.py:35
  93.8 1.9 maximum_select_fusion.1
  95.7 5.6 %collective-permute-done.11 = bf16[2,2,2,1,48,1920]{5,4,3,2,1,0:T(8,128)(2,1)S(1)} collective-permute-done((bf16[2,2,2,1,48,1920]{5,4,3,2,1,0:T(8,128)(2,1)S(1)}, bf16[2,2,2,1,48,1920]{5,4,3,2,1,0:T(8,128)(2,1)S(1)}, u32[]{:S(2)}, u32[]{:S(2)}) %collective-permute-start.11) | collective-permute-done | bytes 1474592 | tf_op jit(solution)/shard_map/ppermute | solution.py:35
  101.3 1.9 maximum_select_fusion
  103.2 4.6 %shard_map.435.own_ref = bf16[1536,768]{1,0:T(8,128)(2,1)} custom-call(bf16[384,1536]{1,0:T(8,128)(2,1)} %copy-done.3, bf16[768,1920]{1,0:T(8,128)(2,1)} %bitcast.67), custom_call_target="tpu_custom_call" | custom-call | flops 905969664 | bytes 8000000 | tf_op jit(solution)/shard_map/pallas_call | solution.py:1062
  112.6 15.4 %shard_map.436 = (bf16[1536,768]{1,0:T(8,128)(2,1)}, bf16[1536,768]{1,0:T(8,128)(2,1)}, bf16[1536,768]{1,0:T(8,128)(2,1)}, f32[1,1536]{1,0:T(1,128)}, bf16[1536,1536]{1,0:T(8,128)(2,1)}, /*index=5*/f32[1,768]{1,0:T(1,128)}) custom-call(bf16[1536,768]{1,0:T(8,128)(2,1)} %shard_map.435.own_ref, bf16[1536,768]{1,0:T(8,128)(2,1)} %collective-permute-done.12.other_ref, ...), custom_call_target="tpu_custom_call" | custom-call | flops 7247757312 | bytes 30000000 | tf_op jit(solution)/shard_map/pallas_call | solution.py:826
  128.3 4.6 %collective-permute-done.13.other_ref = bf16[1536,768]{1,0:T(8,128)(2,1)S(1)} collective-permute-done((bf16[1536,768]{1,0:T(8,128)(2,1)}, bf16[1536,768]{1,0:T(8,128)(2,1)S(1)}, u32[]{:S(2)}, u32[]{:S(2)}) %collective-permute-start.13) | collective-permute-done | bytes 2359328 | tf_op jit(solution)/shard_map/ppermute | solution.py:35
  132.9 1.4 copy-done.43
  134.3 32.0 %shard_map.437 = (f32[1536,768]{1,0:T(8,128)}, bf16[1536,768]{1,0:T(8,128)(2,1)}, bf16[768,1536]{1,0:T(8,128)(2,1)}, bf16[768,1536]{1,0:T(8,128)(2,1)}, bf16[153...) custom-call(bf16[1536,768]{1,0:T(8,128)(2,1)} %get-tuple-element.114.own_ref, ...), custom_call_target="tpu_custom_call" | custom-call | flops 7247757312 | bytes 30000000 | tf_op jit(solution)/shard_map/pallas_call | solution.py:936
  168.2 2.4 constant_dynamic-slice_fusion.3
  173.7 8.4 %shard_map.438 = (bf16[1536,768]{1,0:T(8,128)(2,1)}, bf16[384,1536]{1,0:T(8,128)(2,1)}, f32[8,768]{1,0:T(8,128)}) custom-call(bf16[1536,768]{1,0:T(8,128)(2,1)} %get-tuple-element.118.own_ref, bf16[1536,768]{1,0:T(8,128)(2,1)} %collective-permute-done.14.other_ref, bf16[1536,768]{1,0:T(8,128)(2,1)} %get-tuple-element.119.d_two_ref, ...), custom_call_target="tpu_custom_call" | custom-call | flops 905969664 | bytes 14000000 | tf_op jit(solution)/shard_map/pallas_call | solution.py:1012
  182.1 3.2 convolution_convert_fusion
  187.2 17.3 %shard_map.439 = (bf16[576,1536]{1,0:T(8,128)(2,1)S(1)}, f32[3,256]{1,0:T(4,128)S(1)}) custom-call(s32[1,2]{1,0:T(1,128)S(1)} %copy-done.5, bf16[2,3,192,1536]{3,2,1,0:T(8,128)(2,1)} %shard_map.432.proj_ref, f32[3,256]{1,0:T(4,128)S(1)} %get-tuple-element.199.taps_ref, bf16[384,1536]{1,0:T(8,128)(2,1)S(1)} %copy-done.6, bf16[6,128,1536]{2,1,0:T(8,128)(2,1)} %copy-done.8, ...), custom_call_target="tpu_custom_call" | custom-call | flops 15000000512 | bytes 10000000 | tf_op jit(solution)/shard_map/pallas_call | solution.py:675
  206.8 5.5 %shard_map.440 = bf16[768,576]{1,0:T(8,128)(2,1)} custom-call(bf16[576,1536]{1,0:T(8,128)(2,1)} %copy-done, bf16[1536,768]{1,0:T(8,128)(2,1)} %right_ref.3), custom_call_target="tpu_custom_call" | custom-call | flops 1358954496 | bytes 6000000 | tf_op jit(solution)/shard_map/pallas_call | solution.py:1079
  213.6 1.7 convert_add_fusion.2
  215.4 1.4 copy-done.17
  218.2 2.0 constant_dynamic-slice_fusion.1
  224.4 17.4 %shard_map.441 = (bf16[576,1536]{1,0:T(8,128)(2,1)S(1)}, f32[3,256]{1,0:T(4,128)S(1)}) custom-call(s32[1,2]{1,0:T(1,128)S(1)} %copy-done.5, bf16[2,3,192,1536]{3,2,1,0:T(8,128)(2,1)} %shard_map.432.proj_ref, f32[3,256]{1,0:T(4,128)S(1)} %get-tuple-element.198.taps_ref, bf16[384,1536]{1,0:T(8,128)(2,1)S(1)} %copy-done.6, bf16[6,128,1536]{2,1,0:T(8,128)(2,1)} %copy-done.8, ...), custom_call_target="tpu_custom_call" | custom-call | flops 15000000512 | bytes 10000000 | tf_op jit(solution)/shard_map/pallas_call | solution.py:675
  243.9 5.0 %shard_map.442 = bf16[768,576]{1,0:T(8,128)(2,1)} custom-call(bf16[576,1536]{1,0:T(8,128)(2,1)} %copy-done.2, bf16[1536,768]{1,0:T(8,128)(2,1)} %right_ref.3), custom_call_target="tpu_custom_call" | custom-call | flops 1358954496 | bytes 6000000 | tf_op jit(solution)/shard_map/pallas_call | solution.py:1079
  249.0 1.4 pad_maximum_fusion
  257.4 2.2 collective-permute-start.23
  259.6 7.3 %shard_map.443 = bf16[1536,768]{1,0:T(8,128)(2,1)} custom-call(bf16[576,1536]{1,0:T(8,128)(2,1)} %copy-done, bf16[768,576]{1,0:T(8,128)(2,1)} %bitcast.95, bf16[576,1536]{1,0:T(8,128)(2,1)} %copy-done.2, bf16[768,576]{1,0:T(8,128)(2,1)} %bitcast.93), custom_call_target="tpu_custom_call" | custom-call | flops 2717908992 | bytes 8000000 | tf_op jit(solution)/shard_map/pallas_call | solution.py:1062
  268.2 8.2 %collective-permute-done.27 = bf16[2,2,1,1,50,576]{5,4,3,2,1,0:T(8,128)(2,1)S(1)} collective-permute-done((bf16[2,2,1,1,50,576]{5,4,3,2,1,0:T(8,128)(2,1)S(1)}, bf16[2,2,1,1,50,576]{5,4,3,2,1,0:T(8,128)(2,1)S(1)}, u32[]{:S(2)}, u32[]{:S(2)}) %collective-permute-start.27) | collective-permute-done | bytes 230432 | tf_op jit(solution)/shard_map/ppermute | solution.py:35
  277.4 3.0 collective-permute-start.24
  280.4 2.9 convert_add_fusion
  283.4 5.9 %collective-permute-done.28 = bf16[2,1,1,1,98,576]{5,4,3,2,1,0:T(8,128)(2,1)S(1)} collective-permute-done((bf16[2,1,1,1,98,576]{5,4,3,2,1,0:T(8,128)(2,1)S(1)}, bf16[2,1,1,1,98,576]{5,4,3,2,1,0:T(8,128)(2,1)S(1)}, u32[]{:S(2)}, u32[]{:S(2)}) %collective-permute-start.28) | collective-permute-done | bytes 225824 | tf_op jit(solution)/shard_map/ppermute | solution.py:35
  290.1 9.0 %collective-permute-done.24 = bf16[1,1,1,1,48,3456]{5,4,3,2,1,0:T(8,128)(2,1)S(1)} collective-permute-done((bf16[1,1,1,1,48,3456]{5,4,3,2,1,0:T(8,128)(2,1)S(1)}, bf16[1,1,1,1,48,3456]{5,4,3,2,1,0:T(8,128)(2,1)S(1)}, u32[]{:S(2)}, u32[]{:S(2)}) %collective-permute-start.24) | collective-permute-done | bytes 331808 | tf_op jit(solution)/shard_map/ppermute | solution.py:35
  299.1 1.6 collective-permute-done.29
  301.4 2.6 shard_map.444
  305.7 1.7 collective-permute-start.32
  308.6 1.8 collective-permute-done.32
  311.1 2.9 collective-permute-start.34
  314.1 1.4 collective-permute-start.35
  315.6 3.8 %collective-permute-done.35 = f32[1,384]{1,0:T(1,128)S(1)} collective-permute-done((f32[1,384]{1,0:T(1,128)S(1)}, f32[1,384]{1,0:T(1,128)S(1)}, u32[]{:S(2)}, u32[]{:S(2)}) %collective-permute-start.35) | collective-permute-done | bytes 1568 | tf_op jit(solution)/shard_map/ppermute | solution.py:141
  321.2 4.4 %shard_map.445 = (f32[3,48,384]{2,1,0:T(8,128)}, f32[3,48,384]{2,1,0:T(8,128)}, f32[3,48,384]{2,1,0:T(8,128)}, f32[48,384]{1,0:T(8,128)}, f32[48,384]{1,0:T(8,12...) custom-call(f32[1,128]{1,0:T(1,128)} %slice_add_fusion.refs_0_, ...), custom_call_target="tpu_custom_call" | custom-call | flops 5000000 | bytes 6000000 | tf_op jit(solution)/shard_map/pallas_call | solution.py:1257
  (269 shorter events, 55.3 us)
Async XLA Ops:
  0.7 8.0 %copy-start.32 = (f32[48,1536]{1,0:T(8,128)S(1)}, f32[48,1536]{1,0:T(8,128)}, u32[]{:S(2)}) copy-start(f32[48,1536]{1,0:T(8,128)} %refs_13_.1) | copy-start | bytes 884740
  0.7 8.0 %copy-start.36 = (f32[384,48]{0,1:T(8,128)S(1)}, f32[384,48]{0,1:T(8,128)}, u32[]{:S(2)}) copy-start(f32[384,48]{0,1:T(8,128)} %param.32) | copy-start | bytes 221188
  0.7 8.0 %copy-start.38 = (f32[6,33]{1,0:T(8,128)S(1)}, f32[6,33]{1,0:T(8,128)}, u32[]{:S(2)}) copy-start(f32[6,33]{1,0:T(8,128)} %refs_25_.1) | copy-start | bytes 2380
  3.6 10.5 %collective-permute-start = (bf16[1,1,1,1,97,576]{5,4,3,2,1,0:T(8,128)(2,1)S(1)}, bf16[1,1,1,1,97,576]{5,4,3,2,1,0:T(8,128)(2,1)S(1)}, u32[]{:S(2)}, u32[]{:S(2)}) collective-permute-start(bf16[1,1,1,1,97,576]{5,4,3,2,1,0:T(8,128)(2,1)S(1)} %get-tuple-element.187), channel_id=1, source_target_pairs={{0,16},{2,18},{4,20},{6,22},{8,24},{10,26},{12,28},{14,30},{16,0},... | collective-permute-start | bytes 335240 | tf_op jit(solution)/shard_map/ppermute | solution.py:35
  14.2 13.1 %collective-permute-start.1 = (bf16[2,1,1,1,97,576]{5,4,3,2,1,0:T(8,128)(2,1)S(1)}, bf16[2,1,1,1,97,576]{5,4,3,2,1,0:T(8,128)(2,1)S(1)}, u32[]{:S(2)}, u32[]{:S(2)}) collective-permute-start(bf16[2,1,1,1,97,576]{5,4,3,2,1,0:T(8,128)(2,1)S(1)} %maximum_select_fusion.13), channel_id=1, source_target_pairs={{0,8},{2,10},{4,12},{6,14},{8,0},{10,2},{12,4},{14,6},{16,24},{18,... | collective-permute-start | bytes 670472 | tf_op jit(solution)/shard_map/ppermute | solution.py:35
  14.9 18.2 %collective-permute-start.6 = (bf16[1,1,1,1,48,3456]{5,4,3,2,1,0:T(8,128)(2,1)S(1)}, bf16[1,1,1,1,48,3456]{5,4,3,2,1,0:T(8,128)(2,1)S(1)}, u32[]{:S(2)}, u32[]{:S(2)}) collective-permute-start(bf16[1,1,1,1,48,3456]{5,4,3,2,1,0:T(8,128)(2,1)S(1)} %bitcast.76), channel_id=1, source_target_pairs={{0,16},{2,18},{4,20},{6,22},{8,24},{10,26},{12,28},{14,30},{16,0},... | collective-permute-start | bytes 995336 | tf_op jit(solution)/shard_map/ppermute | solution.py:35
  27.5 8.5 %collective-permute-start.2 = (bf16[2,2,1,1,49,576]{5,4,3,2,1,0:T(8,128)(2,1)S(1)}, bf16[2,2,1,1,49,576]{5,4,3,2,1,0:T(8,128)(2,1)S(1)}, u32[]{:S(2)}, u32[]{:S(2)}) collective-permute-start(bf16[2,2,1,1,49,576]{5,4,3,2,1,0:T(8,128)(2,1)S(1)} %slice.235), channel_id=1, source_target_pairs={{0,2},{2,0},{4,6},{6,4},{8,10},{10,8},{12,14},{14,12},{16,18},{18,... | collective-permute-start | bytes 677384 | tf_op jit(solution)/shard_map/ppermute | solution.py:35
  28.8 6.2 %collective-permute-start.4 = (bf16[2,2,1,1,48,576]{5,4,3,2,1,0:T(8,128)(2,1)S(1)}, bf16[2,2,1,1,48,576]{5,4,3,2,1,0:T(8,128)(2,1)S(1)}, u32[]{:S(2)}, u32[]{:S(2)}) collective-permute-start(bf16[2,2,1,1,48,576]{5,4,3,2,1,0:T(8,128)(2,1)S(1)} %slice.237), channel_id=1, source_target_pairs={{0,4},{2,6},{4,0},{6,2},{8,12},{10,14},{12,8},{14,10},{16,20},{18,... | collective-permute-start | bytes 663560 | tf_op jit(solution)/shard_map/ppermute | solution.py:35
  33.3 17.5 %collective-permute-start.7 = (bf16[2,1,1,1,48,3456]{5,4,3,2,1,0:T(8,128)(2,1)S(1)}, bf16[2,1,1,1,48,3456]{5,4,3,2,1,0:T(8,128)(2,1)S(1)}, u32[]{:S(2)}, u32[]{:S(2)}) collective-permute-start(bf16[2,1,1,1,48,3456]{5,4,3,2,1,0:T(8,128)(2,1)S(1)} %maximum_select_fusion.8), channel_id=1, source_target_pairs={{0,8},{2,10},{4,12},{6,14},{8,0},{10,2},{12,4},{14,6},{16,24},{18,... | collective-permute-start | bytes 1990664 | tf_op jit(solution)/shard_map/ppermute | solution.py:35
  35.1 10.7 %collective-permute-start.5 = (bf16[2,2,2,1,48,576]{5,4,3,2,1,0:T(8,128)(2,1)S(1)}, bf16[2,2,2,1,48,576]{5,4,3,2,1,0:T(8,128)(2,1)S(1)}, u32[]{:S(2)}, u32[]{:S(2)}) collective-permute-start(bf16[2,2,2,1,48,576]{5,4,3,2,1,0:T(8,128)(2,1)S(1)} %maximum_select_fusion.11), channel_id=1, source_target_pairs={{0,2},{2,0},{4,6},{6,4},{8,10},{10,8},{12,14},{14,12},{16,18},{18,... | collective-permute-start | bytes 1327112 | tf_op jit(solution)/shard_map/ppermute | solution.py:35
  36.6 11.4 %collective-permute-start.3 = (bf16[2,2,1,2,49,576]{5,3,4,2,1,0:T(2,128)(2,1)S(1)}, bf16[2,2,1,2,49,576]{5,3,4,2,1,0:T(2,128)(2,1)S(1)}, u32[]{:S(2)}, u32[]{:S(2)}) collective-permute-start(bf16[2,2,1,2,49,576]{5,3,4,2,1,0:T(2,128)(2,1)S(1)} %copy.72), channel_id=1, source_target_pairs={{0,4},{2,6},{4,0},{6,2},{8,12},{10,14},{12,8},{14,10},{16,20},{18,... | collective-permute-start | bytes 1354760 | tf_op jit(solution)/shard_map/ppermute | solution.py:35
  51.1 18.1 %collective-permute-start.8 = (bf16[2,2,1,1,48,1920]{5,4,3,2,1,0:T(8,128)(2,1)S(1)}, bf16[2,2,1,1,48,1920]{5,4,3,2,1,0:T(8,128)(2,1)S(1)}, u32[]{:S(2)}, u32[]{:S(2)}) collective-permute-start(bf16[2,2,1,1,48,1920]{5,4,3,2,1,0:T(8,128)(2,1)S(1)} %slice.238), channel_id=1, source_target_pairs={{0,4},{2,6},{4,0},{6,2},{8,12},{10,14},{12,8},{14,10},{16,20},{18,... | collective-permute-start | bytes 2211848 | tf_op jit(solution)/shard_map/ppermute | solution.py:35
  52.7 15.8 %collective-permute-start.9 = (bf16[2,2,1,1,48,1536]{5,4,3,2,1,0:T(8,128)(2,1)S(1)}, bf16[2,2,1,1,48,1536]{5,4,3,2,1,0:T(8,128)(2,1)S(1)}, u32[]{:S(2)}, u32[]{:S(2)}) collective-permute-start(bf16[2,2,1,1,48,1536]{5,4,3,2,1,0:T(8,128)(2,1)S(1)} %slice.239), channel_id=1, source_target_pairs={{0,2},{2,0},{4,6},{6,4},{8,10},{10,8},{12,14},{14,12},{16,18},{18,... | collective-permute-start | bytes 1769480 | tf_op jit(solution)/shard_map/ppermute | solution.py:35
  68.5 118.7 %copy-start.9 = (f32[6,128,128]{2,1,0:T(8,128)}, f32[6,128,128]{2,1,0:T(8,128)S(1)}, u32[]{:S(2)}) copy-start(f32[6,128,128]{2,1,0:T(8,128)S(1)} %get-tuple-element.109.middle_ref) | copy-start | bytes 1179652
  68.5 118.6 %copy-start.11 = (f32[6,128,64]{2,1,0:T(8,128)}, f32[6,128,64]{2,1,0:T(8,128)S(1)}, u32[]{:S(2)}) copy-start(f32[6,128,64]{2,1,0:T(8,128)S(1)} %get-tuple-element.110.values_ref) | copy-start | bytes 589828
  68.7 25.1 %collective-permute-start.10 = (bf16[2,2,1,2,48,1536]{5,4,3,2,1,0:T(8,128)(2,1)S(1)}, bf16[2,2,1,2,48,1536]{5,4,3,2,1,0:T(8,128)(2,1)S(1)}, u32[]{:S(2)}, u32[]{:S(2)}) collective-permute-start(bf16[2,2,1,2,48,1536]{5,4,3,2,1,0:T(8,128)(2,1)S(1)} %maximum_select_fusion.4), channel_id=1, source_target_pairs={{0,4},{2,6},{4,0},{6,2},{8,12},{10,14},{12,8},{14,10},{16,20},{18,... | collective-permute-start | bytes 3538952 | tf_op jit(solution)/shard_map/ppermute | solution.py:35
  69.9 31.4 %collective-permute-start.11 = (bf16[2,2,2,1,48,1920]{5,4,3,2,1,0:T(8,128)(2,1)S(1)}, bf16[2,2,2,1,48,1920]{5,4,3,2,1,0:T(8,128)(2,1)S(1)}, u32[]{:S(2)}, u32[]{:S(2)}) collective-permute-start(bf16[2,2,2,1,48,1920]{5,4,3,2,1,0:T(8,128)(2,1)S(1)} %maximum_select_fusion.2), channel_id=1, source_target_pairs={{0,2},{2,0},{4,6},{6,4},{8,10},{10,8},{12,14},{14,12},{16,18},{18,... | collective-permute-start | bytes 4423688 | tf_op jit(solution)/shard_map/ppermute | solution.py:35
  88.9 98.2 %copy-start.13 = (f32[6,128,64]{2,1,0:T(8,128)}, f32[6,128,64]{2,1,0:T(8,128)S(1)}, u32[]{:S(2)}) copy-start(f32[6,128,64]{2,1,0:T(8,128)S(1)} %get-tuple-element.131.weighted_ref) | copy-start | bytes 589828
  107.8 4.9 %collective-permute-start.12 = (bf16[1536,768]{1,0:T(8,128)(2,1)}, bf16[1536,768]{1,0:T(8,128)(2,1)}, u32[]{:S(2)}, u32[]{:S(2)}) collective-permute-start(bf16[1536,768]{1,0:T(8,128)(2,1)} %shard_map.435.own_ref), channel_id=1, source_target_pairs={{0,1},{1,0},{2,3},{3,2},{4,5},{5,4},{6,7},{7,6},{8,9},{9,8},{10,11... | collective-permute-start | bytes 7077896 | tf_op jit(solution)/shard_map/ppermute | solution.py:35
  128.1 4.8 %collective-permute-start.13 = (bf16[1536,768]{1,0:T(8,128)(2,1)}, bf16[1536,768]{1,0:T(8,128)(2,1)S(1)}, u32[]{:S(2)}, u32[]{:S(2)}) collective-permute-start(bf16[1536,768]{1,0:T(8,128)(2,1)} %get-tuple-element.114.own_ref), channel_id=1, source_target_pairs={{0,1},{1,0},{2,3},{3,2},{4,5},{5,4},{6,7},{7,6},{8,9},{9,8},{10,11... | collective-permute-start | bytes 7077896 | tf_op jit(solution)/shard_map/ppermute | solution.py:35
  166.3 7.3 %collective-permute-start.14 = (bf16[1536,768]{1,0:T(8,128)(2,1)}, bf16[1536,768]{1,0:T(8,128)(2,1)}, u32[]{:S(2)}, u32[]{:S(2)}) collective-permute-start(bf16[1536,768]{1,0:T(8,128)(2,1)} %get-tuple-element.118.own_ref), channel_id=1, source_target_pairs={{0,1},{1,0},{2,3},{3,2},{4,5},{5,4},{6,7},{7,6},{8,9},{9,8},{10,11... | collective-permute-start | bytes 7077896 | tf_op jit(solution)/shard_map/ppermute | solution.py:35
  170.6 35.2 %collective-permute-start.16 = (bf16[2,2,2,1,48,1536]{5,4,3,2,1,0:T(8,128)(2,1)}, bf16[2,2,2,1,48,1536]{5,4,3,2,1,0:T(8,128)(2,1)S(1)}, u32[]{:S(2)}, u32[]{:S(2)}) collective-permute-start(bf16[2,2,2,1,48,1536]{5,4,3,2,1,0:T(8,128)(2,1)} %constant_dynamic-slice_fusion.3), channel_id=1, source_target_pairs={{0,2},{2,0},{4,6},{6,4},{8,10},{10,8},{12,14},{14,12},{16,18},{18,... | collective-permute-start | bytes 3538952 | tf_op jit(solution)/shard_map/ppermute | solution.py:35
  172.7 40.9 %collective-permute-start.15 = (bf16[2,2,1,2,48,1536]{5,4,3,2,1,0:T(8,128)(2,1)}, bf16[2,2,1,2,48,1536]{5,4,3,2,1,0:T(8,128)(2,1)}, u32[]{:S(2)}, u32[]{:S(2)}) collective-permute-start(bf16[2,2,1,2,48,1536]{5,4,3,2,1,0:T(8,128)(2,1)} %constant_dynamic-slice_fusion.4), channel_id=1, source_target_pairs={{0,4},{2,6},{4,0},{6,2},{8,12},{10,14},{12,8},{14,10},{16,20},{18,... | collective-permute-start | bytes 3538952 | tf_op jit(solution)/shard_map/ppermute | solution.py:35
  173.7 8.5 %copy-start.4 = (bf16[384,1536]{1,0:T(8,128)(2,1)S(1)}, bf16[384,1536]{1,0:T(8,128)(2,1)}, u32[]{:S(2)}) copy-start(bf16[384,1536]{1,0:T(8,128)(2,1)} %copy-done.3) | copy-start | bytes 3538948
  186.1 37.1 %collective-permute-start.17 = (bf16[2,2,2,1,48,384]{5,4,3,2,1,0:T(8,128)(2,1)}, bf16[2,2,2,1,48,384]{5,4,3,2,1,0:T(8,128)(2,1)}, u32[]{:S(2)}, u32[]{:S(2)}) collective-permute-start(bf16[2,2,2,1,48,384]{5,4,3,2,1,0:T(8,128)(2,1)} %constant_dynamic-slice_fusion.2), channel_id=1, source_target_pairs={{0,2},{2,0},{4,6},{6,4},{8,10},{10,8},{12,14},{14,12},{16,18},{18,... | collective-permute-start | bytes 884744 | tf_op jit(solution)/shard_map/ppermute | solution.py:35
  187.2 18.5 %copy-start.39 = (f32[8,768]{1,0:T(8,128)S(1)}, f32[8,768]{1,0:T(8,128)}, u32[]{:S(2)}) copy-start(f32[8,768]{1,0:T(8,128)} %get-tuple-element.139) | copy-start | bytes 73732
  220.2 31.8 %collective-permute-start.21 = (bf16[2,2,1,2,48,576]{5,4,3,2,1,0:T(8,128)(2,1)}, bf16[2,2,1,2,48,576]{5,4,3,2,1,0:T(8,128)(2,1)}, u32[]{:S(2)}, u32[]{:S(2)}) collective-permute-start(bf16[2,2,1,2,48,576]{5,4,3,2,1,0:T(8,128)(2,1)} %constant_dynamic-slice_fusion.1), channel_id=1, source_target_pairs={{0,4},{2,6},{4,0},{6,2},{8,12},{10,14},{12,8},{14,10},{16,20},{18,... | collective-permute-start | bytes 1327112 | tf_op jit(solution)/shard_map/ppermute | solution.py:35
  221.3 32.9 %collective-permute-start.18 = (bf16[2,2,1,1,48,1536]{5,4,3,2,1,0:T(8,128)(2,1)}, bf16[2,2,1,1,48,1536]{5,4,3,2,1,0:T(8,128)(2,1)}, u32[]{:S(2)}, u32[]{:S(2)}) collective-permute-start(bf16[2,2,1,1,48,1536]{5,4,3,2,1,0:T(8,128)(2,1)} %dynamic-slice_convert_fusion), channel_id=1, source_target_pairs={{0,4},{2,6},{4,0},{6,2},{8,12},{10,14},{12,8},{14,10},{16,20},{18,... | collective-permute-start | bytes 1769480 | tf_op jit(solution)/shard_map/ppermute | solution.py:35
  222.2 33.5 %collective-permute-start.19 = (bf16[2,2,1,1,48,1536]{5,4,3,2,1,0:T(8,128)(2,1)}, bf16[2,2,1,1,48,1536]{5,4,3,2,1,0:T(8,128)(2,1)}, u32[]{:S(2)}, u32[]{:S(2)}) collective-permute-start(bf16[2,2,1,1,48,1536]{5,4,3,2,1,0:T(8,128)(2,1)} %dynamic-slice_convert_fusion.1), channel_id=1, source_target_pairs={{0,2},{2,0},{4,6},{6,4},{8,10},{10,8},{12,14},{14,12},{16,18},{18,... | collective-permute-start | bytes 1769480 | tf_op jit(solution)/shard_map/ppermute | solution.py:35
  224.4 17.5 %copy-start.26 = (f32[2,2,2,1,48,384]{5,4,3,2,1,0:T(8,128)}, f32[2,2,2,1,48,384]{5,4,3,2,1,0:T(8,128)S(1)}, u32[]{:S(2)}) copy-start(f32[2,2,2,1,48,384]{5,4,3,2,1,0:T(8,128)S(1)} %convert_add_fusion.9) | copy-start | bytes 1769476
  242.0 11.1 %collective-permute-start.20 = (bf16[2,2,1,1,48,384]{5,4,3,2,1,0:T(8,128)(2,1)S(1)}, bf16[2,2,1,1,48,384]{5,4,3,2,1,0:T(8,128)(2,1)S(1)}, u32[]{:S(2)}, u32[]{:S(2)}) collective-permute-start(bf16[2,2,1,1,48,384]{5,4,3,2,1,0:T(8,128)(2,1)S(1)} %dynamic-slice_convert_fusion.8), channel_id=1, source_target_pairs={{0,4},{2,6},{4,0},{6,2},{8,12},{10,14},{12,8},{14,10},{16,20},{18,... | collective-permute-start | bytes 442376 | tf_op jit(solution)/shard_map/ppermute | solution.py:35
  250.8 16.1 %collective-permute-start.26 = (bf16[2,2,2,1,50,576]{5,2,4,3,1,0:T(2,128)(2,1)S(1)}, bf16[2,2,2,1,50,576]{5,2,4,3,1,0:T(2,128)(2,1)S(1)}, u32[]{:S(2)}, u32[]{:S(2)}) collective-permute-start(bf16[2,2,2,1,50,576]{5,2,4,3,1,0:T(2,128)(2,1)S(1)} %copy.81), channel_id=1, source_target_pairs={{0,2},{2,0},{4,6},{6,4},{8,10},{10,8},{12,14},{14,12},{16,18},{18,... | collective-permute-start | bytes 1382408 | tf_op jit(solution)/shard_map/ppermute | solution.py:35
  253.2 15.0 %collective-permute-start.25 = (bf16[2,2,1,1,48,576]{5,4,3,2,1,0:T(8,128)(2,1)S(1)}, bf16[2,2,1,1,48,576]{5,4,3,2,1,0:T(8,128)(2,1)S(1)}, u32[]{:S(2)}, u32[]{:S(2)}) collective-permute-start(bf16[2,2,1,1,48,576]{5,4,3,2,1,0:T(8,128)(2,1)S(1)} %dynamic-slice_convert_fusion.5), channel_id=1, source_target_pairs={{0,2},{2,0},{4,6},{6,4},{8,10},{10,8},{12,14},{14,12},{16,18},{18,... | collective-permute-start | bytes 663560 | tf_op jit(solution)/shard_map/ppermute | solution.py:35
  257.4 19.2 %collective-permute-start.23 = (bf16[2,1,1,1,48,3456]{5,4,3,2,1,0:T(8,128)(2,1)S(1)}, bf16[2,1,1,1,48,3456]{5,4,3,2,1,0:T(8,128)(2,1)S(1)}, u32[]{:S(2)}, u32[]{:S(2)}) collective-permute-start(bf16[2,1,1,1,48,3456]{5,4,3,2,1,0:T(8,128)(2,1)S(1)} %pad_maximum_fusion.1), channel_id=1, source_target_pairs={{0,8},{2,10},{4,12},{6,14},{8,0},{10,2},{12,4},{14,6},{16,24},{18,... | collective-permute-start | bytes 1990664 | tf_op jit(solution)/shard_map/ppermute | solution.py:35
  266.9 13.5 %collective-permute-start.22 = (bf16[1536,768]{1,0:T(8,128)(2,1)}, bf16[1536,768]{1,0:T(8,128)(2,1)S(1)}, u32[]{:S(2)}, u32[]{:S(2)}) collective-permute-start(bf16[1536,768]{1,0:T(8,128)(2,1)} %shard_map.443), channel_id=1, source_target_pairs={{0,1},{1,0},{2,3},{3,2},{4,5},{5,4},{6,7},{7,6},{8,9},{9,8},{10,11... | collective-permute-start | bytes 7077896 | tf_op jit(solution)/shard_map/ppermute | solution.py:35
  267.1 9.3 %collective-permute-start.27 = (bf16[2,2,1,1,50,576]{5,4,3,2,1,0:T(8,128)(2,1)S(1)}, bf16[2,2,1,1,50,576]{5,4,3,2,1,0:T(8,128)(2,1)S(1)}, u32[]{:S(2)}, u32[]{:S(2)}) collective-permute-start(bf16[2,2,1,1,50,576]{5,4,3,2,1,0:T(8,128)(2,1)S(1)} %dynamic-slice_convert_fusion.4), channel_id=1, source_target_pairs={{0,4},{2,6},{4,0},{6,2},{8,12},{10,14},{12,8},{14,10},{16,20},{18,... | collective-permute-start | bytes 691208 | tf_op jit(solution)/shard_map/ppermute | solution.py:35
  276.5 12.7 %collective-permute-start.28 = (bf16[2,1,1,1,98,576]{5,4,3,2,1,0:T(8,128)(2,1)S(1)}, bf16[2,1,1,1,98,576]{5,4,3,2,1,0:T(8,128)(2,1)S(1)}, u32[]{:S(2)}, u32[]{:S(2)}) collective-permute-start(bf16[2,1,1,1,98,576]{5,4,3,2,1,0:T(8,128)(2,1)S(1)} %pad_maximum_fusion.4), channel_id=1, source_target_pairs={{0,8},{2,10},{4,12},{6,14},{8,0},{10,2},{12,4},{14,6},{16,24},{18,... | collective-permute-start | bytes 677384 | tf_op jit(solution)/shard_map/ppermute | solution.py:35
  277.4 21.6 %collective-permute-start.24 = (bf16[1,1,1,1,48,3456]{5,4,3,2,1,0:T(8,128)(2,1)S(1)}, bf16[1,1,1,1,48,3456]{5,4,3,2,1,0:T(8,128)(2,1)S(1)}, u32[]{:S(2)}, u32[]{:S(2)}) collective-permute-start(bf16[1,1,1,1,48,3456]{5,4,3,2,1,0:T(8,128)(2,1)S(1)} %pad_maximum_fusion.3), channel_id=1, source_target_pairs={{0,16},{2,18},{4,20},{6,22},{8,24},{10,26},{12,28},{14,30},{16,0},... | collective-permute-start | bytes 995336 | tf_op jit(solution)/shard_map/ppermute | solution.py:35
  289.3 11.4 %copy-start.28 = (f32[2,1,1,1,50,576]{5,4,3,2,1,0:T(8,128)}, f32[2,1,1,1,50,576]{5,4,3,2,1,0:T(8,128)S(1)}, u32[]{:S(2)}) copy-start(f32[2,1,1,1,50,576]{5,4,3,2,1,0:T(8,128)S(1)} %convert_add_fusion.13) | copy-start | bytes 691204
  289.3 11.4 %copy-start.29 = (f32[2,1,1,1,48,576]{5,4,3,2,1,0:T(8,128)}, f32[2,1,1,1,48,576]{5,4,3,2,1,0:T(8,128)S(1)}, u32[]{:S(2)}) copy-start(f32[2,1,1,1,48,576]{5,4,3,2,1,0:T(8,128)S(1)} %convert_add_fusion.14) | copy-start | bytes 663556
  289.4 11.3 %collective-permute-start.29 = (bf16[1,1,1,1,98,576]{5,4,3,2,1,0:T(8,128)(2,1)S(1)}, bf16[1,1,1,1,98,576]{5,4,3,2,1,0:T(8,128)(2,1)S(1)}, u32[]{:S(2)}, u32[]{:S(2)}) collective-permute-start(bf16[1,1,1,1,98,576]{5,4,3,2,1,0:T(8,128)(2,1)S(1)} %pad_maximum_fusion.6), channel_id=1, source_target_pairs={{0,16},{2,18},{4,20},{6,22},{8,24},{10,26},{12,28},{14,30},{16,0},... | collective-permute-start | bytes 338696 | tf_op jit(solution)/shard_map/ppermute | solution.py:35
  303.9 3.8 %collective-permute-start.30 = (f32[1,384]{1,0:T(1,128)}, f32[1,384]{1,0:T(1,128)S(1)}, u32[]{:S(2)}, u32[]{:S(2)}) collective-permute-start(f32[1,384]{1,0:T(1,128)} %get-tuple-element.152), channel_id=1, source_target_pairs={{0,2},{2,0},{4,6},{6,4},{8,10},{10,8},{12,14},{14,12},{16,18},{18,... | collective-permute-start | bytes 4616 | tf_op jit(solution)/shard_map/ppermute | solution.py:35
  304.8 3.8 %collective-permute-start.31 = (f32[1,384]{1,0:T(1,128)}, f32[1,384]{1,0:T(1,128)S(1)}, u32[]{:S(2)}, u32[]{:S(2)}) collective-permute-start(f32[1,384]{1,0:T(1,128)} %get-tuple-element.152), channel_id=1, source_target_pairs={{0,4},{2,6},{4,0},{6,2},{8,12},{10,14},{12,8},{14,10},{16,20},{18,... | collective-permute-start | bytes 4616 | tf_op jit(solution)/shard_map/ppermute | solution.py:141
  305.7 4.7 %collective-permute-start.32 = (f32[1,384]{1,0:T(1,128)}, f32[1,384]{1,0:T(1,128)S(1)}, u32[]{:S(2)}, u32[]{:S(2)}) collective-permute-start(f32[1,384]{1,0:T(1,128)} %get-tuple-element.152), channel_id=1, source_target_pairs={{0,6},{2,4},{4,2},{6,0},{8,14},{10,12},{12,10},{14,8},{16,22},{18,... | collective-permute-start | bytes 4616 | tf_op jit(solution)/shard_map/ppermute | solution.py:141
  311.1 4.4 %collective-permute-start.33 = (f32[1,384]{1,0:T(1,128)S(1)}, f32[1,384]{1,0:T(1,128)S(1)}, u32[]{:S(2)}, u32[]{:S(2)}) collective-permute-start(f32[1,384]{1,0:T(1,128)S(1)} %add_add_fusion.1), channel_id=1, source_target_pairs={{0,8},{2,10},{4,12},{6,14},{8,0},{10,2},{12,4},{14,6},{16,24},{18,... | collective-permute-start | bytes 4616 | tf_op jit(solution)/shard_map/ppermute | solution.py:35
  311.1 4.5 %collective-permute-start.34 = (f32[1,384]{1,0:T(1,128)S(1)}, f32[1,384]{1,0:T(1,128)S(1)}, u32[]{:S(2)}, u32[]{:S(2)}) collective-permute-start(f32[1,384]{1,0:T(1,128)S(1)} %add_add_fusion.1), channel_id=1, source_target_pairs={{0,16},{2,18},{4,20},{6,22},{8,24},{10,26},{12,28},{14,30},{16,0},... | collective-permute-start | bytes 4616 | tf_op jit(solution)/shard_map/ppermute | solution.py:141
  314.1 5.4 %collective-permute-start.35 = (f32[1,384]{1,0:T(1,128)S(1)}, f32[1,384]{1,0:T(1,128)S(1)}, u32[]{:S(2)}, u32[]{:S(2)}) collective-permute-start(f32[1,384]{1,0:T(1,128)S(1)} %add_add_fusion.1), channel_id=1, source_target_pairs={{0,24},{2,26},{4,28},{6,30},{8,16},{10,18},{12,20},{14,22},{16,8},... | collective-permute-start | bytes 4616 | tf_op jit(solution)/shard_map/ppermute | solution.py:141
  319.4 1.2 collective-permute-start.36
  (33 other events, 122.6 us)
